TPU v7x, 32 devices: a whole 2x2x4 slice. The times are simulated.
32 devices in a mesh: dp: 16 (over z, y, x), mp: 2 (over core).
Axes of the slice: x: 2, y: 2, z: 4, core: 2. Of those that a mesh axis runs over, the one named last changes fastest.
Arguments:
- hidden_in: bfloat16 [16384, 2048], P(('dp', 'mp')), may hold values from -6 to 6
- segments: int32 [16384], P('dp'), may hold values from -1 to 16, as said below
- norm_gain: float32 [2048], replicated, may hold values from 0.25 to 1.75
- w_zx: bfloat16 [2048, 2, 4096], P('dp', None, 'mp'), may hold values from -0.125 to 0.125
- w_dt: bfloat16 [2048, 64], P('dp', 'mp'), may hold values from -0.125 to 0.125
- w_bc: bfloat16 [2048, 256], P('dp'), may hold values from -0.125 to 0.125
- conv_x: float32 [4, 4096], P(None, 'mp'), may hold values from -3 to 3
- conv_x_bias: float32 [4096], P('mp'), may hold values from -3 to 3
- conv_bc: float32 [4, 256], replicated, may hold values from -3 to 3
- conv_bc_bias: float32 [256], replicated, may hold values from -3 to 3
- dt_bias: float32 [64], P('mp'), may hold values from -6.5 to -2.5
- a_log: float32 [64], P('mp'), may hold values from 0 to 2.77
- d_skip: float32 [64], P('mp'), may hold values from 0.5 to 1.5
- gated_gain: float32 [4096], P('mp'), may hold values from 0.25 to 1.75
- w_out: bfloat16 [4096, 2048], P('mp', 'dp'), may hold values from -0.09375 to 0.09375
- cotangent: bfloat16 [16384, 2048], P(('dp', 'mp')), may hold values from -6 to 6
Outputs:
- residual_out: bfloat16 [16384, 2048], P(('dp', 'mp'))
- input_grad: float32 [16384, 2048], P(('dp', 'mp'))
- grad_norm_gain: float32 [2048], replicated
- grad_w_zx: float32 [2048, 2, 4096], P('dp', None, 'mp')
- grad_w_dt: float32 [2048, 64], P('dp', 'mp')
- grad_w_bc: float32 [2048, 256], P('dp')
- grad_conv_x: float32 [4, 4096], P(None, 'mp')
- grad_conv_x_bias: float32 [4096], P('mp')
- grad_conv_bc: float32 [4, 256], replicated
- grad_conv_bc_bias: float32 [256], replicated
- grad_dt_bias: float32 [64], P('mp')
- grad_a_log: float32 [64], P('mp')
- grad_d_skip: float32 [64], P('mp')
- grad_gated_gain: float32 [4096], P('mp')
- grad_w_out: float32 [4096, 2048], P('mp', 'dp')
- rms_residual: float32 [], replicated
- rms_mixer: float32 [], replicated
Inputs may be any that keep to these rules, and one draw needn't show every extreme that they name: `segments`: per token, the number of its document within its sequence of 1024 tokens, counted from 0 in order, or -1 for padding at the sequence's end. Documents hold 60 to 800 tokens, except the last of a sequence, which may be cut short. In every sequence one document holds tokens on both sides of its middle.
All inputs are finite; a program needn't handle non-finite values.
Results may differ from a plain program's by a relative error of at most 0.0064.
The roundings to bfloat16 on the way count: a program that leaves them out, or rounds other values in their place, can miss the bound.
Values may be sent and summed in bfloat16 or wider, within the bound.
A program may use at most 320 MiB of HBM per device.

v0:
```python
import jax
import jax.numpy as jnp
from jax import lax
from jax.sharding import PartitionSpec as P

BLOCK = 256


EPSILON = 1e-05
HIGH = lax.Precision.HIGHEST


def segment_conv(inputs, taps, bias, segment_ids):
    reach = taps.shape[0]
    result = bias[None, :] + taps[reach - 1][None, :] * inputs
    for offset in range(1, reach):
        moved = jnp.concatenate(
            [jnp.zeros((offset, inputs.shape[1]), inputs.dtype), inputs[:-offset]], axis=0
        )
        earlier = jnp.concatenate([jnp.full((offset,), -2, jnp.int32), segment_ids[:-offset]])
        same_doc = (earlier == segment_ids)[:, None]
        result = result + taps[reach - 1 - offset][None, :] * jnp.where(same_doc, moved, 0.0)
    return result


def block_terms(operands):
    block_x, block_dt, block_cum, block_b, block_c, block_seg = operands
    size = block_seg.shape[0]
    causal = lax.broadcasted_iota(jnp.int32, (size, size), 0) >= lax.broadcasted_iota(
        jnp.int32, (size, size), 1
    )
    same_doc = causal & (block_seg[:, None] == block_seg[None, :])
    scores = jnp.dot(block_c, block_b.T, precision=HIGH)
    spread = block_cum[:, None, :] - block_cum[None, :, :]
    decay = jnp.exp(jnp.where(same_doc[:, :, None], spread, -jnp.inf))
    mixing = scores[:, :, None] * decay * block_dt[None, :, :]
    within = jnp.einsum("tsh,shp->thp", mixing, block_x, precision=HIGH)
    last_keep = (block_seg == block_seg[-1]).astype(block_cum.dtype)[:, None]
    tail_weight = jnp.exp(block_cum[-1][None, :] - block_cum) * block_dt * last_keep
    weighted_x = tail_weight[:, :, None] * block_x
    state = jnp.einsum("shp,sn->hpn", weighted_x, block_b, precision=HIGH)
    return (within, state)


def blocked_scan(values, step_sizes, decay_rates, b_rows, c_rows, segment_ids):
    length, head_count, width = values.shape
    nstate = b_rows.shape[1]
    number = length // BLOCK
    x_blocks = values.reshape(number, BLOCK, head_count, width)
    dt_blocks = step_sizes.reshape(number, BLOCK, head_count)
    cum_blocks = jnp.cumsum(
        (step_sizes * decay_rates[None, :]).reshape(number, BLOCK, head_count), axis=1
    )
    b_blocks = b_rows.reshape(number, BLOCK, nstate)
    c_blocks = c_rows.reshape(number, BLOCK, nstate)
    seg_blocks = segment_ids.reshape(number, BLOCK)
    before = jnp.concatenate([jnp.full((1,), -2, jnp.int32), seg_blocks[:-1, -1]])
    within, states = lax.map(
        jax.checkpoint(block_terms),
        (x_blocks, dt_blocks, cum_blocks, b_blocks, c_blocks, seg_blocks),
    )

    def carry_step(state, operands):
        block_state, block_cum, block_seg, prior = operands
        keep_flag = (block_seg[-1] == prior).astype(state.dtype)
        after = state * (jnp.exp(block_cum[-1]) * keep_flag)[:, None, None] + block_state
        return (after, state)

    start_state = jnp.zeros((head_count, width, nstate), values.dtype)
    _, entering = lax.scan(carry_step, start_state, (states, cum_blocks, seg_blocks, before))
    linked = (seg_blocks == before[:, None]).astype(values.dtype)[:, :, None] * jnp.exp(cum_blocks)
    across = jnp.einsum("ctn,chpn->cthp", c_blocks, entering, precision=HIGH) * linked[..., None]
    return (within + across).reshape(length, head_count, width)


def conv_states(proj_bc, taps, tap_bias, segment_ids):
    return jax.nn.silu(segment_conv(proj_bc, taps, tap_bias, segment_ids))


def head_mixer(
    proj_zx, state_inputs, proj_dt, taps, tap_bias, step_bias, rate_logs, skip_gain, segment_ids
):
    inner_width = taps.shape[1]
    head_count = step_bias.shape[0]
    length = proj_zx.shape[0]
    gate_part = proj_zx[:, :inner_width]
    values = proj_zx[:, inner_width:]
    conv_values = jax.nn.silu(segment_conv(values, taps, tap_bias, segment_ids))
    conv_values = conv_values.reshape(length, head_count, inner_width // head_count)
    nstate = state_inputs.shape[1] // 2
    step_sizes = jax.nn.softplus(proj_dt + step_bias)
    decay_rates = -jnp.exp(rate_logs)
    scanned = blocked_scan(
        conv_values,
        step_sizes,
        decay_rates,
        state_inputs[:, :nstate],
        state_inputs[:, nstate:],
        segment_ids,
    )
    scanned = scanned + skip_gain[None, :, None] * conv_values
    return scanned.reshape(length, inner_width) * jax.nn.silu(gate_part)


def fetch_shards(w_zx, w_dt, w_bc, w_out):
    return (
        lax.all_gather(w_zx, "dp", axis=0, tiled=True),
        lax.all_gather(w_dt, "dp", axis=0, tiled=True),
        lax.all_gather(w_bc, "dp", axis=0, tiled=True),
        lax.all_gather(w_out, "dp", axis=1, tiled=True),
    )


def local(
    hidden_in,
    segments,
    norm_gain,
    w_zx,
    w_dt,
    w_bc,
    conv_x,
    conv_x_bias,
    conv_bc,
    conv_bc_bias,
    dt_bias,
    a_log,
    d_skip,
    gated_gain,
    w_out,
    cotangent,
):
    tok_rows = hidden_in.shape[0]
    own_start = lax.axis_index("mp") * tok_rows
    inner_local = conv_x.shape[1]
    inner_total = inner_local * lax.axis_size("mp")
    inputs = hidden_in.astype(jnp.float32)
    inverse_rows = lax.rsqrt(jnp.mean(inputs * inputs, axis=-1, keepdims=True) + EPSILON)
    normed = (inputs * inverse_rows * norm_gain).astype(jnp.bfloat16)
    normed_full = lax.all_gather(normed, "mp", axis=0, tiled=True)
    zx_weight, dt_weight, bc_weight, out_weight = fetch_shards(w_zx, w_dt, w_bc, w_out)
    model_width = zx_weight.shape[0]
    zx_flat = zx_weight.reshape(model_width, 2 * inner_local)
    proj_zx = jnp.dot(normed_full, zx_flat, preferred_element_type=jnp.float32)
    proj_bc = jnp.dot(normed_full, bc_weight, preferred_element_type=jnp.float32)
    proj_dt = jnp.dot(normed_full, dt_weight, preferred_element_type=jnp.float32)

    def state_part(proj_bc, taps, tap_bias):
        return conv_states(proj_bc, taps, tap_bias, segments)

    def head_part(*operands):
        return head_mixer(*operands, segments)

    state_inputs, state_back = jax.vjp(state_part, proj_bc, conv_bc, conv_bc_bias)
    gated, head_back = jax.vjp(
        head_part, proj_zx, state_inputs, proj_dt, conv_x, conv_x_bias, dt_bias, a_log, d_skip
    )
    squares = lax.psum(jnp.sum(gated * gated, axis=-1), "mp")
    inverse_gated = lax.rsqrt(squares / inner_total + EPSILON)[:, None]
    scaled = (gated * inverse_gated * gated_gain).astype(jnp.bfloat16)
    mixer_out = lax.psum_scatter(
        jnp.dot(scaled, out_weight, preferred_element_type=jnp.float32),
        "mp",
        scatter_dimension=0,
        tiled=True,
    )
    residual_out = (inputs + mixer_out).astype(jnp.bfloat16)
    usable = (lax.dynamic_slice_in_dim(segments, own_start, tok_rows, 0) >= 0).astype(jnp.float32)[
        :, None
    ]
    sum_inputs = jnp.sum(usable * inputs * inputs)
    sum_mixer = jnp.sum(usable * mixer_out * mixer_out)
    usable_count = jnp.sum(usable)
    sum_inputs, sum_mixer, usable_count = lax.psum(
        (sum_inputs, sum_mixer, usable_count), ("dp", "mp")
    )
    cot_full = lax.all_gather(cotangent, "mp", axis=0, tiled=True)
    zx_weight, dt_weight, bc_weight, out_weight = fetch_shards(w_zx, w_dt, w_bc, w_out)
    zx_flat = zx_weight.reshape(model_width, 2 * inner_local)
    d_scaled = jnp.einsum("td,cd->tc", cot_full, out_weight, preferred_element_type=jnp.float32)
    grad_out_weight = jnp.einsum("tc,td->cd", scaled, cot_full, preferred_element_type=jnp.float32)
    grad_out_weight = lax.psum_scatter(grad_out_weight, "dp", scatter_dimension=1, tiled=True)
    cross_sum = lax.psum(jnp.sum(gated * gated_gain * d_scaled, axis=-1), "mp")[:, None]
    grad_gated_gain = jnp.sum(d_scaled * gated * inverse_gated, axis=0)
    inverse_cube = inverse_gated * inverse_gated * inverse_gated
    d_gated = inverse_gated * gated_gain * d_scaled - gated * inverse_cube / inner_total * cross_sum
    d_zx, d_states, d_dt, grad_conv_x, grad_conv_x_bias, grad_dt_bias, grad_a_log, grad_d_skip = (
        head_back(d_gated)
    )
    d_states = lax.psum(d_states, "mp")
    d_bc, grad_conv_bc, grad_conv_bc_bias = state_back(d_states)
    zx_grad = d_zx.astype(jnp.bfloat16)
    dt_grad = d_dt.astype(jnp.bfloat16)
    bc_grad = d_bc.astype(jnp.bfloat16)
    first = jnp.einsum("tk,dk->td", zx_grad, zx_flat, preferred_element_type=jnp.float32)
    d_normed = lax.psum_scatter(
        first + jnp.einsum("th,dh->td", dt_grad, dt_weight, preferred_element_type=jnp.float32),
        "mp",
        scatter_dimension=0,
        tiled=True,
    )
    own_bc = lax.dynamic_slice_in_dim(bc_grad, own_start, tok_rows, 0)
    d_normed = d_normed + jnp.einsum(
        "tk,dk->td", own_bc, bc_weight, preferred_element_type=jnp.float32
    )
    all_grads = jnp.concatenate([zx_grad, dt_grad, bc_grad], axis=1)
    zx_cols = zx_grad.shape[1]
    dt_cols = dt_grad.shape[1]
    owned = lax.psum_scatter(
        jnp.einsum("tr,tk->rk", normed_full, all_grads, preferred_element_type=jnp.float32),
        "dp",
        scatter_dimension=0,
        tiled=True,
    )
    own_width = owned.shape[0]
    grad_zx_weight = owned[:, :zx_cols].reshape(own_width, 2, inner_local)
    grad_dt_weight = owned[:, zx_cols : zx_cols + dt_cols]
    grad_bc_weight = owned[:, zx_cols + dt_cols :]
    small_sums = lax.psum(
        (
            grad_conv_x,
            grad_conv_x_bias,
            grad_conv_bc,
            grad_conv_bc_bias,
            grad_dt_bias,
            grad_a_log,
            grad_d_skip,
            grad_gated_gain,
        ),
        "dp",
    )
    grad_norm_gain = jnp.sum(d_normed * inputs * inverse_rows, axis=0)
    inverse_cube_rows = inverse_rows * inverse_rows * inverse_rows
    input_grad = (
        cotangent.astype(jnp.float32)
        + inverse_rows * norm_gain * d_normed
        - inputs
        * inverse_cube_rows
        * jnp.mean(inputs * norm_gain * d_normed, axis=-1, keepdims=True)
    )
    grad_norm_gain = lax.psum(grad_norm_gain, ("dp", "mp"))
    rms_residual = jnp.sqrt(sum_inputs / (usable_count * model_width))
    rms_mixer = jnp.sqrt(sum_mixer / (usable_count * model_width))
    return (
        residual_out,
        input_grad,
        grad_norm_gain,
        grad_zx_weight,
        grad_dt_weight,
        grad_bc_weight,
        small_sums[0],
        small_sums[1],
        small_sums[2],
        small_sums[3],
        small_sums[4],
        small_sums[5],
        small_sums[6],
        small_sums[7],
        grad_out_weight,
        rms_residual,
        rms_mixer,
    )


def solution(mesh):
    in_specs = (
        P(("dp", "mp"), None),
        P("dp"),
        P(),
        P("dp", None, "mp"),
        P("dp", "mp"),
        P("dp", None),
        P(None, "mp"),
        P("mp"),
        P(),
        P(),
        P("mp"),
        P("mp"),
        P("mp"),
        P("mp"),
        P("mp", "dp"),
        P(("dp", "mp"), None),
    )
    out_specs = (
        P(("dp", "mp"), None),
        P(("dp", "mp"), None),
        P(),
        P("dp", None, "mp"),
        P("dp", "mp"),
        P("dp", None),
        P(None, "mp"),
        P("mp"),
        P(),
        P(),
        P("mp"),
        P("mp"),
        P("mp"),
        P("mp"),
        P("mp", "dp"),
        P(),
        P(),
    )
    return jax.shard_map(local, mesh=mesh, in_specs=in_specs, out_specs=out_specs, check_vma=False)
```

profile of v0, /device:TPU:0, one launch (start us, length us, event | category | flops | bytes accessed | tf_op | source)
XLA Modules:
  0.0 2166.9 jit_solution(15688621336362691921)
XLA Ops:
  19.4 43.2 %all_gather.25 = bf16[2048,32]{0,1:T(8,128)(2,1)S(1)} all-gather(bf16[128,32]{0,1:T(8,128)(2,1)S(1)} %copy-done.62), channel_id=1, replica_groups=mesh['dp'=16,'mp'=2] {'dp'}, dimensions={0}, use_global_device_ids=true | all-gather | bytes 139264 | tf_op jit(solution)/shard_map/all_gather | solution.py:108
  73.5 15.7 all-gather.10.cloned.1.call-done
  96.5 186.0 %all-gather.8.cloned.1.call-done = bf16[2048,2,2048]{2,1,0:T(2,128)(2,1)} async-done(((bf16[128,2,2048]{2,1,0:T(2,128)(2,1)}), bf16[2048,2,2048]{2,1,0:T(2,128)(2,1)}) %all-gather.8.cloned.1.call-update) | async-done | bytes 16777232 | tf_op jit(solution)/shard_map/all_gather | solution.py:107
  282.5 17.9 copy.258
  300.4 20.3 fusion.151
  334.3 20.8 fusion.89
  355.2 14.4 reshape.485
  369.6 14.4 copy.164
  390.9 87.4 %while.75 = (s32[]{:T(128)}, f32[4,256,32,64]{1,3,2,0:T(8,128)}, f32[4,32,64,128]{3,2,1,0:T(8,128)}, f32[4,256,32,64]{1,3,2,0:T(8,128)}, f32[4,256,128]{2,1,0:T(...) while((s32[]{:T(128)}, f32[4,256,32,64]{1,3,2,0:T(8,128)}, ...), condition=%wide.region_4.5_spmd.clone, body=%wide.region_3.4_spmd.clone.sunk | while | flops 2525716992 | bytes 8792109 | solution.py:58
  480.7 26.0 %while.76 = (s32[]{:T(128)}, f32[32,64,128]{2,1,0:T(8,128)S(1)}, f32[4,32,64,128]{3,2,1,0:T(8,128)}, f32[4,32]{1,0:T(4,128)S(1)}, f32[4]{0:T(128)S(1)}, /*index=...) while((s32[]{:T(128)}, f32[32,64,128]{2,1,0:T(8,128)S(1)}, ...), condition=%wide.region_6.7_spmd.clone, body=%wide.region_5.6_spmd.clone.sunk | while | flops 1048646 | bytes 5244906 | solution.py:70
  506.7 13.5 multiply_add_fusion.2
  520.2 16.2 copy.192
  536.4 15.1 reshape.483
  567.4 16.9 multiply_reduce_fusion.2
  586.8 21.6 multiply_reduce_fusion.3
  608.4 14.4 reshape.486
  622.8 14.2 copy.176
  650.6 17.2 while.77
  675.1 176.2 %while.74 = (s32[]{:T(128)}, f32[4,256,32,64]{1,3,2,0:T(8,128)}, f32[4,256,32]{1,2,0:T(8,128)}, f32[4,256,32]{1,2,0:T(8,128)}, f32[4,256,128]{2,1,0:T(8,128)}, /...) while((s32[]{:T(128)}, f32[4,256,32,64]{1,3,2,0:T(8,128)}, ...), condition=%wide.region_22.23_spmd, body=%wide.region_15.22_spmd.sunk | while | flops 5172363776 | bytes 34026664 | solution.py:58
  851.3 16.4 fusion.113
  868.9 15.9 fusion.134
  905.3 16.3 copy.193
  921.6 14.9 reshape.484
  942.0 21.2 fusion.135
  999.0 22.4 %convolution_add_fusion.1 = f32[1024,2048]{1,0:T(8,128)} fusion(f32[1024,2048]{1,0:T(8,128)} %fusion.153, bf16[1024,4096]{1,0:T(8,128)(2,1)S(1)} %add_convert_fusion, bf16[2048,4096]{1,0:T(8,128)(2,1)} %bitcast.378), kind=kOutput, calls=%fused_computation.159 | convolution fusion | flops 17181966336 | bytes 41943040 | tf_op jit(solution)/shard_map/tk,dk->td/dot_general | solution.py:194
  1027.2 14.3 concatenate.46
  1041.6 26.9 %fusion.154 = f32[2048,4384]{0,1:T(8,128)} fusion(bf16[1024,2048]{1,0:T(8,128)(2,1)} %all-gather.6.cloned.1.call-done, bf16[1024,4384]{1,0:T(8,128)(2,1)} %concatenate.46), kind=kOutput, calls=%fused_computation.258 | convolution fusion | flops 18387828736 | bytes 49086464 | tf_op jit(solution)/shard_map/tr,tk->rk/dot_general | solution.py:209
  1069.1 16.2 fusion.133
  1087.0 77.5 %all-reduce.29 = (f32[4,2048]{1,0:T(4,128)}, f32[2048]{0:T(1024)}, f32[4,256]{1,0:T(4,128)}, f32[256]{0:T(256)}, f32[32]{0:T(128)}, /*index=5*/f32[32]{0:T(128)}, f32[32]{0:T(128)}, f32[2048]{0:T(1024)}) all-reduce(f32[4,2048]{1,0:T(4,128)S(1)} %pad_add_fusion.1, ...), channel_id=1, replica_groups=mesh['dp'=16,'mp'=2] {'dp'}, use_global_device_ids=true, to_apply=%region_36.37 | all-reduce | flops 13664 | bytes 109312 | tf_op jit(solution)/shard_map/psum | solution.py:218
  1172.2 46.4 %all-reduce.28 = (f32[2048]{0:T(1024)}, f32[]{:T(128)}, f32[]{:T(128)}, f32[]{:T(128)}) all-reduce(f32[2048]{0:T(1024)S(1)} %get-tuple-element.1113, f32[]{:T(128)} %get-tuple-element.1111, f32[]{:T(128)} %get-tuple-element.1089, f32[]{:T(128)} %get-tuple-element.1109), channel_id=1, replica_groups=mesh['dp'=16,'mp'=2] {'dp','mp'}, use_global_device_ids=true, to_apply=%region_30.31 | all-reduce | flops 2051 | bytes 16408 | tf_op jit(solution)/shard_map/psum | solution.py:240
  1226.8 575.9 %reduce-scatter.9.cloned.1.call-done = f32[128,4384]{0,1:T(8,128)} async-done(((f32[2048,4384]{0,1:T(8,128)}), f32[128,4384]{0,1:T(8,128)}) %reduce-scatter.9.cloned.1.call-update) | async-done | bytes 2244624 | tf_op jit(solution)/shard_map/reduce_scatter | solution.py:208
  1808.8 348.7 %reduce-scatter.11.cloned.1.call-done = f32[2048,128]{1,0:T(8,128)} async-done(((f32[2048,2048]{1,0:T(8,128)}), f32[2048,128]{1,0:T(8,128)}) %reduce-scatter.11.cloned.1.call-update) | async-done | bytes 1048592 | tf_op jit(solution)/shard_map/reduce_scatter | solution.py:181
  (480 shorter events, 483.1 us)
Async XLA Ops:
  7.3 55.5 %copy-start.74 = (f32[32]{0:T(128)S(1)}, f32[32]{0:T(128)}, u32[]{:S(2)}) copy-start(f32[32]{0:T(128)} %param.34) | copy-start | bytes 388
  7.3 55.5 %all-gather.6.cloned.1.call-start = ((), (), s32[]{:S(2)}) async-start(), calls=%async_computation.4 | async-start | bytes 6291456 | tf_op jit(solution)/shard_map/all_gather | solution.py:139
  13.5 75.8 %all-gather.10.cloned.1.call-start = ((), (), s32[]{:S(2)}) async-start(), calls=%async_computation.6 | async-start | bytes 1114112 | tf_op jit(solution)/shard_map/all_gather | solution.py:109
  14.2 268.3 %all-gather.8.cloned.1.call-start = ((), (), s32[]{:S(2)}) async-start(), calls=%async_computation.5 | async-start | bytes 17825792 | tf_op jit(solution)/shard_map/all_gather | solution.py:107
  14.9 552.4 %all-gather.14.cloned.1.call-start = ((), (), s32[]{:S(2)}) async-start(), calls=%async_computation.9 | async-start | bytes 6291456 | tf_op jit(solution)/shard_map/all_gather | solution.py:176
  15.5 551.9 %all-gather.12.cloned.1.call-start = ((), (), s32[]{:S(2)}) async-start(), calls=%async_computation.7 | async-start | bytes 8912896 | tf_op jit(solution)/shard_map/all_gather | solution.py:110
  16.1 1005.4 %all-reduce.32.cloned.1.call-start = ((), (), s32[]{:S(2)}) async-start(), calls=%async_computation.11 | async-start | bytes 2097152 | tf_op jit(solution)/shard_map/psum | solution.py:189
  16.2 76.8 %copy-start.70 = (f32[32]{0:T(128)}, f32[32]{0:T(128)S(1)}, u32[]{:S(2)}) copy-start(f32[32]{0:T(128)S(1)} %exponential_negate_fusion) | copy-start | bytes 388
  18.6 74.5 %copy-start.36 = (f32[4,256]{1,0:T(4,128)}, f32[4,256]{1,0:T(4,128)S(1)}, u32[]{:S(2)}) copy-start(f32[4,256]{1,0:T(4,128)S(1)} %compare_convert_fusion.2) | copy-start | bytes 12292
  18.6 74.5 %copy-start.51 = (f32[1,256]{1,0:T(1,128)}, f32[1,256]{1,0:T(1,128)S(1)}, u32[]{:S(2)}) copy-start(f32[1,256]{1,0:T(1,128)S(1)} %get-tuple-element.1127) | copy-start | bytes 3076
  18.6 74.5 %copy-start.53 = (f32[1,256]{1,0:T(1,128)}, f32[1,256]{1,0:T(1,128)S(1)}, u32[]{:S(2)}) copy-start(f32[1,256]{1,0:T(1,128)S(1)} %get-tuple-element.1128) | copy-start | bytes 3076
  18.6 74.5 %copy-start.55 = (f32[1,256]{1,0:T(1,128)}, f32[1,256]{1,0:T(1,128)S(1)}, u32[]{:S(2)}) copy-start(f32[1,256]{1,0:T(1,128)S(1)} %get-tuple-element.1126) | copy-start | bytes 3076
  18.6 74.5 %copy-start.57 = (f32[1,256]{1,0:T(1,128)}, f32[1,256]{1,0:T(1,128)S(1)}, u32[]{:S(2)}) copy-start(f32[1,256]{1,0:T(1,128)S(1)} %get-tuple-element.1125) | copy-start | bytes 3076
  19.4 314.6 %copy-start.26 = (f32[1,2048]{1,0:T(1,128)}, f32[1,2048]{1,0:T(1,128)S(1)}, u32[]{:S(2)}) copy-start(f32[1,2048]{1,0:T(1,128)S(1)} %get-tuple-element.1121) | copy-start | bytes 24580
  19.4 314.6 %copy-start.28 = (f32[1,2048]{1,0:T(1,128)}, f32[1,2048]{1,0:T(1,128)S(1)}, u32[]{:S(2)}) copy-start(f32[1,2048]{1,0:T(1,128)S(1)} %get-tuple-element.1122) | copy-start | bytes 24580
  19.4 314.6 %copy-start.30 = (f32[1,2048]{1,0:T(1,128)}, f32[1,2048]{1,0:T(1,128)S(1)}, u32[]{:S(2)}) copy-start(f32[1,2048]{1,0:T(1,128)S(1)} %get-tuple-element.1120) | copy-start | bytes 24580
  19.4 314.6 %copy-start.32 = (f32[1,2048]{1,0:T(1,128)}, f32[1,2048]{1,0:T(1,128)S(1)}, u32[]{:S(2)}) copy-start(f32[1,2048]{1,0:T(1,128)S(1)} %get-tuple-element.1119) | copy-start | bytes 24580
  62.7 271.4 %copy-start.38 = (pred[1024]{0:T(1024)(128)(4,1)}, pred[1024]{0:T(1024)(128)(4,1)S(1)}, u32[]{:S(2)}) copy-start(pred[1024]{0:T(1024)(128)(4,1)S(1)} %get-tuple-element.1129) | copy-start | bytes 3076
  62.7 271.4 %copy-start.40 = (pred[1024]{0:T(1024)(128)(4,1)}, pred[1024]{0:T(1024)(128)(4,1)S(1)}, u32[]{:S(2)}) copy-start(pred[1024]{0:T(1024)(128)(4,1)S(1)} %get-tuple-element.1130) | copy-start | bytes 3076
  62.7 271.4 %copy-start.42 = (pred[1024]{0:T(1024)(128)(4,1)}, pred[1024]{0:T(1024)(128)(4,1)S(1)}, u32[]{:S(2)}) copy-start(pred[1024]{0:T(1024)(128)(4,1)S(1)} %get-tuple-element.1131) | copy-start | bytes 3076
  62.7 31.3 %copy-start.68 = (f32[256]{0:T(256)S(1)}, f32[256]{0:T(256)}, u32[]{:S(2)}) copy-start(f32[256]{0:T(256)} %param.33) | copy-start | bytes 3076
  70.4 22.6 %copy-start.7 = (f32[4,32,2,128]{3,1,2,0:T(8,128)}, f32[4,32,2,128]{3,1,2,0:T(8,128)S(1)}, u32[]{:S(2)}) copy-start(f32[4,32,2,128]{3,1,2,0:T(8,128)S(1)} %reduce-window.14) | copy-start | bytes 393220
  70.7 22.4 %copy-start.34 = (f32[4,32,2]{1,2,0:T(2,128)}, f32[4,32,2]{1,2,0:T(2,128)S(1)}, u32[]{:S(2)}) copy-start(f32[4,32,2]{1,2,0:T(2,128)S(1)} %copy.162) | copy-start | bytes 3076
  71.6 565.4 %copy-start.9 = (f32[4,256,32]{1,2,0:T(8,128)}, f32[4,256,32]{1,2,0:T(8,128)S(1)}, u32[]{:S(2)}) copy-start(f32[4,256,32]{1,2,0:T(8,128)S(1)} %exponential_multiply_fusion) | copy-start | bytes 393220
  868.8 295.6 %reduce-scatter.5.cloned.1.call-start = ((), (), s32[]{:S(2)}) async-start(), calls=%async_computation.8 | async-start | bytes 12582912 | tf_op jit(solution)/shard_map/reduce_scatter | solution.py:160
  884.9 279.6 %reduce-scatter.7.cloned.1.call-start = ((), (), s32[]{:S(2)}) async-start(), calls=%async_computation.10 | async-start | bytes 12582912 | tf_op jit(solution)/shard_map/reduce_scatter | solution.py:195
  1021.5 781.2 %reduce-scatter.9.cloned.1.call-start = ((), (), s32[]{:S(2)}) async-start(), calls=%async_computation.12 | async-start | bytes 38158336 | tf_op jit(solution)/shard_map/reduce_scatter | solution.py:208
  1068.5 1089.1 %reduce-scatter.11.cloned.1.call-start = ((), (), s32[]{:S(2)}) async-start(), calls=%async_computation.13 | async-start | bytes 17825792 | tf_op jit(solution)/shard_map/reduce_scatter | solution.py:181
  1085.4 79.1 %copy-start.5 = (bf16[512,2048]{1,0:T(8,128)(2,1)S(1)}, bf16[512,2048]{1,0:T(8,128)(2,1)}, u32[]{:S(2)}) copy-start(bf16[512,2048]{1,0:T(8,128)(2,1)} %param.24) | copy-start | bytes 6291460
  1085.4 79.1 %copy-start.25 = (f32[2048]{0:T(1024)S(1)}, f32[2048]{0:T(1024)}, u32[]{:S(2)}) copy-start(f32[2048]{0:T(1024)} %param.26) | copy-start | bytes 24580
  1085.4 79.1 %copy-start.47 = (f32[512]{0:T(512)S(1)}, f32[512]{0:T(512)}, u32[]{:S(2)}) copy-start(f32[512]{0:T(512)} %copy-done.46) | copy-start | bytes 6148
  1164.5 56.2 %copy-start.64 = (f32[512]{0:T(512)S(1)}, f32[512]{0:T(512)}, u32[]{:S(2)}) copy-start(f32[512]{0:T(512)} %get-tuple-element.1132) | copy-start | bytes 6148
  (65 other events, 627.9 us)
Sparse Core Ops, SparseCore 0:
  13.6 16.3 all-gather.5
  32.7 56.4 all-gather.9
  92.0 190.4 all-gather.7
  283.9 11.8 all-gather.13
  298.3 143.5 all-gather.11
  869.0 18.0 all-reduce.31
  889.4 17.9 reduce-scatter.4
  1021.6 15.5 reduce-scatter.6
  1068.6 734.0 reduce-scatter.8
  1805.5 352.0 reduce-scatter.10
where the time goes:
time: 2190 us; the launch traced here: 2170 us
  waiting for transfers between devices  1130 us (52%)
  matrix products  374 us (17%)
  local copies, waits for them, and re-layouts  258 us (12%)
  other arithmetic  208 us (9%)
  blocking collectives  172 us (8%)
    reduce_scatter x1, waiting for transfers between devices, local(): lax.psum_scatter(jnp.einsum('tr,tk->rk', normed_full, all_grads, preferre...  576 us
    reduce_scatter x1, waiting for transfers between devices, local(): lax.psum_scatter(grad_out_weight, 'dp', scatter_dimension=1, tiled=True)  349 us
    all_gather x1, waiting for transfers between devices, fetch_shards(): lax.all_gather(w_zx, 'dp', axis=0, tiled=True)  186 us
    dot_general x12, matrix products, block_terms(): within = jnp.einsum('tsh,shp->thp', mixing, block_x, precision=HIGH)  138 us
    psum x1, blocking collectives, local(): lax.psum((grad_conv_x, grad_conv_x_bias, grad_conv_bc, grad_conv_bc_bias,...  77.5 us
    psum x1, blocking collectives, local(): grad_norm_gain = lax.psum(grad_norm_gain, ('dp', 'mp'))  46.4 us
    unnamed x154, local copies, waits for them, and re-layouts  46 us
    reshape x3, local copies, waits for them, and re-layouts, blocked_scan(): return (within + across).reshape(length, head_count, width)  45.7 us
  transfers between devices with their start and end apart: 10, of which 4 were waited for; matrix products, arithmetic and copies ran while one was open for 24% of the time, Pallas kernels for 0%

commit v1 on v0

v1 whole, which is shorter than its diff:
```python
import functools

import jax
import jax.numpy as jnp
from jax import lax
from jax.experimental import pallas as pl
from jax.experimental.pallas import tpu as pltpu
from jax.sharding import PartitionSpec as P

BLOCK = 256
LANES = 128
TILE = 256
WIDTH = 64
GROUP = TILE // WIDTH
EPSILON = 1e-05
HIGH = lax.Precision.HIGHEST
BF16 = jnp.bfloat16
F32 = jnp.float32
VMEM_LIMIT = 56 * 2**20

NN = (((1,), (0,)), ((), ()))
NT = (((1,), (1,)), ((), ()))
TN = (((0,), (0,)), ((), ()))


def dot(a, b, dims=NN, precision=None):
    return lax.dot_general(a, b, dims, precision=precision, preferred_element_type=F32)


def low_dot(a, b, dims=NN):
    return dot(a.astype(BF16), b.astype(BF16), dims)


def flip(a, axis, bit):
    size = lax.axis_size(axis)
    return lax.ppermute(a, axis, [(i, i ^ bit) for i in range(size)])


def sigmoid(q):
    return 1.0 / (1.0 + jnp.exp(-q))


def owner_block(number, dp, extent):
    y, z, x = number // (extent // 2), (number // 2) % (extent // 4), number % 2
    return jnp.bitwise_xor(dp - lax.rem(dp, 2), (y * 2) + (z * 4) + x)


def norm_kernel(place_ref, hidden_ref, cot_ref, gain_ref, normed_ref, cot_out_ref, inv_ref, *, extent):
    u = hidden_ref[...].astype(F32)
    inv = lax.rsqrt(jnp.mean(u * u, axis=-1, keepdims=True) + EPSILON)
    inv_ref[...] = inv
    for number in range(extent):
        start = pl.multiple_of(owner_block(number, place_ref[0], extent) * LANES, LANES)
        piece = hidden_ref[:, pl.ds(start, LANES)].astype(F32)
        gain = gain_ref[:, pl.ds(start, LANES)]
        normed_ref[:, number * LANES : (number + 1) * LANES] = (piece * inv * gain).astype(BF16)
        cot_out_ref[:, number * LANES : (number + 1) * LANES] = cot_ref[:, pl.ds(start, LANES)]


def input_norm(hidden, cot, gain, dp, extent):
    rows, width = hidden.shape
    if width // extent != LANES:
        u = hidden.astype(F32)
        inv = lax.rsqrt(jnp.mean(u * u, axis=-1, keepdims=True) + EPSILON)
        normed = (u * inv * gain).astype(BF16)
        order = owner_block(jnp.arange(extent), dp, extent)

        def arranged(a):
            return jnp.take(a.reshape(rows, extent, -1), order, axis=1).reshape(rows, width)

        return arranged(normed), arranged(cot), inv
    step = 128
    tile = pl.BlockSpec((step, width), lambda i: (i, 0))
    return pl.pallas_call(
        functools.partial(norm_kernel, extent=extent),
        grid=(rows // step,),
        in_specs=[
            pl.BlockSpec(memory_space=pltpu.SMEM),
            tile,
            tile,
            pl.BlockSpec((1, width), lambda i: (0, 0)),
        ],
        out_specs=[tile, tile, pl.BlockSpec((step, 1), lambda i: (i, 0))],
        out_shape=[
            jax.ShapeDtypeStruct((rows, width), BF16),
            jax.ShapeDtypeStruct((rows, width), BF16),
            jax.ShapeDtypeStruct((rows, 1), F32),
        ],
        compiler_params=pltpu.CompilerParams(vmem_limit_bytes=VMEM_LIMIT),
    )(dp.reshape(1), hidden, cot, gain.reshape(1, width))


def restore_kernel(place_ref, in_ref, out_ref, *, extent):
    for number in range(extent):
        start = pl.multiple_of(owner_block(number, place_ref[0], extent) * LANES, LANES)
        out_ref[:, pl.ds(start, LANES)] = in_ref[:, number * LANES : (number + 1) * LANES]


def restore_order(a, dp, extent):
    rows, width = a.shape
    if width // extent != LANES:
        order = owner_block(jnp.arange(extent), dp, extent)
        back = jnp.argsort(order)
        return jnp.take(a.reshape(rows, extent, -1), back, axis=1).reshape(rows, width)
    step = 128
    tile = pl.BlockSpec((step, width), lambda i: (i, 0))
    return pl.pallas_call(
        functools.partial(restore_kernel, extent=extent),
        grid=(rows // step,),
        in_specs=[pl.BlockSpec(memory_space=pltpu.SMEM), tile],
        out_specs=tile,
        out_shape=jax.ShapeDtypeStruct((rows, width), a.dtype),
        compiler_params=pltpu.CompilerParams(vmem_limit_bytes=VMEM_LIMIT),
    )(dp.reshape(1), a)


DT, CUM, SEG, VALID, LINK, KEEP, INV, CROSS = 0, 4, 8, 9, 12, 13, 14, 15
COLS = 16
TAPS, BIAS, SKIP, GAIN = 0, 4, 5, 6


def spread(col, first):
    rows = col.shape[0]
    lane = lax.broadcasted_iota(jnp.int32, (rows, TILE), 1)
    wide = jnp.broadcast_to(col[:, first : first + 1], (rows, TILE))
    for head in range(1, GROUP):
        wide = jnp.where(
            lane < head * WIDTH,
            wide,
            jnp.broadcast_to(col[:, first + head : first + head + 1], (rows, TILE)),
        )
    return wide


def conv_of(v, col_ref, par_ref):
    result = par_ref[BIAS : BIAS + 1, :] + par_ref[TAPS + 3 : TAPS + 4, :] * v
    for offset in range(1, 4):
        valid = col_ref[:, VALID + offset - 1 : VALID + offset]
        result = result + par_ref[TAPS + 3 - offset : TAPS + 4 - offset, :] * (
            pltpu.roll(v, offset, 0) * valid
        )
    return result


def pair_mask(seg_col, seg_row, transposed):
    down = lax.broadcasted_iota(jnp.int32, (BLOCK, BLOCK), 0)
    across = lax.broadcasted_iota(jnp.int32, (BLOCK, BLOCK), 1)
    causal = down <= across if transposed else down >= across
    return causal & (seg_col == seg_row)


def forward_kernel(z_ref, dyn_ref, bc_ref, col_ref, row_ref, par_ref, y_ref, state_ref, sum_ref, xs_ref, carry_ref):
    blocks = xs_ref.shape[0] // BLOCK
    conv = conv_of(z_ref[:, TILE:], col_ref, par_ref)
    xs_ref[...] = conv * sigmoid(conv)
    carry_ref[...] = jnp.zeros_like(carry_ref)

    def one_block(number, carried):
        rows = pl.ds(pl.multiple_of(number * BLOCK, BLOCK), BLOCK)
        b_rows, c_rows = bc_ref[rows, :LANES], bc_ref[rows, LANES:]
        col = col_ref[rows, :]
        scores = dot(c_rows, b_rows, NT, HIGH)
        mask = pair_mask(col[:, SEG : SEG + 1], row_ref[GROUP : GROUP + 1, rows], False)
        scores = jnp.where(mask, scores, 0.0)
        x = xs_ref[rows, :]
        cum_wide = spread(col, CUM)
        dtx = x * spread(col, DT)
        dtx_low = dtx.astype(BF16)
        parts = []
        for head in range(GROUP):
            gap = col[:, CUM + head : CUM + head + 1] - row_ref[head : head + 1, rows]
            mixing = scores * jnp.exp(jnp.minimum(gap, 0.0))
            parts.append(dot(mixing.astype(BF16), dtx_low[:, head * WIDTH : (head + 1) * WIDTH]))
        within = jnp.concatenate(parts, axis=1)
        state = carry_ref[...]
        state_ref[number] = state
        decay = jnp.exp(cum_wide) * col[:, LINK : LINK + 1]
        y = within + low_dot(c_rows, state) * decay + par_ref[SKIP : SKIP + 1, :] * x
        weight = jnp.exp(cum_wide[BLOCK - 1 :, :] - cum_wide) * col[:, KEEP : KEEP + 1]
        carry_ref[...] = state * decay[BLOCK - 1 :, :] + low_dot(b_rows, dtx * weight, TN)
        y_ref[rows, :] = y
        z = z_ref[rows, :TILE]
        yg = y * z * sigmoid(z)
        first = jnp.sum(yg * yg, axis=1, keepdims=True)
        second = jnp.sum(yg * par_ref[GAIN : GAIN + 1, :] * dyn_ref[rows, :], axis=1, keepdims=True)
        lane = lax.broadcasted_iota(jnp.int32, (BLOCK, 8), 1)
        sum_ref[rows, :] = jnp.where(lane == 0, first, jnp.where(lane == 1, second, 0.0))
        return carried

    lax.fori_loop(0, blocks, one_block, 0)


def backward_kernel(
    z_ref, y_ref, dyn_ref, bc_ref, col_ref, row_ref, par_ref, state_ref, dbc_in_ref,
    dzx_ref, yn_ref, dbc_ref, steps_ref, small_ref, xs_ref, dconv_ref, carry_ref,
):
    blocks = xs_ref.shape[0] // BLOCK
    conv = conv_of(z_ref[:, TILE:], col_ref, par_ref)
    gate = sigmoid(conv)
    xs_ref[...] = conv * gate
    dconv_ref[...] = gate * (1.0 + conv * (1.0 - gate))
    carry_ref[...] = jnp.zeros_like(carry_ref)
    small_ref[...] = jnp.zeros_like(small_ref)
    down = lax.broadcasted_iota(jnp.int32, (BLOCK, BLOCK), 0)
    across = lax.broadcasted_iota(jnp.int32, (BLOCK, BLOCK), 1)

    def one_block(step, carried):
        number = blocks - 1 - step
        rows = pl.ds(pl.multiple_of(number * BLOCK, BLOCK), BLOCK)
        col = col_ref[rows, :]
        z, y, dyn = z_ref[rows, :TILE], y_ref[rows, :], dyn_ref[rows, :]
        gain = par_ref[GAIN : GAIN + 1, :]
        inv, cross = col[:, INV : INV + 1], col[:, CROSS : CROSS + 1]
        gate = sigmoid(z)
        silu = z * gate
        yg = y * silu
        yg_inv = yg * inv
        d_yg = inv * gain * dyn - yg * cross
        dzx_ref[rows, :TILE] = (d_yg * y * (gate * (1.0 + z * (1.0 - gate)))).astype(BF16)
        yn_ref[rows, :] = (yg_inv * gain).astype(BF16)
        small_ref[GAIN : GAIN + 1, :] += jnp.sum(dyn * yg_inv, axis=0, keepdims=True)
        e = d_yg * silu
        b_rows, c_rows = bc_ref[rows, :LANES], bc_ref[rows, LANES:]
        b_low, c_low = b_rows.astype(BF16), c_rows.astype(BF16)
        scores = dot(b_rows, c_rows, NT, HIGH)
        mask = pair_mask(col[:, SEG : SEG + 1], row_ref[GROUP : GROUP + 1, rows], True)
        scores = jnp.where(mask, scores, 0.0)
        x = xs_ref[rows, :]
        dt_wide, cum_wide = spread(col, DT), spread(col, CUM)
        dtx = x * dt_wide
        dtx_low, e_low = dtx.astype(BF16), e.astype(BF16)
        reach = (down >= across).astype(BF16)
        d_scores = jnp.zeros((BLOCK, BLOCK), F32)
        parts, between = [], []
        for head in range(GROUP):
            lanes = slice(head * WIDTH, (head + 1) * WIDTH)
            gap = row_ref[head : head + 1, rows] - col[:, CUM + head : CUM + head + 1]
            decay = jnp.exp(jnp.minimum(gap, 0.0))
            mixing = scores * decay
            parts.append(dot(mixing.astype(BF16), e_low[:, lanes]))
            d_mixing = dot(dtx_low[:, lanes], e_low[:, lanes], NT)
            d_scores = d_scores + d_mixing * decay
            later = dot((d_mixing * mixing).astype(BF16), reach)
            between.append(jnp.sum(jnp.where(down < across, later, 0.0), axis=0, keepdims=True))
        d_dtx = jnp.concatenate(parts, axis=1)
        d_scores = jnp.where(mask, d_scores, 0.0).astype(BF16)
        d_b = dot(d_scores, c_low)
        d_c = dot(d_scores, b_low, TN)
        state, d_state = state_ref[number], carry_ref[...]
        state_low, d_state_low = state.astype(BF16), d_state.astype(BF16)
        decay = jnp.exp(cum_wide) * col[:, LINK : LINK + 1]
        e_in = e * decay
        e_in_low = e_in.astype(BF16)
        from_state = e_in * dot(c_low, state_low)
        d_c = d_c + dot(e_in_low, state_low, NT)
        carry_ref[...] = decay[BLOCK - 1 :, :] * d_state + dot(c_low, e_in_low, TN)
        weight = jnp.exp(cum_wide[BLOCK - 1 :, :] - cum_wide) * col[:, KEEP : KEEP + 1]
        d_tail = weight * dot(b_low, d_state_low)
        to_state = d_tail * dtx
        d_b = d_b + low_dot(weight * dtx, d_state_low, NT)
        d_dtx = d_dtx + d_tail
        through = decay[BLOCK - 1 :, :] * jnp.sum(state * d_state, axis=0, keepdims=True)
        d_x = dt_wide * d_dtx + par_ref[SKIP : SKIP + 1, :] * e
        small_ref[SKIP : SKIP + 1, :] += jnp.sum(x * e, axis=0, keepdims=True)
        dconv_ref[rows, :] = dconv_ref[rows, :] * d_x
        dbc_ref[rows, :LANES] = dbc_in_ref[rows, :LANES] + d_b
        dbc_ref[rows, LANES:] = dbc_in_ref[rows, LANES:] + d_c
        owner = lax.broadcasted_iota(jnp.int32, (8, TILE), 1) // WIDTH
        pick = (owner == lax.broadcasted_iota(jnp.int32, (8, TILE), 0)).astype(F32)
        q_rows = dot(pick, from_state, NT, HIGH)
        p_rows = dot(pick, to_state, NT, HIGH)
        dt_rows = dot(pick, d_dtx * x, NT, HIGH)
        const = dot(pick, jnp.broadcast_to(through, (8, TILE)), NT, HIGH)[:, :1]
        run = (
            dot(q_rows, (down >= across).astype(F32), NN, HIGH)
            + dot(p_rows, (down < across).astype(F32), NN, HIGH)
            + const
        )
        steps_ref[:GROUP, rows] = run[:GROUP] + jnp.concatenate(between, axis=0)
        steps_ref[GROUP:, rows] = dt_rows[:GROUP]
        return carried

    lax.fori_loop(0, blocks, one_block, 0)
    v, d_conv = z_ref[:, TILE:], dconv_ref[...]
    length = v.shape[0]
    d_v = par_ref[TAPS + 3 : TAPS + 4, :] * d_conv
    small_ref[TAPS + 3 : TAPS + 4, :] = jnp.sum(d_conv * v, axis=0, keepdims=True)
    small_ref[BIAS : BIAS + 1, :] = jnp.sum(d_conv, axis=0, keepdims=True)
    for offset in range(1, 4):
        place = TAPS + 3 - offset
        counted = d_conv * col_ref[:, VALID + offset - 1 : VALID + offset]
        small_ref[place : place + 1, :] = jnp.sum(
            counted * pltpu.roll(v, offset, 0), axis=0, keepdims=True
        )
        d_v = d_v + par_ref[place : place + 1, :] * pltpu.roll(counted, length - offset, 0)
    dzx_ref[:, TILE:] = d_v.astype(BF16)


def by_sequence(rows, width):
    return pl.BlockSpec((rows, width), lambda i: (i, 0))


def whole(shape):
    return pl.BlockSpec(shape, lambda i: (0,) * len(shape))


def run_forward(zv, dyn, bc, col, row, par, length):
    tokens = zv.shape[0]
    number, blocks = tokens // length, length // BLOCK
    return pl.pallas_call(
        forward_kernel,
        grid=(number,),
        in_specs=[
            by_sequence(length, 2 * TILE),
            by_sequence(length, TILE),
            by_sequence(length, 2 * LANES),
            by_sequence(length, COLS),
            pl.BlockSpec((8, length), lambda i: (0, i)),
            whole((8, TILE)),
        ],
        out_specs=[
            by_sequence(length, TILE),
            pl.BlockSpec((blocks, LANES, TILE), lambda i: (i, 0, 0)),
            by_sequence(length, 8),
        ],
        out_shape=[
            jax.ShapeDtypeStruct((tokens, TILE), F32),
            jax.ShapeDtypeStruct((number * blocks, LANES, TILE), F32),
            jax.ShapeDtypeStruct((tokens, 8), F32),
        ],
        scratch_shapes=[pltpu.VMEM((length, TILE), F32), pltpu.VMEM((LANES, TILE), F32)],
        compiler_params=pltpu.CompilerParams(vmem_limit_bytes=VMEM_LIMIT),
        cost_estimate=pl.CostEstimate(flops=10**10, bytes_accessed=10**7, transcendentals=10**7),
    )(zv, dyn, bc, col, row, par)


def run_backward(zv, y, dyn, bc, col, row, par, state, dbc, length):
    tokens = zv.shape[0]
    number, blocks = tokens // length, length // BLOCK
    return pl.pallas_call(
        backward_kernel,
        grid=(number,),
        in_specs=[
            by_sequence(length, 2 * TILE),
            by_sequence(length, TILE),
            by_sequence(length, TILE),
            by_sequence(length, 2 * LANES),
            by_sequence(length, COLS),
            pl.BlockSpec((8, length), lambda i: (0, i)),
            whole((8, TILE)),
            pl.BlockSpec((blocks, LANES, TILE), lambda i: (i, 0, 0)),
            by_sequence(length, 2 * LANES),
        ],
        out_specs=[
            by_sequence(length, 2 * TILE),
            by_sequence(length, TILE),
            by_sequence(length, 2 * LANES),
            pl.BlockSpec((8, length), lambda i: (0, i)),
            pl.BlockSpec((8, TILE), lambda i: (i, 0)),
        ],
        out_shape=[
            jax.ShapeDtypeStruct((tokens, 2 * TILE), BF16),
            jax.ShapeDtypeStruct((tokens, TILE), BF16),
            jax.ShapeDtypeStruct((tokens, 2 * LANES), F32),
            jax.ShapeDtypeStruct((8, tokens), F32),
            jax.ShapeDtypeStruct((8 * number, TILE), F32),
        ],
        scratch_shapes=[
            pltpu.VMEM((length, TILE), F32),
            pltpu.VMEM((length, TILE), F32),
            pltpu.VMEM((LANES, TILE), F32),
        ],
        compiler_params=pltpu.CompilerParams(vmem_limit_bytes=VMEM_LIMIT),
        cost_estimate=pl.CostEstimate(flops=2 * 10**10, bytes_accessed=10**7, transcendentals=10**7),
    )(zv, y, dyn, bc, col, row, par, state, dbc)


def segment_conv(inputs, taps, bias, masks):
    reach = taps.shape[0]
    result = bias[None, :] + taps[reach - 1][None, :] * inputs
    for offset in range(1, reach):
        moved = jnp.concatenate(
            [jnp.zeros((offset, inputs.shape[1]), inputs.dtype), inputs[:-offset]], axis=0
        )
        result = result + taps[reach - 1 - offset][None, :] * (
            moved * masks[:, offset - 1 : offset]
        )
    return result


def sequence_masks(ids):
    masks = []
    for offset in range(1, 4):
        earlier = jnp.concatenate([jnp.full((offset,), -2, jnp.int32), ids[:-offset]])
        masks.append(earlier == ids)
    blocks = ids.reshape(-1, BLOCK)
    last = blocks[:, -1]
    before = jnp.concatenate([jnp.full((1,), -2, jnp.int32), last[:-1]])
    masks.append((blocks == before[:, None]).reshape(-1))
    masks.append((blocks == last[:, None]).reshape(-1))
    return jnp.stack(masks, axis=1).astype(F32)


def local(
    hidden_in,
    segments,
    norm_gain,
    w_zx,
    w_dt,
    w_bc,
    conv_x,
    conv_x_bias,
    conv_bc,
    conv_bc_bias,
    dt_bias,
    a_log,
    d_skip,
    gated_gain,
    w_out,
    cotangent,
):
    dp, mp = lax.axis_index("dp"), lax.axis_index("mp")
    extent = lax.axis_size("dp")
    far = extent // 4
    x_side = lax.rem(dp, 2)
    rows, width = hidden_in.shape
    length = segments.shape[0]
    inner = conv_x.shape[1]
    inner_total = inner * lax.axis_size("mp")
    heads = dt_bias.shape[0]
    quarter, own_heads = inner // 2, heads // 2
    tiles = quarter // TILE
    depth = w_zx.shape[0]

    def by_side(own, other, axis):
        return jnp.where(
            x_side == 0,
            jnp.concatenate([own, other], axis=axis),
            jnp.concatenate([other, own], axis=axis),
        )

    def by_core(own, other, axis):
        return jnp.where(
            mp == 0,
            jnp.concatenate([own, other], axis=axis),
            jnp.concatenate([other, own], axis=axis),
        )

    def of_side(a, side, axis):
        size = a.shape[axis] // 2
        return lax.dynamic_slice_in_dim(a, side * size, size, axis)

    packed = jnp.concatenate([w_zx[:, 0], w_zx[:, 1], w_out.T], axis=1)
    packed = packed.reshape(depth, 3, 2, tiles, TILE).transpose(2, 3, 0, 1, 4)
    packed = packed.reshape(2, tiles, depth, 3 * TILE)
    small_weights = jnp.concatenate([w_bc, w_dt], axis=1)
    small_other = flip(small_weights, "dp", 1)
    packed_own = lax.dynamic_index_in_dim(packed, x_side, 0, False)
    packed_other = flip(lax.dynamic_index_in_dim(packed, 1 - x_side, 0, False), "dp", 1)

    def gathered(piece):
        near = [piece] + [flip(piece, "dp", 4 * k) for k in range(1, far)]
        return near + [flip(p, "dp", 2) for p in near]

    bc_weight = jnp.concatenate(gathered(by_side(small_weights, small_other, 0)), axis=0)

    normed, cot, inverse_rows = input_norm(hidden_in, cotangent, norm_gain, dp, extent)

    def both_sequences(a):
        near = flip(a, "dp", 1)
        return by_core(a, flip(a, "mp", 1), 0), by_core(near, flip(near, "mp", 1), 0)

    normed_own, normed_near = both_sequences(normed)
    normed_all = jnp.concatenate([normed_own, normed_near], axis=0)
    weights = []
    for tile in range(tiles):
        piece = by_side(packed_own[tile], packed_other[tile], 0)
        weights.append(jnp.concatenate(gathered(piece), axis=0))
    cot_all = jnp.concatenate(both_sequences(cot), axis=0)
    ids = (segments, flip(segments, "dp", 1))

    proj_small = dot(normed_all, bc_weight)
    proj_bc = proj_small[:, : 2 * LANES]
    proj_dt = of_side(proj_small[:, 2 * LANES :], x_side, 1)
    masks = [sequence_masks(one) for one in ids]

    def state_part(values, taps, bias, mask):
        return jax.nn.silu(segment_conv(values, taps, bias, mask))

    bc_own, state_back = jax.vjp(
        lambda values, taps, bias: state_part(values, taps, bias, masks[0]),
        proj_bc[:length],
        conv_bc,
        conv_bc_bias,
    )
    bc_near = state_part(proj_bc[length:], conv_bc, conv_bc_bias, masks[1])
    bc = jnp.concatenate([bc_own, bc_near], axis=0)
    side_bias = of_side(dt_bias, x_side, 0)
    rate = -jnp.exp(of_side(a_log, x_side, 0))
    raw_dt = proj_dt + side_bias
    dt = jax.nn.softplus(raw_dt)
    tokens = dt.shape[0]
    lower = (jnp.arange(BLOCK)[:, None] >= jnp.arange(BLOCK)[None, :]).astype(F32)
    cum = jnp.einsum(
        "ts,csh->cth", lower, (dt * rate).reshape(-1, BLOCK, own_heads), precision=HIGH
    ).reshape(tokens, own_heads)
    mask_all = jnp.concatenate(masks, axis=0)
    ids_all = jnp.concatenate(ids, axis=0).astype(F32)
    cum_rows = cum.T

    def tile_of(a, tile):
        return of_side(a, x_side, a.ndim - 1)[..., tile * TILE : (tile + 1) * TILE]

    skip_wide = jnp.repeat(d_skip, WIDTH)
    params, cols, row_sets = [], [], []
    for tile in range(tiles):
        params.append(
            jnp.concatenate(
                [
                    tile_of(conv_x, tile),
                    tile_of(conv_x_bias, tile)[None],
                    tile_of(skip_wide, tile)[None],
                    tile_of(gated_gain, tile)[None],
                    jnp.zeros((1, TILE), F32),
                ],
                axis=0,
            )
        )
        own = slice(tile * GROUP, (tile + 1) * GROUP)
        cols.append(
            jnp.concatenate([dt[:, own], cum[:, own], ids_all[:, None], mask_all], axis=1)
        )
        row_sets.append(
            jnp.concatenate(
                [cum_rows[own], ids_all[None], jnp.zeros((3, tokens), F32)], axis=0
            )
        )

    zvs, dyns, ys, states, sums = [], [], [], [], 0.0
    for tile in range(tiles):
        dyns.append(dot(cot_all, weights[tile][:, 2 * TILE :]))
        zvs.append(dot(normed_all, weights[tile][:, : 2 * TILE]))
        y, state, part = run_forward(
            zvs[tile],
            dyns[tile],
            bc,
            jnp.pad(cols[tile], ((0, 0), (0, 2))),
            row_sets[tile],
            params[tile],
            length,
        )
        ys.append(y)
        states.append(state)
        sums = sums + part[:, :2]
    sums = sums + flip(sums, "mp", 1)
    near = flip(sums, "dp", 1)
    sums = sums + jnp.concatenate([near[length:], near[:length]], axis=0)
    inverse_gated = lax.rsqrt(sums[:, :1] / inner_total + EPSILON)
    cross = inverse_gated * inverse_gated * inverse_gated / inner_total * sums[:, 1:2]

    dzxs, yns, mine, theirs, d_steps, smalls = [], [], [], [], [], []
    dbc = jnp.zeros((tokens, 2 * LANES), F32)
    half = width // 2
    for tile in range(tiles):
        dzx, yn, dbc, steps, small = run_backward(
            zvs[tile],
            ys[tile],
            dyns[tile],
            bc,
            jnp.concatenate([cols[tile], inverse_gated, cross], axis=1),
            row_sets[tile],
            params[tile],
            states[tile],
            dbc,
            length,
        )
        dzxs.append(dzx)
        yns.append(yn)
        d_steps.append(steps)
        smalls.append(small[:8] + small[8:])

        def share(start):
            part = slice(start, start + half)
            return jnp.concatenate(
                [dot(normed_all[:, part], dzx, TN), dot(cot_all[:, part], yn, TN)], axis=1
            )

        sent = flip(share(half).astype(BF16), "dp", 2)
        total = (share(0) + sent.astype(F32)).reshape(far, 2 * depth, 3 * TILE)
        out = total.astype(BF16)
        total = total[0]
        for k in range(1, far):
            total = total + flip(out[k], "dp", 4 * k).astype(F32)
        mine.append(of_side(total, x_side, 0))
        theirs.append(flip(of_side(total, 1 - x_side, 0).astype(BF16), "dp", 1).astype(F32))

    def assembled(parts):
        stacked = jnp.stack([p.reshape(depth, 3, TILE) for p in parts], axis=2)
        return stacked.reshape(depth, 3, quarter)

    full = by_side(assembled(mine), assembled(theirs), 2)
    grad_zx_weight = full[:, :2]
    grad_out_weight = full[:, 2].T

    dbc = dbc + flip(dbc, "mp", 1)
    dbc = dbc[:length] + flip(dbc[length:], "dp", 1)
    d_bc, grad_conv_bc, grad_conv_bc_bias = state_back(dbc)
    bc_grad = d_bc.astype(BF16)

    steps = jnp.concatenate([s[:GROUP] for s in d_steps], axis=0).T
    direct = jnp.concatenate([s[GROUP:] for s in d_steps], axis=0).T
    d_dt = (direct + rate * steps) * jax.nn.sigmoid(raw_dt)
    grad_dt_bias = jnp.sum(d_dt, axis=0)
    grad_a_log = jnp.sum(steps * dt, axis=0) * rate
    dt_grad = d_dt.astype(BF16)

    def placed(a):
        zero = jnp.zeros_like(a)
        return by_side(a, zero, a.ndim - 1)

    small_grad = jnp.concatenate(
        [
            dot(normed_own, lax.dynamic_slice_in_dim(bc_grad, mp * LANES, LANES, 1), TN),
            placed(dot(normed_all, dt_grad, TN)),
        ],
        axis=1,
    )
    small_grad = small_grad.reshape(2 * far, 2, depth, -1)
    small_grad = of_side(small_grad, x_side, 1) + flip(
        of_side(small_grad, 1 - x_side, 1).astype(BF16), "dp", 1
    ).astype(F32)
    small_grad = small_grad.reshape(2, far, depth, -1)
    small_grad = small_grad[0] + flip(small_grad[1].astype(BF16), "dp", 2).astype(F32)
    out = small_grad.astype(BF16)
    small_grad = small_grad[0]
    for k in range(1, far):
        small_grad = small_grad + flip(out[k], "dp", 4 * k).astype(F32)
    grad_dt_weight = small_grad[:, LANES:]
    own_bc = small_grad[:, :LANES]
    grad_bc_weight = by_core(own_bc, flip(own_bc, "mp", 1), 1)

    def token_sum(products):
        def part(core):
            return products(lambda a: of_side(a.reshape(2, 2, rows, -1), core, 1).reshape(2 * rows, -1))

        total = part(mp) + flip(part(1 - mp).astype(BF16), "mp", 1).astype(F32)
        return total[:rows] + flip(total[rows:].astype(BF16), "dp", 1).astype(F32)

    out_all = jnp.concatenate([w[:, 2 * TILE :] for w in weights], axis=1)
    yn_all = jnp.concatenate(yns, axis=1)
    mixer_out = restore_order(token_sum(lambda pick: dot(pick(yn_all), out_all, NT)), dp, extent)
    inputs = hidden_in.astype(F32)
    residual_out = (inputs + mixer_out).astype(BF16)
    usable = (lax.dynamic_slice_in_dim(segments, mp * rows, rows, 0) >= 0).astype(F32)[:, None]
    totals = jnp.stack(
        [
            jnp.sum(usable * inputs * inputs),
            jnp.sum(usable * mixer_out * mixer_out),
            jnp.sum(usable),
        ]
    )

    zv_all = jnp.concatenate([w[:, : 2 * TILE] for w in weights], axis=1)
    dt_weight = of_side(bc_weight[:, 2 * LANES :], x_side, 1)
    dzx_all = jnp.concatenate(dzxs, axis=1)
    d_normed = token_sum(
        lambda pick: dot(pick(dzx_all), zv_all, NT) + dot(pick(dt_grad), dt_weight, NT)
    )
    d_normed = d_normed + dot(
        lax.dynamic_slice_in_dim(bc_grad, mp * rows, rows, 0), bc_weight[:, : 2 * LANES], NT
    )
    d_normed = restore_order(d_normed, dp, extent)
    grad_norm_gain = jnp.sum(d_normed * inputs * inverse_rows, axis=0)
    inverse_cube_rows = inverse_rows * inverse_rows * inverse_rows
    input_grad = (
        cotangent.astype(F32)
        + inverse_rows * norm_gain * d_normed
        - inputs
        * inverse_cube_rows
        * jnp.mean(inputs * norm_gain * d_normed, axis=-1, keepdims=True)
    )

    def summed(a, axes):
        for axis in axes:
            bit = 1
            while bit < lax.axis_size(axis):
                a = a + flip(a, axis, bit)
                bit *= 2
        return a

    small = jnp.concatenate(smalls, axis=1)
    channel = placed(small[: GAIN + 1])
    skip_grad = jnp.sum(channel[SKIP].reshape(heads, WIDTH), axis=1)
    pieces = [
        channel[TAPS:BIAS],
        channel[BIAS],
        grad_conv_bc,
        grad_conv_bc_bias,
        placed(grad_dt_bias),
        placed(grad_a_log),
        skip_grad,
        channel[GAIN],
    ]
    flat = summed(jnp.concatenate([p.reshape(-1) for p in pieces]), ("dp",))
    small_sums, start = [], 0
    for piece in pieces:
        small_sums.append(flat[start : start + piece.size].reshape(piece.shape))
        start += piece.size
    last = summed(jnp.concatenate([grad_norm_gain, totals]), ("mp", "dp"))
    grad_norm_gain = last[:width]
    sum_inputs, sum_mixer, usable_count = last[width], last[width + 1], last[width + 2]
    rms_residual = jnp.sqrt(sum_inputs / (usable_count * width))
    rms_mixer = jnp.sqrt(sum_mixer / (usable_count * width))
    return (
        residual_out,
        input_grad,
        grad_norm_gain,
        grad_zx_weight,
        grad_dt_weight,
        grad_bc_weight,
        small_sums[0],
        small_sums[1],
        small_sums[2],
        small_sums[3],
        small_sums[4],
        small_sums[5],
        small_sums[6],
        small_sums[7],
        grad_out_weight,
        rms_residual,
        rms_mixer,
    )


def solution(mesh):
    in_specs = (
        P(("dp", "mp"), None),
        P("dp"),
        P(),
        P("dp", None, "mp"),
        P("dp", "mp"),
        P("dp", None),
        P(None, "mp"),
        P("mp"),
        P(),
        P(),
        P("mp"),
        P("mp"),
        P("mp"),
        P("mp"),
        P("mp", "dp"),
        P(("dp", "mp"), None),
    )
    out_specs = (
        P(("dp", "mp"), None),
        P(("dp", "mp"), None),
        P(),
        P("dp", None, "mp"),
        P("dp", "mp"),
        P("dp", None),
        P(None, "mp"),
        P("mp"),
        P(),
        P(),
        P("mp"),
        P("mp"),
        P("mp"),
        P("mp"),
        P("mp", "dp"),
        P(),
        P(),
    )
    return jax.shard_map(local, mesh=mesh, in_specs=in_specs, out_specs=out_specs, check_vma=False)
```

time: 2190 us -> 1140 us (0.52)
  waiting for transfers between devices: 1130 us -> 345 us
  matrix products: 374 us -> 162 us
  Pallas kernels: 0 us -> 202 us
  blocking collectives: 172 us -> 0 us
  starting transfers between devices: 0.4 us -> 167 us
  local copies, waits for them, and re-layouts: 258 us -> 129 us
  other arithmetic: 208 us -> 120 us
    reduce_scatter x4 -> x0, waiting for transfers between devices: 925 us -> none  [the longest x1 576 us: local(): lax.psum_scatter(jnp.einsum('tr,tk->rk', normed_full, all_grads, preferre...]
    ppermute x0 -> x87, waiting for transfers between devices: none -> 345 us  [flip(): return lax.ppermute(a, axis, [(i, i ^ bit) for i in range(size)])]
    dot_general x53 -> x35, matrix products: 374 us -> 162 us  [the longest x34 161 us: dot(): lax.dot_general(a, b, dims, precision=precision, preferred_element_type=F32)]
    pallas_call x0 -> x11, Pallas kernels: none -> 202 us  [the longest x4 129 us: run_backward(): pl.pallas_call(backward_kernel, grid=(number,), in_specs=[by_sequence(len...]
    all_gather x5 -> x0, waiting for transfers between devices: 202 us -> none  [the longest x1 186 us: fetch_shards(): lax.all_gather(w_zx, 'dp', axis=0, tiled=True)]
    ppermute x0 -> x87, starting transfers between devices: none -> 167 us  [flip(): return lax.ppermute(a, axis, [(i, i ^ bit) for i in range(size)])]
    psum x4 -> x0, blocking collectives: 129 us -> none  [the longest x1 77.5 us: local(): lax.psum((grad_conv_x, grad_conv_x_bias, grad_conv_bc, grad_conv_bc_bias,...]
    reshape x13 -> x8, local copies, waits for them, and re-layouts: 95 us -> 2.55 us  [the longest x2 1.23 us: local(): small_sums.append(flat[start:start + piece.size].reshape(piece.shape))]
  transfers between devices with their start and end apart: 10 -> 87, of which waited for: 4 -> 32; matrix products, arithmetic and copies ran while one was open for 24% -> 21% of each run, Pallas kernels for 0% -> 1%
where the time goes in v1:
time: 1140 us; the launch traced here: 1130 us
  waiting for transfers between devices  345 us (30%)
  Pallas kernels  202 us (18%)
  starting transfers between devices  167 us (15%)
  matrix products  162 us (14%)
  local copies, waits for them, and re-layouts  129 us (11%)
  other arithmetic  120 us (11%)
    ppermute x87, waiting for transfers between devices, flip(): return lax.ppermute(a, axis, [(i, i ^ bit) for i in range(size)])  345 us
    ppermute x87, starting transfers between devices, flip(): return lax.ppermute(a, axis, [(i, i ^ bit) for i in range(size)])  167 us
    dot_general x34, matrix products, dot(): lax.dot_general(a, b, dims, precision=precision, preferred_element_type=F32)  161 us
    pallas_call x4, Pallas kernels, run_backward(): pl.pallas_call(backward_kernel, grid=(number,), in_specs=[by_sequence(len...  129 us
    pallas_call x4, Pallas kernels, run_forward(): pl.pallas_call(forward_kernel, grid=(number,), in_specs=[by_sequence(leng...  57.5 us
    unnamed x306, local copies, waits for them, and re-layouts  29.3 us
  transfers between devices with their start and end apart: 87, of which 32 were waited for; matrix products, arithmetic and copies ran while one was open for 21% of the time, Pallas kernels for 1%

profile of v1, /device:TPU:0, one launch (start us, length us, event | category | flops | bytes accessed | tf_op | source)
XLA Modules:
  0.0 1132.3 jit_solution(12226299533727120118)
XLA Ops:
  75.8 28.3 %collective-permute-done.38 = bf16[256,768]{0,1:T(8,128)(2,1)S(1)} collective-permute-done((bf16[256,768]{0,1:T(8,128)(2,1)}, bf16[256,768]{0,1:T(8,128)(2,1)S(1)}, u32[]{:S(2)}, u32[]{:S(2)}) %collective-permute-start.38) | collective-permute-done | bytes 393248 | tf_op jit(solution)/shard_map/ppermute | solution.py:36
  107.5 10.3 collective-permute-start.23
  120.9 8.5 collective-permute-done.31
  134.5 17.0 %collective-permute-start.4 = (bf16[256,768]{0,1:T(8,128)(2,1)S(1)}, bf16[256,768]{0,1:T(8,128)(2,1)S(1)}, u32[]{:S(2)}, u32[]{:S(2)}) collective-permute-start(bf16[256,768]{0,1:T(8,128)(2,1)S(1)} %get-tuple-element.249), channel_id=1, source_target_pairs={{0,8},{2,10},{4,12},{6,14},{8,0},{10,2},{12,4},{14,6},{16,24},{18,... | collective-permute-start | bytes 1179656 | tf_op jit(solution)/shard_map/ppermute | solution.py:36
  154.7 8.4 collective-permute-done.24
  171.2 21.4 %collective-permute-done.5 = bf16[256,768]{0,1:T(8,128)(2,1)S(1)} collective-permute-done((bf16[256,768]{0,1:T(8,128)(2,1)S(1)}, bf16[256,768]{0,1:T(8,128)(2,1)S(1)}, u32[]{:S(2)}, u32[]{:S(2)}) %collective-permute-start.5) | collective-permute-done | bytes 393248 | tf_op jit(solution)/shard_map/ppermute | solution.py:36
  271.1 8.5 collective-permute-done.9
  387.1 14.3 %shard_map.291 = (f32[2048,256]{1,0:T(8,128)}, f32[8,128,256]{2,1,0:T(8,128)}, f32[2048,8]{1,0:T(8,128)}) custom-call(f32[2048,512]{1,0:T(8,128)} %fusion.79.z_ref, f32[2048,256]{1,0:T(8,128)} %fusion.71.dyn_ref, f32[2048,256]{1,0:T(8,128)} %pad_maximum_fusion.6.bc_ref, f32[2048,16]{1,0:T(8,128)} %pad.55.col_ref, f32[8,2048]{1,0:T(8,128)} %get-tuple-element.362.row_ref, ...), custom_call_target="tpu_custom_call" | custom-call | flops 10000000000 | bytes 10000000 | tf_op jit(solution)/shard_map/pallas_call | solution.py:310
  401.3 14.5 %shard_map.290 = (f32[2048,256]{1,0:T(8,128)}, f32[8,128,256]{2,1,0:T(8,128)}, f32[2048,8]{1,0:T(8,128)}) custom-call(f32[2048,512]{1,0:T(8,128)} %fusion.81.z_ref, f32[2048,256]{1,0:T(8,128)} %fusion.73.dyn_ref, f32[2048,256]{1,0:T(8,128)} %pad_maximum_fusion.6.bc_ref, f32[2048,16]{1,0:T(8,128)} %pad.54.col_ref, f32[8,2048]{1,0:T(8,128)} %get-tuple-element.361.row_ref, ...), custom_call_target="tpu_custom_call" | custom-call | flops 10000000000 | bytes 10000000 | tf_op jit(solution)/shard_map/pallas_call | solution.py:310
  415.8 14.3 %shard_map.289 = (f32[2048,256]{1,0:T(8,128)}, f32[8,128,256]{2,1,0:T(8,128)}, f32[2048,8]{1,0:T(8,128)}) custom-call(f32[2048,512]{1,0:T(8,128)} %fusion.83.z_ref, f32[2048,256]{1,0:T(8,128)} %fusion.75.dyn_ref, f32[2048,256]{1,0:T(8,128)} %pad_maximum_fusion.6.bc_ref, f32[2048,16]{1,0:T(8,128)} %pad.53.col_ref, f32[8,2048]{1,0:T(8,128)} %get-tuple-element.360.row_ref, ...), custom_call_target="tpu_custom_call" | custom-call | flops 10000000000 | bytes 10000000 | tf_op jit(solution)/shard_map/pallas_call | solution.py:310
  430.1 14.4 %shard_map.288 = (f32[2048,256]{1,0:T(8,128)}, f32[8,128,256]{2,1,0:T(8,128)}, f32[2048,8]{1,0:T(8,128)}) custom-call(f32[2048,512]{1,0:T(8,128)} %fusion.85.z_ref, f32[2048,256]{1,0:T(8,128)} %fusion.77.dyn_ref, f32[2048,256]{1,0:T(8,128)} %pad_maximum_fusion.6.bc_ref, f32[2048,16]{1,0:T(8,128)} %pad.52.col_ref, f32[8,2048]{1,0:T(8,128)} %get-tuple-element.359.row_ref, ...), custom_call_target="tpu_custom_call" | custom-call | flops 10000000000 | bytes 10000000 | tf_op jit(solution)/shard_map/pallas_call | solution.py:310
  486.2 32.3 %shard_map.292 = (bf16[2048,512]{1,0:T(8,128)(2,1)}, bf16[2048,256]{1,0:T(8,128)(2,1)}, f32[2048,256]{1,0:T(8,128)}, f32[8,2048]{1,0:T(8,128)}, f32[16,256]{1,0:T(8,128)}) custom-call(f32[2048,512]{1,0:T(8,128)} %fusion.85.z_ref, f32[2048,256]{1,0:T(8,128)} %get-tuple-element.54.y_ref, f32[2048,256]{1,0:T(8,128)} %fusion.77.dyn_ref, ...), custom_call_target="tpu_custom_call" | custom-call | flops 20000000000 | bytes 10000000 | tf_op jit(solution)/shard_map/pallas_call | solution.py:340
  518.5 32.0 %shard_map.293 = (bf16[2048,512]{1,0:T(8,128)(2,1)}, bf16[2048,256]{1,0:T(8,128)(2,1)}, f32[2048,256]{1,0:T(8,128)}, f32[8,2048]{1,0:T(8,128)}, f32[16,256]{1,0:T(8,128)}) custom-call(f32[2048,512]{1,0:T(8,128)} %fusion.83.z_ref, f32[2048,256]{1,0:T(8,128)} %get-tuple-element.61.y_ref, f32[2048,256]{1,0:T(8,128)} %fusion.75.dyn_ref, ...), custom_call_target="tpu_custom_call" | custom-call | flops 20000000000 | bytes 10000000 | tf_op jit(solution)/shard_map/pallas_call | solution.py:340
  550.5 32.2 %shard_map.294 = (bf16[2048,512]{1,0:T(8,128)(2,1)}, bf16[2048,256]{1,0:T(8,128)(2,1)}, f32[2048,256]{1,0:T(8,128)}, f32[8,2048]{1,0:T(8,128)}, f32[16,256]{1,0:T(8,128)}) custom-call(f32[2048,512]{1,0:T(8,128)} %fusion.81.z_ref, f32[2048,256]{1,0:T(8,128)} %get-tuple-element.65.y_ref, f32[2048,256]{1,0:T(8,128)} %fusion.73.dyn_ref, ...), custom_call_target="tpu_custom_call" | custom-call | flops 20000000000 | bytes 10000000 | tf_op jit(solution)/shard_map/pallas_call | solution.py:340
  582.6 32.2 %shard_map.295 = (bf16[2048,512]{1,0:T(8,128)(2,1)}, bf16[2048,256]{1,0:T(8,128)(2,1)}, f32[2048,256]{1,0:T(8,128)}, f32[8,2048]{1,0:T(8,128)}, f32[16,256]{1,0:T(8,128)}) custom-call(f32[2048,512]{1,0:T(8,128)} %fusion.79.z_ref, f32[2048,256]{1,0:T(8,128)} %get-tuple-element.69.y_ref, f32[2048,256]{1,0:T(8,128)} %fusion.71.dyn_ref, ...), custom_call_target="tpu_custom_call" | custom-call | flops 20000000000 | bytes 10000000 | tf_op jit(solution)/shard_map/pallas_call | solution.py:340
  692.1 13.0 %fusion.14 = f32[1024,2048]{1,0:T(8,128)} fusion(bf16[1024,2048]{1,0:T(8,128)(2,1)S(1)} %bitcast.210, bf16[2048,512]{0,1:T(8,128)(2,1)S(1)} %copy-done.45, bf16[2048,512]{0,1:T(8,128)(2,1)} %slice.716, bf16[2048,512]{0,1:T(8,128)(2,1)} %slice.710, bf16[2048,512]{0,1:T(8,128)(2,1)} %slice.685), kind=kOutput, calls=%fused_computation.66 | convolution fusion | flops 8623489024 | bytes 20971520 | tf_op jit(solution)/shard_map/dot_general | solution.py:27
  705.1 14.3 %add_convert_fusion = bf16[1024,2048]{1,0:T(8,128)(2,1)} fusion(f32[1024,2048]{1,0:T(8,128)S(1)} %fusion.42, bf16[1024,2048]{1,0:T(8,128)(2,1)} %bitcast.209, bf16[2048,512]{0,1:T(8,128)(2,1)} %slice.722, bf16[2048,512]{0,1:T(8,128)(2,1)} %slice.716, bf16[2048,512]{0,1:T(8,128)(2,1)} %slice.710, bf16[2048,512]{0,1:T(8,128)(2,1)} %slice.685), kind=kOutput, calls=%fused_computation.19 | convolution fusion | flops 8627683328 | bytes 25165824 | tf_op jit(solution)/shard_map/dot_general | solution.py:27
  719.4 9.5 convolution_convert_fusion
  741.1 11.0 collective-permute-done.65
  752.1 15.3 %collective-permute-start.71 = (bf16[256,768]{0,1:T(8,128)(2,1)S(1)}, bf16[256,768]{0,1:T(8,128)(2,1)S(1)}, u32[]{:S(2)}, u32[]{:S(2)}) collective-permute-start(bf16[256,768]{0,1:T(8,128)(2,1)S(1)} %get-tuple-element.297), channel_id=1, source_target_pairs={{0,16},{2,18},{4,20},{6,22},{8,24},{10,26},{12,28},{14,30},{16,0},... | collective-permute-start | bytes 1179656 | tf_op jit(solution)/shard_map/ppermute | solution.py:36
  769.6 16.2 %collective-permute-done.61 = bf16[1024,768]{0,1:T(8,128)(2,1)} collective-permute-done((bf16[1024,768]{0,1:T(8,128)(2,1)}, bf16[1024,768]{0,1:T(8,128)(2,1)}, u32[]{:S(2)}, u32[]{:S(2)}) %collective-permute-start.61) | collective-permute-done | bytes 1572896 | tf_op jit(solution)/shard_map/ppermute | solution.py:36
  785.8 16.1 %collective-permute-start.70 = (bf16[256,768]{0,1:T(8,128)(2,1)S(1)}, bf16[256,768]{0,1:T(8,128)(2,1)S(1)}, u32[]{:S(2)}, u32[]{:S(2)}) collective-permute-start(bf16[256,768]{0,1:T(8,128)(2,1)S(1)} %get-tuple-element.295), channel_id=1, source_target_pairs={{0,8},{2,10},{4,12},{6,14},{8,0},{10,2},{12,4},{14,6},{16,24},{18,... | collective-permute-start | bytes 1179656 | tf_op jit(solution)/shard_map/ppermute | solution.py:36
  804.3 14.8 %collective-permute-done.57 = bf16[1024,768]{0,1:T(8,128)(2,1)} collective-permute-done((bf16[1024,768]{0,1:T(8,128)(2,1)}, bf16[1024,768]{0,1:T(8,128)(2,1)}, u32[]{:S(2)}, u32[]{:S(2)}) %collective-permute-start.57) | collective-permute-done | bytes 1572896 | tf_op jit(solution)/shard_map/ppermute | solution.py:36
  822.5 16.6 %collective-permute-start.67 = (bf16[256,768]{0,1:T(8,128)(2,1)S(1)}, bf16[256,768]{0,1:T(8,128)(2,1)S(1)}, u32[]{:S(2)}, u32[]{:S(2)}) collective-permute-start(bf16[256,768]{0,1:T(8,128)(2,1)S(1)} %get-tuple-element.294), channel_id=1, source_target_pairs={{0,16},{2,18},{4,20},{6,22},{8,24},{10,26},{12,28},{14,30},{16,0},... | collective-permute-start | bytes 1179656 | tf_op jit(solution)/shard_map/ppermute | solution.py:36
  840.8 14.3 %collective-permute-start.63 = (bf16[256,768]{0,1:T(8,128)(2,1)S(1)}, bf16[256,768]{0,1:T(8,128)(2,1)S(1)}, u32[]{:S(2)}, u32[]{:S(2)}) collective-permute-start(bf16[256,768]{0,1:T(8,128)(2,1)S(1)} %get-tuple-element.291), channel_id=1, source_target_pairs={{0,16},{2,18},{4,20},{6,22},{8,24},{10,26},{12,28},{14,30},{16,0},... | collective-permute-start | bytes 1179656 | tf_op jit(solution)/shard_map/ppermute | solution.py:36
  855.1 25.3 %collective-permute-done.67 = bf16[256,768]{0,1:T(8,128)(2,1)S(1)} collective-permute-done((bf16[256,768]{0,1:T(8,128)(2,1)S(1)}, bf16[256,768]{0,1:T(8,128)(2,1)S(1)}, u32[]{:S(2)}, u32[]{:S(2)}) %collective-permute-start.67) | collective-permute-done | bytes 393248 | tf_op jit(solution)/shard_map/ppermute | solution.py:36
  881.9 29.7 %collective-permute-done.63 = bf16[256,768]{0,1:T(8,128)(2,1)S(1)} collective-permute-done((bf16[256,768]{0,1:T(8,128)(2,1)S(1)}, bf16[256,768]{0,1:T(8,128)(2,1)S(1)}, u32[]{:S(2)}, u32[]{:S(2)}) %collective-permute-start.63) | collective-permute-done | bytes 393248 | tf_op jit(solution)/shard_map/ppermute | solution.py:36
  913.7 15.9 %collective-permute-done.59 = bf16[256,768]{0,1:T(8,128)(2,1)S(1)} collective-permute-done((bf16[256,768]{0,1:T(8,128)(2,1)S(1)}, bf16[256,768]{0,1:T(8,128)(2,1)S(1)}, u32[]{:S(2)}, u32[]{:S(2)}) %collective-permute-start.59) | collective-permute-done | bytes 393248 | tf_op jit(solution)/shard_map/ppermute | solution.py:36
  941.7 24.5 %collective-permute-done.73 = bf16[128,768]{0,1:T(8,128)(2,1)S(1)} collective-permute-done((bf16[128,768]{0,1:T(8,128)(2,1)S(1)}, bf16[128,768]{0,1:T(8,128)(2,1)S(1)}, u32[]{:S(2)}, u32[]{:S(2)}) %collective-permute-start.73) | collective-permute-done | bytes 196640 | tf_op jit(solution)/shard_map/ppermute | solution.py:36
  982.7 8.6 convert_add_fusion.2
  997.4 13.7 %convert_add_fusion.1 = f32[1024,2048]{1,0:T(8,128)} fusion(bf16[1024,2048]{1,0:T(8,128)(2,1)} %collective-permute-done.48, f32[1024,2048]{1,0:T(8,128)} %fusion.14, f32[1024,2048]{1,0:T(8,128)} %fusion.44), kind=kLoop, calls=%fused_computation.18 | loop fusion | flops 6291456 | bytes 29360128 | tf_op jit(solution)/shard_map/add | solution.py:646
  1055.9 29.9 %collective-permute-done.49 = bf16[512,2048]{1,0:T(8,128)(2,1)} collective-permute-done((bf16[512,2048]{1,0:T(8,128)(2,1)}, bf16[512,2048]{1,0:T(8,128)(2,1)}, u32[]{:S(2)}, u32[]{:S(2)}) %collective-permute-start.49) | collective-permute-done | bytes 2097184 | tf_op jit(solution)/shard_map/ppermute | solution.py:36
  (722 shorter events, 547.6 us)
Async XLA Ops:
  62.9 41.1 %collective-permute-start.38 = (bf16[256,768]{0,1:T(8,128)(2,1)}, bf16[256,768]{0,1:T(8,128)(2,1)S(1)}, u32[]{:S(2)}, u32[]{:S(2)}) collective-permute-start(bf16[256,768]{0,1:T(8,128)(2,1)} %get-tuple-element.261), channel_id=1, source_target_pairs={{0,16},{2,18},{4,20},{6,22},{8,24},{10,26},{12,28},{14,30},{16,0},... | collective-permute-start | bytes 1179656 | tf_op jit(solution)/shard_map/ppermute | solution.py:36
  66.1 40.9 %collective-permute-start.39 = (bf16[256,768]{0,1:T(8,128)(2,1)}, bf16[256,768]{0,1:T(8,128)(2,1)S(1)}, u32[]{:S(2)}, u32[]{:S(2)}) collective-permute-start(bf16[256,768]{0,1:T(8,128)(2,1)} %get-tuple-element.261), channel_id=1, source_target_pairs={{0,24},{2,26},{4,28},{6,30},{8,16},{10,18},{12,20},{14,22},{16,8},... | collective-permute-start | bytes 1179656 | tf_op jit(solution)/shard_map/ppermute | solution.py:36
  67.5 40.0 %collective-permute-start.40 = (bf16[256,768]{0,1:T(8,128)(2,1)}, bf16[256,768]{0,1:T(8,128)(2,1)S(1)}, u32[]{:S(2)}, u32[]{:S(2)}) collective-permute-start(bf16[256,768]{0,1:T(8,128)(2,1)} %get-tuple-element.261), channel_id=1, source_target_pairs={{0,4},{2,6},{4,0},{6,2},{8,12},{10,14},{12,8},{14,10},{16,20},{18,... | collective-permute-start | bytes 1179656 | tf_op jit(solution)/shard_map/ppermute | solution.py:36
  69.3 50.1 %collective-permute-start.30 = (bf16[256,768]{0,1:T(8,128)(2,1)S(1)}, bf16[256,768]{0,1:T(8,128)(2,1)S(1)}, u32[]{:S(2)}, u32[]{:S(2)}) collective-permute-start(bf16[256,768]{0,1:T(8,128)(2,1)S(1)} %get-tuple-element.253), channel_id=1, source_target_pairs={{0,8},{2,10},{4,12},{6,14},{8,0},{10,2},{12,4},{14,6},{16,24},{18,... | collective-permute-start | bytes 1179656 | tf_op jit(solution)/shard_map/ppermute | solution.py:36
  69.4 60.0 %collective-permute-start.31 = (bf16[256,768]{0,1:T(8,128)(2,1)S(1)}, bf16[256,768]{0,1:T(8,128)(2,1)S(1)}, u32[]{:S(2)}, u32[]{:S(2)}) collective-permute-start(bf16[256,768]{0,1:T(8,128)(2,1)S(1)} %get-tuple-element.253), channel_id=1, source_target_pairs={{0,16},{2,18},{4,20},{6,22},{8,24},{10,26},{12,28},{14,30},{16,0},... | collective-permute-start | bytes 1179656 | tf_op jit(solution)/shard_map/ppermute | solution.py:36
  107.5 44.0 %collective-permute-start.23 = (bf16[256,768]{0,1:T(8,128)(2,1)S(1)}, bf16[256,768]{0,1:T(8,128)(2,1)S(1)}, u32[]{:S(2)}, u32[]{:S(2)}) collective-permute-start(bf16[256,768]{0,1:T(8,128)(2,1)S(1)} %get-tuple-element.251), channel_id=1, source_target_pairs={{0,8},{2,10},{4,12},{6,14},{8,0},{10,2},{12,4},{14,6},{16,24},{18,... | collective-permute-start | bytes 1179656 | tf_op jit(solution)/shard_map/ppermute | solution.py:36
  119.4 43.7 %collective-permute-start.24 = (bf16[256,768]{0,1:T(8,128)(2,1)S(1)}, bf16[256,768]{0,1:T(8,128)(2,1)S(1)}, u32[]{:S(2)}, u32[]{:S(2)}) collective-permute-start(bf16[256,768]{0,1:T(8,128)(2,1)S(1)} %get-tuple-element.251), channel_id=1, source_target_pairs={{0,16},{2,18},{4,20},{6,22},{8,24},{10,26},{12,28},{14,30},{16,0},... | collective-permute-start | bytes 1179656 | tf_op jit(solution)/shard_map/ppermute | solution.py:36
  151.5 41.1 %collective-permute-start.5 = (bf16[256,768]{0,1:T(8,128)(2,1)S(1)}, bf16[256,768]{0,1:T(8,128)(2,1)S(1)}, u32[]{:S(2)}, u32[]{:S(2)}) collective-permute-start(bf16[256,768]{0,1:T(8,128)(2,1)S(1)} %get-tuple-element.249), channel_id=1, source_target_pairs={{0,16},{2,18},{4,20},{6,22},{8,24},{10,26},{12,28},{14,30},{16,0},... | collective-permute-start | bytes 1179656 | tf_op jit(solution)/shard_map/ppermute | solution.py:36
  163.1 98.7 %collective-permute-start.1 = (bf16[512,2048]{1,0:T(8,128)(2,1)S(1)}, bf16[512,2048]{1,0:T(8,128)(2,1)S(1)}, u32[]{:S(2)}, u32[]{:S(2)}) collective-permute-start(bf16[512,2048]{1,0:T(8,128)(2,1)S(1)} %copy-done.47), channel_id=1, source_target_pairs={{0,2},{2,0},{4,6},{6,4},{8,10},{10,8},{12,14},{14,12},{16,18},{18,... | collective-permute-start | bytes 6291464 | tf_op jit(solution)/shard_map/ppermute | solution.py:36
  221.5 69.5 %collective-permute-start = (bf16[512,2048]{1,0:T(8,128)(2,1)S(1)}, bf16[512,2048]{1,0:T(8,128)(2,1)S(1)}, u32[]{:S(2)}, u32[]{:S(2)}) collective-permute-start(bf16[512,2048]{1,0:T(8,128)(2,1)S(1)} %copy-done.47), channel_id=1, source_target_pairs={{0,1},{1,0},{2,3},{3,2},{4,5},{5,4},{6,7},{7,6},{8,9},{9,8},{10,11... | collective-permute-start | bytes 6291464 | tf_op jit(solution)/shard_map/ppermute | solution.py:36
  230.0 61.1 %collective-permute-start.12 = (bf16[512,2048]{1,0:T(8,128)(2,1)S(1)}, bf16[512,2048]{1,0:T(8,128)(2,1)}, u32[]{:S(2)}, u32[]{:S(2)}) collective-permute-start(bf16[512,2048]{1,0:T(8,128)(2,1)S(1)} %copy-done.46), channel_id=1, source_target_pairs={{0,2},{2,0},{4,6},{6,4},{8,10},{10,8},{12,14},{14,12},{16,18},{18,... | collective-permute-start | bytes 6291464 | tf_op jit(solution)/shard_map/ppermute | solution.py:36
  255.2 38.5 %collective-permute-start.11 = (bf16[512,2048]{1,0:T(8,128)(2,1)S(1)}, bf16[512,2048]{1,0:T(8,128)(2,1)S(1)}, u32[]{:S(2)}, u32[]{:S(2)}) collective-permute-start(bf16[512,2048]{1,0:T(8,128)(2,1)S(1)} %copy-done.46), channel_id=1, source_target_pairs={{0,1},{1,0},{2,3},{3,2},{4,5},{5,4},{6,7},{7,6},{8,9},{9,8},{10,11... | collective-permute-start | bytes 6291464 | tf_op jit(solution)/shard_map/ppermute | solution.py:36
  679.5 252.4 %collective-permute-start.50 = (f32[2048,256]{1,0:T(8,128)}, f32[2048,256]{1,0:T(8,128)}, u32[]{:S(2)}, u32[]{:S(2)}) collective-permute-start(f32[2048,256]{1,0:T(8,128)} %get-tuple-element.82), channel_id=1, source_target_pairs={{0,1},{1,0},{2,3},{3,2},{4,5},{5,4},{6,7},{7,6},{8,9},{9,8},{10,11... | collective-permute-start | bytes 6291464 | tf_op jit(solution)/shard_map/ppermute | solution.py:36
  680.9 56.5 %collective-permute-start.69 = (bf16[1024,768]{0,1:T(8,128)(2,1)}, bf16[1024,768]{0,1:T(8,128)(2,1)}, u32[]{:S(2)}, u32[]{:S(2)}) collective-permute-start(bf16[1024,768]{0,1:T(8,128)(2,1)} %pad_maximum_fusion.10), channel_id=1, source_target_pairs={{0,4},{2,6},{4,0},{6,2},{8,12},{10,14},{12,8},{14,10},{16,20},{18,... | collective-permute-start | bytes 4718600 | tf_op jit(solution)/shard_map/ppermute | solution.py:36
  683.7 68.4 %collective-permute-start.65 = (bf16[1024,768]{0,1:T(8,128)(2,1)}, bf16[1024,768]{0,1:T(8,128)(2,1)}, u32[]{:S(2)}, u32[]{:S(2)}) collective-permute-start(bf16[1024,768]{0,1:T(8,128)(2,1)} %pad_maximum_fusion.9), channel_id=1, source_target_pairs={{0,4},{2,6},{4,0},{6,2},{8,12},{10,14},{12,8},{14,10},{16,20},{18,... | collective-permute-start | bytes 4718600 | tf_op jit(solution)/shard_map/ppermute | solution.py:36
  685.5 100.3 %collective-permute-start.61 = (bf16[1024,768]{0,1:T(8,128)(2,1)}, bf16[1024,768]{0,1:T(8,128)(2,1)}, u32[]{:S(2)}, u32[]{:S(2)}) collective-permute-start(bf16[1024,768]{0,1:T(8,128)(2,1)} %pad_maximum_fusion.8), channel_id=1, source_target_pairs={{0,4},{2,6},{4,0},{6,2},{8,12},{10,14},{12,8},{14,10},{16,20},{18,... | collective-permute-start | bytes 4718600 | tf_op jit(solution)/shard_map/ppermute | solution.py:36
  688.3 130.8 %collective-permute-start.57 = (bf16[1024,768]{0,1:T(8,128)(2,1)}, bf16[1024,768]{0,1:T(8,128)(2,1)}, u32[]{:S(2)}, u32[]{:S(2)}) collective-permute-start(bf16[1024,768]{0,1:T(8,128)(2,1)} %pad_maximum_fusion.7), channel_id=1, source_target_pairs={{0,4},{2,6},{4,0},{6,2},{8,12},{10,14},{12,8},{14,10},{16,20},{18,... | collective-permute-start | bytes 4718600 | tf_op jit(solution)/shard_map/ppermute | solution.py:36
  739.9 82.5 %collective-permute-start.72 = (bf16[256,768]{0,1:T(8,128)(2,1)S(1)}, bf16[256,768]{0,1:T(8,128)(2,1)S(1)}, u32[]{:S(2)}, u32[]{:S(2)}) collective-permute-start(bf16[256,768]{0,1:T(8,128)(2,1)S(1)} %get-tuple-element.296), channel_id=1, source_target_pairs={{0,24},{2,26},{4,28},{6,30},{8,16},{10,18},{12,20},{14,22},{16,8},... | collective-permute-start | bytes 1179656 | tf_op jit(solution)/shard_map/ppermute | solution.py:36
  752.1 87.0 %collective-permute-start.71 = (bf16[256,768]{0,1:T(8,128)(2,1)S(1)}, bf16[256,768]{0,1:T(8,128)(2,1)S(1)}, u32[]{:S(2)}, u32[]{:S(2)}) collective-permute-start(bf16[256,768]{0,1:T(8,128)(2,1)S(1)} %get-tuple-element.297), channel_id=1, source_target_pairs={{0,16},{2,18},{4,20},{6,22},{8,24},{10,26},{12,28},{14,30},{16,0},... | collective-permute-start | bytes 1179656 | tf_op jit(solution)/shard_map/ppermute | solution.py:36
  785.8 53.5 %collective-permute-start.70 = (bf16[256,768]{0,1:T(8,128)(2,1)S(1)}, bf16[256,768]{0,1:T(8,128)(2,1)S(1)}, u32[]{:S(2)}, u32[]{:S(2)}) collective-permute-start(bf16[256,768]{0,1:T(8,128)(2,1)S(1)} %get-tuple-element.295), channel_id=1, source_target_pairs={{0,8},{2,10},{4,12},{6,14},{8,0},{10,2},{12,4},{14,6},{16,24},{18,... | collective-permute-start | bytes 1179656 | tf_op jit(solution)/shard_map/ppermute | solution.py:36
  822.5 57.9 %collective-permute-start.67 = (bf16[256,768]{0,1:T(8,128)(2,1)S(1)}, bf16[256,768]{0,1:T(8,128)(2,1)S(1)}, u32[]{:S(2)}, u32[]{:S(2)}) collective-permute-start(bf16[256,768]{0,1:T(8,128)(2,1)S(1)} %get-tuple-element.294), channel_id=1, source_target_pairs={{0,16},{2,18},{4,20},{6,22},{8,24},{10,26},{12,28},{14,30},{16,0},... | collective-permute-start | bytes 1179656 | tf_op jit(solution)/shard_map/ppermute | solution.py:36
  839.1 41.5 %collective-permute-start.66 = (bf16[256,768]{0,1:T(8,128)(2,1)S(1)}, bf16[256,768]{0,1:T(8,128)(2,1)S(1)}, u32[]{:S(2)}, u32[]{:S(2)}) collective-permute-start(bf16[256,768]{0,1:T(8,128)(2,1)S(1)} %get-tuple-element.292), channel_id=1, source_target_pairs={{0,8},{2,10},{4,12},{6,14},{8,0},{10,2},{12,4},{14,6},{16,24},{18,... | collective-permute-start | bytes 1179656 | tf_op jit(solution)/shard_map/ppermute | solution.py:36
  839.3 41.6 %collective-permute-start.64 = (bf16[256,768]{0,1:T(8,128)(2,1)S(1)}, bf16[256,768]{0,1:T(8,128)(2,1)S(1)}, u32[]{:S(2)}, u32[]{:S(2)}) collective-permute-start(bf16[256,768]{0,1:T(8,128)(2,1)S(1)} %get-tuple-element.290), channel_id=1, source_target_pairs={{0,24},{2,26},{4,28},{6,30},{8,16},{10,18},{12,20},{14,22},{16,8},... | collective-permute-start | bytes 1179656 | tf_op jit(solution)/shard_map/ppermute | solution.py:36
  840.8 70.8 %collective-permute-start.63 = (bf16[256,768]{0,1:T(8,128)(2,1)S(1)}, bf16[256,768]{0,1:T(8,128)(2,1)S(1)}, u32[]{:S(2)}, u32[]{:S(2)}) collective-permute-start(bf16[256,768]{0,1:T(8,128)(2,1)S(1)} %get-tuple-element.291), channel_id=1, source_target_pairs={{0,16},{2,18},{4,20},{6,22},{8,24},{10,26},{12,28},{14,30},{16,0},... | collective-permute-start | bytes 1179656 | tf_op jit(solution)/shard_map/ppermute | solution.py:36
  880.6 102.1 %collective-permute-start.46 = (bf16[1024,2048]{1,0:T(8,128)(2,1)}, bf16[1024,2048]{1,0:T(8,128)(2,1)}, u32[]{:S(2)}, u32[]{:S(2)}) collective-permute-start(bf16[1024,2048]{1,0:T(8,128)(2,1)} %convolution_convert_fusion), channel_id=1, source_target_pairs={{0,1},{1,0},{2,3},{3,2},{4,5},{5,4},{6,7},{7,6},{8,9},{9,8},{10,11... | collective-permute-start | bytes 12582920 | tf_op jit(solution)/shard_map/ppermute | solution.py:36
  937.5 59.9 %collective-permute-start.48 = (bf16[1024,2048]{1,0:T(8,128)(2,1)}, bf16[1024,2048]{1,0:T(8,128)(2,1)}, u32[]{:S(2)}, u32[]{:S(2)}) collective-permute-start(bf16[1024,2048]{1,0:T(8,128)(2,1)} %add_convert_fusion), channel_id=1, source_target_pairs={{0,1},{1,0},{2,3},{3,2},{4,5},{5,4},{6,7},{7,6},{8,9},{9,8},{10,11... | collective-permute-start | bytes 12582920 | tf_op jit(solution)/shard_map/ppermute | solution.py:36
  981.7 43.0 %collective-permute-start.77 = (bf16[8,1,128,160]{3,2,0,1:T(8,128)(2,1)}, bf16[8,1,128,160]{3,2,0,1:T(8,128)(2,1)}, u32[]{:S(2)}, u32[]{:S(2)}) collective-permute-start(bf16[8,1,128,160]{3,2,0,1:T(8,128)(2,1)} %copy.392), channel_id=1, source_target_pairs={{0,2},{2,0},{4,6},{6,4},{8,10},{10,8},{12,14},{14,12},{16,18},{18,... | collective-permute-start | bytes 983048 | tf_op jit(solution)/shard_map/ppermute | solution.py:36
  996.3 48.9 %collective-permute-start.47 = (bf16[512,2048]{1,0:T(8,128)(2,1)}, bf16[512,2048]{1,0:T(8,128)(2,1)}, u32[]{:S(2)}, u32[]{:S(2)}) collective-permute-start(bf16[512,2048]{1,0:T(8,128)(2,1)} %slice.924), channel_id=1, source_target_pairs={{0,2},{2,0},{4,6},{6,4},{8,10},{10,8},{12,14},{14,12},{16,18},{18,... | collective-permute-start | bytes 6291464 | tf_op jit(solution)/shard_map/ppermute | solution.py:36
  1015.1 70.7 %collective-permute-start.49 = (bf16[512,2048]{1,0:T(8,128)(2,1)}, bf16[512,2048]{1,0:T(8,128)(2,1)}, u32[]{:S(2)}, u32[]{:S(2)}) collective-permute-start(bf16[512,2048]{1,0:T(8,128)(2,1)} %slice.923), channel_id=1, source_target_pairs={{0,2},{2,0},{4,6},{6,4},{8,10},{10,8},{12,14},{14,12},{16,18},{18,... | collective-permute-start | bytes 6291464 | tf_op jit(solution)/shard_map/ppermute | solution.py:36
  1032.4 72.9 %collective-permute-start.81 = (bf16[128,160]{1,0:T(8,128)(2,1)S(1)}, bf16[128,160]{1,0:T(8,128)(2,1)S(1)}, u32[]{:S(2)}, u32[]{:S(2)}) collective-permute-start(bf16[128,160]{1,0:T(8,128)(2,1)S(1)} %get-tuple-element.318), channel_id=1, source_target_pairs={{0,24},{2,26},{4,28},{6,30},{8,16},{10,18},{12,20},{14,22},{16,8},... | collective-permute-start | bytes 122888 | tf_op jit(solution)/shard_map/ppermute | solution.py:36
  1034.0 71.3 %collective-permute-start.80 = (bf16[128,160]{1,0:T(8,128)(2,1)S(1)}, bf16[128,160]{1,0:T(8,128)(2,1)S(1)}, u32[]{:S(2)}, u32[]{:S(2)}) collective-permute-start(bf16[128,160]{1,0:T(8,128)(2,1)S(1)} %get-tuple-element.319), channel_id=1, source_target_pairs={{0,16},{2,18},{4,20},{6,22},{8,24},{10,26},{12,28},{14,30},{16,0},... | collective-permute-start | bytes 122888 | tf_op jit(solution)/shard_map/ppermute | solution.py:36
  1036.0 69.3 %collective-permute-start.79 = (bf16[128,160]{1,0:T(8,128)(2,1)S(1)}, bf16[128,160]{1,0:T(8,128)(2,1)S(1)}, u32[]{:S(2)}, u32[]{:S(2)}) collective-permute-start(bf16[128,160]{1,0:T(8,128)(2,1)S(1)} %get-tuple-element.317), channel_id=1, source_target_pairs={{0,8},{2,10},{4,12},{6,14},{8,0},{10,2},{12,4},{14,6},{16,24},{18,... | collective-permute-start | bytes 122888 | tf_op jit(solution)/shard_map/ppermute | solution.py:36
  (184 other events, 3149.6 us)

commit v2 on v1

v2 whole, which is shorter than its diff:
```python
import functools

import jax
import jax.numpy as jnp
from jax import lax
from jax.experimental import pallas as pl
from jax.experimental.pallas import tpu as pltpu
from jax.sharding import PartitionSpec as P

BLOCK = 256
LANES = 128
TILE = 256
WIDTH = 64
GROUP = TILE // WIDTH
EPSILON = 1e-05
HIGH = lax.Precision.HIGHEST
BF16 = jnp.bfloat16
F32 = jnp.float32
VMEM_LIMIT = 58 * 2**20

NN = (((1,), (0,)), ((), ()))
NT = (((1,), (1,)), ((), ()))
TN = (((0,), (0,)), ((), ()))


def dot(a, b, dims=NN, precision=None):
    return lax.dot_general(a, b, dims, precision=precision, preferred_element_type=F32)


def low_dot(a, b, dims=NN):
    return dot(a.astype(BF16), b.astype(BF16), dims)


def flip(a, axis, bit):
    size = lax.axis_size(axis)
    return lax.ppermute(a, axis, [(i, i ^ bit) for i in range(size)])


def sigmoid(q):
    return 1.0 / (1.0 + jnp.exp(-q))


def owner_block(number, dp, extent):
    y, z, x = number // (extent // 2), (number // 2) % (extent // 4), number % 2
    return jnp.bitwise_xor(dp - lax.rem(dp, 2), (y * 2) + (z * 4) + x)


def norm_kernel(place_ref, hidden_ref, cot_ref, gain_ref, normed_ref, cot_out_ref, inv_ref, *, extent):
    u = hidden_ref[...].astype(F32)
    inv = lax.rsqrt(jnp.mean(u * u, axis=-1, keepdims=True) + EPSILON)
    inv_ref[...] = inv
    for number in range(extent):
        start = pl.multiple_of(owner_block(number, place_ref[0], extent) * LANES, LANES)
        piece = hidden_ref[:, pl.ds(start, LANES)].astype(F32)
        gain = gain_ref[:, pl.ds(start, LANES)]
        normed_ref[:, number * LANES : (number + 1) * LANES] = (piece * inv * gain).astype(BF16)
        cot_out_ref[:, number * LANES : (number + 1) * LANES] = cot_ref[:, pl.ds(start, LANES)]


def input_norm(hidden, cot, gain, dp, extent):
    rows, width = hidden.shape
    if width // extent != LANES:
        u = hidden.astype(F32)
        inv = lax.rsqrt(jnp.mean(u * u, axis=-1, keepdims=True) + EPSILON)
        normed = (u * inv * gain).astype(BF16)
        order = owner_block(jnp.arange(extent), dp, extent)

        def arranged(a):
            return jnp.take(a.reshape(rows, extent, -1), order, axis=1).reshape(rows, width)

        return arranged(normed), arranged(cot), inv
    step = 128
    tile = pl.BlockSpec((step, width), lambda i: (i, 0))
    return pl.pallas_call(
        functools.partial(norm_kernel, extent=extent),
        grid=(rows // step,),
        in_specs=[
            pl.BlockSpec(memory_space=pltpu.SMEM),
            tile,
            tile,
            pl.BlockSpec((1, width), lambda i: (0, 0)),
        ],
        out_specs=[tile, tile, pl.BlockSpec((step, 1), lambda i: (i, 0))],
        out_shape=[
            jax.ShapeDtypeStruct((rows, width), BF16),
            jax.ShapeDtypeStruct((rows, width), BF16),
            jax.ShapeDtypeStruct((rows, 1), F32),
        ],
        compiler_params=pltpu.CompilerParams(vmem_limit_bytes=VMEM_LIMIT),
    )(dp.reshape(1), hidden, cot, gain.reshape(1, width))


def restore_kernel(place_ref, in_ref, out_ref, *, extent):
    for number in range(extent):
        start = pl.multiple_of(owner_block(number, place_ref[0], extent) * LANES, LANES)
        out_ref[:, pl.ds(start, LANES)] = in_ref[:, number * LANES : (number + 1) * LANES]


def restore_order(a, dp, extent):
    rows, width = a.shape
    if width // extent != LANES:
        order = owner_block(jnp.arange(extent), dp, extent)
        back = jnp.argsort(order)
        return jnp.take(a.reshape(rows, extent, -1), back, axis=1).reshape(rows, width)
    step = 128
    tile = pl.BlockSpec((step, width), lambda i: (i, 0))
    return pl.pallas_call(
        functools.partial(restore_kernel, extent=extent),
        grid=(rows // step,),
        in_specs=[pl.BlockSpec(memory_space=pltpu.SMEM), tile],
        out_specs=tile,
        out_shape=jax.ShapeDtypeStruct((rows, width), a.dtype),
        compiler_params=pltpu.CompilerParams(vmem_limit_bytes=VMEM_LIMIT),
    )(dp.reshape(1), a)


VALID, LINK, KEEP, SEG = 0, 3, 4, 5
COLS = 8
HEADS = 16
TAPS, BIAS, SKIP, GAIN = 0, 4, 5, 6
ANY = pl.BlockSpec(memory_space=pl.ANY)


def iota(shape, axis):
    return lax.broadcasted_iota(jnp.int32, shape, axis)


def thirds(a):
    high = a.astype(BF16)
    rest = a - high.astype(F32)
    mid = rest.astype(BF16)
    return [high, mid, (rest - mid.astype(F32)).astype(BF16)]


def halves(a):
    high = a.astype(BF16)
    return [high, (a - high.astype(F32)).astype(BF16)]


def conv_of(v, col_ref, par_ref, length):
    result = par_ref[BIAS : BIAS + 1, :] + par_ref[TAPS + 3 : TAPS + 4, :] * v
    for offset in range(1, 4):
        valid = col_ref[:, VALID + offset - 1 : VALID + offset]
        result = result + par_ref[TAPS + 3 - offset : TAPS + 4 - offset, :] * (
            pltpu.roll(v, offset, 0) * valid
        )
    return result


def pair_mask(seg_col, seg_row, transposed):
    down, across = iota((BLOCK, BLOCK), 0), iota((BLOCK, BLOCK), 1)
    causal = down <= across if transposed else down >= across
    return causal & (seg_col == seg_row)


def table_kernel(
    normed_ref, weight_ref, seg_col_ref, seg_row_ref, par_ref, head_ref,
    proj_ref, bc_ref, wide_ref, col_ref, row_ref, score_ref, turned_ref,
):
    length = seg_col_ref.shape[0]
    proj = dot(normed_ref[...], weight_ref[...])
    proj_ref[...] = proj[:, : 2 * LANES]
    raw = proj[:, 2 * LANES :] + head_ref[0:1, :HEADS]
    dt = jnp.maximum(raw, 0.0) + jnp.log1p(jnp.exp(-jnp.abs(raw)))
    step = dt * head_ref[1:2, :HEADS]
    seg = seg_col_ref[...]
    place = iota((length, 1), 0)
    number = place // BLOCK
    before, last = jnp.full((length, 1), -2.0, F32), jnp.zeros((length, 1), F32)
    for block in range(length // BLOCK):
        end = seg[(block + 1) * BLOCK - 1 : (block + 1) * BLOCK, :]
        last = jnp.where(number == block, end, last)
        before = jnp.where(number == block + 1, end, before)
    lower = (iota((BLOCK, BLOCK), 0) >= iota((BLOCK, BLOCK), 1)).astype(F32)
    upper = (iota((BLOCK, BLOCK), 0) <= iota((BLOCK, BLOCK), 1)).astype(F32)
    eye = (iota((BLOCK, BLOCK), 0) == iota((BLOCK, BLOCK), 1)).astype(F32)
    cums = []
    for block in range(length // BLOCK):
        rows = slice(block * BLOCK, (block + 1) * BLOCK)
        cums.append(dot(lower, step[rows], NN, HIGH))
        cum_rows = dot(step[rows], upper, TN, HIGH)
        raw_rows = dot(raw[rows], eye, TN, HIGH)
        for tile in range(HEADS // GROUP):
            heads = slice(tile * GROUP, (tile + 1) * GROUP)
            row_ref[tile * 8 : (tile + 1) * 8, rows] = jnp.concatenate(
                [cum_rows[heads], raw_rows[heads]], axis=0
            )
    cum = jnp.concatenate(cums, axis=0)
    lane = iota((length, COLS), 1)
    col = jnp.zeros((length, COLS), F32)
    for offset in range(1, 4):
        valid = (pltpu.roll(seg, offset, 0) == seg) & (place >= offset)
        col = jnp.where(lane == VALID + offset - 1, valid.astype(F32), col)
    col = jnp.where(lane == LINK, (seg == before).astype(F32), col)
    col = jnp.where(lane == KEEP, (seg == last).astype(F32), col)
    col_ref[...] = jnp.where(lane == SEG, seg, col)
    wide_ref[...] = jnp.concatenate(
        thirds(dt) + thirds(cum) + [jnp.zeros((length, LANES - 6 * HEADS), BF16)], axis=1
    )
    conv = conv_of(proj_ref[...], col_ref, par_ref, length)
    bc_ref[...] = conv * sigmoid(conv)
    for block in range(length // BLOCK):
        rows = slice(block * BLOCK, (block + 1) * BLOCK)
        b_rows, c_rows = bc_ref[rows, :LANES], bc_ref[rows, LANES:]
        seg_col, seg_row = seg[rows], seg_row_ref[:, rows]
        score_ref[rows, :] = jnp.where(
            pair_mask(seg_col, seg_row, False), dot(c_rows, b_rows, NT, HIGH), 0.0
        )
        turned_ref[rows, :] = jnp.where(
            pair_mask(seg_col, seg_row, True), dot(b_rows, c_rows, NT, HIGH), 0.0
        )


def forward_kernel(*refs, pieces):
    (
        normed_ref, cot_ref, bc_ref, wide_ref, pick_ref, col_ref, row_ref, score_ref, par_ref, sum_in_ref,
        w_ref, z_ref, dyn_ref, y_ref, state_ref, sum_ref, xs_ref, carry_ref,
    ) = refs[pieces:]
    length = xs_ref.shape[0]
    blocks = length // BLOCK

    @pl.when(pl.program_id(0) == 0)
    def _():
        depth = refs[0].shape[0]
        for number in range(pieces):
            w_ref[number * depth : (number + 1) * depth, :] = refs[number][...]

    def project(number, carried):
        rows = pl.ds(pl.multiple_of(number * BLOCK, BLOCK), BLOCK)
        z_ref[rows, :] = dot(normed_ref[rows, :], w_ref[:, : 2 * TILE])
        dyn_ref[rows, :] = dot(cot_ref[rows, :], w_ref[:, 2 * TILE :])
        return carried

    lax.fori_loop(0, blocks, project, 0)
    conv = conv_of(z_ref[:, TILE:], col_ref, par_ref, length)
    xs_ref[...] = conv * sigmoid(conv)
    carry_ref[...] = jnp.zeros_like(carry_ref)

    def one_block(number, carried):
        rows = pl.ds(pl.multiple_of(number * BLOCK, BLOCK), BLOCK)
        b_rows, c_rows = bc_ref[rows, :LANES], bc_ref[rows, LANES:]
        col = col_ref[rows, :]
        scores = score_ref[rows, :]
        x = xs_ref[rows, :]
        wide = dot(wide_ref[rows, :], pick_ref[...])
        dt_wide, cum_wide = wide[:, :TILE], wide[:, TILE:]
        dtx = x * dt_wide
        dtx_low = dtx.astype(BF16)
        parts = []
        for head in range(GROUP):
            gap = cum_wide[:, head * WIDTH : head * WIDTH + 1] - row_ref[head : head + 1, rows]
            mixing = scores * jnp.exp(jnp.minimum(gap, 0.0))
            parts.append(dot(mixing.astype(BF16), dtx_low[:, head * WIDTH : (head + 1) * WIDTH]))
        within = jnp.concatenate(parts, axis=1)
        state = carry_ref[...]
        state_ref[number] = state
        decay = jnp.exp(cum_wide) * col[:, LINK : LINK + 1]
        y = within + low_dot(c_rows, state) * decay + par_ref[SKIP : SKIP + 1, :] * x
        weight = jnp.exp(cum_wide[BLOCK - 1 :, :] - cum_wide) * col[:, KEEP : KEEP + 1]
        carry_ref[...] = state * decay[BLOCK - 1 :, :] + low_dot(b_rows, dtx * weight, TN)
        y_ref[rows, :] = y
        z = z_ref[rows, :TILE]
        yg = y * z * sigmoid(z)
        first = jnp.sum(yg * yg, axis=1, keepdims=True)
        second = jnp.sum(yg * par_ref[GAIN : GAIN + 1, :] * dyn_ref[rows, :], axis=1, keepdims=True)
        lane = iota((BLOCK, 8), 1)
        sum_ref[rows, :] = sum_in_ref[rows, :] + jnp.where(
            lane == 0, first, jnp.where(lane == 1, second, 0.0)
        )
        return carried

    lax.fori_loop(0, blocks, one_block, 0)


def backward_tile(
    origin, z_ref, y_ref, dyn_ref, bc_ref, wide_ref, pick_ref, col_ref, row_ref, seg_ref, turned_ref, norm_ref,
    par_ref, state_ref, grad_ref, dbc_ref, step_row_ref, step_col_ref, small_ref, turn_ref, xs_ref, dconv_ref,
    carry_ref,
):
    length = xs_ref.shape[0]
    blocks = length // BLOCK
    conv = conv_of(z_ref[:, TILE:], col_ref, par_ref, length)
    gate = sigmoid(conv)
    xs_ref[...] = conv * gate
    dconv_ref[...] = gate * (1.0 + conv * (1.0 - gate))
    carry_ref[...] = jnp.zeros_like(carry_ref)
    small_ref[...] = jnp.zeros_like(small_ref)
    down, across = iota((BLOCK, BLOCK), 0), iota((BLOCK, BLOCK), 1)

    def one_block(step, carried):
        number = blocks - 1 - step
        rows = pl.ds(pl.multiple_of(number * BLOCK, BLOCK), BLOCK)
        col = col_ref[rows, :]
        z, y, dyn = z_ref[rows, :TILE], y_ref[rows, :], dyn_ref[rows, :]
        gain = par_ref[GAIN : GAIN + 1, :]
        inv, cross = norm_ref[rows, 0:1], norm_ref[rows, 1:2]
        gate = sigmoid(z)
        silu = z * gate
        yg = y * silu
        yg_inv = yg * inv
        d_yg = inv * gain * dyn - yg * cross
        grad_ref[rows, :TILE] = (d_yg * y * (gate * (1.0 + z * (1.0 - gate)))).astype(BF16)
        grad_ref[rows, 2 * TILE :] = (yg_inv * gain).astype(BF16)
        small_ref[GAIN : GAIN + 1, :] += jnp.sum(dyn * yg_inv, axis=0, keepdims=True)
        e = d_yg * silu
        b_rows, c_rows = bc_ref[rows, :LANES], bc_ref[rows, LANES:]
        b_low, c_low = b_rows.astype(BF16), c_rows.astype(BF16)
        scores = turned_ref[rows, :]
        x = xs_ref[rows, :]
        wide = dot(wide_ref[rows, :], pick_ref[...])
        dt_wide, cum_wide = wide[:, :TILE], wide[:, TILE:]
        dtx = x * dt_wide
        dtx_low, e_low = dtx.astype(BF16), e.astype(BF16)
        reach = (down >= across).astype(BF16)
        d_scores = jnp.zeros((BLOCK, BLOCK), F32)
        parts, between = [], []
        for head in range(GROUP):
            lanes = slice(head * WIDTH, (head + 1) * WIDTH)
            gap = row_ref[head : head + 1, rows] - cum_wide[:, head * WIDTH : head * WIDTH + 1]
            decay = jnp.exp(jnp.minimum(gap, 0.0))
            mixing = scores * decay
            parts.append(dot(mixing.astype(BF16), e_low[:, lanes]))
            d_mixing = dot(dtx_low[:, lanes], e_low[:, lanes], NT)
            d_scores = d_scores + d_mixing * decay
            later = dot((d_mixing * mixing).astype(BF16), reach)
            between.append(jnp.sum(jnp.where(down < across, later, 0.0), axis=0, keepdims=True))
        d_dtx = jnp.concatenate(parts, axis=1)
        mask = pair_mask(col[:, SEG : SEG + 1], seg_ref[:, rows], True)
        d_scores = jnp.where(mask, d_scores, 0.0).astype(BF16)
        d_b = dot(d_scores, c_low)
        d_c = dot(d_scores, b_low, TN)
        state, d_state = state_ref[number], carry_ref[...]
        state_low, d_state_low = state.astype(BF16), d_state.astype(BF16)
        decay = jnp.exp(cum_wide) * col[:, LINK : LINK + 1]
        e_in = e * decay
        e_in_low = e_in.astype(BF16)
        from_state = e_in * dot(c_low, state_low)
        d_c = d_c + dot(e_in_low, state_low, NT)
        carry_ref[...] = decay[BLOCK - 1 :, :] * d_state + dot(c_low, e_in_low, TN)
        weight = jnp.exp(cum_wide[BLOCK - 1 :, :] - cum_wide) * col[:, KEEP : KEEP + 1]
        d_tail = weight * dot(b_low, d_state_low)
        to_state = d_tail * dtx
        d_b = d_b + low_dot(weight * dtx, d_state_low, NT)
        d_dtx = d_dtx + d_tail
        through = decay[BLOCK - 1 :, :] * jnp.sum(state * d_state, axis=0, keepdims=True)
        d_x = dt_wide * d_dtx + par_ref[SKIP : SKIP + 1, :] * e
        small_ref[SKIP : SKIP + 1, :] += jnp.sum(x * e, axis=0, keepdims=True)
        dconv_ref[rows, :] = dconv_ref[rows, :] * d_x
        spot = pl.ds(pl.multiple_of(origin + number * BLOCK, BLOCK), BLOCK)
        dbc_ref[spot, :LANES] += d_b
        dbc_ref[spot, LANES:] += d_c
        owner = (iota((TILE, 8), 0) // WIDTH == iota((TILE, 8), 1)).astype(BF16)

        def head_sum(a):
            return sum(dot(part, owner) for part in halves(a))

        after = (down <= across).astype(BF16)
        prior = (down > across).astype(BF16)
        run = sum(dot(after, part) for part in halves(head_sum(from_state)))
        run = run + sum(dot(prior, part) for part in halves(head_sum(to_state)))
        run = run + head_sum(jnp.broadcast_to(through, (8, TILE)))[:1]
        step_col_ref[rows, 0:8] = run
        step_col_ref[rows, 8:16] = head_sum(d_dtx * x)
        step_row_ref[:, rows] = jnp.concatenate(between + between, axis=0)
        return carried

    lax.fori_loop(0, blocks, one_block, 0)
    v, d_conv = z_ref[:, TILE:], dconv_ref[...]
    d_v = par_ref[TAPS + 3 : TAPS + 4, :] * d_conv
    small_ref[TAPS + 3 : TAPS + 4, :] = jnp.sum(d_conv * v, axis=0, keepdims=True)
    small_ref[BIAS : BIAS + 1, :] = jnp.sum(d_conv, axis=0, keepdims=True)
    for offset in range(1, 4):
        place = TAPS + 3 - offset
        counted = d_conv * col_ref[:, VALID + offset - 1 : VALID + offset]
        small_ref[place : place + 1, :] = jnp.sum(
            counted * pltpu.roll(v, offset, 0), axis=0, keepdims=True
        )
        d_v = d_v + par_ref[place : place + 1, :] * pltpu.roll(counted, length - offset, 0)
    grad_ref[:, TILE : 2 * TILE] = d_v.astype(BF16)
    for number in range(blocks):
        rows = slice(number * BLOCK, (number + 1) * BLOCK)
        spot = pl.ds(pl.multiple_of(origin + number * BLOCK, BLOCK), BLOCK)
        turn_ref[:, spot] = grad_ref[rows, :].T


def backward_kernel(
    normed_ref, cot_ref, z_ref, y_ref, dyn_ref, bc_ref, wide_ref, pick_ref, col_ref, row_ref, seg_ref,
    turned_ref, norm_ref, par_ref, state_ref,
    grad_ref, dbc_ref, step_row_ref, step_col_ref, small_ref, far_out_ref, near_out_ref, total_ref,
    turn_ref, xs_ref, dconv_ref, carry_ref, stream_ref, far_ref, near_ref, y_recv_ref, z_send_ref, z_own_ref,
    z_recv_ref, stream_sem, out_sem, y_send_sem, y_recv_sem, z_send_sem, z_recv_sem,
    *, inside, tiles, spans,
):
    tile, sequence = pl.program_id(0), pl.program_id(1)
    length = xs_ref.shape[0]
    parts = turn_ref.shape[0], near_ref.shape[2]
    halves_of = near_ref.shape[0]
    dp, mp = lax.axis_index("dp"), lax.axis_index("mp")

    def partner(bits):
        return (jnp.bitwise_xor(dp, bits), mp)

    def y_copy(number, part):
        slot = lax.rem(number, 2)
        return pltpu.make_async_remote_copy(
            src_ref=far_ref.at[part],
            dst_ref=y_recv_ref.at[slot, part],
            send_sem=y_send_sem.at[part],
            recv_sem=y_recv_sem.at[slot, part],
            device_id=partner(2),
            device_id_type=pl.DeviceIdType.MESH,
        )

    def z_copy(number, k):
        slot = lax.rem(number, 2)
        return pltpu.make_async_remote_copy(
            src_ref=z_send_ref.at[k - 1],
            dst_ref=z_recv_ref.at[slot, k - 1],
            send_sem=z_send_sem.at[k - 1],
            recv_sem=z_recv_sem.at[slot, k - 1],
            device_id=partner(4 * k),
            device_id_type=pl.DeviceIdType.MESH,
        )

    def finish(number):
        slot = lax.rem(number, 2)
        total = z_own_ref[...]
        for k in range(1, spans):
            z_copy(number, k).wait()
            total = total + z_recv_ref[slot, k - 1].astype(F32)
        total_ref[number] = total

    def pass_on(number):
        slot = lax.rem(number, 2)
        for part in range(spans):
            y_copy(number, part).wait()
            whole_part = near_ref[part] + y_recv_ref[slot, part].astype(F32)
            if part == 0:
                z_own_ref[...] = whole_part
            else:
                z_send_ref[part - 1] = whole_part.astype(BF16)
                z_copy(number, part).start()

    @pl.when((tile == 0) & (sequence == 0))
    def _():
        dbc_ref[...] = jnp.zeros_like(dbc_ref)
        if inside:
            barrier = pltpu.get_barrier_semaphore()
            others = [2] + [4 * k for k in range(1, spans)]
            for bits in others:
                pl.semaphore_signal(
                    barrier, inc=1, device_id=partner(bits), device_id_type=pl.DeviceIdType.MESH
                )
            pl.semaphore_wait(barrier, len(others))

    if inside > 1:

        @pl.when((sequence == 1) & (tile >= 2) & (tile < inside + 2))
        def _():
            finish(tile - 2)

    if inside:

        @pl.when((sequence == 1) & (tile >= 1) & (tile < inside + 1))
        def _():
            pass_on(tile - 1)

    backward_tile(
        sequence * length, z_ref, y_ref, dyn_ref, bc_ref, wide_ref, pick_ref, col_ref, row_ref, seg_ref,
        turned_ref, norm_ref, par_ref, state_ref, grad_ref, dbc_ref, step_row_ref, step_col_ref, small_ref,
        turn_ref, xs_ref, dconv_ref, carry_ref,
    )

    def fetch(number, slot):
        lanes = pl.ds(pl.multiple_of(number * parts[1], LANES), parts[1])
        return [
            pltpu.make_async_copy(ref.at[:, lanes], stream_ref.at[slot, at], stream_sem.at[slot, at])
            for at, ref in enumerate((normed_ref, cot_ref))
        ]

    def out_copies():
        place = tile - inside
        return [
            pltpu.make_async_copy(far_ref, far_out_ref.at[place], out_sem.at[0]),
            pltpu.make_async_copy(near_ref, near_out_ref.at[place], out_sem.at[1]),
        ]

    @pl.when(sequence == 1)
    def _():
        for copy in fetch(halves_of, 0):
            copy.start()

        def one_part(step, carried):
            number = lax.rem(step + halves_of, 2 * halves_of)
            slot = lax.rem(step, 2)

            @pl.when(step + 1 < 2 * halves_of)
            def _():
                for copy in fetch(lax.rem(step + 1 + halves_of, 2 * halves_of), lax.rem(step + 1, 2)):
                    copy.start()

            for copy in fetch(number, slot):
                copy.wait()
            upper = dot(turn_ref[: 2 * TILE, :], stream_ref[slot, 0])
            lower = dot(turn_ref[2 * TILE :, :], stream_ref[slot, 1])

            @pl.when(step < halves_of)
            def _():
                far_ref[step, : 2 * TILE, :] = upper.astype(BF16)
                far_ref[step, 2 * TILE :, :] = lower.astype(BF16)

            @pl.when(step >= halves_of)
            def _():
                near_ref[step - halves_of, : 2 * TILE, :] = upper
                near_ref[step - halves_of, 2 * TILE :, :] = lower

            return carried

        def run(first, last):
            lax.fori_loop(first, last, one_part, 0)

        run(0, halves_of)
        if inside:

            @pl.when(tile < inside)
            def _():
                for part in range(spans):
                    y_copy(tile, part).start()

        run(halves_of, 2 * halves_of)
        if inside < tiles:

            @pl.when(tile >= inside)
            def _():
                for copy in out_copies():
                    copy.start()
                for copy in out_copies():
                    copy.wait()

    if inside:

        @pl.when((sequence == 1) & (tile == tiles - 1))
        def _():
            finish(tile - 1)


def by_sequence(rows, width):
    return pl.BlockSpec((rows, width), lambda i: (i, 0))


def by_columns(rows, length):
    return pl.BlockSpec((rows, length), lambda i: (0, i))


def whole(shape):
    return pl.BlockSpec(shape, lambda i: (0,) * len(shape))


def shaped(shape, kind=F32):
    return jax.ShapeDtypeStruct(shape, kind)


def cost(flops):
    return pl.CostEstimate(flops=int(flops), bytes_accessed=10**7, transcendentals=10**6)


def run_tables(normed, weight, ids, par, head, length):
    tokens, width = normed.shape
    cols = weight.shape[1]
    return pl.pallas_call(
        table_kernel,
        grid=(tokens // length,),
        in_specs=[
            by_sequence(length, width),
            whole((width, cols)),
            by_sequence(length, 1),
            by_columns(1, length),
            whole((8, 2 * LANES)),
            whole((8, LANES)),
        ],
        out_specs=[
            by_sequence(length, 2 * LANES),
            by_sequence(length, 2 * LANES),
            by_sequence(length, LANES),
            by_sequence(length, COLS),
            by_columns(2 * HEADS, length),
            by_sequence(length, BLOCK),
            by_sequence(length, BLOCK),
        ],
        out_shape=[
            shaped((tokens, 2 * LANES)),
            shaped((tokens, 2 * LANES)),
            shaped((tokens, LANES), BF16),
            shaped((tokens, COLS)),
            shaped((2 * HEADS, tokens)),
            shaped((tokens, BLOCK)),
            shaped((tokens, BLOCK)),
        ],
        compiler_params=pltpu.CompilerParams(vmem_limit_bytes=VMEM_LIMIT),
        cost_estimate=cost(1e10),
    )(normed, weight, ids[:, None], ids[None, :], par, head)


def pick_table(tile):
    row, lane = jnp.arange(LANES)[:, None], jnp.arange(2 * TILE)[None, :]
    head = tile * GROUP + (lane % TILE) // WIDTH
    return ((row % HEADS == head) & (row // (3 * HEADS) == lane // TILE)).astype(BF16)


def run_forward(pieces, normed, cot, bc, wide, col, rows, score, par, sums, tile, length):
    tokens, width = normed.shape
    number, blocks = tokens // length, length // BLOCK
    return pl.pallas_call(
        functools.partial(forward_kernel, pieces=len(pieces)),
        grid=(number,),
        in_specs=[whole(p.shape) for p in pieces]
        + [
            by_sequence(length, width),
            by_sequence(length, width),
            by_sequence(length, 2 * LANES),
            by_sequence(length, LANES),
            whole((LANES, 2 * TILE)),
            by_sequence(length, COLS),
            pl.BlockSpec((8, length), lambda i: (tile, i)),
            by_sequence(length, BLOCK),
            whole((8, TILE)),
            by_sequence(length, 8),
        ],
        out_specs=[
            whole((width, 3 * TILE)),
            by_sequence(length, 2 * TILE),
            by_sequence(length, TILE),
            by_sequence(length, TILE),
            pl.BlockSpec((blocks, LANES, TILE), lambda i: (i, 0, 0)),
            by_sequence(length, 8),
        ],
        out_shape=[
            shaped((width, 3 * TILE), BF16),
            shaped((tokens, 2 * TILE)),
            shaped((tokens, TILE)),
            shaped((tokens, TILE)),
            shaped((number * blocks, LANES, TILE)),
            shaped((tokens, 8)),
        ],
        scratch_shapes=[pltpu.VMEM((length, TILE), F32), pltpu.VMEM((LANES, TILE), F32)],
        compiler_params=pltpu.CompilerParams(vmem_limit_bytes=VMEM_LIMIT),
        cost_estimate=cost(2e10),
    )(*pieces, normed, cot, bc, wide, pick_table(tile), col, rows, score, par, sums)


def run_backward(normed, cot, zv, y, dyn, bc, wide, col, rows, ids, turned, norms, par, state, length, spans):
    tiles, tokens = zv.shape[:2]
    width = normed.shape[1]
    number, blocks = tokens // length, length // BLOCK
    part = 2 * LANES
    near = width // part // 2
    inside = tiles - 1 if near == spans else 0

    def by_tile(size, cols):
        return pl.BlockSpec((None, size, cols), lambda j, i: (j, i, 0))

    def shared(size, cols):
        return pl.BlockSpec((size, cols), lambda j, i: (i, 0))

    def fixed(*shape):
        return pl.BlockSpec((None,) + shape, lambda j, i: (j,) + (0,) * len(shape))

    params = dict(vmem_limit_bytes=VMEM_LIMIT)
    if inside:
        params.update(collective_id=1, has_side_effects=True)
    return inside, pl.pallas_call(
        functools.partial(backward_kernel, inside=inside, tiles=tiles, spans=spans),
        grid=(tiles, number),
        in_specs=[
            ANY,
            ANY,
            by_tile(length, 2 * TILE),
            by_tile(length, TILE),
            by_tile(length, TILE),
            shared(length, 2 * LANES),
            shared(length, LANES),
            fixed(LANES, 2 * TILE),
            shared(length, COLS),
            pl.BlockSpec((8, length), lambda j, i: (j, i)),
            pl.BlockSpec((1, length), lambda j, i: (0, i)),
            shared(length, BLOCK),
            shared(length, 8),
            fixed(8, TILE),
            pl.BlockSpec((None, blocks, LANES, TILE), lambda j, i: (j, i, 0, 0)),
        ],
        out_specs=[
            by_tile(length, 3 * TILE),
            pl.BlockSpec((tokens, 2 * LANES), lambda j, i: (0, 0)),
            pl.BlockSpec((8, length), lambda j, i: (j, i)),
            by_tile(length, 16),
            pl.BlockSpec((None, None, 8, TILE), lambda j, i: (j, i, 0, 0)),
            ANY,
            ANY,
            pl.BlockSpec((max(inside, 1), 3 * TILE, part), lambda j, i: (0, 0, 0)),
        ],
        out_shape=[
            shaped((tiles, tokens, 3 * TILE), BF16),
            shaped((tokens, 2 * LANES)),
            shaped((tiles * 8, tokens)),
            shaped((tiles, tokens, 16)),
            shaped((tiles, number, 8, TILE)),
            shaped((tiles - inside, near, 3 * TILE, part), BF16),
            shaped((tiles - inside, near, 3 * TILE, part)),
            shaped((max(inside, 1), 3 * TILE, part)),
        ],
        scratch_shapes=[
            pltpu.VMEM((3 * TILE, tokens), BF16),
            pltpu.VMEM((length, TILE), F32),
            pltpu.VMEM((length, TILE), F32),
            pltpu.VMEM((LANES, TILE), F32),
            pltpu.VMEM((2, 2, tokens, part), BF16),
            pltpu.VMEM((near, 3 * TILE, part), BF16),
            pltpu.VMEM((near, 3 * TILE, part), F32),
            pltpu.VMEM((2, near, 3 * TILE, part), BF16),
            pltpu.VMEM((3, 3 * TILE, part), BF16),
            pltpu.VMEM((3 * TILE, part), F32),
            pltpu.VMEM((2, 3, 3 * TILE, part), BF16),
            pltpu.SemaphoreType.DMA((2, 2)),
            pltpu.SemaphoreType.DMA((2,)),
            pltpu.SemaphoreType.DMA((near,)),
            pltpu.SemaphoreType.DMA((2, near)),
            pltpu.SemaphoreType.DMA((3,)),
            pltpu.SemaphoreType.DMA((2, 3)),
        ],
        compiler_params=pltpu.CompilerParams(**params),
        cost_estimate=cost(2e11),
    )(
        normed, cot, zv, y, dyn, bc, wide, jnp.stack([pick_table(tile) for tile in range(tiles)]), col, rows,
        ids[None, :], turned, norms, par, state,
    )


def segment_conv(inputs, taps, bias, masks):
    reach = taps.shape[0]
    result = bias[None, :] + taps[reach - 1][None, :] * inputs
    for offset in range(1, reach):
        moved = jnp.concatenate(
            [jnp.zeros((offset, inputs.shape[1]), inputs.dtype), inputs[:-offset]], axis=0
        )
        result = result + taps[reach - 1 - offset][None, :] * (
            moved * masks[:, offset - 1 : offset]
        )
    return result


def local(
    hidden_in,
    segments,
    norm_gain,
    w_zx,
    w_dt,
    w_bc,
    conv_x,
    conv_x_bias,
    conv_bc,
    conv_bc_bias,
    dt_bias,
    a_log,
    d_skip,
    gated_gain,
    w_out,
    cotangent,
):
    dp, mp = lax.axis_index("dp"), lax.axis_index("mp")
    extent = lax.axis_size("dp")
    far = extent // 4
    x_side = lax.rem(dp, 2)
    rows, width = hidden_in.shape
    length = segments.shape[0]
    inner = conv_x.shape[1]
    inner_total = inner * lax.axis_size("mp")
    heads = dt_bias.shape[0]
    quarter, own_heads = inner // 2, heads // 2
    tiles = quarter // TILE
    depth = w_zx.shape[0]

    def by_side(own, other, axis):
        return jnp.where(
            x_side == 0,
            jnp.concatenate([own, other], axis=axis),
            jnp.concatenate([other, own], axis=axis),
        )

    def by_core(own, other, axis):
        return jnp.where(
            mp == 0,
            jnp.concatenate([own, other], axis=axis),
            jnp.concatenate([other, own], axis=axis),
        )

    def of_side(a, side, axis):
        size = a.shape[axis] // 2
        return lax.dynamic_slice_in_dim(a, side * size, size, axis)

    packed = jnp.concatenate([w_zx[:, 0], w_zx[:, 1], w_out.T], axis=1)
    packed = packed.reshape(depth, 3, 2, tiles, TILE).transpose(2, 3, 0, 1, 4)
    packed = packed.reshape(2, tiles, depth, 3 * TILE)

    def small_weights(side):
        return jnp.concatenate([w_bc, of_side(w_dt, side, 1)], axis=1)

    small_other = flip(small_weights(1 - x_side), "dp", 1)
    packed_own = lax.dynamic_index_in_dim(packed, x_side, 0, False)
    packed_other = flip(lax.dynamic_index_in_dim(packed, 1 - x_side, 0, False), "dp", 1)

    def gathered(piece):
        near = [piece] + [flip(piece, "dp", 4 * k) for k in range(1, far)]
        return near + [flip(p, "dp", 2) for p in near]

    bc_weight = jnp.concatenate(
        gathered(by_side(small_weights(x_side), small_other, 0)), axis=0
    )

    normed, cot, inverse_rows = input_norm(hidden_in, cotangent, norm_gain, dp, extent)

    def both_sequences(a):
        near = flip(a, "dp", 1)
        return by_core(a, flip(a, "mp", 1), 0), by_core(near, flip(near, "mp", 1), 0)

    normed_own, normed_near = both_sequences(normed)
    normed_all = jnp.concatenate([normed_own, normed_near], axis=0)
    pieces = [gathered(by_side(packed_own[tile], packed_other[tile], 0)) for tile in range(tiles)]
    cot_all = jnp.concatenate(both_sequences(cot), axis=0)
    ids = (segments, flip(segments, "dp", 1))

    ids_all = jnp.concatenate(ids, axis=0).astype(F32)
    side_bias = of_side(dt_bias, x_side, 0)
    rate = -jnp.exp(of_side(a_log, x_side, 0))
    bc_par = jnp.concatenate([conv_bc, conv_bc_bias[None], jnp.zeros((3, 2 * LANES), F32)], axis=0)
    head_par = jnp.pad(jnp.stack([side_bias, rate]), ((0, 6), (0, LANES - own_heads)))
    proj_bc, bc, wide, col, rows_all, score, turned = run_tables(
        normed_all, bc_weight, ids_all, bc_par, head_par, length
    )
    tokens = normed_all.shape[0]

    def tile_of(a, tile):
        return of_side(a, x_side, a.ndim - 1)[..., tile * TILE : (tile + 1) * TILE]

    skip_wide = jnp.repeat(d_skip, WIDTH)
    params = [
        jnp.concatenate(
            [
                tile_of(conv_x, tile),
                tile_of(conv_x_bias, tile)[None],
                tile_of(skip_wide, tile)[None],
                tile_of(gated_gain, tile)[None],
                jnp.zeros((1, TILE), F32),
            ],
            axis=0,
        )
        for tile in range(tiles)
    ]

    weights, zvs, dyns, ys, states = [], [], [], [], []
    sums = jnp.zeros((tokens, 8), F32)
    for tile in range(tiles):
        weight, zv, dyn, y, state, sums = run_forward(
            pieces[tile], normed_all, cot_all, bc, wide, col, rows_all, score, params[tile], sums, tile, length
        )
        weights.append(weight)
        zvs.append(zv)
        dyns.append(dyn)
        ys.append(y)
        states.append(state)
    sums = sums + flip(sums, "mp", 1)
    near = flip(sums, "dp", 1)
    sums = sums + jnp.concatenate([near[length:], near[:length]], axis=0)
    inverse_gated = lax.rsqrt(sums[:, :1] / inner_total + EPSILON)
    cross = inverse_gated * inverse_gated * inverse_gated / inner_total * sums[:, 1:2]
    lane = jnp.arange(8)[None, :]
    norms = jnp.where(lane == 0, inverse_gated, jnp.where(lane == 1, cross, 0.0))

    inside, (grads, dbc, step_rows, step_cols, smalls, far_share, near_share, inner_totals) = run_backward(
        normed_all, cot_all, jnp.stack(zvs), jnp.stack(ys), jnp.stack(dyns), bc, wide, col, rows_all, ids_all,
        turned, norms, jnp.stack(params), jnp.stack(states), length, far,
    )

    def spread_sum(far_part, near_part):
        def arranged(a):
            return a.transpose(1, 0, 2).reshape(3 * TILE, far, 2 * depth).transpose(1, 0, 2)

        total = arranged(near_part) + arranged(flip(far_part, "dp", 2)).astype(F32)
        out = total.astype(BF16)
        total = total[0]
        for k in range(1, far):
            total = total + flip(out[k], "dp", 4 * k).astype(F32)
        return total

    totals_of = [inner_totals[tile] for tile in range(inside)]
    totals_of += [spread_sum(far_share[at], near_share[at]) for at in range(tiles - inside)]
    stacked = jnp.stack(totals_of)
    mine = of_side(stacked, x_side, 2)
    theirs = flip(of_side(stacked, 1 - x_side, 2).astype(BF16), "dp", 1).astype(F32)

    def assembled(parts):
        return parts.reshape(tiles, 3, TILE, depth).transpose(1, 0, 2, 3).reshape(3, quarter, depth)

    full = by_side(assembled(mine), assembled(theirs), 1)
    grad_zx_weight = full[:2].transpose(2, 0, 1)
    grad_out_weight = full[2]

    dbc = dbc + flip(dbc, "mp", 1)
    dbc = dbc[:length] + flip(dbc[length:], "dp", 1)
    own_masks = col[:length, VALID : VALID + 3]
    _, state_back = jax.vjp(
        lambda values, taps, bias: jax.nn.silu(segment_conv(values, taps, bias, own_masks)),
        proj_bc[:length],
        conv_bc,
        conv_bc_bias,
    )
    d_bc, grad_conv_bc, grad_conv_bc_bias = state_back(dbc)
    bc_grad = d_bc.astype(BF16)

    raw_dt = rows_all.reshape(tiles, 2, GROUP, tokens)[:, 1].reshape(own_heads, tokens)
    run_steps = step_cols.transpose(0, 2, 1)
    steps = (step_rows.reshape(tiles, 8, tokens)[:, :GROUP] + run_steps[:, :GROUP]).reshape(own_heads, tokens)
    direct = run_steps[:, 8 : 8 + GROUP].reshape(own_heads, tokens)
    d_dt = (direct + rate[:, None] * steps) * jax.nn.sigmoid(raw_dt)
    grad_dt_bias = jnp.sum(d_dt, axis=1)
    grad_a_log = jnp.sum(steps * jax.nn.softplus(raw_dt), axis=1) * rate
    dt_grad = d_dt.T.astype(BF16)

    def placed(a):
        zero = jnp.zeros_like(a)
        return by_side(a, zero, a.ndim - 1)

    small_grad = jnp.concatenate(
        [
            dot(normed_own, lax.dynamic_slice_in_dim(bc_grad, mp * LANES, LANES, 1), TN),
            placed(dot(normed_all, dt_grad, TN)),
        ],
        axis=1,
    )
    small_grad = small_grad.reshape(2 * far, 2, depth, -1)
    small_grad = of_side(small_grad, x_side, 1) + flip(
        of_side(small_grad, 1 - x_side, 1).astype(BF16), "dp", 1
    ).astype(F32)
    small_grad = small_grad.reshape(2, far, depth, -1)
    small_grad = small_grad[0] + flip(small_grad[1].astype(BF16), "dp", 2).astype(F32)
    out = small_grad.astype(BF16)
    small_grad = small_grad[0]
    for k in range(1, far):
        small_grad = small_grad + flip(out[k], "dp", 4 * k).astype(F32)
    grad_dt_weight = small_grad[:, LANES:]
    own_bc = small_grad[:, :LANES]
    grad_bc_weight = by_core(own_bc, flip(own_bc, "mp", 1), 1)

    def token_sum(products):
        def part(core):
            return products(lambda a: of_side(a.reshape(2, 2, rows, -1), core, 1).reshape(2 * rows, -1))

        total = part(mp) + flip(part(1 - mp).astype(BF16), "mp", 1).astype(F32)
        return total[:rows] + flip(total[rows:].astype(BF16), "dp", 1).astype(F32)

    out_all = jnp.concatenate([w[:, 2 * TILE :] for w in weights], axis=1)
    yn_all = jnp.concatenate([g[:, 2 * TILE :] for g in grads], axis=1)
    mixer_out = restore_order(token_sum(lambda pick: dot(pick(yn_all), out_all, NT)), dp, extent)
    inputs = hidden_in.astype(F32)
    residual_out = (inputs + mixer_out).astype(BF16)
    usable = (lax.dynamic_slice_in_dim(segments, mp * rows, rows, 0) >= 0).astype(F32)[:, None]
    totals = jnp.stack(
        [
            jnp.sum(usable * inputs * inputs),
            jnp.sum(usable * mixer_out * mixer_out),
            jnp.sum(usable),
        ]
    )

    zv_all = jnp.concatenate([w[:, : 2 * TILE] for w in weights], axis=1)
    dt_weight = bc_weight[:, 2 * LANES :]
    dzx_all = jnp.concatenate([g[:, : 2 * TILE] for g in grads], axis=1)
    d_normed = token_sum(
        lambda pick: dot(pick(dzx_all), zv_all, NT) + dot(pick(dt_grad), dt_weight, NT)
    )
    d_normed = d_normed + dot(
        lax.dynamic_slice_in_dim(bc_grad, mp * rows, rows, 0), bc_weight[:, : 2 * LANES], NT
    )
    d_normed = restore_order(d_normed, dp, extent)
    grad_norm_gain = jnp.sum(d_normed * inputs * inverse_rows, axis=0)
    inverse_cube_rows = inverse_rows * inverse_rows * inverse_rows
    input_grad = (
        cotangent.astype(F32)
        + inverse_rows * norm_gain * d_normed
        - inputs
        * inverse_cube_rows
        * jnp.mean(inputs * norm_gain * d_normed, axis=-1, keepdims=True)
    )

    def summed(a, axes):
        for axis in axes:
            bit = 1
            while bit < lax.axis_size(axis):
                a = a + flip(a, axis, bit)
                bit *= 2
        return a

    small = jnp.sum(smalls, axis=1).transpose(1, 0, 2).reshape(8, quarter)
    channel = placed(small[: GAIN + 1])
    skip_grad = jnp.sum(channel[SKIP].reshape(heads, WIDTH), axis=1)
    pieces = [
        channel[TAPS:BIAS],
        channel[BIAS],
        grad_conv_bc,
        grad_conv_bc_bias,
        placed(grad_dt_bias),
        placed(grad_a_log),
        skip_grad,
        channel[GAIN],
    ]
    flat = summed(jnp.concatenate([p.reshape(-1) for p in pieces]), ("dp",))
    small_sums, start = [], 0
    for piece in pieces:
        small_sums.append(flat[start : start + piece.size].reshape(piece.shape))
        start += piece.size
    last = summed(jnp.concatenate([grad_norm_gain, totals]), ("mp", "dp"))
    grad_norm_gain = last[:width]
    sum_inputs, sum_mixer, usable_count = last[width], last[width + 1], last[width + 2]
    rms_residual = jnp.sqrt(sum_inputs / (usable_count * width))
    rms_mixer = jnp.sqrt(sum_mixer / (usable_count * width))
    return (
        residual_out,
        input_grad,
        grad_norm_gain,
        grad_zx_weight,
        grad_dt_weight,
        grad_bc_weight,
        small_sums[0],
        small_sums[1],
        small_sums[2],
        small_sums[3],
        small_sums[4],
        small_sums[5],
        small_sums[6],
        small_sums[7],
        grad_out_weight,
        rms_residual,
        rms_mixer,
    )


def solution(mesh):
    in_specs = (
        P(("dp", "mp"), None),
        P("dp"),
        P(),
        P("dp", None, "mp"),
        P("dp", "mp"),
        P("dp", None),
        P(None, "mp"),
        P("mp"),
        P(),
        P(),
        P("mp"),
        P("mp"),
        P("mp"),
        P("mp"),
        P("mp", "dp"),
        P(("dp", "mp"), None),
    )
    out_specs = (
        P(("dp", "mp"), None),
        P(("dp", "mp"), None),
        P(),
        P("dp", None, "mp"),
        P("dp", "mp"),
        P("dp", None),
        P(None, "mp"),
        P("mp"),
        P(),
        P(),
        P("mp"),
        P("mp"),
        P("mp"),
        P("mp"),
        P("mp", "dp"),
        P(),
        P(),
    )
    return jax.shard_map(local, mesh=mesh, in_specs=in_specs, out_specs=out_specs, check_vma=False)
```

time: 1140 us -> 1010 us (0.89)
  Pallas kernels: 202 us -> 348 us
  waiting for transfers between devices: 345 us -> 243 us
  matrix products: 162 us -> 63.2 us
  starting transfers between devices: 167 us -> 97.5 us
    pallas_call x8 -> x6, Pallas kernels: 186 us -> 332 us  [the longest x1 203 us: run_backward(): pl.pallas_call(functools.partial(backward_kernel, inside=inside, tiles=ti...]
    ppermute x87 -> x72, waiting for transfers between devices: 345 us -> 243 us  [flip(): return lax.ppermute(a, axis, [(i, i ^ bit) for i in range(size)])]
    dot_general x34 -> x9, matrix products: 161 us -> 63.2 us  [dot(): lax.dot_general(a, b, dims, precision=precision, preferred_element_type=F32)]
    ppermute x87 -> x72, starting transfers between devices: 167 us -> 97.5 us  [flip(): return lax.ppermute(a, axis, [(i, i ^ bit) for i in range(size)])]
    concatenate x14 -> x2, local copies, waits for them, and re-layouts: 22.8 us -> 0.11 us  [the longest x1 0.07 us: local(): jnp.concatenate([conv_bc, conv_bc_bias[None], jnp.zeros((3, 2 * LANES), F...]
    another operation x1 -> x10, other arithmetic: 0.11 us -> 20.5 us  [the longest x1 6.74 us: local(): jnp.stack(zvs)]
    add x10 -> x2, other arithmetic: 16 us -> 0.02 us  [pick_table(): head = tile * GROUP + lane % TILE // WIDTH]
    unnamed x306 -> x263, local copies, waits for them, and re-layouts: 29.3 us -> 35.9 us
  transfers between devices with their start and end apart: 87 -> 72, of which waited for: 32 -> 22; matrix products, arithmetic and copies ran while one was open for 21% -> 27% of each run, Pallas kernels for 1% -> 12%
where the time goes in v2:
time: 1010 us; the launch traced here: 1000 us
  Pallas kernels  348 us (34%)
  waiting for transfers between devices  243 us (24%)
  other arithmetic  126 us (12%)
  local copies, waits for them, and re-layouts  120 us (12%)
  starting transfers between devices  97.5 us (10%)
  matrix products  63.2 us (6%)
    ppermute x72, waiting for transfers between devices, flip(): return lax.ppermute(a, axis, [(i, i ^ bit) for i in range(size)])  243 us
    pallas_call x1, Pallas kernels, run_backward(): pl.pallas_call(functools.partial(backward_kernel, inside=inside, tiles=ti...  203 us
    pallas_call x4, Pallas kernels, run_forward(): pl.pallas_call(functools.partial(forward_kernel, pieces=len(pieces)), gri...  110 us
    ppermute x72, starting transfers between devices, flip(): return lax.ppermute(a, axis, [(i, i ^ bit) for i in range(size)])  97.5 us
    dot_general x9, matrix products, dot(): lax.dot_general(a, b, dims, precision=precision, preferred_element_type=F32)  63.2 us
    unnamed x263, local copies, waits for them, and re-layouts  35.9 us
  transfers between devices with their start and end apart: 72, of which 22 were waited for; matrix products, arithmetic and copies ran while one was open for 27% of the time, Pallas kernels for 12%

profile of v2, /device:TPU:0, one launch (start us, length us, event | category | flops | bytes accessed | tf_op | source)
XLA Modules:
  0.0 1005.0 jit_solution(15114351664356904243)
XLA Ops:
  42.8 16.0 %collective-permute-done.22 = s32[1024]{0:T(1024)} collective-permute-done((s32[1024]{0:T(1024)S(1)}, s32[1024]{0:T(1024)}, u32[]{:S(2)}, u32[]{:S(2)}) %collective-permute-start.22) | collective-permute-done | bytes 4128 | tf_op jit(solution)/shard_map/ppermute | solution.py:36
  86.5 44.6 %collective-permute-done.6 = bf16[4,128,768]{2,1,0:T(8,128)(2,1)S(1)} collective-permute-done((bf16[4,128,768]{2,1,0:T(8,128)(2,1)S(1)}, bf16[4,128,768]{2,1,0:T(8,128)(2,1)S(1)}, u32[]{:S(2)}, u32[]{:S(2)}) %collective-permute-start.6) | collective-permute-done | bytes 786464 | tf_op jit(solution)/shard_map/ppermute | solution.py:36
  151.7 8.4 pad_maximum_fusion.1.normed_ref.refs_8_
  160.1 19.3 %shard_map.288 = (f32[2048,256]{1,0:T(8,128)}, f32[2048,256]{1,0:T(8,128)}, bf16[2048,128]{1,0:T(8,128)(2,1)}, f32[2048,8]{1,0:T(8,128)}, f32[32,2048]{1,0:T(8,1...) custom-call(bf16[2048,2048]{1,0:T(8,128)(2,1)} %pad_maximum_fusion.1.normed_ref.refs_8_, bf16[2048,272]{1,0:T(8,128)(2,1)} %copy-done.17, ...), custom_call_target="tpu_custom_call" | custom-call | flops 10000000000 | bytes 10000000 | tf_op jit(solution)/shard_map/pallas_call | solution.py:570
  189.7 9.6 collective-permute-done.23.refs_1_
  199.3 10.8 %collective-permute-done.24.refs_2_ = bf16[256,768]{1,0:T(8,128)(2,1)S(1)} collective-permute-done((bf16[256,768]{1,0:T(8,128)(2,1)S(1)}, bf16[256,768]{1,0:T(8,128)(2,1)S(1)}, u32[]{:S(2)}, u32[]{:S(2)}) %collective-permute-start.24) | collective-permute-done | bytes 393248 | tf_op jit(solution)/shard_map/ppermute | solution.py:36
  217.2 8.5 pad_maximum_fusion.2.refs_9_.cot_ref
  225.7 18.1 %collective-permute-done.31.refs_2_ = bf16[256,768]{1,0:T(8,128)(2,1)S(1)} collective-permute-done((bf16[256,768]{1,0:T(8,128)(2,1)S(1)}, bf16[256,768]{1,0:T(8,128)(2,1)S(1)}, u32[]{:S(2)}, u32[]{:S(2)}) %collective-permute-start.31) | collective-permute-done | bytes 393248 | tf_op jit(solution)/shard_map/ppermute | solution.py:36
  244.4 7.8 collective-permute-start.37
  255.7 28.7 %shard_map.289 = (bf16[2048,768]{1,0:T(8,128)(2,1)}, f32[2048,512]{1,0:T(8,128)}, f32[2048,256]{1,0:T(8,128)}, f32[2048,256]{1,0:T(8,128)}, f32[8,128,256]{2,1,0:T(8,128)}, /*index=5*/f32[2048,8]{1,0:T(8,128)}) custom-call(bf16[256,768]{1,0:T(8,128)(2,1)} %maximum_select_fusion.5.refs_0_, bf16[256,768]{1,0:T(8,128)(2,1)} %collective-permute-done.7.refs_1_, ...), custom_call_target="tpu_custom_call" | custom-call | flops 20000000000 | bytes 10000000 | tf_op jit(solution)/shard_map/pallas_call | solution.py:613
  284.4 12.1 %collective-permute-start.38 = (bf16[256,768]{1,0:T(8,128)(2,1)S(1)}, bf16[256,768]{1,0:T(8,128)(2,1)}, u32[]{:S(2)}, u32[]{:S(2)}) collective-permute-start(bf16[256,768]{1,0:T(8,128)(2,1)S(1)} %maximum_select_fusion.8.refs_0_), channel_id=1, source_target_pairs={{0,16},{2,18},{4,20},{6,22},{8,24},{10,26},{12,28},{14,30},{16,0},... | collective-permute-start | bytes 1179656 | tf_op jit(solution)/shard_map/ppermute | solution.py:36
  301.7 27.3 %shard_map.290 = (bf16[2048,768]{1,0:T(8,128)(2,1)}, f32[2048,512]{1,0:T(8,128)}, f32[2048,256]{1,0:T(8,128)}, f32[2048,256]{1,0:T(8,128)}, f32[8,128,256]{2,1,0:T(8,128)}, /*index=5*/f32[2048,8]{1,0:T(8,128)}) custom-call(bf16[256,768]{1,0:T(8,128)(2,1)} %maximum_select_fusion.6.refs_0_, bf16[256,768]{1,0:T(8,128)(2,1)} %copy-done.101, ...), custom_call_target="tpu_custom_call" | custom-call | flops 20000000000 | bytes 10000000 | tf_op jit(solution)/shard_map/pallas_call | solution.py:613
  333.9 27.2 %shard_map.291 = (bf16[2048,768]{1,0:T(8,128)(2,1)}, f32[2048,512]{1,0:T(8,128)}, f32[2048,256]{1,0:T(8,128)}, f32[2048,256]{1,0:T(8,128)}, f32[8,128,256]{2,1,0:T(8,128)}, /*index=5*/f32[2048,8]{1,0:T(8,128)}) custom-call(bf16[256,768]{1,0:T(8,128)(2,1)} %copy-done.51, bf16[256,768]{1,0:T(8,128)(2,1)} %copy-done.97, bf16[256,768]{1,0:T(8,128)(2,1)} %copy-done.99, ...), custom_call_target="tpu_custom_call" | custom-call | flops 20000000000 | bytes 10000000 | tf_op jit(solution)/shard_map/pallas_call | solution.py:613
  361.9 27.2 %shard_map.292 = (bf16[2048,768]{1,0:T(8,128)(2,1)}, f32[2048,512]{1,0:T(8,128)}, f32[2048,256]{1,0:T(8,128)}, f32[2048,256]{1,0:T(8,128)}, f32[8,128,256]{2,1,0:T(8,128)}, /*index=5*/f32[2048,8]{1,0:T(8,128)}) custom-call(bf16[256,768]{1,0:T(8,128)(2,1)} %copy-done.50, bf16[256,768]{1,0:T(8,128)(2,1)} %copy-done.103, ...), custom_call_target="tpu_custom_call" | custom-call | flops 20000000000 | bytes 10000000 | tf_op jit(solution)/shard_map/pallas_call | solution.py:613
  414.0 6.7 pad_maximum_fusion.z_ref
  451.4 202.6 %shard_map.293 = (bf16[4,2048,768]{2,1,0:T(8,128)(2,1)}, f32[2048,256]{1,0:T(8,128)}, f32[32,2048]{1,0:T(8,128)}, f32[4,2048,16]{2,1,0:T(8,128)}, f32[4,2,8,256]...) custom-call(bf16[2048,2048]{1,0:T(8,128)(2,1)} %pad_maximum_fusion.1.normed_, ...), custom_call_target="tpu_custom_call" | custom-call | flops 199999995904 | bytes 10000000 | tf_op jit(solution)/shard_map/pallas_call | solution.py:671
  670.9 10.4 %fusion.10 = (f32[4,4]{1,0:T(4,128)S(1)}, f32[4,4]{1,0:T(4,128)S(1)}, f32[4,4,2048]{1,2,0:T(8,128)}, f32[4,4,2048]{1,2,0:T(8,128)}) fusion(f32[4,1,4,2048]{2,3,0,1:T(8,128)} %copy.175, f32[4,4]{1,0:T(4,128)S(1)} %copy-done.81, f32[4,16,2048]{1,2,0:T(8,128)} %bitcast.214, f32[4,4,2048]{1,2,0:T(8,128)} %copy.174), kind=kLoop, calls=%fused_computation.28 | loop fusion | flops 524256 | bytes 786624 | tf_op jit(solution)/shard_map/reduce_sum | solution.py:925
  700.6 14.1 %add_convert_fusion = bf16[1024,2048]{1,0:T(8,128)(2,1)} fusion(f32[1024,2048]{1,0:T(8,128)} %fusion.44, bf16[1024,2048]{1,0:T(8,128)(2,1)S(1)} %bitcast.222, bf16[2048,512]{1,0:T(8,128)(2,1)} %slice.370, bf16[2048,512]{1,0:T(8,128)(2,1)} %slice.369, bf16[2048,512]{1,0:T(8,128)(2,1)} %slice.368, bf16[2048,512]{1,0:T(8,128)(2,1)} %slice.367), kind=kOutput, calls=%fused_computation.15 | convolution fusion | flops 8627683328 | bytes 25165824 | tf_op jit(solution)/shard_map/dot_general | solution.py:27
  724.0 6.2 convolution_convert_fusion
  730.2 23.5 %collective-permute-done.57 = bf16[4,768,256]{2,1,0:T(8,128)(2,1)S(1)} collective-permute-done((bf16[4,768,256]{2,1,0:T(8,128)(2,1)}, bf16[4,768,256]{2,1,0:T(8,128)(2,1)S(1)}, u32[]{:S(2)}, u32[]{:S(2)}) %collective-permute-start.57) | collective-permute-done | bytes 1572896 | tf_op jit(solution)/shard_map/ppermute | solution.py:36
  760.0 11.5 %collective-permute-done.58 = bf16[768,256]{1,0:T(8,128)(2,1)S(1)} collective-permute-done((bf16[768,256]{1,0:T(8,128)(2,1)S(1)}, bf16[768,256]{1,0:T(8,128)(2,1)S(1)}, u32[]{:S(2)}, u32[]{:S(2)}) %collective-permute-start.58) | collective-permute-done | bytes 393248 | tf_op jit(solution)/shard_map/ppermute | solution.py:36
  771.5 13.2 %collective-permute-done.59 = bf16[768,256]{1,0:T(8,128)(2,1)S(1)} collective-permute-done((bf16[768,256]{1,0:T(8,128)(2,1)S(1)}, bf16[768,256]{1,0:T(8,128)(2,1)S(1)}, u32[]{:S(2)}, u32[]{:S(2)}) %collective-permute-start.59) | collective-permute-done | bytes 393248 | tf_op jit(solution)/shard_map/ppermute | solution.py:36
  796.7 9.0 collective-permute-done.61
  806.5 16.0 %collective-permute-done.51 = f32[1024,256]{1,0:T(8,128)S(1)} collective-permute-done((f32[1024,256]{1,0:T(8,128)S(1)}, f32[1024,256]{1,0:T(8,128)S(1)}, u32[]{:S(2)}, u32[]{:S(2)}) %collective-permute-start.51) | collective-permute-done | bytes 1048608 | tf_op jit(solution)/shard_map/ppermute | solution.py:36
  839.5 9.5 collective-permute-start.70
  849.1 16.7 %convert_add_fusion.1 = f32[1024,2048]{1,0:T(8,128)} fusion(bf16[1024,2048]{1,0:T(8,128)(2,1)} %collective-permute-done.48, f32[1024,2048]{1,0:T(8,128)} %fusion.46, bf16[1024,2048]{1,0:T(8,128)(2,1)} %bitcast.221, bf16[2048,512]{1,0:T(8,128)(2,1)} %slice.370, bf16[2048,512]{1,0:T(8,128)(2,1)} %slice.369, bf16[2048,512]{1,0:T(8,128)(2,1)} %slice.368, ...), kind=kOutput, calls=%fused_computation.14 | convolution fusion | flops 8629780480 | bytes 33554432 | tf_op jit(solution)/shard_map/dot_general | solution.py:27
  871.6 7.1 convert_add_fusion.2
  906.5 12.2 %collective-permute-done.49 = bf16[512,2048]{1,0:T(8,128)(2,1)} collective-permute-done((bf16[512,2048]{1,0:T(8,128)(2,1)}, bf16[512,2048]{1,0:T(8,128)(2,1)}, u32[]{:S(2)}, u32[]{:S(2)}) %collective-permute-start.49) | collective-permute-done | bytes 2097184 | tf_op jit(solution)/shard_map/ppermute | solution.py:36
  929.4 29.3 %collective-permute-done.47 = bf16[512,2048]{1,0:T(8,128)(2,1)} collective-permute-done((bf16[512,2048]{1,0:T(8,128)(2,1)}, bf16[512,2048]{1,0:T(8,128)(2,1)}, u32[]{:S(2)}, u32[]{:S(2)}) %collective-permute-start.47) | collective-permute-done | bytes 2097184 | tf_op jit(solution)/shard_map/ppermute | solution.py:36
  958.7 5.8 slice_add_fusion.2.in_ref
  969.9 6.4 fusion
  992.4 6.7 fusion.3
  (577 shorter events, 325.5 us)
Async XLA Ops:
  11.3 73.1 %collective-permute-start.1 = (bf16[512,2048]{1,0:T(8,128)(2,1)}, bf16[512,2048]{1,0:T(8,128)(2,1)}, u32[]{:S(2)}, u32[]{:S(2)}) collective-permute-start(bf16[512,2048]{1,0:T(8,128)(2,1)} %get-tuple-element.59), channel_id=1, source_target_pairs={{0,2},{2,0},{4,6},{6,4},{8,10},{10,8},{12,14},{14,12},{16,18},{18,... | collective-permute-start | bytes 6291464 | tf_op jit(solution)/shard_map/ppermute | solution.py:36
  11.3 47.5 %collective-permute-start.22 = (s32[1024]{0:T(1024)S(1)}, s32[1024]{0:T(1024)}, u32[]{:S(2)}, u32[]{:S(2)}) collective-permute-start(s32[1024]{0:T(1024)S(1)} %copy-done.68), channel_id=1, source_target_pairs={{0,2},{2,0},{4,6},{6,4},{8,10},{10,8},{12,14},{14,12},{16,18},{18,... | collective-permute-start | bytes 12296 | tf_op jit(solution)/shard_map/ppermute | solution.py:36
  58.8 75.9 %collective-permute-start = (bf16[512,2048]{1,0:T(8,128)(2,1)}, bf16[512,2048]{1,0:T(8,128)(2,1)}, u32[]{:S(2)}, u32[]{:S(2)}) collective-permute-start(bf16[512,2048]{1,0:T(8,128)(2,1)} %get-tuple-element.59), channel_id=1, source_target_pairs={{0,1},{1,0},{2,3},{3,2},{4,5},{5,4},{6,7},{7,6},{8,9},{9,8},{10,11... | collective-permute-start | bytes 6291464 | tf_op jit(solution)/shard_map/ppermute | solution.py:36
  67.3 74.4 %collective-permute-start.4 = (bf16[512,2048]{1,0:T(8,128)(2,1)}, bf16[512,2048]{1,0:T(8,128)(2,1)}, u32[]{:S(2)}, u32[]{:S(2)}) collective-permute-start(bf16[512,2048]{1,0:T(8,128)(2,1)} %get-tuple-element.60), channel_id=1, source_target_pairs={{0,2},{2,0},{4,6},{6,4},{8,10},{10,8},{12,14},{14,12},{16,18},{18,... | collective-permute-start | bytes 6291464 | tf_op jit(solution)/shard_map/ppermute | solution.py:36
  71.5 70.8 %collective-permute-start.3 = (bf16[512,2048]{1,0:T(8,128)(2,1)}, bf16[512,2048]{1,0:T(8,128)(2,1)S(1)}, u32[]{:S(2)}, u32[]{:S(2)}) collective-permute-start(bf16[512,2048]{1,0:T(8,128)(2,1)} %get-tuple-element.60), channel_id=1, source_target_pairs={{0,1},{1,0},{2,3},{3,2},{4,5},{5,4},{6,7},{7,6},{8,9},{9,8},{10,11... | collective-permute-start | bytes 6291464 | tf_op jit(solution)/shard_map/ppermute | solution.py:36
  82.1 49.0 %collective-permute-start.6 = (bf16[4,128,768]{2,1,0:T(8,128)(2,1)S(1)}, bf16[4,128,768]{2,1,0:T(8,128)(2,1)S(1)}, u32[]{:S(2)}, u32[]{:S(2)}) collective-permute-start(bf16[4,128,768]{2,1,0:T(8,128)(2,1)S(1)} %bitcast.244), channel_id=1, source_target_pairs={{0,2},{2,0},{4,6},{6,4},{8,10},{10,8},{12,14},{14,12},{16,18},{18,... | collective-permute-start | bytes 2359304 | tf_op jit(solution)/shard_map/ppermute | solution.py:36
  84.4 61.5 %collective-permute-start.2 = (bf16[512,2048]{1,0:T(8,128)(2,1)}, bf16[512,2048]{1,0:T(8,128)(2,1)S(1)}, u32[]{:S(2)}, u32[]{:S(2)}) collective-permute-start(bf16[512,2048]{1,0:T(8,128)(2,1)} %collective-permute-done.1), channel_id=1, source_target_pairs={{0,1},{1,0},{2,3},{3,2},{4,5},{5,4},{6,7},{7,6},{8,9},{9,8},{10,11... | collective-permute-start | bytes 6291464 | tf_op jit(solution)/shard_map/ppermute | solution.py:36
  132.1 47.2 %collective-permute-start.7 = (bf16[256,768]{1,0:T(8,128)(2,1)}, bf16[256,768]{1,0:T(8,128)(2,1)}, u32[]{:S(2)}, u32[]{:S(2)}) collective-permute-start(bf16[256,768]{1,0:T(8,128)(2,1)} %maximum_select_fusion.5.refs_0_), channel_id=1, source_target_pairs={{0,8},{2,10},{4,12},{6,14},{8,0},{10,2},{12,4},{14,6},{16,24},{18,... | collective-permute-start | bytes 1179656 | tf_op jit(solution)/shard_map/ppermute | solution.py:36
  134.7 45.3 %collective-permute-start.8 = (bf16[256,768]{1,0:T(8,128)(2,1)}, bf16[256,768]{1,0:T(8,128)(2,1)}, u32[]{:S(2)}, u32[]{:S(2)}) collective-permute-start(bf16[256,768]{1,0:T(8,128)(2,1)} %maximum_select_fusion.5.refs_0_), channel_id=1, source_target_pairs={{0,16},{2,18},{4,20},{6,22},{8,24},{10,26},{12,28},{14,30},{16,0},... | collective-permute-start | bytes 1179656 | tf_op jit(solution)/shard_map/ppermute | solution.py:36
  141.7 41.6 %collective-permute-start.9 = (bf16[256,768]{1,0:T(8,128)(2,1)}, bf16[256,768]{1,0:T(8,128)(2,1)}, u32[]{:S(2)}, u32[]{:S(2)}) collective-permute-start(bf16[256,768]{1,0:T(8,128)(2,1)} %maximum_select_fusion.5.refs_0_), channel_id=1, source_target_pairs={{0,24},{2,26},{4,28},{6,30},{8,16},{10,18},{12,20},{14,22},{16,8},... | collective-permute-start | bytes 1179656 | tf_op jit(solution)/shard_map/ppermute | solution.py:36
  142.3 42.0 %collective-permute-start.5 = (bf16[512,2048]{1,0:T(8,128)(2,1)}, bf16[512,2048]{1,0:T(8,128)(2,1)S(1)}, u32[]{:S(2)}, u32[]{:S(2)}) collective-permute-start(bf16[512,2048]{1,0:T(8,128)(2,1)} %collective-permute-done.4), channel_id=1, source_target_pairs={{0,1},{1,0},{2,3},{3,2},{4,5},{5,4},{6,7},{7,6},{8,9},{9,8},{10,11... | collective-permute-start | bytes 6291464 | tf_op jit(solution)/shard_map/ppermute | solution.py:36
  145.9 37.9 %collective-permute-start.10 = (bf16[256,768]{1,0:T(8,128)(2,1)}, bf16[256,768]{1,0:T(8,128)(2,1)}, u32[]{:S(2)}, u32[]{:S(2)}) collective-permute-start(bf16[256,768]{1,0:T(8,128)(2,1)} %maximum_select_fusion.5.refs_0_), channel_id=1, source_target_pairs={{0,4},{2,6},{4,0},{6,2},{8,12},{10,14},{12,8},{14,10},{16,20},{18,... | collective-permute-start | bytes 1179656 | tf_op jit(solution)/shard_map/ppermute | solution.py:36
  199.3 44.5 %collective-permute-start.31 = (bf16[256,768]{1,0:T(8,128)(2,1)S(1)}, bf16[256,768]{1,0:T(8,128)(2,1)S(1)}, u32[]{:S(2)}, u32[]{:S(2)}) collective-permute-start(bf16[256,768]{1,0:T(8,128)(2,1)S(1)} %maximum_select_fusion.7.refs_0_), channel_id=1, source_target_pairs={{0,16},{2,18},{4,20},{6,22},{8,24},{10,26},{12,28},{14,30},{16,0},... | collective-permute-start | bytes 1179656 | tf_op jit(solution)/shard_map/ppermute | solution.py:36
  212.6 39.5 %collective-permute-start.11 = (bf16[256,768]{1,0:T(8,128)(2,1)}, bf16[256,768]{1,0:T(8,128)(2,1)}, u32[]{:S(2)}, u32[]{:S(2)}) collective-permute-start(bf16[256,768]{1,0:T(8,128)(2,1)} %collective-permute-done.7.refs_1_), channel_id=1, source_target_pairs={{0,4},{2,6},{4,0},{6,2},{8,12},{10,14},{12,8},{14,10},{16,20},{18,... | collective-permute-start | bytes 1179656 | tf_op jit(solution)/shard_map/ppermute | solution.py:36
  213.1 39.5 %collective-permute-start.12 = (bf16[256,768]{1,0:T(8,128)(2,1)}, bf16[256,768]{1,0:T(8,128)(2,1)}, u32[]{:S(2)}, u32[]{:S(2)}) collective-permute-start(bf16[256,768]{1,0:T(8,128)(2,1)} %collective-permute-done.8.refs_2_), channel_id=1, source_target_pairs={{0,4},{2,6},{4,0},{6,2},{8,12},{10,14},{12,8},{14,10},{16,20},{18,... | collective-permute-start | bytes 1179656 | tf_op jit(solution)/shard_map/ppermute | solution.py:36
  216.7 37.5 %collective-permute-start.13 = (bf16[256,768]{1,0:T(8,128)(2,1)}, bf16[256,768]{1,0:T(8,128)(2,1)}, u32[]{:S(2)}, u32[]{:S(2)}) collective-permute-start(bf16[256,768]{1,0:T(8,128)(2,1)} %collective-permute-done.9.refs_3_), channel_id=1, source_target_pairs={{0,4},{2,6},{4,0},{6,2},{8,12},{10,14},{12,8},{14,10},{16,20},{18,... | collective-permute-start | bytes 1179656 | tf_op jit(solution)/shard_map/ppermute | solution.py:36
  243.9 40.5 %collective-permute-start.33 = (bf16[256,768]{1,0:T(8,128)(2,1)S(1)}, bf16[256,768]{1,0:T(8,128)(2,1)S(1)}, u32[]{:S(2)}, u32[]{:S(2)}) collective-permute-start(bf16[256,768]{1,0:T(8,128)(2,1)S(1)} %maximum_select_fusion.7.refs_0_), channel_id=1, source_target_pairs={{0,4},{2,6},{4,0},{6,2},{8,12},{10,14},{12,8},{14,10},{16,20},{18,... | collective-permute-start | bytes 1179656 | tf_op jit(solution)/shard_map/ppermute | solution.py:36
  244.4 52.2 %collective-permute-start.37 = (bf16[256,768]{1,0:T(8,128)(2,1)S(1)}, bf16[256,768]{1,0:T(8,128)(2,1)S(1)}, u32[]{:S(2)}, u32[]{:S(2)}) collective-permute-start(bf16[256,768]{1,0:T(8,128)(2,1)S(1)} %maximum_select_fusion.8.refs_0_), channel_id=1, source_target_pairs={{0,8},{2,10},{4,12},{6,14},{8,0},{10,2},{12,4},{14,6},{16,24},{18,... | collective-permute-start | bytes 1179656 | tf_op jit(solution)/shard_map/ppermute | solution.py:36
  252.1 45.8 %collective-permute-start.27 = (bf16[256,768]{1,0:T(8,128)(2,1)S(1)}, bf16[256,768]{1,0:T(8,128)(2,1)S(1)}, u32[]{:S(2)}, u32[]{:S(2)}) collective-permute-start(bf16[256,768]{1,0:T(8,128)(2,1)S(1)} %copy-done.102), channel_id=1, source_target_pairs={{0,4},{2,6},{4,0},{6,2},{8,12},{10,14},{12,8},{14,10},{16,20},{18,... | collective-permute-start | bytes 1179656 | tf_op jit(solution)/shard_map/ppermute | solution.py:36
  252.6 46.9 %collective-permute-start.28 = (bf16[256,768]{1,0:T(8,128)(2,1)S(1)}, bf16[256,768]{1,0:T(8,128)(2,1)S(1)}, u32[]{:S(2)}, u32[]{:S(2)}) collective-permute-start(bf16[256,768]{1,0:T(8,128)(2,1)S(1)} %copy-done.105), channel_id=1, source_target_pairs={{0,4},{2,6},{4,0},{6,2},{8,12},{10,14},{12,8},{14,10},{16,20},{18,... | collective-permute-start | bytes 1179656 | tf_op jit(solution)/shard_map/ppermute | solution.py:36
  254.2 45.9 %collective-permute-start.29 = (bf16[256,768]{1,0:T(8,128)(2,1)S(1)}, bf16[256,768]{1,0:T(8,128)(2,1)S(1)}, u32[]{:S(2)}, u32[]{:S(2)}) collective-permute-start(bf16[256,768]{1,0:T(8,128)(2,1)S(1)} %copy-done.107), channel_id=1, source_target_pairs={{0,4},{2,6},{4,0},{6,2},{8,12},{10,14},{12,8},{14,10},{16,20},{18,... | collective-permute-start | bytes 1179656 | tf_op jit(solution)/shard_map/ppermute | solution.py:36
  284.4 44.5 %collective-permute-start.38 = (bf16[256,768]{1,0:T(8,128)(2,1)S(1)}, bf16[256,768]{1,0:T(8,128)(2,1)}, u32[]{:S(2)}, u32[]{:S(2)}) collective-permute-start(bf16[256,768]{1,0:T(8,128)(2,1)S(1)} %maximum_select_fusion.8.refs_0_), channel_id=1, source_target_pairs={{0,16},{2,18},{4,20},{6,22},{8,24},{10,26},{12,28},{14,30},{16,0},... | collective-permute-start | bytes 1179656 | tf_op jit(solution)/shard_map/ppermute | solution.py:36
  668.1 124.9 %collective-permute-start.50 = (f32[2048,256]{1,0:T(8,128)}, f32[2048,256]{1,0:T(8,128)}, u32[]{:S(2)}, u32[]{:S(2)}) collective-permute-start(f32[2048,256]{1,0:T(8,128)} %get-tuple-element.95), channel_id=1, source_target_pairs={{0,1},{1,0},{2,3},{3,2},{4,5},{5,4},{6,7},{7,6},{8,9},{9,8},{10,11... | collective-permute-start | bytes 6291464 | tf_op jit(solution)/shard_map/ppermute | solution.py:36
  714.6 134.4 %collective-permute-start.48 = (bf16[1024,2048]{1,0:T(8,128)(2,1)}, bf16[1024,2048]{1,0:T(8,128)(2,1)}, u32[]{:S(2)}, u32[]{:S(2)}) collective-permute-start(bf16[1024,2048]{1,0:T(8,128)(2,1)} %add_convert_fusion), channel_id=1, source_target_pairs={{0,1},{1,0},{2,3},{3,2},{4,5},{5,4},{6,7},{7,6},{8,9},{9,8},{10,11... | collective-permute-start | bytes 12582920 | tf_op jit(solution)/shard_map/ppermute | solution.py:36
  771.5 100.1 %collective-permute-start.46 = (bf16[1024,2048]{1,0:T(8,128)(2,1)}, bf16[1024,2048]{1,0:T(8,128)(2,1)}, u32[]{:S(2)}, u32[]{:S(2)}) collective-permute-start(bf16[1024,2048]{1,0:T(8,128)(2,1)} %convolution_convert_fusion), channel_id=1, source_target_pairs={{0,1},{1,0},{2,3},{3,2},{4,5},{5,4},{6,7},{7,6},{8,9},{9,8},{10,11... | collective-permute-start | bytes 12582920 | tf_op jit(solution)/shard_map/ppermute | solution.py:36
  839.3 54.5 %collective-permute-start.62 = (bf16[8,1,128,160]{3,2,0,1:T(8,128)(2,1)}, bf16[8,1,128,160]{3,2,0,1:T(8,128)(2,1)}, u32[]{:S(2)}, u32[]{:S(2)}) collective-permute-start(bf16[8,1,128,160]{3,2,0,1:T(8,128)(2,1)} %copy.179), channel_id=1, source_target_pairs={{0,2},{2,0},{4,6},{6,4},{8,10},{10,8},{12,14},{14,12},{16,18},{18,... | collective-permute-start | bytes 983048 | tf_op jit(solution)/shard_map/ppermute | solution.py:36
  839.5 49.0 %collective-permute-start.70 = (f32[13664]{0:T(1024)S(1)}, f32[13664]{0:T(1024)S(1)}, u32[]{:S(2)}, u32[]{:S(2)}) collective-permute-start(f32[13664]{0:T(1024)S(1)} %add.444), channel_id=1, source_target_pairs={{0,8},{2,10},{4,12},{6,14},{8,0},{10,2},{12,4},{14,6},{16,24},{18,... | collective-permute-start | bytes 163976 | tf_op jit(solution)/shard_map/ppermute | solution.py:36
  869.9 48.9 %collective-permute-start.49 = (bf16[512,2048]{1,0:T(8,128)(2,1)}, bf16[512,2048]{1,0:T(8,128)(2,1)}, u32[]{:S(2)}, u32[]{:S(2)}) collective-permute-start(bf16[512,2048]{1,0:T(8,128)(2,1)} %slice.554), channel_id=1, source_target_pairs={{0,2},{2,0},{4,6},{6,4},{8,10},{10,8},{12,14},{14,12},{16,18},{18,... | collective-permute-start | bytes 6291464 | tf_op jit(solution)/shard_map/ppermute | solution.py:36
  883.6 75.0 %collective-permute-start.47 = (bf16[512,2048]{1,0:T(8,128)(2,1)}, bf16[512,2048]{1,0:T(8,128)(2,1)}, u32[]{:S(2)}, u32[]{:S(2)}) collective-permute-start(bf16[512,2048]{1,0:T(8,128)(2,1)} %slice.555), channel_id=1, source_target_pairs={{0,2},{2,0},{4,6},{6,4},{8,10},{10,8},{12,14},{14,12},{16,18},{18,... | collective-permute-start | bytes 6291464 | tf_op jit(solution)/shard_map/ppermute | solution.py:36
  902.1 76.2 %collective-permute-start.64 = (bf16[128,160]{1,0:T(8,128)(2,1)}, bf16[128,160]{1,0:T(8,128)(2,1)S(1)}, u32[]{:S(2)}, u32[]{:S(2)}) collective-permute-start(bf16[128,160]{1,0:T(8,128)(2,1)} %get-tuple-element.259), channel_id=1, source_target_pairs={{0,8},{2,10},{4,12},{6,14},{8,0},{10,2},{12,4},{14,6},{16,24},{18,... | collective-permute-start | bytes 122888 | tf_op jit(solution)/shard_map/ppermute | solution.py:36
  902.1 76.2 %collective-permute-start.65 = (bf16[128,160]{1,0:T(8,128)(2,1)S(1)}, bf16[128,160]{1,0:T(8,128)(2,1)S(1)}, u32[]{:S(2)}, u32[]{:S(2)}) collective-permute-start(bf16[128,160]{1,0:T(8,128)(2,1)S(1)} %get-tuple-element.261), channel_id=1, source_target_pairs={{0,16},{2,18},{4,20},{6,22},{8,24},{10,26},{12,28},{14,30},{16,0},... | collective-permute-start | bytes 122888 | tf_op jit(solution)/shard_map/ppermute | solution.py:36
  904.6 73.8 %collective-permute-start.66 = (bf16[128,160]{1,0:T(8,128)(2,1)S(1)}, bf16[128,160]{1,0:T(8,128)(2,1)S(1)}, u32[]{:S(2)}, u32[]{:S(2)}) collective-permute-start(bf16[128,160]{1,0:T(8,128)(2,1)S(1)} %get-tuple-element.260), channel_id=1, source_target_pairs={{0,24},{2,26},{4,28},{6,30},{8,16},{10,18},{12,20},{14,22},{16,8},... | collective-permute-start | bytes 122888 | tf_op jit(solution)/shard_map/ppermute | solution.py:36
  (159 other events, 2706.2 us)

commit v3 on v2

--- a/solution.py
+++ b/solution.py
@@ -137,10 +137,10 @@
     return [high, (a - high.astype(F32)).astype(BF16)]
 
 
-def conv_of(v, col_ref, par_ref, length):
+def conv_of(v, col, par_ref):
     result = par_ref[BIAS : BIAS + 1, :] + par_ref[TAPS + 3 : TAPS + 4, :] * v
     for offset in range(1, 4):
-        valid = col_ref[:, VALID + offset - 1 : VALID + offset]
+        valid = col[:, VALID + offset - 1 : VALID + offset]
         result = result + par_ref[TAPS + 3 - offset : TAPS + 4 - offset, :] * (
             pltpu.roll(v, offset, 0) * valid
         )
@@ -153,21 +153,26 @@
     return causal & (seg_col == seg_row)
 
 
-def table_kernel(
-    normed_ref, weight_ref, seg_col_ref, seg_row_ref, par_ref, head_ref,
+def table_part(
+    origin, length, normed_ref, weight_ref, seg_col_ref, seg_row_ref, par_ref, head_ref,
     proj_ref, bc_ref, wide_ref, col_ref, row_ref, score_ref, turned_ref,
 ):
-    length = seg_col_ref.shape[0]
-    proj = dot(normed_ref[...], weight_ref[...])
-    proj_ref[...] = proj[:, : 2 * LANES]
-    raw = proj[:, 2 * LANES :] + head_ref[0:1, :HEADS]
+    every = pl.ds(origin, length)
+    blocks = length // BLOCK
+
+    def spot(block):
+        return pl.ds(pl.multiple_of(origin + block * BLOCK, BLOCK), BLOCK)
+
+    proj = dot(normed_ref[every, :], weight_ref[...])
+    proj_ref[every, :] = proj[:, : 2 * LANES]
+    raw = proj[:, 2 * LANES : 2 * LANES + HEADS] + head_ref[0:1, :HEADS]
     dt = jnp.maximum(raw, 0.0) + jnp.log1p(jnp.exp(-jnp.abs(raw)))
     step = dt * head_ref[1:2, :HEADS]
-    seg = seg_col_ref[...]
+    seg = seg_col_ref[every, :]
     place = iota((length, 1), 0)
     number = place // BLOCK
     before, last = jnp.full((length, 1), -2.0, F32), jnp.zeros((length, 1), F32)
-    for block in range(length // BLOCK):
+    for block in range(blocks):
         end = seg[(block + 1) * BLOCK - 1 : (block + 1) * BLOCK, :]
         last = jnp.where(number == block, end, last)
         before = jnp.where(number == block + 1, end, before)
@@ -175,14 +180,14 @@
     upper = (iota((BLOCK, BLOCK), 0) <= iota((BLOCK, BLOCK), 1)).astype(F32)
     eye = (iota((BLOCK, BLOCK), 0) == iota((BLOCK, BLOCK), 1)).astype(F32)
     cums = []
-    for block in range(length // BLOCK):
+    for block in range(blocks):
         rows = slice(block * BLOCK, (block + 1) * BLOCK)
         cums.append(dot(lower, step[rows], NN, HIGH))
         cum_rows = dot(step[rows], upper, TN, HIGH)
         raw_rows = dot(raw[rows], eye, TN, HIGH)
         for tile in range(HEADS // GROUP):
             heads = slice(tile * GROUP, (tile + 1) * GROUP)
-            row_ref[tile * 8 : (tile + 1) * 8, rows] = jnp.concatenate(
+            row_ref[tile * 8 : (tile + 1) * 8, spot(block)] = jnp.concatenate(
                 [cum_rows[heads], raw_rows[heads]], axis=0
             )
     cum = jnp.concatenate(cums, axis=0)
@@ -193,62 +198,69 @@
         col = jnp.where(lane == VALID + offset - 1, valid.astype(F32), col)
     col = jnp.where(lane == LINK, (seg == before).astype(F32), col)
     col = jnp.where(lane == KEEP, (seg == last).astype(F32), col)
-    col_ref[...] = jnp.where(lane == SEG, seg, col)
-    wide_ref[...] = jnp.concatenate(
+    col = jnp.where(lane == SEG, seg, col)
+    col_ref[every, :] = col
+    wide_ref[every, :] = jnp.concatenate(
         thirds(dt) + thirds(cum) + [jnp.zeros((length, LANES - 6 * HEADS), BF16)], axis=1
     )
-    conv = conv_of(proj_ref[...], col_ref, par_ref, length)
-    bc_ref[...] = conv * sigmoid(conv)
-    for block in range(length // BLOCK):
+    conv = conv_of(proj[:, : 2 * LANES], col, par_ref)
+    bc_ref[every, :] = conv * sigmoid(conv)
+    for block in range(blocks):
         rows = slice(block * BLOCK, (block + 1) * BLOCK)
-        b_rows, c_rows = bc_ref[rows, :LANES], bc_ref[rows, LANES:]
-        seg_col, seg_row = seg[rows], seg_row_ref[:, rows]
-        score_ref[rows, :] = jnp.where(
+        at = spot(block)
+        b_rows, c_rows = bc_ref[at, :LANES], bc_ref[at, LANES:]
+        seg_col, seg_row = seg[rows], seg_row_ref[:, at]
+        score_ref[at, :] = jnp.where(
             pair_mask(seg_col, seg_row, False), dot(c_rows, b_rows, NT, HIGH), 0.0
         )
-        turned_ref[rows, :] = jnp.where(
+        turned_ref[at, :] = jnp.where(
             pair_mask(seg_col, seg_row, True), dot(b_rows, c_rows, NT, HIGH), 0.0
         )
 
 
-def forward_kernel(*refs, pieces):
-    (
-        normed_ref, cot_ref, bc_ref, wide_ref, pick_ref, col_ref, row_ref, score_ref, par_ref, sum_in_ref,
-        w_ref, z_ref, dyn_ref, y_ref, state_ref, sum_ref, xs_ref, carry_ref,
-    ) = refs[pieces:]
+def table_kernel(*refs):
+    table_part(0, refs[0].shape[0], *refs)
+
+
+def forward_tile(
+    origin, first_row, normed_ref, cot_ref, w_ref, bc_ref, wide_ref, pick_ref, col_ref, row_ref, score_ref,
+    par_ref, z_ref, dyn_ref, y_ref, state_ref, sum_ref, xs_ref, carry_ref,
+):
     length = xs_ref.shape[0]
     blocks = length // BLOCK
 
-    @pl.when(pl.program_id(0) == 0)
-    def _():
-        depth = refs[0].shape[0]
-        for number in range(pieces):
-            w_ref[number * depth : (number + 1) * depth, :] = refs[number][...]
+    def spot(number):
+        return pl.ds(pl.multiple_of(origin + number * BLOCK, BLOCK), BLOCK)
 
     def project(number, carried):
         rows = pl.ds(pl.multiple_of(number * BLOCK, BLOCK), BLOCK)
-        z_ref[rows, :] = dot(normed_ref[rows, :], w_ref[:, : 2 * TILE])
-        dyn_ref[rows, :] = dot(cot_ref[rows, :], w_ref[:, 2 * TILE :])
+        z_ref[rows, :] = dot(normed_ref[spot(number), :], w_ref[:, : 2 * TILE])
+        dyn_ref[rows, :] = dot(cot_ref[spot(number), :], w_ref[:, 2 * TILE :])
         return carried
 
     lax.fori_loop(0, blocks, project, 0)
-    conv = conv_of(z_ref[:, TILE:], col_ref, par_ref, length)
+    conv = conv_of(z_ref[:, TILE:], col_ref[pl.ds(origin, length), :], par_ref)
     xs_ref[...] = conv * sigmoid(conv)
     carry_ref[...] = jnp.zeros_like(carry_ref)
+    ones = jnp.ones((8, TILE), BF16)
+
+    def row_sum(a):
+        return sum(dot(ones, part, NT) for part in halves(a))
 
     def one_block(number, carried):
-        rows = pl.ds(pl.multiple_of(number * BLOCK, BLOCK), BLOCK)
-        b_rows, c_rows = bc_ref[rows, :LANES], bc_ref[rows, LANES:]
-        col = col_ref[rows, :]
-        scores = score_ref[rows, :]
+        rows, at = pl.ds(pl.multiple_of(number * BLOCK, BLOCK), BLOCK), spot(number)
+        b_rows, c_rows = bc_ref[at, :LANES], bc_ref[at, LANES:]
+        col = col_ref[at, :]
+        scores = score_ref[at, :]
         x = xs_ref[rows, :]
-        wide = dot(wide_ref[rows, :], pick_ref[...])
+        wide = dot(wide_ref[at, :], pick_ref[...])
         dt_wide, cum_wide = wide[:, :TILE], wide[:, TILE:]
+        cum_rows = row_ref[pl.ds(first_row, 8), at]
         dtx = x * dt_wide
         dtx_low = dtx.astype(BF16)
         parts = []
         for head in range(GROUP):
-            gap = cum_wide[:, head * WIDTH : head * WIDTH + 1] - row_ref[head : head + 1, rows]
+            gap = cum_wide[:, head * WIDTH : head * WIDTH + 1] - cum_rows[head : head + 1, :]
             mixing = scores * jnp.exp(jnp.minimum(gap, 0.0))
             parts.append(dot(mixing.astype(BF16), dtx_low[:, head * WIDTH : (head + 1) * WIDTH]))
         within = jnp.concatenate(parts, axis=1)
@@ -261,15 +273,235 @@
         y_ref[rows, :] = y
         z = z_ref[rows, :TILE]
         yg = y * z * sigmoid(z)
-        first = jnp.sum(yg * yg, axis=1, keepdims=True)
-        second = jnp.sum(yg * par_ref[GAIN : GAIN + 1, :] * dyn_ref[rows, :], axis=1, keepdims=True)
-        lane = iota((BLOCK, 8), 1)
-        sum_ref[rows, :] = sum_in_ref[rows, :] + jnp.where(
-            lane == 0, first, jnp.where(lane == 1, second, 0.0)
-        )
+        first = row_sum(yg * yg)
+        second = row_sum(yg * par_ref[GAIN : GAIN + 1, :] * dyn_ref[rows, :])
+        place = iota((8, BLOCK), 0)
+        sum_ref[:, at] += jnp.where(place == 0, first, jnp.where(place == 1, second, 0.0))
         return carried
 
     lax.fori_loop(0, blocks, one_block, 0)
+
+
+def forward_kernel(*refs, pieces):
+    normed_ref, cot_ref, bc_ref, wide_ref, pick_ref, col_ref, row_ref, score_ref, par_ref = refs[pieces : pieces + 9]
+    w_ref, z_ref, dyn_ref, y_ref, state_ref, sum_ref, xs_ref, carry_ref = refs[pieces + 9 :]
+
+    @pl.when(pl.program_id(0) == 0)
+    def _():
+        depth = refs[0].shape[0]
+        for number in range(pieces):
+            w_ref[number * depth : (number + 1) * depth, :] = refs[number][...]
+
+    sum_ref[...] = jnp.zeros_like(sum_ref)
+    forward_tile(
+        0, 0, normed_ref, cot_ref, w_ref, bc_ref, wide_ref, pick_ref, col_ref, row_ref, score_ref, par_ref,
+        z_ref, dyn_ref, y_ref, state_ref, sum_ref, xs_ref, carry_ref,
+    )
+
+
+def gather_kernel(
+    normed_ref, cot_ref, own_ref, other_ref, small_own_ref, small_other_ref, seg_col_ref, seg_row_ref,
+    bc_par_ref, head_ref, pick_ref, par_ref,
+    normed_out, cot_out, w_out, small_out, z_ref, dyn_ref, y_ref, state_ref, proj_out, bc_out, wide_out, col_out, row_out,
+    turned_out, norm_ref,
+    normed_all, cot_all, w_all, small_all, proj_all, bc_all, wide_all, col_all, row_all, score_all, turned_all,
+    sum_ref, sum_recv, xs_ref, carry_ref,
+    here_sem, out_sem, act_send, act_recv, x_send, x_recv, z_send, z_recv, y_send, y_recv, sum_send, sum_recv_sem,
+    *, tiles, spans, inner_total,
+):
+    tile, sequence = pl.program_id(0), pl.program_id(1)
+    length = xs_ref.shape[0]
+    rows = normed_ref.shape[0]
+    depth = own_ref.shape[1]
+    part = 2 * depth
+    dp, mp = lax.axis_index("dp"), lax.axis_index("mp")
+    side = lax.rem(dp, 2)
+    mine = pl.ds(pl.multiple_of(mp * rows, rows), rows)
+    theirs = pl.ds(pl.multiple_of(length + mp * rows, rows), rows)
+    slab = pl.ds(pl.multiple_of(side * depth, depth), depth)
+    other_core = (dp, 1 - mp)
+
+    def along(bits):
+        return (jnp.bitwise_xor(dp, bits), mp)
+
+    def remote(src, dst, send, recv, device):
+        return pltpu.make_async_remote_copy(
+            src_ref=src, dst_ref=dst, send_sem=send, recv_sem=recv, device_id=device,
+            device_id_type=pl.DeviceIdType.MESH,
+        )
+
+    arrays = ((normed_ref, normed_all), (cot_ref, cot_all))
+
+    def act_here(a):
+        return pltpu.make_async_copy(arrays[a][0], arrays[a][1].at[mine, :], here_sem.at[a])
+
+    def act_core(a):
+        return remote(
+            arrays[a][0], arrays[a][1].at[mine, :], act_send.at[a, 0], act_recv.at[a, 0], other_core
+        )
+
+    def act_x(a):
+        return remote(
+            arrays[a][0], arrays[a][1].at[theirs, :], act_send.at[a, 1], act_recv.at[a, 1], along(1)
+        )
+
+    def act_pass(a):
+        return remote(
+            arrays[a][1].at[theirs, :], arrays[a][1].at[theirs, :], act_send.at[a, 2], act_recv.at[a, 2], other_core
+        )
+
+    def weight_of(number):
+        return small_all if number == 0 else w_all.at[number - 1]
+
+    def w_here(number):
+        src = small_own_ref if number == 0 else own_ref.at[number - 1]
+        return pltpu.make_async_copy(src, weight_of(number).at[slab, :], here_sem.at[2 + number])
+
+    def w_x(number):
+        src = small_other_ref if number == 0 else other_ref.at[number - 1]
+        return remote(src, weight_of(number).at[slab, :], x_send.at[number], x_recv.at[number], along(1))
+
+    def w_z(number, k):
+        ref = weight_of(number)
+        return remote(
+            ref.at[pl.ds(0, part), :], ref.at[pl.ds(k * part, part), :],
+            z_send.at[number, k - 1], z_recv.at[number, k - 1], along(4 * k),
+        )
+
+    def w_y(number, k):
+        ref = weight_of(number)
+        return remote(
+            ref.at[pl.ds(k * part, part), :], ref.at[pl.ds((spans + k) * part, part), :],
+            y_send.at[number, k], y_recv.at[number, k], along(2),
+        )
+
+    def begin_z(number):
+        w_here(number).wait()
+        w_x(number).wait_recv()
+        for k in range(1, spans):
+            w_z(number, k).start()
+        w_y(number, 0).start()
+
+    def begin_y(number):
+        for k in range(1, spans):
+            w_z(number, k).wait_recv()
+            w_y(number, k).start()
+
+    def complete(number):
+        for k in range(spans):
+            w_y(number, k).wait_recv()
+
+    tables = (
+        (normed_all, normed_out), (cot_all, cot_out), (proj_all, proj_out), (bc_all, bc_out),
+        (wide_all, wide_out), (col_all, col_out), (row_all, row_out), (turned_all, turned_out),
+        (small_all, small_out),
+    )
+
+    def table_out(at):
+        return pltpu.make_async_copy(tables[at][0], tables[at][1], out_sem.at[at])
+
+    def weight_out(number):
+        return pltpu.make_async_copy(w_all.at[number], w_out.at[number], out_sem.at[len(tables) + number])
+
+    def make_tables(origin):
+        table_part(
+            origin, length, normed_all, small_all, seg_col_ref, seg_row_ref, bc_par_ref, head_ref,
+            proj_all, bc_all, wide_all, col_all, row_all, score_all, turned_all,
+        )
+
+    @pl.when((tile == 0) & (sequence == 0))
+    def _():
+        barrier = pltpu.get_barrier_semaphore()
+        partners = [along(1), along(2), other_core] + [along(4 * k) for k in range(1, spans)]
+        for device in partners:
+            pl.semaphore_signal(barrier, inc=1, device_id=device, device_id_type=pl.DeviceIdType.MESH)
+        for number in range(tiles + 1):
+            w_here(number).start()
+        act_here(0).start()
+        act_here(1).start()
+        sum_ref[...] = jnp.zeros_like(sum_ref)
+        pl.semaphore_wait(barrier, len(partners))
+        w_x(0).start()
+        w_x(1).start()
+        act_core(0).start()
+        act_core(1).start()
+        act_x(0).start()
+        begin_z(0)
+        begin_z(1)
+        for number in range(2, tiles + 1):
+            w_x(number).start()
+        act_x(1).start()
+        begin_y(0)
+        begin_z(2)
+        act_here(0).wait()
+        act_core(0).wait_recv()
+        complete(0)
+        make_tables(0)
+        begin_y(1)
+        act_x(0).wait_recv()
+        act_pass(0).start()
+        act_here(1).wait()
+        act_core(1).wait_recv()
+
+    for number in range(tiles):
+
+        @pl.when((tile == number) & (sequence == 0))
+        def _(number=number):
+            if number + 3 <= tiles:
+                begin_z(number + 3)
+            if number + 2 <= tiles:
+                begin_y(number + 2)
+            complete(number + 1)
+            weight_out(number).start()
+
+    @pl.when((tile == 0) & (sequence == 1))
+    def _():
+        act_pass(0).wait_recv()
+        make_tables(length)
+        act_x(1).wait_recv()
+        act_pass(1).start()
+        act_pass(1).wait_recv()
+        for at in range(len(tables)):
+            table_out(at).start()
+
+    forward_tile(
+        sequence * length, tile * 8, normed_all, cot_all, w_all.at[tile], bc_all, wide_all, pick_ref, col_all,
+        row_all, score_all, par_ref, z_ref, dyn_ref, y_ref, state_ref, sum_ref, xs_ref, carry_ref,
+    )
+
+    @pl.when((tile == tiles - 1) & (sequence == 1))
+    def _():
+        between = remote(sum_ref, sum_recv.at[0], sum_send.at[0], sum_recv_sem.at[0], other_core)
+        between.start()
+        between.wait()
+        sum_ref[...] += sum_recv[0]
+        across = remote(sum_ref, sum_recv.at[1], sum_send.at[1], sum_recv_sem.at[1], along(1))
+        across.start()
+        across.wait()
+        norm_ref[...] = norm_rows(
+            sum_ref[...] + jnp.concatenate([sum_recv[1, :, length:], sum_recv[1, :, :length]], axis=1),
+            inner_total,
+        )
+        for a in range(2):
+            act_core(a).wait_send()
+            act_x(a).wait_send()
+            act_pass(a).wait_send()
+        for number in range(tiles + 1):
+            w_x(number).wait_send()
+            for k in range(1, spans):
+                w_z(number, k).wait_send()
+            for k in range(spans):
+                w_y(number, k).wait_send()
+        for at in range(len(tables)):
+            table_out(at).wait()
+        for number in range(tiles):
+            weight_out(number).wait()
+
+
+def norm_rows(sums, inner_total):
+    inverse = lax.rsqrt(sums[0:1] / inner_total + EPSILON)
+    cross = inverse * inverse * inverse / inner_total * sums[1:2]
+    return jnp.concatenate([inverse, cross, jnp.zeros((6, sums.shape[1]), F32)], axis=0)
 
 
 def backward_tile(
@@ -279,7 +511,7 @@
 ):
     length = xs_ref.shape[0]
     blocks = length // BLOCK
-    conv = conv_of(z_ref[:, TILE:], col_ref, par_ref, length)
+    conv = conv_of(z_ref[:, TILE:], col_ref[...], par_ref)
     gate = sigmoid(conv)
     xs_ref[...] = conv * gate
     dconv_ref[...] = gate * (1.0 + conv * (1.0 - gate))
@@ -293,7 +525,8 @@
         col = col_ref[rows, :]
         z, y, dyn = z_ref[rows, :TILE], y_ref[rows, :], dyn_ref[rows, :]
         gain = par_ref[GAIN : GAIN + 1, :]
-        inv, cross = norm_ref[rows, 0:1], norm_ref[rows, 1:2]
+        norms = dot(norm_ref[:, rows], (iota((8, 8), 0) == iota((8, 8), 1)).astype(F32), TN, HIGH)
+        inv, cross = norms[:, 0:1], norms[:, 1:2]
         gate = sigmoid(z)
         silu = z * gate
         yg = y * silu
@@ -607,7 +840,7 @@
     return ((row % HEADS == head) & (row // (3 * HEADS) == lane // TILE)).astype(BF16)
 
 
-def run_forward(pieces, normed, cot, bc, wide, col, rows, score, par, sums, tile, length):
+def run_forward(pieces, normed, cot, bc, wide, col, rows, score, par, tile, length):
     tokens, width = normed.shape
     number, blocks = tokens // length, length // BLOCK
     return pl.pallas_call(
@@ -624,7 +857,6 @@
             pl.BlockSpec((8, length), lambda i: (tile, i)),
             by_sequence(length, BLOCK),
             whole((8, TILE)),
-            by_sequence(length, 8),
         ],
         out_specs=[
             whole((width, 3 * TILE)),
@@ -632,7 +864,7 @@
             by_sequence(length, TILE),
             by_sequence(length, TILE),
             pl.BlockSpec((blocks, LANES, TILE), lambda i: (i, 0, 0)),
-            by_sequence(length, 8),
+            by_columns(8, length),
         ],
         out_shape=[
             shaped((width, 3 * TILE), BF16),
@@ -640,12 +872,109 @@
             shaped((tokens, TILE)),
             shaped((tokens, TILE)),
             shaped((number * blocks, LANES, TILE)),
-            shaped((tokens, 8)),
+            shaped((8, tokens)),
         ],
         scratch_shapes=[pltpu.VMEM((length, TILE), F32), pltpu.VMEM((LANES, TILE), F32)],
         compiler_params=pltpu.CompilerParams(vmem_limit_bytes=VMEM_LIMIT),
         cost_estimate=cost(2e10),
-    )(*pieces, normed, cot, bc, wide, pick_table(tile), col, rows, score, par, sums)
+    )(*pieces, normed, cot, bc, wide, pick_table(tile), col, rows, score, par)
+
+
+def run_gather(normed, cot, own, other, small_own, small_other, ids, bc_par, head_par, pars, length, spans, inner_total):
+    rows, width = normed.shape
+    tiles, _, cols = own.shape
+    small_cols = small_own.shape[1]
+    tokens, blocks = 2 * length, length // BLOCK
+
+    def by_tile(size, count):
+        return pl.BlockSpec((None, size, count), lambda j, i: (j, i, 0))
+
+    def fixed(*shape):
+        return pl.BlockSpec((None,) + shape, lambda j, i: (j,) + (0,) * len(shape))
+
+    def constant(*shape):
+        return pl.BlockSpec(shape, lambda j, i: (0,) * len(shape))
+
+    dma = pltpu.SemaphoreType.DMA
+    table_shapes = [
+        ((tokens, 2 * LANES), F32),
+        ((tokens, 2 * LANES), F32),
+        ((tokens, LANES), BF16),
+        ((tokens, COLS), F32),
+        ((2 * HEADS, tokens), F32),
+        ((tokens, BLOCK), F32),
+    ]
+    return pl.pallas_call(
+        functools.partial(gather_kernel, tiles=tiles, spans=spans, inner_total=inner_total),
+        grid=(tiles, 2),
+        in_specs=[ANY] * 6
+        + [
+            constant(tokens, 1),
+            constant(1, tokens),
+            constant(8, 2 * LANES),
+            constant(8, LANES),
+            fixed(LANES, 2 * TILE),
+            fixed(8, TILE),
+        ],
+        out_specs=[
+            ANY,
+            ANY,
+            ANY,
+            ANY,
+            by_tile(length, 2 * TILE),
+            by_tile(length, TILE),
+            by_tile(length, TILE),
+            pl.BlockSpec((None, blocks, LANES, TILE), lambda j, i: (j, i, 0, 0)),
+        ]
+        + [ANY] * 6
+        + [constant(8, tokens)],
+        out_shape=[
+            shaped((tokens, width), BF16),
+            shaped((tokens, width), BF16),
+            shaped((tiles, width, cols), BF16),
+            shaped((width, small_cols), BF16),
+            shaped((tiles, tokens, 2 * TILE)),
+            shaped((tiles, tokens, TILE)),
+            shaped((tiles, tokens, TILE)),
+            shaped((tiles, 2 * blocks, LANES, TILE)),
+        ]
+        + [shaped(*one) for one in table_shapes]
+        + [shaped((8, tokens))],
+        scratch_shapes=[
+            pltpu.VMEM((tokens, width), BF16),
+            pltpu.VMEM((tokens, width), BF16),
+            pltpu.VMEM((tiles, width, cols), BF16),
+            pltpu.VMEM((width, small_cols), BF16),
+        ]
+        + [pltpu.VMEM(*one) for one in table_shapes[:5]]
+        + [
+            pltpu.VMEM((tokens, BLOCK), F32),
+            pltpu.VMEM((tokens, BLOCK), F32),
+            pltpu.VMEM((8, tokens), F32),
+            pltpu.VMEM((2, 8, tokens), F32),
+            pltpu.VMEM((length, TILE), F32),
+            pltpu.VMEM((LANES, TILE), F32),
+            dma((3 + tiles,)),
+            dma((9 + tiles,)),
+            dma((2, 3)),
+            dma((2, 3)),
+            dma((1 + tiles,)),
+            dma((1 + tiles,)),
+            dma((1 + tiles, spans - 1)),
+            dma((1 + tiles, spans - 1)),
+            dma((1 + tiles, spans)),
+            dma((1 + tiles, spans)),
+            dma((2,)),
+            dma((2,)),
+        ],
+        compiler_params=pltpu.CompilerParams(
+            vmem_limit_bytes=VMEM_LIMIT, collective_id=2, has_side_effects=True
+        ),
+        cost_estimate=cost(2e11),
+    )(
+        normed, cot, own, other, small_own, small_other, ids[:, None], ids[None, :], bc_par, head_par,
+        jnp.stack([pick_table(tile) for tile in range(tiles)]), pars,
+    )
 
 
 def run_backward(normed, cot, zv, y, dyn, bc, wide, col, rows, ids, turned, norms, par, state, length, spans):
@@ -684,7 +1013,7 @@
             pl.BlockSpec((8, length), lambda j, i: (j, i)),
             pl.BlockSpec((1, length), lambda j, i: (0, i)),
             shared(length, BLOCK),
-            shared(length, 8),
+            pl.BlockSpec((8, length), lambda j, i: (0, i)),
             fixed(8, TILE),
             pl.BlockSpec((None, blocks, LANES, TILE), lambda j, i: (j, i, 0, 0)),
         ],
@@ -802,82 +1131,76 @@
     packed = packed.reshape(2, tiles, depth, 3 * TILE)
 
     def small_weights(side):
-        return jnp.concatenate([w_bc, of_side(w_dt, side, 1)], axis=1)
-
-    small_other = flip(small_weights(1 - x_side), "dp", 1)
+        filler = jnp.zeros((depth, LANES - own_heads), BF16)
+        return jnp.concatenate([w_bc, of_side(w_dt, side, 1), filler], axis=1)
+
     packed_own = lax.dynamic_index_in_dim(packed, x_side, 0, False)
-    packed_other = flip(lax.dynamic_index_in_dim(packed, 1 - x_side, 0, False), "dp", 1)
+    packed_other = lax.dynamic_index_in_dim(packed, 1 - x_side, 0, False)
 
     def gathered(piece):
         near = [piece] + [flip(piece, "dp", 4 * k) for k in range(1, far)]
         return near + [flip(p, "dp", 2) for p in near]
 
-    bc_weight = jnp.concatenate(
-        gathered(by_side(small_weights(x_side), small_other, 0)), axis=0
-    )
-
     normed, cot, inverse_rows = input_norm(hidden_in, cotangent, norm_gain, dp, extent)
 
-    def both_sequences(a):
-        near = flip(a, "dp", 1)
-        return by_core(a, flip(a, "mp", 1), 0), by_core(near, flip(near, "mp", 1), 0)
-
-    normed_own, normed_near = both_sequences(normed)
-    normed_all = jnp.concatenate([normed_own, normed_near], axis=0)
-    pieces = [gathered(by_side(packed_own[tile], packed_other[tile], 0)) for tile in range(tiles)]
-    cot_all = jnp.concatenate(both_sequences(cot), axis=0)
     ids = (segments, flip(segments, "dp", 1))
-
     ids_all = jnp.concatenate(ids, axis=0).astype(F32)
     side_bias = of_side(dt_bias, x_side, 0)
     rate = -jnp.exp(of_side(a_log, x_side, 0))
     bc_par = jnp.concatenate([conv_bc, conv_bc_bias[None], jnp.zeros((3, 2 * LANES), F32)], axis=0)
     head_par = jnp.pad(jnp.stack([side_bias, rate]), ((0, 6), (0, LANES - own_heads)))
-    proj_bc, bc, wide, col, rows_all, score, turned = run_tables(
-        normed_all, bc_weight, ids_all, bc_par, head_par, length
-    )
-    tokens = normed_all.shape[0]
-
-    def tile_of(a, tile):
-        return of_side(a, x_side, a.ndim - 1)[..., tile * TILE : (tile + 1) * TILE]
-
-    skip_wide = jnp.repeat(d_skip, WIDTH)
-    params = [
-        jnp.concatenate(
-            [
-                tile_of(conv_x, tile),
-                tile_of(conv_x_bias, tile)[None],
-                tile_of(skip_wide, tile)[None],
-                tile_of(gated_gain, tile)[None],
-                jnp.zeros((1, TILE), F32),
-            ],
-            axis=0,
-        )
-        for tile in range(tiles)
-    ]
-
-    weights, zvs, dyns, ys, states = [], [], [], [], []
-    sums = jnp.zeros((tokens, 8), F32)
-    for tile in range(tiles):
-        weight, zv, dyn, y, state, sums = run_forward(
-            pieces[tile], normed_all, cot_all, bc, wide, col, rows_all, score, params[tile], sums, tile, length
-        )
-        weights.append(weight)
-        zvs.append(zv)
-        dyns.append(dyn)
-        ys.append(y)
-        states.append(state)
-    sums = sums + flip(sums, "mp", 1)
-    near = flip(sums, "dp", 1)
-    sums = sums + jnp.concatenate([near[length:], near[:length]], axis=0)
-    inverse_gated = lax.rsqrt(sums[:, :1] / inner_total + EPSILON)
-    cross = inverse_gated * inverse_gated * inverse_gated / inner_total * sums[:, 1:2]
-    lane = jnp.arange(8)[None, :]
-    norms = jnp.where(lane == 0, inverse_gated, jnp.where(lane == 1, cross, 0.0))
+    params = jnp.concatenate(
+        [
+            of_side(conv_x, x_side, 1),
+            of_side(conv_x_bias, x_side, 0)[None],
+            of_side(jnp.repeat(d_skip, WIDTH), x_side, 0)[None],
+            of_side(gated_gain, x_side, 0)[None],
+            jnp.zeros((1, quarter), F32),
+        ],
+        axis=0,
+    )
+    params = params.reshape(8, tiles, TILE).transpose(1, 0, 2)
+    tokens = 2 * length
+    if depth == LANES:
+        (
+            normed_all, cot_all, weights, bc_weight, zvs, dyns, ys, states, proj_bc, bc, wide, col, rows_all, turned, norms,
+        ) = run_gather(
+            normed, cot, packed_own, packed_other, small_weights(x_side), small_weights(1 - x_side), ids_all,
+            bc_par, head_par, params, length, far, inner_total,
+        )
+    else:
+
+        def both_sequences(a):
+            near = flip(a, "dp", 1)
+            return jnp.concatenate(
+                [by_core(a, flip(a, "mp", 1), 0), by_core(near, flip(near, "mp", 1), 0)], axis=0
+            )
+
+        normed_all, cot_all = both_sequences(normed), both_sequences(cot)
+        packed_other = flip(packed_other, "dp", 1)
+        small_other = flip(small_weights(1 - x_side), "dp", 1)
+        bc_weight = jnp.concatenate(gathered(by_side(small_weights(x_side), small_other, 0)), axis=0)
+        proj_bc, bc, wide, col, rows_all, score, turned = run_tables(
+            normed_all, bc_weight, ids_all, bc_par, head_par, length
+        )
+        results = []
+        for tile in range(tiles):
+            pieces = gathered(by_side(packed_own[tile], packed_other[tile], 0))
+            results.append(
+                run_forward(
+                    pieces, normed_all, cot_all, bc, wide, col, rows_all, score, params[tile], tile, length
+                )
+            )
+        weights, zvs, dyns, ys, states, sums = [jnp.stack(part) for part in zip(*results)]
+        sums = jnp.sum(sums, axis=0)
+        sums = sums + flip(sums, "mp", 1)
+        near = flip(sums, "dp", 1)
+        sums = sums + jnp.concatenate([near[:, length:], near[:, :length]], axis=1)
+        norms = norm_rows(sums, inner_total)
 
     inside, (grads, dbc, step_rows, step_cols, smalls, far_share, near_share, inner_totals) = run_backward(
-        normed_all, cot_all, jnp.stack(zvs), jnp.stack(ys), jnp.stack(dyns), bc, wide, col, rows_all, ids_all,
-        turned, norms, jnp.stack(params), jnp.stack(states), length, far,
+        normed_all, cot_all, zvs, ys, dyns, bc, wide, col, rows_all, ids_all, turned, norms, params, states,
+        length, far,
     )
 
     def spread_sum(far_part, near_part):
@@ -931,7 +1254,7 @@
 
     small_grad = jnp.concatenate(
         [
-            dot(normed_own, lax.dynamic_slice_in_dim(bc_grad, mp * LANES, LANES, 1), TN),
+            dot(normed_all[:length], lax.dynamic_slice_in_dim(bc_grad, mp * LANES, LANES, 1), TN),
             placed(dot(normed_all, dt_grad, TN)),
         ],
         axis=1,
@@ -972,7 +1295,7 @@
     )
 
     zv_all = jnp.concatenate([w[:, : 2 * TILE] for w in weights], axis=1)
-    dt_weight = bc_weight[:, 2 * LANES :]
+    dt_weight = bc_weight[:, 2 * LANES : 2 * LANES + own_heads]
     dzx_all = jnp.concatenate([g[:, : 2 * TILE] for g in grads], axis=1)
     d_normed = token_sum(
         lambda pick: dot(pick(dzx_all), zv_all, NT) + dot(pick(dt_grad), dt_weight, NT)

time: 1010 us -> 839 us (0.83)
  waiting for transfers between devices: 243 us -> 120 us
  Pallas kernels: 348 us -> 452 us
  starting transfers between devices: 97.5 us -> 28 us
  other arithmetic: 126 us -> 64.4 us
  local copies, waits for them, and re-layouts: 120 us -> 103 us
    ppermute x72 -> x27, waiting for transfers between devices: 243 us -> 120 us  [flip(): return lax.ppermute(a, axis, [(i, i ^ bit) for i in range(size)])]
    pallas_call x5 -> x1, Pallas kernels: 130 us -> 218 us  [run_gather(): pl.pallas_call(functools.partial(gather_kernel, tiles=tiles, spans=spans,...]
    ppermute x72 -> x27, starting transfers between devices: 97.5 us -> 28 us  [flip(): return lax.ppermute(a, axis, [(i, i ^ bit) for i in range(size)])]
    another operation x6 -> x1, other arithmetic: 19.5 us -> 0.92 us  [run_gather(): jnp.stack([pick_table(tile) for tile in range(tiles)])]
    concatenate x5 -> x2, other arithmetic: 19.6 us -> 1.85 us  [the longest x1 1.15 us: local(): jnp.concatenate([dot(normed_all[:length], lax.dynamic_slice_in_dim(bc_gra...]
    select_n x5 -> x1, other arithmetic: 18.1 us -> 0.67 us  [by_core(): jnp.where(mp == 0, jnp.concatenate([own, other], axis=axis), jnp.concaten...]
    pallas_call x1, Pallas kernels: 203 us -> 219 us  [run_backward(): pl.pallas_call(functools.partial(backward_kernel, inside=inside, tiles=ti...]
    unnamed x263 -> x133, local copies, waits for them, and re-layouts: 35.9 us -> 21.1 us
  transfers between devices with their start and end apart: 72 -> 27, of which waited for: 22 -> 13; matrix products, arithmetic and copies ran while one was open for 27% -> 21% of each run, Pallas kernels for 12% -> 2%
where the time goes in v3:
time: 839 us; the launch traced here: 834 us
  Pallas kernels  452 us (54%)
  waiting for transfers between devices  120 us (14%)
  local copies, waits for them, and re-layouts  103 us (12%)
  other arithmetic  64.4 us (8%)
  matrix products  59.2 us (7%)
  starting transfers between devices  28 us (3%)
    pallas_call x1, Pallas kernels, run_backward(): pl.pallas_call(functools.partial(backward_kernel, inside=inside, tiles=ti...  219 us
    pallas_call x1, Pallas kernels, run_gather(): pl.pallas_call(functools.partial(gather_kernel, tiles=tiles, spans=spans,...  218 us
    ppermute x27, waiting for transfers between devices, flip(): return lax.ppermute(a, axis, [(i, i ^ bit) for i in range(size)])  120 us
    dot_general x9, matrix products, dot(): lax.dot_general(a, b, dims, precision=precision, preferred_element_type=F32)  59.2 us
    ppermute x27, starting transfers between devices, flip(): return lax.ppermute(a, axis, [(i, i ^ bit) for i in range(size)])  28 us
    unnamed x133, local copies, waits for them, and re-layouts  21.1 us
  transfers between devices with their start and end apart: 27, of which 13 were waited for; matrix products, arithmetic and copies ran while one was open for 21% of the time, Pallas kernels for 2%

profile of v3, /device:TPU:0, one launch (start us, length us, event | category | flops | bytes accessed | tf_op | source)
XLA Modules:
  0.0 833.6 jit_solution(14359270670593965407)
XLA Ops:
  9.5 3.5 fusion.79
  15.1 5.2 shard_map.287
  31.4 217.9 %shard_map.288 = (bf16[2048,2048]{1,0:T(8,128)(2,1)}, bf16[2048,2048]{1,0:T(8,128)(2,1)}, bf16[4,2048,768]{2,1,0:T(8,128)(2,1)}, bf16[2048,384]{1,0:T(8,128)(2,1...) custom-call(bf16[512,2048]{1,0:T(8,128)(2,1)} %get-tuple-element.43., ...), custom_call_target="tpu_custom_call" | custom-call | flops 199999995904 | bytes 10000000 | tf_op jit(solution)/shard_map/pallas_call | solution.py:907
  253.9 218.9 %shard_map.289 = (bf16[4,2048,768]{2,1,0:T(8,128)(2,1)}, f32[2048,256]{1,0:T(8,128)}, f32[32,2048]{1,0:T(8,128)}, f32[4,2048,16]{2,1,0:T(8,128)}, f32[4,2,8,256]...) custom-call(bf16[2048,2048]{1,0:T(8,128)(2,1)} %get-tuple-element.45.normed_, ...), custom_call_target="tpu_custom_call" | custom-call | flops 199999995904 | bytes 10000000 | tf_op jit(solution)/shard_map/pallas_call | solution.py:1000
  473.6 5.1 slice_bitcast_fusion.7
  512.3 5.3 add_divide_fusion
  520.5 10.4 %fusion.10 = (f32[4,4]{1,0:T(4,128)S(1)}, f32[4,4]{1,0:T(4,128)S(1)}, f32[4,4,2048]{1,2,0:T(8,128)}, f32[4,4,2048]{1,2,0:T(8,128)}) fusion(f32[4,1,4,2048]{2,3,0,1:T(8,128)} %copy.156, f32[4,4]{1,0:T(4,128)S(1)} %copy-done.44, f32[4,16,2048]{1,2,0:T(8,128)} %bitcast.183, f32[4,4,2048]{1,2,0:T(8,128)} %copy.155), kind=kLoop, calls=%fused_computation.23 | loop fusion | flops 524256 | bytes 786624 | tf_op jit(solution)/shard_map/reduce_sum | solution.py:1248
  537.1 3.8 pad_maximum_fusion
  544.2 12.4 %fusion.26 = f32[1024,2048]{1,0:T(8,128)S(1)} fusion(bf16[1024,2048]{1,0:T(8,128)(2,1)} %bitcast.192, bf16[2048,512]{1,0:T(8,128)(2,1)} %slice.329, bf16[2048,512]{1,0:T(8,128)(2,1)} %slice.328, bf16[2048,512]{1,0:T(8,128)(2,1)} %slice.327, bf16[2048,512]{1,0:T(8,128)(2,1)} %slice.326), kind=kOutput, calls=%fused_computation.69 | convolution fusion | flops 8623489024 | bytes 20971520 | tf_op jit(solution)/shard_map/dot_general | solution.py:27
  556.7 13.6 %fusion.27 = f32[1024,2048]{1,0:T(8,128)} fusion(bf16[1024,2048]{1,0:T(8,128)(2,1)S(1)} %bitcast.191, bf16[2048,512]{1,0:T(8,128)(2,1)} %slice.329, bf16[2048,512]{1,0:T(8,128)(2,1)} %slice.328, bf16[2048,512]{1,0:T(8,128)(2,1)} %slice.327, bf16[2048,512]{1,0:T(8,128)(2,1)} %slice.326), kind=kOutput, calls=%fused_computation.70 | convolution fusion | flops 8623489024 | bytes 20971520 | tf_op jit(solution)/shard_map/dot_general | solution.py:27
  570.3 4.5 add_convert_fusion
  578.8 6.1 convolution_convert_fusion
  591.7 7.2 collective-permute-done.13
  598.9 8.6 %collective-permute-done.15 = bf16[768,256]{1,0:T(8,128)(2,1)S(1)} collective-permute-done((bf16[768,256]{1,0:T(8,128)(2,1)S(1)}, bf16[768,256]{1,0:T(8,128)(2,1)S(1)}, u32[]{:S(2)}, u32[]{:S(2)}) %collective-permute-start.15) | collective-permute-done | bytes 393248 | tf_op jit(solution)/shard_map/ppermute | solution.py:36
  607.5 17.0 %collective-permute-done.14 = bf16[768,256]{1,0:T(8,128)(2,1)S(1)} collective-permute-done((bf16[768,256]{1,0:T(8,128)(2,1)S(1)}, bf16[768,256]{1,0:T(8,128)(2,1)S(1)}, u32[]{:S(2)}, u32[]{:S(2)}) %collective-permute-start.14) | collective-permute-done | bytes 393248 | tf_op jit(solution)/shard_map/ppermute | solution.py:36
  630.5 14.9 %collective-permute-done.16 = bf16[4,768,128]{2,1,0:T(8,128)(2,1)S(1)} collective-permute-done((bf16[4,768,128]{2,1,0:T(8,128)(2,1)S(1)}, bf16[4,768,128]{2,1,0:T(8,128)(2,1)S(1)}, u32[]{:S(2)}, u32[]{:S(2)}) %collective-permute-start.16) | collective-permute-done | bytes 786464 | tf_op jit(solution)/shard_map/ppermute | solution.py:36
  646.2 19.5 %collective-permute-done.6 = f32[1024,256]{1,0:T(8,128)S(1)} collective-permute-done((f32[1024,256]{1,0:T(8,128)S(1)}, f32[1024,256]{1,0:T(8,128)S(1)}, u32[]{:S(2)}, u32[]{:S(2)}) %collective-permute-start.6) | collective-permute-done | bytes 1048608 | tf_op jit(solution)/shard_map/ppermute | solution.py:36
  673.1 3.2 fusion.20
  677.5 3.2 reshape.766
  686.0 6.3 convert_add_fusion.1
  692.3 3.3 copy-done.3
  698.5 6.4 convert_add_fusion.2
  704.9 3.3 copy-done.8
  723.9 4.2 collective-permute-done.18
  732.3 13.8 %collective-permute-done.4 = bf16[512,2048]{1,0:T(8,128)(2,1)} collective-permute-done((bf16[512,2048]{1,0:T(8,128)(2,1)}, bf16[512,2048]{1,0:T(8,128)(2,1)}, u32[]{:S(2)}, u32[]{:S(2)}) %collective-permute-start.4) | collective-permute-done | bytes 2097184 | tf_op jit(solution)/shard_map/ppermute | solution.py:36
  746.1 5.7 fusion.11.in_ref
  751.8 4.9 shard_map.291
  756.7 30.4 %collective-permute-done.2 = bf16[512,2048]{1,0:T(8,128)(2,1)} collective-permute-done((bf16[512,2048]{1,0:T(8,128)(2,1)}, bf16[512,2048]{1,0:T(8,128)(2,1)}, u32[]{:S(2)}, u32[]{:S(2)}) %collective-permute-start.2) | collective-permute-done | bytes 2097184 | tf_op jit(solution)/shard_map/ppermute | solution.py:36
  787.1 5.8 slice_add_fusion.2.in_ref
  792.9 5.5 shard_map.290
  798.4 6.7 fusion
  821.1 6.7 fusion.3
  (323 shorter events, 144.5 us)
Async XLA Ops:
  0.7 22.9 %copy-start = (f32[4,2048]{1,0:T(4,128)S(1)}, f32[4,2048]{1,0:T(4,128)}, u32[]{:S(2)}) copy-start(f32[4,2048]{1,0:T(4,128)} %param.22) | copy-start | bytes 98308
  0.7 28.8 %collective-permute-start = (s32[1024]{0:T(1024)}, s32[1024]{0:T(1024)S(1)}, u32[]{:S(2)}, u32[]{:S(2)}) collective-permute-start(s32[1024]{0:T(1024)} %param.17), channel_id=1, source_target_pairs={{0,2},{2,0},{4,6},{6,4},{8,10},{10,8},{12,14},{14,12},{16,18},{18,... | collective-permute-start | bytes 12296 | tf_op jit(solution)/shard_map/ppermute | solution.py:36
  505.3 79.6 %collective-permute-start.12 = (bf16[4,768,256]{2,1,0:T(8,128)(2,1)}, bf16[4,768,256]{2,1,0:T(8,128)(2,1)}, u32[]{:S(2)}, u32[]{:S(2)}) collective-permute-start(bf16[4,768,256]{2,1,0:T(8,128)(2,1)} %bitcast.236), channel_id=1, source_target_pairs={{0,4},{2,6},{4,0},{6,2},{8,12},{10,14},{12,8},{14,10},{16,20},{18,... | collective-permute-start | bytes 4718600 | tf_op jit(solution)/shard_map/ppermute | solution.py:36
  506.9 120.0 %collective-permute-start.5 = (f32[2048,256]{1,0:T(8,128)}, f32[2048,256]{1,0:T(8,128)}, u32[]{:S(2)}, u32[]{:S(2)}) collective-permute-start(f32[2048,256]{1,0:T(8,128)} %get-tuple-element.63), channel_id=1, source_target_pairs={{0,1},{1,0},{2,3},{3,2},{4,5},{5,4},{6,7},{7,6},{8,9},{9,8},{10,11... | collective-permute-start | bytes 6291464 | tf_op jit(solution)/shard_map/ppermute | solution.py:36
  574.8 111.2 %collective-permute-start.3 = (bf16[1024,2048]{1,0:T(8,128)(2,1)}, bf16[1024,2048]{1,0:T(8,128)(2,1)}, u32[]{:S(2)}, u32[]{:S(2)}) collective-permute-start(bf16[1024,2048]{1,0:T(8,128)(2,1)} %add_convert_fusion), channel_id=1, source_target_pairs={{0,1},{1,0},{2,3},{3,2},{4,5},{5,4},{6,7},{7,6},{8,9},{9,8},{10,11... | collective-permute-start | bytes 12582920 | tf_op jit(solution)/shard_map/ppermute | solution.py:36
  586.9 12.0 %collective-permute-start.13 = (bf16[768,256]{1,0:T(8,128)(2,1)S(1)}, bf16[768,256]{1,0:T(8,128)(2,1)S(1)}, u32[]{:S(2)}, u32[]{:S(2)}) collective-permute-start(bf16[768,256]{1,0:T(8,128)(2,1)S(1)} %get-tuple-element.214), channel_id=1, source_target_pairs={{0,8},{2,10},{4,12},{6,14},{8,0},{10,2},{12,4},{14,6},{16,24},{18,... | collective-permute-start | bytes 1179656 | tf_op jit(solution)/shard_map/ppermute | solution.py:36
  587.6 19.9 %collective-permute-start.15 = (bf16[768,256]{1,0:T(8,128)(2,1)S(1)}, bf16[768,256]{1,0:T(8,128)(2,1)S(1)}, u32[]{:S(2)}, u32[]{:S(2)}) collective-permute-start(bf16[768,256]{1,0:T(8,128)(2,1)S(1)} %get-tuple-element.215), channel_id=1, source_target_pairs={{0,24},{2,26},{4,28},{6,30},{8,16},{10,18},{12,20},{14,22},{16,8},... | collective-permute-start | bytes 1179656 | tf_op jit(solution)/shard_map/ppermute | solution.py:36
  589.0 35.5 %collective-permute-start.14 = (bf16[768,256]{1,0:T(8,128)(2,1)S(1)}, bf16[768,256]{1,0:T(8,128)(2,1)S(1)}, u32[]{:S(2)}, u32[]{:S(2)}) collective-permute-start(bf16[768,256]{1,0:T(8,128)(2,1)S(1)} %get-tuple-element.216), channel_id=1, source_target_pairs={{0,16},{2,18},{4,20},{6,22},{8,24},{10,26},{12,28},{14,30},{16,0},... | collective-permute-start | bytes 1179656 | tf_op jit(solution)/shard_map/ppermute | solution.py:36
  591.7 33.0 %copy-start.5 = (f32[3,768,256]{2,1,0:T(8,128)S(1)}, f32[3,768,256]{2,1,0:T(8,128)}, u32[]{:S(2)}) copy-start(f32[3,768,256]{2,1,0:T(8,128)} %get-tuple-element.65) | copy-start | bytes 7077892
  591.7 33.8 %copy-start.53 = (f32[32]{0:T(128)S(1)}, f32[32]{0:T(128)}, u32[]{:S(2)}) copy-start(f32[32]{0:T(128)} %param.27) | copy-start | bytes 388
  598.9 98.9 %collective-permute-start.1 = (bf16[1024,2048]{1,0:T(8,128)(2,1)}, bf16[1024,2048]{1,0:T(8,128)(2,1)}, u32[]{:S(2)}, u32[]{:S(2)}) collective-permute-start(bf16[1024,2048]{1,0:T(8,128)(2,1)} %convolution_convert_fusion), channel_id=1, source_target_pairs={{0,1},{1,0},{2,3},{3,2},{4,5},{5,4},{6,7},{7,6},{8,9},{9,8},{10,11... | collective-permute-start | bytes 12582920 | tf_op jit(solution)/shard_map/ppermute | solution.py:36
  624.8 20.5 %collective-permute-start.16 = (bf16[4,768,128]{2,1,0:T(8,128)(2,1)S(1)}, bf16[4,768,128]{2,1,0:T(8,128)(2,1)S(1)}, u32[]{:S(2)}, u32[]{:S(2)}) collective-permute-start(bf16[4,768,128]{2,1,0:T(8,128)(2,1)S(1)} %fusion.24), channel_id=1, source_target_pairs={{0,2},{2,0},{4,6},{6,4},{8,10},{10,8},{12,14},{14,12},{16,18},{18,... | collective-permute-start | bytes 2359304 | tf_op jit(solution)/shard_map/ppermute | solution.py:36
  628.9 36.7 %collective-permute-start.6 = (f32[1024,256]{1,0:T(8,128)S(1)}, f32[1024,256]{1,0:T(8,128)S(1)}, u32[]{:S(2)}, u32[]{:S(2)}) collective-permute-start(f32[1024,256]{1,0:T(8,128)S(1)} %slice.337), channel_id=1, source_target_pairs={{0,2},{2,0},{4,6},{6,4},{8,10},{10,8},{12,14},{14,12},{16,18},{18,... | collective-permute-start | bytes 3145736 | tf_op jit(solution)/shard_map/ppermute | solution.py:36
  668.8 11.9 %collective-permute-start.23 = (f32[13664]{0:T(1024)S(1)}, f32[13664]{0:T(1024)S(1)}, u32[]{:S(2)}, u32[]{:S(2)}) collective-permute-start(f32[13664]{0:T(1024)S(1)} %concatenate.163), channel_id=1, source_target_pairs={{0,2},{2,0},{4,6},{6,4},{8,10},{10,8},{12,14},{14,12},{16,18},{18,... | collective-permute-start | bytes 163976 | tf_op jit(solution)/shard_map/ppermute | solution.py:36
  680.7 5.2 collective-permute-start.24
  684.4 36.1 %collective-permute-start.17 = (bf16[8,1,128,160]{3,2,0,1:T(8,128)(2,1)}, bf16[8,1,128,160]{3,2,0,1:T(8,128)(2,1)}, u32[]{:S(2)}, u32[]{:S(2)}) collective-permute-start(bf16[8,1,128,160]{3,2,0,1:T(8,128)(2,1)} %copy.160), channel_id=1, source_target_pairs={{0,2},{2,0},{4,6},{6,4},{8,10},{10,8},{12,14},{14,12},{16,18},{18,... | collective-permute-start | bytes 983048 | tf_op jit(solution)/shard_map/ppermute | solution.py:36
  685.9 29.4 %collective-permute-start.25 = (f32[13664]{0:T(1024)S(1)}, f32[13664]{0:T(1024)S(1)}, u32[]{:S(2)}, u32[]{:S(2)}) collective-permute-start(f32[13664]{0:T(1024)S(1)} %add.394), channel_id=1, source_target_pairs={{0,8},{2,10},{4,12},{6,14},{8,0},{10,2},{12,4},{14,6},{16,24},{18,... | collective-permute-start | bytes 163976 | tf_op jit(solution)/shard_map/ppermute | solution.py:36
  697.3 48.9 %collective-permute-start.4 = (bf16[512,2048]{1,0:T(8,128)(2,1)}, bf16[512,2048]{1,0:T(8,128)(2,1)}, u32[]{:S(2)}, u32[]{:S(2)}) collective-permute-start(bf16[512,2048]{1,0:T(8,128)(2,1)} %slice.430), channel_id=1, source_target_pairs={{0,2},{2,0},{4,6},{6,4},{8,10},{10,8},{12,14},{14,12},{16,18},{18,... | collective-permute-start | bytes 6291464 | tf_op jit(solution)/shard_map/ppermute | solution.py:36
  709.8 77.3 %collective-permute-start.2 = (bf16[512,2048]{1,0:T(8,128)(2,1)}, bf16[512,2048]{1,0:T(8,128)(2,1)}, u32[]{:S(2)}, u32[]{:S(2)}) collective-permute-start(bf16[512,2048]{1,0:T(8,128)(2,1)} %slice.431), channel_id=1, source_target_pairs={{0,2},{2,0},{4,6},{6,4},{8,10},{10,8},{12,14},{14,12},{16,18},{18,... | collective-permute-start | bytes 6291464 | tf_op jit(solution)/shard_map/ppermute | solution.py:36
  715.3 30.9 %copy-start.17 = (bf16[2048,384]{1,0:T(8,128)(2,1)S(1)}, bf16[2048,384]{1,0:T(8,128)(2,1)}, u32[]{:S(2)}) copy-start(bf16[2048,384]{1,0:T(8,128)(2,1)} %get-tuple-element.62) | copy-start | bytes 4718596
  715.3 5.1 collective-permute-start.26
  719.8 26.4 %copy-start.21 = (bf16[1024,256]{1,0:T(8,128)(2,1)S(1)}, bf16[1024,256]{1,0:T(8,128)(2,1)}, u32[]{:S(2)}) copy-start(bf16[1024,256]{1,0:T(8,128)(2,1)} %copy-done.20) | copy-start | bytes 1572868
  721.6 6.4 collective-permute-start.18
  728.8 78.3 %collective-permute-start.19 = (bf16[128,160]{1,0:T(8,128)(2,1)}, bf16[128,160]{1,0:T(8,128)(2,1)S(1)}, u32[]{:S(2)}, u32[]{:S(2)}) collective-permute-start(bf16[128,160]{1,0:T(8,128)(2,1)} %get-tuple-element.221), channel_id=1, source_target_pairs={{0,8},{2,10},{4,12},{6,14},{8,0},{10,2},{12,4},{14,6},{16,24},{18,... | collective-permute-start | bytes 122888 | tf_op jit(solution)/shard_map/ppermute | solution.py:36
  730.8 76.3 %collective-permute-start.21 = (bf16[128,160]{1,0:T(8,128)(2,1)}, bf16[128,160]{1,0:T(8,128)(2,1)S(1)}, u32[]{:S(2)}, u32[]{:S(2)}) collective-permute-start(bf16[128,160]{1,0:T(8,128)(2,1)} %get-tuple-element.222), channel_id=1, source_target_pairs={{0,24},{2,26},{4,28},{6,30},{8,16},{10,18},{12,20},{14,22},{16,8},... | collective-permute-start | bytes 122888 | tf_op jit(solution)/shard_map/ppermute | solution.py:36
  732.3 74.9 %collective-permute-start.20 = (bf16[128,160]{1,0:T(8,128)(2,1)S(1)}, bf16[128,160]{1,0:T(8,128)(2,1)S(1)}, u32[]{:S(2)}, u32[]{:S(2)}) collective-permute-start(bf16[128,160]{1,0:T(8,128)(2,1)S(1)} %get-tuple-element.223), channel_id=1, source_target_pairs={{0,16},{2,18},{4,20},{6,22},{8,24},{10,26},{12,28},{14,30},{16,0},... | collective-permute-start | bytes 122888 | tf_op jit(solution)/shard_map/ppermute | solution.py:36
  807.1 1.2 collective-permute-start.7
  807.2 6.3 collective-permute-start.22
  808.3 3.7 collective-permute-start.8
  812.0 3.7 collective-permute-start.9
  815.7 3.7 collective-permute-start.10
  819.4 8.4 %collective-permute-start.11 = (f32[2051]{0:T(1024)S(1)}, f32[2051]{0:T(1024)S(1)}, u32[]{:S(2)}, u32[]{:S(2)}) collective-permute-start(f32[2051]{0:T(1024)S(1)} %add.376), channel_id=1, source_target_pairs={{0,16},{2,18},{4,20},{6,22},{8,24},{10,26},{12,28},{14,30},{16,0},... | collective-permute-start | bytes 24620 | tf_op jit(solution)/shard_map/ppermute | solution.py:36
  (57 other events, 502.1 us)

commit v4 on v3

--- a/solution.py
+++ b/solution.py
@@ -118,6 +118,7 @@
 COLS = 8
 HEADS = 16
 TAPS, BIAS, SKIP, GAIN = 0, 4, 5, 6
+STEPS, OUT, SHARE = 2 * TILE, 2 * TILE + 16, 3 * TILE + 16
 ANY = pl.BlockSpec(memory_space=pl.ANY)
 
 
@@ -506,7 +507,7 @@
 
 def backward_tile(
     origin, z_ref, y_ref, dyn_ref, bc_ref, wide_ref, pick_ref, col_ref, row_ref, seg_ref, turned_ref, norm_ref,
-    par_ref, state_ref, grad_ref, dbc_ref, step_row_ref, step_col_ref, small_ref, turn_ref, xs_ref, dconv_ref,
+    par_ref, rate_ref, state_ref, grad_ref, dbc_ref, dt_ref, head_ref, small_ref, turn_ref, xs_ref, dconv_ref,
     carry_ref,
 ):
     length = xs_ref.shape[0]
@@ -517,6 +518,7 @@
     dconv_ref[...] = gate * (1.0 + conv * (1.0 - gate))
     carry_ref[...] = jnp.zeros_like(carry_ref)
     small_ref[...] = jnp.zeros_like(small_ref)
+    head_ref[...] = jnp.zeros_like(head_ref)
     down, across = iota((BLOCK, BLOCK), 0), iota((BLOCK, BLOCK), 1)
 
     def one_block(step, carried):
@@ -592,9 +594,18 @@
         run = sum(dot(after, part) for part in halves(head_sum(from_state)))
         run = run + sum(dot(prior, part) for part in halves(head_sum(to_state)))
         run = run + head_sum(jnp.broadcast_to(through, (8, TILE)))[:1]
-        step_col_ref[rows, 0:8] = run
-        step_col_ref[rows, 8:16] = head_sum(d_dtx * x)
-        step_row_ref[:, rows] = jnp.concatenate(between + between, axis=0)
+        sums = jnp.concatenate(
+            [run, head_sum(d_dtx * x), jnp.zeros((BLOCK, LANES - 16), F32)], axis=1
+        ).T
+        run_rows = sums[:GROUP] + jnp.concatenate(between, axis=0)
+        raw = row_ref[GROUP : 2 * GROUP, rows]
+        d_dt = (sums[8 : 8 + GROUP] + rate_ref[:GROUP, :1] * run_rows) * sigmoid(raw)
+        dt = jnp.maximum(raw, 0.0) + jnp.log1p(jnp.exp(-jnp.abs(raw)))
+        head_ref[:GROUP, :] += jnp.sum(d_dt, axis=1, keepdims=True)
+        head_ref[GROUP:, :] += jnp.sum(run_rows * dt, axis=1, keepdims=True)
+        d_dt = jnp.concatenate([d_dt, jnp.zeros((16 - GROUP, BLOCK), F32)], axis=0).astype(BF16)
+        dt_ref[:, rows] = d_dt
+        turn_ref[STEPS:OUT, spot] = d_dt
         return carried
 
     lax.fori_loop(0, blocks, one_block, 0)
@@ -613,17 +624,19 @@
     for number in range(blocks):
         rows = slice(number * BLOCK, (number + 1) * BLOCK)
         spot = pl.ds(pl.multiple_of(origin + number * BLOCK, BLOCK), BLOCK)
-        turn_ref[:, spot] = grad_ref[rows, :].T
-
-
-def backward_kernel(
-    normed_ref, cot_ref, z_ref, y_ref, dyn_ref, bc_ref, wide_ref, pick_ref, col_ref, row_ref, seg_ref,
-    turned_ref, norm_ref, par_ref, state_ref,
-    grad_ref, dbc_ref, step_row_ref, step_col_ref, small_ref, far_out_ref, near_out_ref, total_ref,
-    turn_ref, xs_ref, dconv_ref, carry_ref, stream_ref, far_ref, near_ref, y_recv_ref, z_send_ref, z_own_ref,
-    z_recv_ref, stream_sem, out_sem, y_send_sem, y_recv_sem, z_send_sem, z_recv_sem,
-    *, inside, tiles, spans,
-):
+        turned = grad_ref[rows, :].T
+        turn_ref[:STEPS, spot] = turned[: 2 * TILE]
+        turn_ref[OUT:, spot] = turned[2 * TILE :]
+
+
+def backward_kernel(*refs, ties, inside, tiles, spans):
+    (
+        normed_ref, cot_ref, z_ref, y_ref, dyn_ref, bc_ref, wide_ref, pick_ref, col_ref, row_ref, seg_ref,
+        turned_ref, norm_ref, par_ref, rate_ref, state_ref,
+        grad_ref, dbc_ref, dt_ref, head_ref, small_ref, far_out_ref, near_out_ref, total_ref,
+        turn_ref, xs_ref, dconv_ref, carry_ref, stream_ref, far_ref, near_ref, y_recv_ref, z_send_ref, z_own_ref,
+        z_recv_ref, stream_sem, out_sem, y_send_sem, y_recv_sem, z_send_sem, z_recv_sem,
+    ) = refs[ties:]
     tile, sequence = pl.program_id(0), pl.program_id(1)
     length = xs_ref.shape[0]
     parts = turn_ref.shape[0], near_ref.shape[2]
@@ -700,7 +713,7 @@
 
     backward_tile(
         sequence * length, z_ref, y_ref, dyn_ref, bc_ref, wide_ref, pick_ref, col_ref, row_ref, seg_ref,
-        turned_ref, norm_ref, par_ref, state_ref, grad_ref, dbc_ref, step_row_ref, step_col_ref, small_ref,
+        turned_ref, norm_ref, par_ref, rate_ref, state_ref, grad_ref, dbc_ref, dt_ref, head_ref, small_ref,
         turn_ref, xs_ref, dconv_ref, carry_ref,
     )
 
@@ -734,18 +747,18 @@
 
             for copy in fetch(number, slot):
                 copy.wait()
-            upper = dot(turn_ref[: 2 * TILE, :], stream_ref[slot, 0])
-            lower = dot(turn_ref[2 * TILE :, :], stream_ref[slot, 1])
+            upper = dot(turn_ref[:OUT, :], stream_ref[slot, 0])
+            lower = dot(turn_ref[OUT:, :], stream_ref[slot, 1])
 
             @pl.when(step < halves_of)
             def _():
-                far_ref[step, : 2 * TILE, :] = upper.astype(BF16)
-                far_ref[step, 2 * TILE :, :] = lower.astype(BF16)
+                far_ref[step, :OUT, :] = upper.astype(BF16)
+                far_ref[step, OUT:, :] = lower.astype(BF16)
 
             @pl.when(step >= halves_of)
             def _():
-                near_ref[step - halves_of, : 2 * TILE, :] = upper
-                near_ref[step - halves_of, 2 * TILE :, :] = lower
+                near_ref[step - halves_of, :OUT, :] = upper
+                near_ref[step - halves_of, OUT:, :] = lower
 
             return carried
 
@@ -977,7 +990,9 @@
     )
 
 
-def run_backward(normed, cot, zv, y, dyn, bc, wide, col, rows, ids, turned, norms, par, state, length, spans):
+def run_backward(
+    ties, normed, cot, zv, y, dyn, bc, wide, col, rows, ids, turned, norms, par, rate, state, length, spans
+):
     tiles, tokens = zv.shape[:2]
     width = normed.shape[1]
     number, blocks = tokens // length, length // BLOCK
@@ -998,9 +1013,10 @@
     if inside:
         params.update(collective_id=1, has_side_effects=True)
     return inside, pl.pallas_call(
-        functools.partial(backward_kernel, inside=inside, tiles=tiles, spans=spans),
+        functools.partial(backward_kernel, ties=len(ties), inside=inside, tiles=tiles, spans=spans),
         grid=(tiles, number),
-        in_specs=[
+        in_specs=[ANY for _ in ties]
+        + [
             ANY,
             ANY,
             by_tile(length, 2 * TILE),
@@ -1015,40 +1031,41 @@
             shared(length, BLOCK),
             pl.BlockSpec((8, length), lambda j, i: (0, i)),
             fixed(8, TILE),
+            fixed(8, LANES),
             pl.BlockSpec((None, blocks, LANES, TILE), lambda j, i: (j, i, 0, 0)),
         ],
         out_specs=[
             by_tile(length, 3 * TILE),
             pl.BlockSpec((tokens, 2 * LANES), lambda j, i: (0, 0)),
-            pl.BlockSpec((8, length), lambda j, i: (j, i)),
-            by_tile(length, 16),
+            pl.BlockSpec((16, length), lambda j, i: (j, i)),
+            pl.BlockSpec((None, None, 8, LANES), lambda j, i: (j, i, 0, 0)),
             pl.BlockSpec((None, None, 8, TILE), lambda j, i: (j, i, 0, 0)),
             ANY,
             ANY,
-            pl.BlockSpec((max(inside, 1), 3 * TILE, part), lambda j, i: (0, 0, 0)),
+            pl.BlockSpec((max(inside, 1), SHARE, part), lambda j, i: (0, 0, 0)),
         ],
         out_shape=[
             shaped((tiles, tokens, 3 * TILE), BF16),
             shaped((tokens, 2 * LANES)),
-            shaped((tiles * 8, tokens)),
-            shaped((tiles, tokens, 16)),
+            shaped((tiles * 16, tokens), BF16),
+            shaped((tiles, number, 8, LANES)),
             shaped((tiles, number, 8, TILE)),
-            shaped((tiles - inside, near, 3 * TILE, part), BF16),
-            shaped((tiles - inside, near, 3 * TILE, part)),
-            shaped((max(inside, 1), 3 * TILE, part)),
+            shaped((tiles - inside, near, SHARE, part), BF16),
+            shaped((tiles - inside, near, SHARE, part)),
+            shaped((max(inside, 1), SHARE, part)),
         ],
         scratch_shapes=[
-            pltpu.VMEM((3 * TILE, tokens), BF16),
+            pltpu.VMEM((SHARE, tokens), BF16),
             pltpu.VMEM((length, TILE), F32),
             pltpu.VMEM((length, TILE), F32),
             pltpu.VMEM((LANES, TILE), F32),
             pltpu.VMEM((2, 2, tokens, part), BF16),
-            pltpu.VMEM((near, 3 * TILE, part), BF16),
-            pltpu.VMEM((near, 3 * TILE, part), F32),
-            pltpu.VMEM((2, near, 3 * TILE, part), BF16),
-            pltpu.VMEM((3, 3 * TILE, part), BF16),
-            pltpu.VMEM((3 * TILE, part), F32),
-            pltpu.VMEM((2, 3, 3 * TILE, part), BF16),
+            pltpu.VMEM((near, SHARE, part), BF16),
+            pltpu.VMEM((near, SHARE, part), F32),
+            pltpu.VMEM((2, near, SHARE, part), BF16),
+            pltpu.VMEM((3, SHARE, part), BF16),
+            pltpu.VMEM((SHARE, part), F32),
+            pltpu.VMEM((2, 3, SHARE, part), BF16),
             pltpu.SemaphoreType.DMA((2, 2)),
             pltpu.SemaphoreType.DMA((2,)),
             pltpu.SemaphoreType.DMA((near,)),
@@ -1059,8 +1076,457 @@
         compiler_params=pltpu.CompilerParams(**params),
         cost_estimate=cost(2e11),
     )(
-        normed, cot, zv, y, dyn, bc, wide, jnp.stack([pick_table(tile) for tile in range(tiles)]), col, rows,
-        ids[None, :], turned, norms, par, state,
+        *ties, normed, cot, zv, y, dyn, bc, wide, jnp.stack([pick_table(tile) for tile in range(tiles)]), col,
+        rows, ids[None, :], turned, norms, par, rate, state,
+    )
+
+
+def mixer_kernel(place_ref, z_ref, y_ref, norm_ref, par_ref, w_ref, out_ref, *, spans):
+    tiles, rows = y_ref.shape[:2]
+    norms = dot(norm_ref[...], (iota((8, 8), 0) == iota((8, 8), 1)).astype(F32), TN, HIGH)
+    parts = []
+    for tile in range(tiles):
+        z = z_ref[tile]
+        yg = y_ref[tile] * (z * sigmoid(z))
+        parts.append((yg * norms[:, 0:1] * par_ref[tile, GAIN : GAIN + 1, :]).astype(BF16))
+    part = 2 * LANES
+    for number in range(2 * spans):
+        total = jnp.zeros((rows, part), F32)
+        for tile in range(tiles):
+            total = total + dot(parts[tile], w_ref[tile, number * part : (number + 1) * part, :], NT)
+        out_ref[:, pl.ds(pair_start(number, place_ref[0], spans), part)] = total.astype(BF16)
+
+
+def pair_start(number, dp, spans):
+    bits = number // spans * 2 + number % spans * 4
+    return pl.multiple_of(jnp.bitwise_xor(dp - lax.rem(dp, 2), bits) * LANES, 2 * LANES)
+
+
+def run_mixer(place, zvs, ys, norms, params, weights, rows, spans):
+    tiles, tokens, _ = ys.shape
+    width = weights.shape[1]
+
+    def at(i, place_ref):
+        half = jnp.bitwise_xor(i // 2, place_ref[1])
+        return i % 2 * 2 + half
+
+    return pl.pallas_call(
+        functools.partial(mixer_kernel, spans=spans),
+        grid_spec=pltpu.PrefetchScalarGridSpec(
+            num_scalar_prefetch=1,
+            grid=(4,),
+            in_specs=[
+                pl.BlockSpec((tiles, rows, TILE), lambda i, p: (0, at(i, p), 0)),
+                pl.BlockSpec((tiles, rows, TILE), lambda i, p: (0, at(i, p), 0)),
+                pl.BlockSpec((8, rows), lambda i, p: (0, at(i, p))),
+                pl.BlockSpec((tiles, 8, TILE), lambda i, p: (0, 0, 0)),
+                pl.BlockSpec((tiles, width, TILE), lambda i, p: (0, 0, 2)),
+            ],
+            out_specs=pl.BlockSpec((None, rows, width), lambda i, p: (i, 0, 0)),
+        ),
+        out_shape=shaped((4, rows, width), BF16),
+        compiler_params=pltpu.CompilerParams(vmem_limit_bytes=VMEM_LIMIT),
+        cost_estimate=cost(1e10),
+    )(place, zvs, ys, norms, params, weights)
+
+
+def tail_kernel(
+    hidden_ref, cot_ref, inv_ref, gain_ref, grads_hbm, weights_hbm, small_ref, dt_ref, far_hbm, near_ref,
+    totals_ref, dbc_ref, proj_ref, col_ref, par_ref, normed_hbm, pack_ref, sums_ref,
+    grad_out, mine_ref, theirs_ref, bc_out_ref, pack_out_ref, last_ref,
+    grads_seq, wblk, acc_ref, give_ref, core_recv, own_ref, x_give, x_recv, y_recv, z_send, z_own, z_recv, w_send,
+    dbc_core, dbc_x, dbc_low, dt_cols, normed_blk, bc_grad, bc_xs, bc_own, bc_xr, bc_yr, bc_zr, bc_core, pack_recv,
+    last_recv,
+    seq_sem, blk_sem, out_sem, core_send, core_rsem, xs_sem, xr_sem, ys_sem, yr_sem, zs_sem, zr_sem, ws_sem, wr_sem,
+    ds_sem, dr_sem, bs_sem, br_sem, ps_sem, pr_sem, ls_sem, lr_sem,
+    *, spans, inside, extent,
+):
+    tiles = grads_seq.shape[0]
+    length = grads_seq.shape[1]
+    rows, width = hidden_ref.shape
+    part = 2 * LANES
+    count = 2 * spans
+    dp, mp = lax.axis_index("dp"), lax.axis_index("mp")
+    side = lax.rem(dp, 2)
+    ours = pl.ds(pl.multiple_of(side * LANES, LANES), LANES)
+    others = pl.ds(pl.multiple_of((1 - side) * LANES, LANES), LANES)
+    other_core = (dp, 1 - mp)
+
+    def along(bits):
+        return (jnp.bitwise_xor(dp, bits), mp)
+
+    def remote(src, dst, send, recv, device):
+        return pltpu.make_async_remote_copy(
+            src_ref=src, dst_ref=dst, send_sem=send, recv_sem=recv, device_id=device,
+            device_id_type=pl.DeviceIdType.MESH,
+        )
+
+    def lanes_of(number):
+        return pl.ds(pair_start(number, dp, spans), part)
+
+    def seq_fetch(sequence):
+        return pltpu.make_async_copy(
+            grads_hbm.at[:, pl.ds(sequence * length, length), pl.ds(0, 2 * TILE)], grads_seq, seq_sem.at[0]
+        )
+
+    def w_fetch(number, slot):
+        at = pl.ds(pl.multiple_of(number * part, part), part)
+        return pltpu.make_async_copy(
+            weights_hbm.at[:, at, pl.ds(0, 2 * TILE)], wblk.at[slot], blk_sem.at[slot]
+        )
+
+    def normed_fetch(number, slot):
+        at = pl.ds(pl.multiple_of(number * part, part), part)
+        return pltpu.make_async_copy(
+            normed_hbm.at[pl.ds(0, length), at], normed_blk.at[slot], blk_sem.at[2 + slot]
+        )
+
+    def core_copy(sequence, number):
+        at = lanes_of(number)
+        return remote(
+            give_ref.at[:, at], core_recv.at[sequence, :, at], core_send.at[sequence, number],
+            core_rsem.at[sequence, number], other_core,
+        )
+
+    def x_copy(number):
+        at = lanes_of(number)
+        return remote(x_give.at[:, at], x_recv.at[:, at], xs_sem.at[number], xr_sem.at[number], along(1))
+
+    def y_copy(k):
+        return remote(far_hbm.at[0, k], y_recv.at[k], ys_sem.at[k], yr_sem.at[k], along(2))
+
+    def z_copy(k):
+        return remote(z_send.at[k - 1], z_recv.at[k - 1], zs_sem.at[k - 1], zr_sem.at[k - 1], along(4 * k))
+
+    def w_copy(tile):
+        return remote(w_send.at[tile], theirs_ref.at[tile], ws_sem.at[tile], wr_sem.at[tile], along(1))
+
+    dbc_between = remote(dbc_ref, dbc_core, ds_sem.at[0], dr_sem.at[0], other_core)
+    dbc_across = remote(dbc_core.at[pl.ds(length, length), :], dbc_x, ds_sem.at[1], dr_sem.at[1], along(1))
+    bc_x = remote(bc_xs, bc_xr, bs_sem.at[0], br_sem.at[0], along(1))
+    bc_y = remote(bc_own.at[pl.ds(spans, spans)], bc_yr, bs_sem.at[1], br_sem.at[1], along(2))
+
+    def bc_z(k):
+        return remote(bc_own.at[k], bc_zr.at[k - 1], bs_sem.at[1 + k], br_sem.at[1 + k], along(4 * k))
+
+    bc_between = remote(bc_own.at[0], bc_core, bs_sem.at[1 + spans], br_sem.at[1 + spans], other_core)
+    bits = [1 << place for place in range(extent.bit_length() - 1)]
+
+    def pack_copy(step):
+        return remote(pack_out_ref, pack_recv.at[step], ps_sem.at[step], pr_sem.at[step], along(bits[step]))
+
+    def pack_step(step):
+        pack_copy(step).wait()
+        pack_out_ref[...] += pack_recv[step]
+        if step + 1 < len(bits):
+            pack_copy(step + 1).start()
+
+    def last_copy(step):
+        device = along(bits[step]) if step < len(bits) else other_core
+        return remote(last_ref, last_recv.at[step], ls_sem.at[step], lr_sem.at[step], device)
+
+    def give_total(tile, total_ref):
+        mine_ref[tile] = total_ref[:, ours]
+        w_send[tile] = total_ref[:, others].astype(BF16)
+        w_copy(tile).start()
+
+    def products(sequence):
+        dt_rows = jnp.concatenate(
+            [
+                dt_ref[tile * 16 : tile * 16 + GROUP, sequence * length : (sequence + 1) * length].astype(F32)
+                for tile in range(tiles)
+            ],
+            axis=0,
+        )
+        dt_rows = jnp.concatenate([dt_rows, jnp.zeros((LANES - tiles * GROUP, length), F32)], axis=0)
+        dt_cols[...] = dt_rows.T.astype(BF16)
+        seq_fetch(sequence).wait()
+
+        def one(number, carried):
+            slot = lax.rem(number, 2)
+
+            @pl.when(number + 1 < count)
+            def _():
+                w_fetch(number + 1, 1 - slot).start()
+
+            w_fetch(number, slot).wait()
+            at = pl.ds(pl.multiple_of(number * part, part), part)
+            total = dot(dt_cols[...], small_ref[at, 2 * LANES :], NT)
+            for tile in range(tiles):
+                total = total + dot(grads_seq[tile], wblk[slot, tile], NT)
+            acc_ref[...] = total
+            lanes = lanes_of(number)
+            away = pl.ds(pl.multiple_of((1 - mp) * rows, rows), rows)
+            here = pl.ds(pl.multiple_of(mp * rows, rows), rows)
+            give_ref[:, lanes] = acc_ref[away, :].astype(BF16)
+            core_copy(sequence, number).start()
+            own_ref[:, lanes] = acc_ref[here, :]
+            return carried
+
+        lax.fori_loop(0, count, one, 0)
+
+    seq_fetch(1).start()
+    w_fetch(0, 0).start()
+    pack_out_ref[...] = pack_ref[...]
+    barrier = pltpu.get_barrier_semaphore()
+    partners = [along(1), along(2), other_core] + [along(4 * k) for k in range(1, spans)]
+    for device in partners:
+        pl.semaphore_signal(barrier, inc=1, device_id=device, device_id_type=pl.DeviceIdType.MESH)
+    pl.semaphore_wait(barrier, len(partners))
+    for k in range(spans):
+        y_copy(k).start()
+    dbc_between.start()
+    pack_copy(0).start()
+    for tile in range(inside):
+        give_total(tile, totals_ref.at[tile])
+    products(1)
+    seq_fetch(0).start()
+    w_fetch(0, 0).start()
+    dbc_between.wait()
+    dbc_core[...] += dbc_ref[...]
+    dbc_across.start()
+    pack_step(0)
+
+    def pass_on(number, carried):
+        core_copy(1, number).wait()
+        lanes = lanes_of(number)
+        x_give[:, lanes] = (own_ref[:, lanes] + core_recv[1, :, lanes].astype(F32)).astype(BF16)
+        x_copy(number).start()
+        return carried
+
+    lax.fori_loop(0, count, pass_on, 0)
+    products(0)
+    pack_step(1)
+    normed_fetch(0, 0).start()
+    dbc_across.wait()
+    conv = conv_of(proj_ref[...], col_ref[...], par_ref)
+    gate = sigmoid(conv)
+    d_conv = (dbc_core[:length, :] + dbc_x[...]) * (gate * (1.0 + conv * (1.0 - gate)))
+    d_proj = par_ref[TAPS + 3 : TAPS + 4, :] * d_conv
+    small = [None] * 4
+    small[3] = jnp.sum(d_conv * proj_ref[...], axis=0, keepdims=True)
+    for offset in range(1, 4):
+        place = TAPS + 3 - offset
+        counted = d_conv * col_ref[:, VALID + offset - 1 : VALID + offset]
+        small[place] = jnp.sum(counted * pltpu.roll(proj_ref[...], offset, 0), axis=0, keepdims=True)
+        d_proj = d_proj + par_ref[place : place + 1, :] * pltpu.roll(counted, length - offset, 0)
+    small.append(jnp.sum(d_conv, axis=0, keepdims=True))
+    conv_grads = jnp.concatenate(small + [jnp.zeros((3, part), F32)], axis=0)
+    dbc_low[...] = d_proj.astype(BF16)
+    for k in range(spans):
+        y_copy(k).wait()
+        total = near_ref[0, k] + y_recv[k].astype(F32)
+        if k == 0:
+            z_own[...] = total
+        else:
+            z_send[k - 1] = total.astype(BF16)
+            z_copy(k).start()
+    half = pl.ds(pl.multiple_of(mp * LANES, LANES), LANES)
+    turned = dbc_low[:, half].T
+
+    def bc_product(number, carried):
+        slot = lax.rem(number, 2)
+
+        @pl.when(number + 1 < count)
+        def _():
+            normed_fetch(number + 1, 1 - slot).start()
+
+        normed_fetch(number, slot).wait()
+        bc_grad[...] = dot(turned, normed_blk[slot])
+        bc_own[number] = bc_grad[:, ours]
+        bc_xs[number] = bc_grad[:, others]
+        return carried
+
+    lax.fori_loop(0, count, bc_product, 0)
+    bc_x.start()
+    pack_step(2)
+    here = pl.ds(pl.multiple_of(mp * rows, rows), rows)
+
+    def add_core(number, carried):
+        core_copy(0, number).wait_recv()
+        lanes = lanes_of(number)
+        at = pl.ds(pl.multiple_of(number * part, part), part)
+        own_ref[:, lanes] += core_recv[0, :, lanes].astype(F32) + dot(
+            dbc_low[here, :], small_ref[at, : 2 * LANES], NT
+        )
+        return carried
+
+    lax.fori_loop(0, count, add_core, 0)
+    pack_step(3)
+    for step in range(4, len(bits)):
+        pack_step(step)
+    bc_x.wait()
+    bc_own[...] += bc_xr[...]
+    bc_y.start()
+    total = z_own[...]
+    for k in range(1, spans):
+        z_copy(k).wait()
+        total = total + z_recv[k - 1].astype(F32)
+    z_own[...] = total
+    give_total(inside, z_own)
+    bc_y.wait()
+    bc_own[:spans] += bc_yr[...]
+    for k in range(1, spans):
+        bc_z(k).start()
+
+    def add_x(number, carried):
+        x_copy(number).wait_recv()
+        lanes = lanes_of(number)
+        own_ref[:, lanes] += x_recv[:, lanes].astype(F32)
+        return carried
+
+    lax.fori_loop(0, count, add_x, 0)
+    last_ref[...] = jnp.zeros_like(last_ref)
+    last_ref[:, part : 2 * part] = 0.5 * conv_grads
+    last_ref[:, 2 * part : 2 * part + LANES] = sums_ref[...]
+    step_rows = 64
+
+    def finish(number, gain_sum):
+        at = pl.ds(pl.multiple_of(number * step_rows, step_rows), step_rows)
+        u, d_normed = hidden_ref[at, :].astype(F32), own_ref[at, :]
+        inv = inv_ref[at, :]
+        scaled = gain_ref[...] * d_normed
+        mean = jnp.mean(u * scaled, axis=-1, keepdims=True)
+        own_ref[at, :] = cot_ref[at, :].astype(F32) + inv * scaled - u * (inv * inv * inv * mean)
+        return gain_sum + jnp.sum(d_normed * u * inv, axis=0, keepdims=True)
+
+    gain_sum = lax.fori_loop(0, rows // step_rows, finish, jnp.zeros((1, width), F32))
+    out = pltpu.make_async_copy(own_ref, grad_out, out_sem.at[0])
+    out.start()
+    for number in range(8):
+        last_ref[number : number + 1, :part] = gain_sum[:, number * part : (number + 1) * part]
+    for step in range(len(bits) + 1):
+        last_copy(step).start()
+        if step == 1:
+            total = bc_own[0]
+            for k in range(1, spans):
+                bc_z(k).wait()
+                total = total + bc_zr[k - 1]
+            bc_own[0] = total
+            bc_between.start()
+        last_copy(step).wait()
+        last_ref[...] += last_recv[step]
+    bc_between.wait()
+    first = jnp.where(mp == 0, 1.0, 0.0)
+    bc_out_ref[:LANES, :] = first * bc_own[0] + (1.0 - first) * bc_core[...]
+    bc_out_ref[LANES:, :] = (1.0 - first) * bc_own[0] + first * bc_core[...]
+    for tile in range(inside + 1):
+        w_copy(tile).wait()
+    for number in range(count):
+        core_copy(0, number).wait_send()
+        x_copy(number).wait_send()
+    out.wait()
+
+
+def run_tail(
+    hidden, cot, inv, gain, grads, weights, small, dts, far_share, near_share, totals, dbc, proj, col, bc_par,
+    normed, pack, sums, length, spans, extent,
+):
+    rows, width = hidden.shape
+    tiles, tokens = grads.shape[:2]
+    part, inside = 2 * LANES, tiles - 1
+    hops = extent.bit_length() - 1
+    dma = pltpu.SemaphoreType.DMA
+
+    def full(*shape):
+        return pl.BlockSpec(shape, lambda i: (0,) * len(shape))
+
+    return pl.pallas_call(
+        functools.partial(tail_kernel, spans=spans, inside=inside, extent=extent),
+        grid=(1,),
+        in_specs=[
+            full(rows, width),
+            full(rows, width),
+            full(rows, 1),
+            full(1, width),
+            ANY,
+            ANY,
+            full(*small.shape),
+            full(*dts.shape),
+            ANY,
+            full(*near_share.shape),
+            full(*totals.shape),
+            full(*dbc.shape),
+            full(length, part),
+            full(length, COLS),
+            full(8, part),
+            ANY,
+            full(*pack.shape),
+            full(8, LANES),
+        ],
+        out_specs=[
+            ANY,
+            full(tiles, SHARE, LANES),
+            full(tiles, SHARE, LANES),
+            full(part, LANES),
+            full(*pack.shape),
+            full(8, 3 * part),
+        ],
+        out_shape=[
+            shaped((rows, width)),
+            shaped((tiles, SHARE, LANES)),
+            shaped((tiles, SHARE, LANES), BF16),
+            shaped((part, LANES)),
+            shaped(pack.shape),
+            shaped((8, 3 * part)),
+        ],
+        scratch_shapes=[
+            pltpu.VMEM((tiles, length, 2 * TILE), BF16),
+            pltpu.VMEM((2, tiles, part, 2 * TILE), BF16),
+            pltpu.VMEM((length, part), F32),
+            pltpu.VMEM((rows, width), BF16),
+            pltpu.VMEM((2, rows, width), BF16),
+            pltpu.VMEM((rows, width), F32),
+            pltpu.VMEM((rows, width), BF16),
+            pltpu.VMEM((rows, width), BF16),
+            pltpu.VMEM((spans, SHARE, part), BF16),
+            pltpu.VMEM((spans - 1, SHARE, part), BF16),
+            pltpu.VMEM((SHARE, part), F32),
+            pltpu.VMEM((spans - 1, SHARE, part), BF16),
+            pltpu.VMEM((tiles, SHARE, LANES), BF16),
+            pltpu.VMEM((tokens, part), F32),
+            pltpu.VMEM((length, part), F32),
+            pltpu.VMEM((length, part), BF16),
+            pltpu.VMEM((length, LANES), BF16),
+            pltpu.VMEM((2, length, part), BF16),
+            pltpu.VMEM((LANES, part), F32),
+            pltpu.VMEM((2 * spans, LANES, LANES), F32),
+            pltpu.VMEM((2 * spans, LANES, LANES), F32),
+            pltpu.VMEM((2 * spans, LANES, LANES), F32),
+            pltpu.VMEM((spans, LANES, LANES), F32),
+            pltpu.VMEM((spans - 1, LANES, LANES), F32),
+            pltpu.VMEM((LANES, LANES), F32),
+            pltpu.VMEM((hops,) + pack.shape, F32),
+            pltpu.VMEM((hops + 1, 8, 3 * part), F32),
+            dma((1,)),
+            dma((4,)),
+            dma((1,)),
+            dma((2, 2 * spans)),
+            dma((2, 2 * spans)),
+            dma((2 * spans,)),
+            dma((2 * spans,)),
+            dma((spans,)),
+            dma((spans,)),
+            dma((spans - 1,)),
+            dma((spans - 1,)),
+            dma((tiles,)),
+            dma((tiles,)),
+            dma((2,)),
+            dma((2,)),
+            dma((2 + spans,)),
+            dma((2 + spans,)),
+            dma((hops,)),
+            dma((hops,)),
+            dma((hops + 1,)),
+            dma((hops + 1,)),
+        ],
+        compiler_params=pltpu.CompilerParams(
+            vmem_limit_bytes=VMEM_LIMIT, collective_id=3, has_side_effects=True
+        ),
+        cost_estimate=cost(1e11),
+    )(
+        hidden, cot, inv, gain, grads, weights, small, dts, far_share, near_share, totals, dbc, proj, col, bc_par,
+        normed, pack, sums,
     )
 
 
@@ -1198,121 +1664,35 @@
         sums = sums + jnp.concatenate([near[:, length:], near[:, :length]], axis=1)
         norms = norm_rows(sums, inner_total)
 
-    inside, (grads, dbc, step_rows, step_cols, smalls, far_share, near_share, inner_totals) = run_backward(
-        normed_all, cot_all, zvs, ys, dyns, bc, wide, col, rows_all, ids_all, turned, norms, params, states,
-        length, far,
+    place = jnp.stack([dp, mp])
+    inputs = hidden_in.astype(F32)
+    usable = (lax.dynamic_slice_in_dim(segments, mp * rows, rows, 0) >= 0).astype(F32)[:, None]
+    native = depth == LANES
+    ties = []
+    if native:
+        mixer = run_mixer(place, zvs, ys, norms, params, weights, rows, far)
+        ties = [mixer]
+        mixer_near = flip(mixer[2:], "mp", 1)
+        mixer_send = (mixer[1].astype(F32) + mixer_near[1].astype(F32)).astype(BF16)
+        mixer_out = mixer[0].astype(F32) + mixer_near[0].astype(F32) + flip(mixer_send, "dp", 1).astype(F32)
+
+    rate_rows = jnp.pad(rate.reshape(tiles, GROUP, 1), ((0, 0), (0, 8 - GROUP), (0, 0)))
+    inside, (grads, dbc, dts, head_sums, smalls, far_share, near_share, inner_totals) = run_backward(
+        ties, normed_all, cot_all, zvs, ys, dyns, bc, wide, col, rows_all, ids_all, turned, norms, params,
+        jnp.broadcast_to(rate_rows, (tiles, 8, LANES)), states, length, far,
     )
-
-    def spread_sum(far_part, near_part):
-        def arranged(a):
-            return a.transpose(1, 0, 2).reshape(3 * TILE, far, 2 * depth).transpose(1, 0, 2)
-
-        total = arranged(near_part) + arranged(flip(far_part, "dp", 2)).astype(F32)
-        out = total.astype(BF16)
-        total = total[0]
-        for k in range(1, far):
-            total = total + flip(out[k], "dp", 4 * k).astype(F32)
-        return total
-
-    totals_of = [inner_totals[tile] for tile in range(inside)]
-    totals_of += [spread_sum(far_share[at], near_share[at]) for at in range(tiles - inside)]
-    stacked = jnp.stack(totals_of)
-    mine = of_side(stacked, x_side, 2)
-    theirs = flip(of_side(stacked, 1 - x_side, 2).astype(BF16), "dp", 1).astype(F32)
-
-    def assembled(parts):
-        return parts.reshape(tiles, 3, TILE, depth).transpose(1, 0, 2, 3).reshape(3, quarter, depth)
-
-    full = by_side(assembled(mine), assembled(theirs), 1)
-    grad_zx_weight = full[:2].transpose(2, 0, 1)
-    grad_out_weight = full[2]
-
-    dbc = dbc + flip(dbc, "mp", 1)
-    dbc = dbc[:length] + flip(dbc[length:], "dp", 1)
-    own_masks = col[:length, VALID : VALID + 3]
-    _, state_back = jax.vjp(
-        lambda values, taps, bias: jax.nn.silu(segment_conv(values, taps, bias, own_masks)),
-        proj_bc[:length],
-        conv_bc,
-        conv_bc_bias,
-    )
-    d_bc, grad_conv_bc, grad_conv_bc_bias = state_back(dbc)
-    bc_grad = d_bc.astype(BF16)
-
-    raw_dt = rows_all.reshape(tiles, 2, GROUP, tokens)[:, 1].reshape(own_heads, tokens)
-    run_steps = step_cols.transpose(0, 2, 1)
-    steps = (step_rows.reshape(tiles, 8, tokens)[:, :GROUP] + run_steps[:, :GROUP]).reshape(own_heads, tokens)
-    direct = run_steps[:, 8 : 8 + GROUP].reshape(own_heads, tokens)
-    d_dt = (direct + rate[:, None] * steps) * jax.nn.sigmoid(raw_dt)
-    grad_dt_bias = jnp.sum(d_dt, axis=1)
-    grad_a_log = jnp.sum(steps * jax.nn.softplus(raw_dt), axis=1) * rate
-    dt_grad = d_dt.T.astype(BF16)
 
     def placed(a):
         zero = jnp.zeros_like(a)
         return by_side(a, zero, a.ndim - 1)
 
-    small_grad = jnp.concatenate(
-        [
-            dot(normed_all[:length], lax.dynamic_slice_in_dim(bc_grad, mp * LANES, LANES, 1), TN),
-            placed(dot(normed_all, dt_grad, TN)),
-        ],
-        axis=1,
-    )
-    small_grad = small_grad.reshape(2 * far, 2, depth, -1)
-    small_grad = of_side(small_grad, x_side, 1) + flip(
-        of_side(small_grad, 1 - x_side, 1).astype(BF16), "dp", 1
-    ).astype(F32)
-    small_grad = small_grad.reshape(2, far, depth, -1)
-    small_grad = small_grad[0] + flip(small_grad[1].astype(BF16), "dp", 2).astype(F32)
-    out = small_grad.astype(BF16)
-    small_grad = small_grad[0]
-    for k in range(1, far):
-        small_grad = small_grad + flip(out[k], "dp", 4 * k).astype(F32)
-    grad_dt_weight = small_grad[:, LANES:]
-    own_bc = small_grad[:, :LANES]
-    grad_bc_weight = by_core(own_bc, flip(own_bc, "mp", 1), 1)
-
-    def token_sum(products):
-        def part(core):
-            return products(lambda a: of_side(a.reshape(2, 2, rows, -1), core, 1).reshape(2 * rows, -1))
-
-        total = part(mp) + flip(part(1 - mp).astype(BF16), "mp", 1).astype(F32)
-        return total[:rows] + flip(total[rows:].astype(BF16), "dp", 1).astype(F32)
-
-    out_all = jnp.concatenate([w[:, 2 * TILE :] for w in weights], axis=1)
-    yn_all = jnp.concatenate([g[:, 2 * TILE :] for g in grads], axis=1)
-    mixer_out = restore_order(token_sum(lambda pick: dot(pick(yn_all), out_all, NT)), dp, extent)
-    inputs = hidden_in.astype(F32)
-    residual_out = (inputs + mixer_out).astype(BF16)
-    usable = (lax.dynamic_slice_in_dim(segments, mp * rows, rows, 0) >= 0).astype(F32)[:, None]
-    totals = jnp.stack(
-        [
-            jnp.sum(usable * inputs * inputs),
-            jnp.sum(usable * mixer_out * mixer_out),
-            jnp.sum(usable),
-        ]
-    )
-
-    zv_all = jnp.concatenate([w[:, : 2 * TILE] for w in weights], axis=1)
-    dt_weight = bc_weight[:, 2 * LANES : 2 * LANES + own_heads]
-    dzx_all = jnp.concatenate([g[:, : 2 * TILE] for g in grads], axis=1)
-    d_normed = token_sum(
-        lambda pick: dot(pick(dzx_all), zv_all, NT) + dot(pick(dt_grad), dt_weight, NT)
-    )
-    d_normed = d_normed + dot(
-        lax.dynamic_slice_in_dim(bc_grad, mp * rows, rows, 0), bc_weight[:, : 2 * LANES], NT
-    )
-    d_normed = restore_order(d_normed, dp, extent)
-    grad_norm_gain = jnp.sum(d_normed * inputs * inverse_rows, axis=0)
-    inverse_cube_rows = inverse_rows * inverse_rows * inverse_rows
-    input_grad = (
-        cotangent.astype(F32)
-        + inverse_rows * norm_gain * d_normed
-        - inputs
-        * inverse_cube_rows
-        * jnp.mean(inputs * norm_gain * d_normed, axis=-1, keepdims=True)
-    )
+    small = jnp.sum(smalls, axis=1).transpose(1, 0, 2).reshape(8, quarter)
+    head_sums = jnp.sum(head_sums[..., 0], axis=1)
+    grad_dt_bias = placed(head_sums[:, :GROUP].reshape(own_heads))
+    grad_a_log = placed(head_sums[:, GROUP:].reshape(own_heads) * rate)
+    channel = placed(small[: GAIN + 1])
+    head_row = jnp.pad(jnp.concatenate([grad_dt_bias, grad_a_log]), (0, inner - 2 * heads))
+    pack = jnp.concatenate([channel, head_row[None]], axis=0)
 
     def summed(a, axes):
         for axis in axes:
@@ -1322,27 +1702,117 @@
                 bit *= 2
         return a
 
-    small = jnp.sum(smalls, axis=1).transpose(1, 0, 2).reshape(8, quarter)
-    channel = placed(small[: GAIN + 1])
-    skip_grad = jnp.sum(channel[SKIP].reshape(heads, WIDTH), axis=1)
-    pieces = [
-        channel[TAPS:BIAS],
-        channel[BIAS],
-        grad_conv_bc,
-        grad_conv_bc_bias,
-        placed(grad_dt_bias),
-        placed(grad_a_log),
-        skip_grad,
-        channel[GAIN],
-    ]
-    flat = summed(jnp.concatenate([p.reshape(-1) for p in pieces]), ("dp",))
-    small_sums, start = [], 0
-    for piece in pieces:
-        small_sums.append(flat[start : start + piece.size].reshape(piece.shape))
-        start += piece.size
-    last = summed(jnp.concatenate([grad_norm_gain, totals]), ("mp", "dp"))
-    grad_norm_gain = last[:width]
-    sum_inputs, sum_mixer, usable_count = last[width], last[width + 1], last[width + 2]
+    def mixer_sums(mixer_out):
+        return jnp.stack(
+            [
+                jnp.sum(usable * inputs * inputs),
+                jnp.sum(usable * mixer_out * mixer_out),
+                jnp.sum(usable),
+            ]
+        )
+
+    if native:
+        sums = jnp.pad(mixer_sums(mixer_out)[None], ((0, 7), (0, LANES - 3)))
+        input_grad, mine, theirs, grad_bc, pack, last = run_tail(
+            hidden_in, cotangent, inverse_rows, norm_gain[None], grads, weights, bc_weight, dts, far_share,
+            near_share, inner_totals, dbc, proj_bc, col, bc_par, normed_all, pack, sums, length, far, extent,
+        )
+        theirs = theirs.astype(F32)
+        grad_bc_weight = grad_bc.T
+        part = 2 * LANES
+        grad_norm_gain = last[:, :part].reshape(width)
+        grad_conv_bc, grad_conv_bc_bias = last[:4, part : 2 * part], last[4, part : 2 * part]
+        totals = last[0, 2 * part : 2 * part + 3]
+    else:
+
+        def spread_sum(far_part, near_part):
+            def arranged(a):
+                return a.transpose(1, 0, 2).reshape(SHARE, far, 2 * depth).transpose(1, 0, 2)
+
+            total = arranged(near_part) + arranged(flip(far_part, "dp", 2)).astype(F32)
+            out = total.astype(BF16)
+            total = total[0]
+            for k in range(1, far):
+                total = total + flip(out[k], "dp", 4 * k).astype(F32)
+            return total
+
+        stacked = jnp.stack([spread_sum(far_share[at], near_share[at]) for at in range(tiles)])
+        mine = of_side(stacked, x_side, 2)
+        theirs = flip(of_side(stacked, 1 - x_side, 2).astype(BF16), "dp", 1).astype(F32)
+
+        dbc = dbc + flip(dbc, "mp", 1)
+        dbc = dbc[:length] + flip(dbc[length:], "dp", 1)
+        own_masks = col[:length, VALID : VALID + 3]
+        _, state_back = jax.vjp(
+            lambda values, taps, bias: jax.nn.silu(segment_conv(values, taps, bias, own_masks)),
+            proj_bc[:length],
+            conv_bc,
+            conv_bc_bias,
+        )
+        d_bc, grad_conv_bc, grad_conv_bc_bias = state_back(dbc)
+        bc_grad = d_bc.astype(BF16)
+        small_grad = dot(normed_all[:length], lax.dynamic_slice_in_dim(bc_grad, mp * LANES, LANES, 1), TN)
+        small_grad = small_grad.reshape(2 * far, 2, depth, -1)
+        small_grad = of_side(small_grad, x_side, 1) + flip(of_side(small_grad, 1 - x_side, 1), "dp", 1)
+        small_grad = small_grad.reshape(2, far, depth, -1)
+        small_grad = small_grad[0] + flip(small_grad[1], "dp", 2)
+        own_bc = small_grad[0]
+        for k in range(1, far):
+            own_bc = own_bc + flip(small_grad[k], "dp", 4 * k)
+        grad_bc_weight = by_core(own_bc, flip(own_bc, "mp", 1), 1)
+
+        def token_sum(products):
+            def part(core):
+                return products(
+                    lambda a: of_side(a.reshape(2, 2, rows, -1), core, 1).reshape(2 * rows, -1)
+                )
+
+            total = part(mp) + flip(part(1 - mp).astype(BF16), "mp", 1).astype(F32)
+            return total[:rows] + flip(total[rows:].astype(BF16), "dp", 1).astype(F32)
+
+        out_all = jnp.concatenate([w[:, 2 * TILE :] for w in weights], axis=1)
+        yn_all = jnp.concatenate([g[:, 2 * TILE :] for g in grads], axis=1)
+        mixer_out = restore_order(token_sum(lambda pick: dot(pick(yn_all), out_all, NT)), dp, extent)
+        zv_all = jnp.concatenate([w[:, : 2 * TILE] for w in weights], axis=1)
+        dt_weight = bc_weight[:, 2 * LANES : 2 * LANES + own_heads]
+        dzx_all = jnp.concatenate([g[:, : 2 * TILE] for g in grads], axis=1)
+        dt_grad = dts.reshape(tiles, 16, tokens)[:, :GROUP].reshape(own_heads, tokens).T
+        d_normed = token_sum(
+            lambda pick: dot(pick(dzx_all), zv_all, NT) + dot(pick(dt_grad), dt_weight, NT)
+        )
+        d_normed = d_normed + dot(
+            lax.dynamic_slice_in_dim(bc_grad, mp * rows, rows, 0), bc_weight[:, : 2 * LANES], NT
+        )
+        d_normed = restore_order(d_normed, dp, extent)
+        grad_norm_gain = jnp.sum(d_normed * inputs * inverse_rows, axis=0)
+        inverse_cube_rows = inverse_rows * inverse_rows * inverse_rows
+        input_grad = (
+            cotangent.astype(F32)
+            + inverse_rows * norm_gain * d_normed
+            - inputs
+            * inverse_cube_rows
+            * jnp.mean(inputs * norm_gain * d_normed, axis=-1, keepdims=True)
+        )
+        pack = summed(pack, ("dp",))
+        conv_sums = jnp.concatenate([grad_conv_bc, grad_conv_bc_bias[None]], axis=0)
+        conv_sums = summed(conv_sums, ("dp",))
+        grad_conv_bc, grad_conv_bc_bias = conv_sums[:4], conv_sums[4]
+        last = summed(jnp.concatenate([grad_norm_gain, mixer_sums(mixer_out)]), ("mp", "dp"))
+        grad_norm_gain, totals = last[:width], last[width:]
+
+    residual_out = (inputs + mixer_out).astype(BF16)
+
+    def assembled(first, last_row):
+        def columns(a):
+            return a[:, first:last_row].reshape(-1, depth)
+
+        return by_side(columns(mine), columns(theirs), 0)
+
+    grad_zx_weight = jnp.stack([assembled(0, TILE).T, assembled(TILE, STEPS).T], axis=1)
+    grad_dt_weight = assembled(STEPS, STEPS + GROUP).T
+    grad_out_weight = assembled(OUT, SHARE)
+    skip_grad = jnp.sum(pack[SKIP].reshape(heads, WIDTH), axis=1)
+    sum_inputs, sum_mixer, usable_count = totals[0], totals[1], totals[2]
     rms_residual = jnp.sqrt(sum_inputs / (usable_count * width))
     rms_mixer = jnp.sqrt(sum_mixer / (usable_count * width))
     return (
@@ -1352,14 +1822,14 @@
         grad_zx_weight,
         grad_dt_weight,
         grad_bc_weight,
-        small_sums[0],
-        small_sums[1],
-        small_sums[2],
-        small_sums[3],
-        small_sums[4],
-        small_sums[5],
-        small_sums[6],
-        small_sums[7],
+        pack[TAPS:BIAS],
+        pack[BIAS],
+        grad_conv_bc,
+        grad_conv_bc_bias,
+        pack[GAIN + 1, :heads],
+        pack[GAIN + 1, heads : 2 * heads],
+        skip_grad,
+        pack[GAIN],
         grad_out_weight,
         rms_residual,
         rms_mixer,

time: 839 us -> 677 us (0.81)
  Pallas kernels: 452 us -> 592 us
  waiting for transfers between devices: 120 us -> 6.07 us
  local copies, waits for them, and re-layouts: 103 us -> 35.4 us
  matrix products: 59.2 us -> 0 us
  other arithmetic: 64.4 us -> 23.9 us
  starting transfers between devices: 28 us -> 3.84 us
    pallas_call x3, Pallas kernels: 229 us -> 369 us  [the longest x1 224 us: run_backward(): pl.pallas_call(functools.partial(backward_kernel, ties=len(ties), inside=...]
    ppermute x27 -> x3, waiting for transfers between devices: 120 us -> 6.07 us  [flip(): return lax.ppermute(a, axis, [(i, i ^ bit) for i in range(size)])]
    dot_general x9 -> x0, matrix products: 59.2 us -> none  [dot(): lax.dot_general(a, b, dims, precision=precision, preferred_element_type=F32)]
    ppermute x27 -> x3, starting transfers between devices: 28 us -> 3.84 us  [flip(): return lax.ppermute(a, axis, [(i, i ^ bit) for i in range(size)])]
    slice x38 -> x11, local copies, waits for them, and re-layouts: 36.1 us -> 12.4 us  [the longest x1 4.81 us: local(): mixer_near = flip(mixer[2:], 'mp', 1)]
    reduce_sum x5 -> x4, other arithmetic: 21.9 us -> 8.28 us  [the longest x1 5.54 us: mixer_sums(): jnp.sum(usable * inputs * inputs)]
    unnamed x133 -> x41, local copies, waits for them, and re-layouts: 21.1 us -> 11.1 us
    dynamic_slice x12 -> x7, local copies, waits for them, and re-layouts: 9.64 us -> 0.72 us  [of_side(): return lax.dynamic_slice_in_dim(a, side * size, size, axis)]
  transfers between devices with their start and end apart: 27 -> 3, of which waited for: 13 -> 1; matrix products, arithmetic and copies ran while one was open for 21% -> 3% of each run, Pallas kernels for 2% -> 34%
where the time goes in v4:
time: 677 us; the launch traced here: 667 us
  Pallas kernels  592 us (87%)
  local copies, waits for them, and re-layouts  35.4 us (5%)
  other arithmetic  23.9 us (4%)
    pallas_call x1, Pallas kernels, run_backward(): pl.pallas_call(functools.partial(backward_kernel, ties=len(ties), inside=...  224 us
    pallas_call x1, Pallas kernels, run_gather(): pl.pallas_call(functools.partial(gather_kernel, tiles=tiles, spans=spans,...  218 us
    pallas_call x1, Pallas kernels, run_tail(): pl.pallas_call(functools.partial(tail_kernel, spans=spans, inside=inside,...  125 us
    pallas_call x1, Pallas kernels, run_mixer(): pl.pallas_call(functools.partial(mixer_kernel, spans=spans), grid_spec=pl...  19.9 us
  transfers between devices with their start and end apart: 3, of which 1 were waited for; matrix products, arithmetic and copies ran while one was open for 3% of the time, Pallas kernels for 34%

profile of v4, /device:TPU:0, one launch (start us, length us, event | category | flops | bytes accessed | tf_op | source)
XLA Modules:
  0.0 666.5 jit_solution(9816806536703653182)
XLA Ops:
  0.7 3.0 collective-permute-start
  3.7 0.7 dynamic-slice_bitcast_fusion
  4.5 0.7 fusion.27
  6.2 3.3 fusion.21
  9.5 0.9 copy.71
  10.3 0.9 copy.72
  14.1 0.8 add_convert_fusion.1.pick_ref.refs_8_
  15.7 1.2 copy.65
  16.9 1.2 copy.64
  18.1 5.2 shard_map.287
  24.0 1.3 copy.68.seg_col_ref
  25.9 217.6 %shard_map.288 = (bf16[2048,2048]{1,0:T(8,128)(2,1)}, bf16[2048,2048]{1,0:T(8,128)(2,1)}, bf16[4,2048,768]{2,1,0:T(8,128)(2,1)}, bf16[2048,384]{1,0:T(8,128)(2,1...) custom-call(bf16[512,2048]{1,0:T(8,128)(2,1)} %get-tuple-element.49., ...), custom_call_target="tpu_custom_call" | custom-call | flops 199999995904 | bytes 10000000 | tf_op jit(solution)/shard_map/pallas_call | solution.py:920
  243.5 19.9 %shard_map.289.refs_0_ = bf16[4,512,2048]{2,1,0:T(8,128)(2,1)} custom-call(s32[2]{0:T(128)} %pad_add_fusion.place_ref, f32[4,2048,512]{2,1,0:T(8,128)} %get-tuple-element.51.z_ref.refs_3_, f32[4,2048,256]{2,1,0:T(8,128)} %get-tuple-element.52.y_ref.refs_4_, f32[8,2048]{1,0:T(8,128)} %get-tuple-element.53.norm_ref.refs_13_, f32[4,8,256]{2,1,0:T(8,128)} %bitcast.92, ...), custom_call_target="tpu_custom_call" | custom-call | flops 10000000000 | bytes 10000000 | tf_op jit(solution)/shard_map/pallas_call | solution.py:1113
  263.4 4.8 slice.136
  268.4 1.3 fusion.18
  269.7 6.1 collective-permute-done.1
  275.8 4.4 fusion.3
  280.2 0.8 collective-permute-start.2
  281.7 224.3 %shard_map.290 = (bf16[4,2048,768]{2,1,0:T(8,128)(2,1)}, f32[2048,256]{1,0:T(8,128)}, bf16[64,2048]{1,0:T(8,128)(2,1)}, f32[4,2,8,128]{3,2,1,0:T(8,128)}, f32[4,...) custom-call(bf16[4,512,2048]{2,1,0:T(8,128)(2,1)} %shard_map.289.ref, ...), custom_call_target="tpu_custom_call" | custom-call | flops 199999995904 | bytes 10000000 | tf_op jit(solution)/shard_map/pallas_call | solution.py:1015
  506.1 0.8 slice_reduce_fusion
  507.2 0.9 reduce_sum.54
  509.0 5.5 fusion.1
  514.5 2.0 maximum_bitcast_fusion.1
  517.1 124.8 %shard_map.291 = (f32[512,2048]{1,0:T(8,128)}, f32[4,784,128]{2,1,0:T(8,128)}, bf16[4,784,128]{2,1,0:T(8,128)(2,1)}, f32[256,128]{1,0:T(8,128)}, f32[8,2048]{1,0:T(8,128)}, /*index=5*/f32[8,768]{1,0:T(8,128)}) custom-call(bf16[512,2048]{1,0:T(8,128)(2,1)} %hidden_ref.3, bf16[512,2048]{1,0:T(8,128)(2,1)} %cot_ref.3, f32[512,1]{1,0:T(8,128)} %get-tuple-element.55.inv_ref, ...), custom_call_target="tpu_custom_call" | custom-call | flops 99999997952 | bytes 10000000 | tf_op jit(solution)/shard_map/pallas_call | solution.py:1434
  642.0 1.3 slice.125
  643.3 1.4 fusion.24
  644.7 1.3 slice.124
  647.4 1.5 fusion.20
  650.9 0.8 copy.70
  655.4 2.3 copy.69
  658.3 1.1 maximum_select_fusion.2
  659.4 4.7 copy.77
  (94 shorter events, 14.2 us)
Async XLA Ops:
  0.7 11.7 %copy-start = (f32[4,2048]{1,0:T(4,128)S(1)}, f32[4,2048]{1,0:T(4,128)}, u32[]{:S(2)}) copy-start(f32[4,2048]{1,0:T(4,128)} %param.22) | copy-start | bytes 98308
  0.7 23.3 %collective-permute-start = (s32[1024]{0:T(1024)}, s32[1024]{0:T(1024)S(1)}, u32[]{:S(2)}, u32[]{:S(2)}) collective-permute-start(s32[1024]{0:T(1024)} %param.17), channel_id=1, source_target_pairs={{0,2},{2,0},{4,6},{6,4},{8,10},{10,8},{12,14},{14,12},{16,18},{18,... | collective-permute-start | bytes 12296 | tf_op jit(solution)/shard_map/ppermute | solution.py:36
  9.4 1.7 copy-start.4
  11.4 1.0 copy-start.11
  11.4 1.0 copy-start.12
  11.6 1.6 copy-start.6
  13.0 2.5 copy-start.13
  18.1 5.2 dynamic-slice-start
  18.1 5.2 dynamic-slice-start.1
  18.1 5.9 copy-start.8
  263.4 4.8 copy-start.14
  263.4 5.0 copy-start.9
  268.3 7.5 %collective-permute-start.1 = (bf16[2,512,2048]{2,1,0:T(8,128)(2,1)}, bf16[2,512,2048]{2,1,0:T(8,128)(2,1)}, u32[]{:S(2)}, u32[]{:S(2)}) collective-permute-start(bf16[2,512,2048]{2,1,0:T(8,128)(2,1)} %slice.136), channel_id=1, source_target_pairs={{0,1},{1,0},{2,3},{3,2},{4,5},{5,4},{6,7},{7,6},{8,9},{9,8},{10,11... | collective-permute-start | bytes 12582920 | tf_op jit(solution)/shard_map/ppermute | solution.py:36
  280.2 228.8 %collective-permute-start.2 = (bf16[512,2048]{1,0:T(8,128)(2,1)}, bf16[512,2048]{1,0:T(8,128)(2,1)}, u32[]{:S(2)}, u32[]{:S(2)}) collective-permute-start(bf16[512,2048]{1,0:T(8,128)(2,1)} %fusion.3), channel_id=1, source_target_pairs={{0,2},{2,0},{4,6},{6,4},{8,10},{10,8},{12,14},{14,12},{16,18},{18,... | collective-permute-start | bytes 6291464 | tf_op jit(solution)/shard_map/ppermute | solution.py:36
  281.7 226.4 %copy-start.15 = (f32[32]{0:T(128)S(1)}, f32[32]{0:T(128)}, u32[]{:S(2)}) copy-start(f32[32]{0:T(128)} %param.27) | copy-start | bytes 388
  281.7 227.3 %copy-start.2 = (bf16[512,2048]{1,0:T(8,128)(2,1)S(1)}, bf16[512,2048]{1,0:T(8,128)(2,1)}, u32[]{:S(2)}) copy-start(bf16[512,2048]{1,0:T(8,128)(2,1)} %hidden_ref.3) | copy-start | bytes 6291460
  281.7 227.3 %copy-start.10 = (f32[512]{0:T(512)S(1)}, f32[512]{0:T(512)}, u32[]{:S(2)}) copy-start(f32[512]{0:T(512)} %get-tuple-element.152) | copy-start | bytes 6148
  642.0 6.9 %copy-start.7 = (f32[8,2048]{1,0:T(8,128)S(1)}, f32[8,2048]{1,0:T(8,128)}, u32[]{:S(2)}) copy-start(f32[8,2048]{1,0:T(8,128)} %get-tuple-element.80) | copy-start | bytes 196612
  642.0 8.7 %copy-start.3 = (bf16[4,784,128]{2,1,0:T(8,128)(2,1)S(1)}, bf16[4,784,128]{2,1,0:T(8,128)(2,1)}, u32[]{:S(2)}) copy-start(bf16[4,784,128]{2,1,0:T(8,128)(2,1)} %get-tuple-element.78) | copy-start | bytes 2408452
  648.9 2.0 copy-start.5
  659.4 4.7 copy-start.1

commit v5 on v4

--- a/solution.py
+++ b/solution.py
@@ -507,28 +507,37 @@
 
 def backward_tile(
     origin, z_ref, y_ref, dyn_ref, bc_ref, wide_ref, pick_ref, col_ref, row_ref, seg_ref, turned_ref, norm_ref,
-    par_ref, rate_ref, state_ref, grad_ref, dbc_ref, dt_ref, head_ref, small_ref, turn_ref, xs_ref, dconv_ref,
-    carry_ref,
+    par_ref, rate_ref, state_ref, grad_ref, dbc_ref, dt_ref, head_ref, small_ref, turn_ref, halo_ref, carry_ref,
 ):
-    length = xs_ref.shape[0]
+    length = z_ref.shape[0]
     blocks = length // BLOCK
-    conv = conv_of(z_ref[:, TILE:], col_ref[...], par_ref)
-    gate = sigmoid(conv)
-    xs_ref[...] = conv * gate
-    dconv_ref[...] = gate * (1.0 + conv * (1.0 - gate))
     carry_ref[...] = jnp.zeros_like(carry_ref)
     small_ref[...] = jnp.zeros_like(small_ref)
     head_ref[...] = jnp.zeros_like(head_ref)
+    halo_ref[...] = jnp.zeros_like(halo_ref)
     down, across = iota((BLOCK, BLOCK), 0), iota((BLOCK, BLOCK), 1)
 
     def one_block(step, carried):
         number = blocks - 1 - step
-        rows = pl.ds(pl.multiple_of(number * BLOCK, BLOCK), BLOCK)
+        start = pl.multiple_of(number * BLOCK, BLOCK)
+        rows = pl.ds(start, BLOCK)
         col = col_ref[rows, :]
+        v = z_ref[rows, TILE:]
+        above = z_ref[pl.ds(pl.multiple_of(jnp.maximum(start - 8, 0), 8), 8), TILE:]
+        joined = jnp.concatenate([above, v], axis=0)
+        moved = [None] + [
+            pltpu.roll(joined, offset, 0)[8:] * col[:, VALID + offset - 1 : VALID + offset]
+            for offset in range(1, 4)
+        ]
+        conv = par_ref[BIAS : BIAS + 1, :] + par_ref[TAPS + 3 : TAPS + 4, :] * v
+        for offset in range(1, 4):
+            conv = conv + par_ref[TAPS + 3 - offset : TAPS + 4 - offset, :] * moved[offset]
+        gate = sigmoid(conv)
+        x = conv * gate
+        slope = gate * (1.0 + conv * (1.0 - gate))
         z, y, dyn = z_ref[rows, :TILE], y_ref[rows, :], dyn_ref[rows, :]
         gain = par_ref[GAIN : GAIN + 1, :]
-        norms = dot(norm_ref[:, rows], (iota((8, 8), 0) == iota((8, 8), 1)).astype(F32), TN, HIGH)
-        inv, cross = norms[:, 0:1], norms[:, 1:2]
+        inv, cross = norm_ref[rows, 0:1], norm_ref[rows, 1:2]
         gate = sigmoid(z)
         silu = z * gate
         yg = y * silu
@@ -538,10 +547,8 @@
         grad_ref[rows, 2 * TILE :] = (yg_inv * gain).astype(BF16)
         small_ref[GAIN : GAIN + 1, :] += jnp.sum(dyn * yg_inv, axis=0, keepdims=True)
         e = d_yg * silu
-        b_rows, c_rows = bc_ref[rows, :LANES], bc_ref[rows, LANES:]
-        b_low, c_low = b_rows.astype(BF16), c_rows.astype(BF16)
+        b_low, c_low = bc_ref[rows, :LANES].astype(BF16), bc_ref[rows, LANES:].astype(BF16)
         scores = turned_ref[rows, :]
-        x = xs_ref[rows, :]
         wide = dot(wide_ref[rows, :], pick_ref[...])
         dt_wide, cum_wide = wide[:, :TILE], wide[:, TILE:]
         dtx = x * dt_wide
@@ -580,19 +587,34 @@
         through = decay[BLOCK - 1 :, :] * jnp.sum(state * d_state, axis=0, keepdims=True)
         d_x = dt_wide * d_dtx + par_ref[SKIP : SKIP + 1, :] * e
         small_ref[SKIP : SKIP + 1, :] += jnp.sum(x * e, axis=0, keepdims=True)
-        dconv_ref[rows, :] = dconv_ref[rows, :] * d_x
-        spot = pl.ds(pl.multiple_of(origin + number * BLOCK, BLOCK), BLOCK)
+        spot = pl.ds(pl.multiple_of(origin + start, BLOCK), BLOCK)
         dbc_ref[spot, :LANES] += d_b
         dbc_ref[spot, LANES:] += d_c
+        d_conv = slope * d_x
+        below = pl.ds(pl.multiple_of(jnp.minimum(start + BLOCK, length - 8), 8), 8)
+        joined = jnp.concatenate([d_conv, halo_ref[...]], axis=0)
+        halo_ref[...] = d_conv[:8]
+        d_v = par_ref[TAPS + 3 : TAPS + 4, :] * d_conv
+        small_ref[TAPS + 3 : TAPS + 4, :] += jnp.sum(d_conv * v, axis=0, keepdims=True)
+        small_ref[BIAS : BIAS + 1, :] += jnp.sum(d_conv, axis=0, keepdims=True)
+        valid = jnp.concatenate([col, col_ref[below, :]], axis=0)
+        for offset in range(1, 4):
+            place = TAPS + 3 - offset
+            small_ref[place : place + 1, :] += jnp.sum(d_conv * moved[offset], axis=0, keepdims=True)
+            counted = joined * valid[:, VALID + offset - 1 : VALID + offset]
+            d_v = d_v + par_ref[place : place + 1, :] * pltpu.roll(counted, BLOCK + 8 - offset, 0)[:BLOCK]
+        grad_ref[rows, TILE : 2 * TILE] = d_v.astype(BF16)
         owner = (iota((TILE, 8), 0) // WIDTH == iota((TILE, 8), 1)).astype(BF16)
 
         def head_sum(a):
             return sum(dot(part, owner) for part in halves(a))
 
-        after = (down <= across).astype(BF16)
-        prior = (down > across).astype(BF16)
-        run = sum(dot(after, part) for part in halves(head_sum(from_state)))
-        run = run + sum(dot(prior, part) for part in halves(head_sum(to_state)))
+        def token_sum(reached, a):
+            both = dot(reached, jnp.concatenate(halves(a), axis=1))
+            return both[:, :8] + both[:, 8:]
+
+        run = token_sum((down <= across).astype(BF16), head_sum(from_state))
+        run = run + token_sum((down > across).astype(BF16), head_sum(to_state))
         run = run + head_sum(jnp.broadcast_to(through, (8, TILE)))[:1]
         sums = jnp.concatenate(
             [run, head_sum(d_dtx * x), jnp.zeros((BLOCK, LANES - 16), F32)], axis=1
@@ -606,66 +628,60 @@
         d_dt = jnp.concatenate([d_dt, jnp.zeros((16 - GROUP, BLOCK), F32)], axis=0).astype(BF16)
         dt_ref[:, rows] = d_dt
         turn_ref[STEPS:OUT, spot] = d_dt
-        return carried
-
-    lax.fori_loop(0, blocks, one_block, 0)
-    v, d_conv = z_ref[:, TILE:], dconv_ref[...]
-    d_v = par_ref[TAPS + 3 : TAPS + 4, :] * d_conv
-    small_ref[TAPS + 3 : TAPS + 4, :] = jnp.sum(d_conv * v, axis=0, keepdims=True)
-    small_ref[BIAS : BIAS + 1, :] = jnp.sum(d_conv, axis=0, keepdims=True)
-    for offset in range(1, 4):
-        place = TAPS + 3 - offset
-        counted = d_conv * col_ref[:, VALID + offset - 1 : VALID + offset]
-        small_ref[place : place + 1, :] = jnp.sum(
-            counted * pltpu.roll(v, offset, 0), axis=0, keepdims=True
-        )
-        d_v = d_v + par_ref[place : place + 1, :] * pltpu.roll(counted, length - offset, 0)
-    grad_ref[:, TILE : 2 * TILE] = d_v.astype(BF16)
-    for number in range(blocks):
-        rows = slice(number * BLOCK, (number + 1) * BLOCK)
-        spot = pl.ds(pl.multiple_of(origin + number * BLOCK, BLOCK), BLOCK)
         turned = grad_ref[rows, :].T
         turn_ref[:STEPS, spot] = turned[: 2 * TILE]
         turn_ref[OUT:, spot] = turned[2 * TILE :]
+        return carried
+
+    lax.fori_loop(0, blocks, one_block, 0)
 
 
 def backward_kernel(*refs, ties, inside, tiles, spans):
     (
         normed_ref, cot_ref, z_ref, y_ref, dyn_ref, bc_ref, wide_ref, pick_ref, col_ref, row_ref, seg_ref,
         turned_ref, norm_ref, par_ref, rate_ref, state_ref,
-        grad_ref, dbc_ref, dt_ref, head_ref, small_ref, far_out_ref, near_out_ref, total_ref,
-        turn_ref, xs_ref, dconv_ref, carry_ref, stream_ref, far_ref, near_ref, y_recv_ref, z_send_ref, z_own_ref,
-        z_recv_ref, stream_sem, out_sem, y_send_sem, y_recv_sem, z_send_sem, z_recv_sem,
+        grad_ref, dbc_ref, dt_ref, head_ref, small_ref, far_out_ref, near_out_ref, z_own_out, z_send_out,
+        mine_ref, theirs_ref, dbc_x_ref,
+        turn_ref, halo_ref, carry_ref, stream_ref, far_ref, near_ref, y_recv_ref, z_send_ref, z_own_ref,
+        z_recv_ref, w_send_ref, w_recv_ref, dbc_core_ref, dbc_send_ref, dbc_recv_ref,
+        stream_sem, out_sem, y_send_sem, y_recv_sem, z_send_sem, z_recv_sem, w_send_sem, w_recv_sem,
+        d_send_sem, d_recv_sem,
     ) = refs[ties:]
-    tile, sequence = pl.program_id(0), pl.program_id(1)
-    length = xs_ref.shape[0]
-    parts = turn_ref.shape[0], near_ref.shape[2]
+    tile, turn = pl.program_id(0), pl.program_id(1)
+    sequence = 1 - turn
+    done = inside - 1
+    length = z_ref.shape[0]
+    part = near_ref.shape[2]
     halves_of = near_ref.shape[0]
+    ahead = stream_ref.shape[0] - 1
     dp, mp = lax.axis_index("dp"), lax.axis_index("mp")
+    side = lax.rem(dp, 2)
 
     def partner(bits):
         return (jnp.bitwise_xor(dp, bits), mp)
 
-    def y_copy(number, part):
+    def remote(src, dst, send, recv, device):
+        return pltpu.make_async_remote_copy(
+            src_ref=src, dst_ref=dst, send_sem=send, recv_sem=recv, device_id=device,
+            device_id_type=pl.DeviceIdType.MESH,
+        )
+
+    def y_copy(number, at):
         slot = lax.rem(number, 2)
-        return pltpu.make_async_remote_copy(
-            src_ref=far_ref.at[part],
-            dst_ref=y_recv_ref.at[slot, part],
-            send_sem=y_send_sem.at[part],
-            recv_sem=y_recv_sem.at[slot, part],
-            device_id=partner(2),
-            device_id_type=pl.DeviceIdType.MESH,
+        return remote(
+            far_ref.at[at], y_recv_ref.at[slot, at], y_send_sem.at[at], y_recv_sem.at[slot, at], partner(2)
         )
 
     def z_copy(number, k):
         slot = lax.rem(number, 2)
-        return pltpu.make_async_remote_copy(
-            src_ref=z_send_ref.at[k - 1],
-            dst_ref=z_recv_ref.at[slot, k - 1],
-            send_sem=z_send_sem.at[k - 1],
-            recv_sem=z_recv_sem.at[slot, k - 1],
-            device_id=partner(4 * k),
-            device_id_type=pl.DeviceIdType.MESH,
+        return remote(
+            z_send_ref.at[k - 1], z_recv_ref.at[slot, k - 1], z_send_sem.at[k - 1], z_recv_sem.at[slot, k - 1],
+            partner(4 * k),
+        )
+
+    def w_copy(number):
+        return remote(
+            w_send_ref.at[number], w_recv_ref.at[number], w_send_sem.at[number], w_recv_sem.at[number], partner(1)
         )
 
     def finish(number):
@@ -674,55 +690,95 @@
         for k in range(1, spans):
             z_copy(number, k).wait()
             total = total + z_recv_ref[slot, k - 1].astype(F32)
-        total_ref[number] = total
+        z_own_ref[...] = total
+        mine_ref[number] = z_own_ref[:, pl.ds(pl.multiple_of(side * LANES, LANES), LANES)]
+        w_send_ref[number] = z_own_ref[:, pl.ds(pl.multiple_of((1 - side) * LANES, LANES), LANES)].astype(BF16)
+        w_copy(number).start()
 
     def pass_on(number):
         slot = lax.rem(number, 2)
-        for part in range(spans):
-            y_copy(number, part).wait()
-            whole_part = near_ref[part] + y_recv_ref[slot, part].astype(F32)
-            if part == 0:
+        for at in range(spans):
+            y_copy(number, at).wait()
+            whole_part = near_ref[at] + y_recv_ref[slot, at].astype(F32)
+            if at == 0:
                 z_own_ref[...] = whole_part
             else:
-                z_send_ref[part - 1] = whole_part.astype(BF16)
-                z_copy(number, part).start()
-
-    @pl.when((tile == 0) & (sequence == 0))
+                z_send_ref[at - 1] = whole_part.astype(BF16)
+
+                @pl.when(number < done)
+                def _(at=at):
+                    z_copy(number, at).start()
+
+    def z_out():
+        return [
+            pltpu.make_async_copy(z_own_ref, z_own_out, out_sem.at[2]),
+            pltpu.make_async_copy(z_send_ref, z_send_out, out_sem.at[3]),
+        ]
+
+    def dbc_core():
+        src = dbc_ref.at[pl.ds(length, length), :]
+        return remote(src, dbc_core_ref, d_send_sem.at[0], d_recv_sem.at[0], (dp, 1 - mp))
+
+    def dbc_x():
+        return remote(dbc_send_ref, dbc_recv_ref, d_send_sem.at[1], d_recv_sem.at[1], partner(1))
+
+    @pl.when((tile == 0) & (turn == 0))
     def _():
         dbc_ref[...] = jnp.zeros_like(dbc_ref)
         if inside:
             barrier = pltpu.get_barrier_semaphore()
-            others = [2] + [4 * k for k in range(1, spans)]
-            for bits in others:
-                pl.semaphore_signal(
-                    barrier, inc=1, device_id=partner(bits), device_id_type=pl.DeviceIdType.MESH
-                )
+            others = [partner(1), partner(2), (dp, 1 - mp)] + [partner(4 * k) for k in range(1, spans)]
+            for device in others:
+                pl.semaphore_signal(barrier, inc=1, device_id=device, device_id_type=pl.DeviceIdType.MESH)
             pl.semaphore_wait(barrier, len(others))
 
-    if inside > 1:
-
-        @pl.when((sequence == 1) & (tile >= 2) & (tile < inside + 2))
-        def _():
-            finish(tile - 2)
-
-    if inside:
-
-        @pl.when((sequence == 1) & (tile >= 1) & (tile < inside + 1))
-        def _():
-            pass_on(tile - 1)
-
-    backward_tile(
-        sequence * length, z_ref, y_ref, dyn_ref, bc_ref, wide_ref, pick_ref, col_ref, row_ref, seg_ref,
-        turned_ref, norm_ref, par_ref, rate_ref, state_ref, grad_ref, dbc_ref, dt_ref, head_ref, small_ref,
-        turn_ref, xs_ref, dconv_ref, carry_ref,
-    )
-
-    def fetch(number, slot):
-        lanes = pl.ds(pl.multiple_of(number * parts[1], LANES), parts[1])
+    def fetch(step):
+        number = lax.rem(step + halves_of, 2 * halves_of)
+        slot = lax.rem(step, ahead + 1)
+        lanes = pl.ds(pl.multiple_of(number * part, LANES), part)
         return [
             pltpu.make_async_copy(ref.at[:, lanes], stream_ref.at[slot, at], stream_sem.at[slot, at])
             for at, ref in enumerate((normed_ref, cot_ref))
         ]
+
+    @pl.when(turn == 1)
+    def _():
+        for step in range(ahead):
+            for copy in fetch(step):
+                copy.start()
+
+    if inside:
+
+        @pl.when((tile == tiles - 1) & (turn == 1))
+        def _():
+            dbc_core().start()
+
+    backward_tile(
+        sequence * length, z_ref, y_ref, dyn_ref, bc_ref, wide_ref, pick_ref, col_ref, row_ref, seg_ref,
+        turned_ref, norm_ref, par_ref, rate_ref, state_ref, grad_ref, dbc_ref, dt_ref, head_ref, small_ref,
+        turn_ref, halo_ref, carry_ref,
+    )
+
+    if inside:
+
+        @pl.when((tile == tiles - 1) & (turn == 1))
+        def _():
+            dbc_core().wait()
+            dbc_send_ref[...] = (dbc_ref[length:, :] + dbc_core_ref[...]).astype(BF16)
+            dbc_x().start()
+
+        @pl.when((turn == 1) & (tile >= 2) & (tile < done + 2))
+        def _():
+            finish(tile - 2)
+
+        @pl.when((turn == 1) & (tile >= 1) & (tile <= inside))
+        def _():
+            pass_on(tile - 1)
+
+        @pl.when((turn == 1) & (tile == inside))
+        def _():
+            for copy in z_out():
+                copy.start()
 
     def out_copies():
         place = tile - inside
@@ -731,21 +787,17 @@
             pltpu.make_async_copy(near_ref, near_out_ref.at[place], out_sem.at[1]),
         ]
 
-    @pl.when(sequence == 1)
+    @pl.when(turn == 1)
     def _():
-        for copy in fetch(halves_of, 0):
-            copy.start()
-
         def one_part(step, carried):
-            number = lax.rem(step + halves_of, 2 * halves_of)
-            slot = lax.rem(step, 2)
-
-            @pl.when(step + 1 < 2 * halves_of)
+            slot = lax.rem(step, ahead + 1)
+
+            @pl.when(step + ahead < 2 * halves_of)
             def _():
-                for copy in fetch(lax.rem(step + 1 + halves_of, 2 * halves_of), lax.rem(step + 1, 2)):
+                for copy in fetch(step + ahead):
                     copy.start()
 
-            for copy in fetch(number, slot):
+            for copy in fetch(step):
                 copy.wait()
             upper = dot(turn_ref[:OUT, :], stream_ref[slot, 0])
             lower = dot(turn_ref[OUT:, :], stream_ref[slot, 1])
@@ -754,6 +806,11 @@
             def _():
                 far_ref[step, :OUT, :] = upper.astype(BF16)
                 far_ref[step, OUT:, :] = lower.astype(BF16)
+                if inside:
+
+                    @pl.when(tile < inside)
+                    def _():
+                        y_copy(tile, step).start()
 
             @pl.when(step >= halves_of)
             def _():
@@ -762,32 +819,26 @@
 
             return carried
 
-        def run(first, last):
-            lax.fori_loop(first, last, one_part, 0)
-
-        run(0, halves_of)
-        if inside:
-
-            @pl.when(tile < inside)
-            def _():
-                for part in range(spans):
-                    y_copy(tile, part).start()
-
-        run(halves_of, 2 * halves_of)
-        if inside < tiles:
-
-            @pl.when(tile >= inside)
-            def _():
-                for copy in out_copies():
-                    copy.start()
-                for copy in out_copies():
-                    copy.wait()
+        lax.fori_loop(0, 2 * halves_of, one_part, 0)
+
+        @pl.when(tile >= inside)
+        def _():
+            for copy in out_copies():
+                copy.start()
+            for copy in out_copies():
+                copy.wait()
 
     if inside:
 
-        @pl.when((sequence == 1) & (tile == tiles - 1))
+        @pl.when((turn == 1) & (tile == tiles - 1))
         def _():
-            finish(tile - 1)
+            for copy in z_out():
+                copy.wait()
+            for number in range(done):
+                w_copy(number).wait()
+            theirs_ref[...] = w_recv_ref[...]
+            dbc_x().wait()
+            dbc_x_ref[...] = dbc_recv_ref[...]
 
 
 def by_sequence(rows, width):
@@ -999,16 +1050,22 @@
     part = 2 * LANES
     near = width // part // 2
     inside = tiles - 1 if near == spans else 0
+    done = max(inside - 1, 1)
+    hops = 3
 
     def by_tile(size, cols):
-        return pl.BlockSpec((None, size, cols), lambda j, i: (j, i, 0))
+        return pl.BlockSpec((None, size, cols), lambda j, i: (j, 1 - i, 0))
 
     def shared(size, cols):
-        return pl.BlockSpec((size, cols), lambda j, i: (i, 0))
+        return pl.BlockSpec((size, cols), lambda j, i: (1 - i, 0))
 
     def fixed(*shape):
         return pl.BlockSpec((None,) + shape, lambda j, i: (j,) + (0,) * len(shape))
 
+    def constant(*shape):
+        return pl.BlockSpec(shape, lambda j, i: (0,) * len(shape))
+
+    dma = pltpu.SemaphoreType.DMA
     params = dict(vmem_limit_bytes=VMEM_LIMIT)
     if inside:
         params.update(collective_id=1, has_side_effects=True)
@@ -1026,23 +1083,27 @@
             shared(length, LANES),
             fixed(LANES, 2 * TILE),
             shared(length, COLS),
-            pl.BlockSpec((8, length), lambda j, i: (j, i)),
-            pl.BlockSpec((1, length), lambda j, i: (0, i)),
+            pl.BlockSpec((8, length), lambda j, i: (j, 1 - i)),
+            pl.BlockSpec((1, length), lambda j, i: (0, 1 - i)),
             shared(length, BLOCK),
-            pl.BlockSpec((8, length), lambda j, i: (0, i)),
+            shared(length, 8),
             fixed(8, TILE),
             fixed(8, LANES),
-            pl.BlockSpec((None, blocks, LANES, TILE), lambda j, i: (j, i, 0, 0)),
+            pl.BlockSpec((None, blocks, LANES, TILE), lambda j, i: (j, 1 - i, 0, 0)),
         ],
         out_specs=[
             by_tile(length, 3 * TILE),
-            pl.BlockSpec((tokens, 2 * LANES), lambda j, i: (0, 0)),
-            pl.BlockSpec((16, length), lambda j, i: (j, i)),
-            pl.BlockSpec((None, None, 8, LANES), lambda j, i: (j, i, 0, 0)),
-            pl.BlockSpec((None, None, 8, TILE), lambda j, i: (j, i, 0, 0)),
+            constant(tokens, 2 * LANES),
+            pl.BlockSpec((16, length), lambda j, i: (j, 1 - i)),
+            pl.BlockSpec((None, None, 8, LANES), lambda j, i: (j, 1 - i, 0, 0)),
+            pl.BlockSpec((None, None, 8, TILE), lambda j, i: (j, 1 - i, 0, 0)),
             ANY,
             ANY,
-            pl.BlockSpec((max(inside, 1), SHARE, part), lambda j, i: (0, 0, 0)),
+            ANY,
+            ANY,
+            constant(done, SHARE, LANES),
+            constant(done, SHARE, LANES),
+            constant(length, part),
         ],
         out_shape=[
             shaped((tiles, tokens, 3 * TILE), BF16),
@@ -1052,26 +1113,38 @@
             shaped((tiles, number, 8, TILE)),
             shaped((tiles - inside, near, SHARE, part), BF16),
             shaped((tiles - inside, near, SHARE, part)),
-            shaped((max(inside, 1), SHARE, part)),
+            shaped((SHARE, part)),
+            shaped((hops, SHARE, part), BF16),
+            shaped((done, SHARE, LANES)),
+            shaped((done, SHARE, LANES), BF16),
+            shaped((length, part), BF16),
         ],
         scratch_shapes=[
             pltpu.VMEM((SHARE, tokens), BF16),
-            pltpu.VMEM((length, TILE), F32),
-            pltpu.VMEM((length, TILE), F32),
+            pltpu.VMEM((8, TILE), F32),
             pltpu.VMEM((LANES, TILE), F32),
-            pltpu.VMEM((2, 2, tokens, part), BF16),
+            pltpu.VMEM((4, 2, tokens, part), BF16),
             pltpu.VMEM((near, SHARE, part), BF16),
             pltpu.VMEM((near, SHARE, part), F32),
             pltpu.VMEM((2, near, SHARE, part), BF16),
-            pltpu.VMEM((3, SHARE, part), BF16),
+            pltpu.VMEM((hops, SHARE, part), BF16),
             pltpu.VMEM((SHARE, part), F32),
-            pltpu.VMEM((2, 3, SHARE, part), BF16),
-            pltpu.SemaphoreType.DMA((2, 2)),
-            pltpu.SemaphoreType.DMA((2,)),
-            pltpu.SemaphoreType.DMA((near,)),
-            pltpu.SemaphoreType.DMA((2, near)),
-            pltpu.SemaphoreType.DMA((3,)),
-            pltpu.SemaphoreType.DMA((2, 3)),
+            pltpu.VMEM((2, hops, SHARE, part), BF16),
+            pltpu.VMEM((done, SHARE, LANES), BF16),
+            pltpu.VMEM((done, SHARE, LANES), BF16),
+            pltpu.VMEM((length, part), F32),
+            pltpu.VMEM((length, part), BF16),
+            pltpu.VMEM((length, part), BF16),
+            dma((4, 2)),
+            dma((4,)),
+            dma((near,)),
+            dma((2, near)),
+            dma((hops,)),
+            dma((2, hops)),
+            dma((done,)),
+            dma((done,)),
+            dma((2,)),
+            dma((2,)),
         ],
         compiler_params=pltpu.CompilerParams(**params),
         cost_estimate=cost(2e11),
@@ -1081,20 +1154,70 @@
     )
 
 
-def mixer_kernel(place_ref, z_ref, y_ref, norm_ref, par_ref, w_ref, out_ref, *, spans):
-    tiles, rows = y_ref.shape[:2]
-    norms = dot(norm_ref[...], (iota((8, 8), 0) == iota((8, 8), 1)).astype(F32), TN, HIGH)
-    parts = []
-    for tile in range(tiles):
-        z = z_ref[tile]
-        yg = y_ref[tile] * (z * sigmoid(z))
-        parts.append((yg * norms[:, 0:1] * par_ref[tile, GAIN : GAIN + 1, :]).astype(BF16))
+def mixer_kernel(
+    z_hbm, y_hbm, norm_ref, par_ref, w_ref, own_ref, give_ref,
+    z_buf, y_buf, norm_buf, away, recv, z_sem, y_sem, send_sem, recv_sem, *, spans, length,
+):
+    tiles, rows = z_buf.shape[1:3]
+    dp, mp = lax.axis_index("dp"), lax.axis_index("mp")
     part = 2 * LANES
-    for number in range(2 * spans):
-        total = jnp.zeros((rows, part), F32)
+    order = ((1, 1 - mp), (0, 1 - mp), (1, mp), (0, mp))
+
+    def rows_of(step):
+        sequence, half = order[step]
+        return pl.ds(pl.multiple_of(sequence * length + half * rows, rows), rows)
+
+    def fetch(step):
+        slot = step % 2
+        at = rows_of(step)
+        return [
+            pltpu.make_async_copy(z_hbm.at[:, at, pl.ds(0, TILE)], z_buf.at[slot], z_sem.at[slot]),
+            pltpu.make_async_copy(y_hbm.at[:, at, :], y_buf.at[slot], y_sem.at[slot]),
+        ]
+
+    def core_copy(step):
+        return pltpu.make_async_remote_copy(
+            src_ref=away.at[step], dst_ref=recv.at[step], send_sem=send_sem.at[step], recv_sem=recv_sem.at[step],
+            device_id=(dp, 1 - mp), device_id_type=pl.DeviceIdType.MESH,
+        )
+
+    for copy in fetch(0):
+        copy.start()
+    barrier = pltpu.get_barrier_semaphore()
+    pl.semaphore_signal(barrier, inc=1, device_id=(dp, 1 - mp), device_id_type=pl.DeviceIdType.MESH)
+    pl.semaphore_wait(barrier, 1)
+    for step in range(4):
+        if step < 3:
+            for copy in fetch(step + 1):
+                copy.start()
+        for copy in fetch(step):
+            copy.wait()
+        norm_buf[...] = norm_ref[rows_of(step), :]
+        parts = []
         for tile in range(tiles):
-            total = total + dot(parts[tile], w_ref[tile, number * part : (number + 1) * part, :], NT)
-        out_ref[:, pl.ds(pair_start(number, place_ref[0], spans), part)] = total.astype(BF16)
+            z = z_buf[step % 2, tile]
+            yg = y_buf[step % 2, tile] * (z * sigmoid(z))
+            parts.append((yg * norm_buf[:, 0:1] * par_ref[tile, GAIN : GAIN + 1, :]).astype(BF16))
+        if step >= 2:
+            core_copy(step - 2).wait()
+
+        def columns(number, carried, step=step, parts=parts):
+            at = pl.ds(pl.multiple_of(number * part, part), part)
+            total = dot(parts[0], w_ref[0, at, :], NT)
+            for tile in range(1, tiles):
+                total = total + dot(parts[tile], w_ref[tile, at, :], NT)
+            lanes = pl.ds(pair_start(number, dp, spans), part)
+            if step < 2:
+                away[step, :, lanes] = total.astype(BF16)
+            elif step == 2:
+                give_ref[:, lanes] = (total + recv[0, :, lanes].astype(F32)).astype(BF16)
+            else:
+                own_ref[:, lanes] = total + recv[1, :, lanes].astype(F32)
+            return carried
+
+        lax.fori_loop(0, 2 * spans, columns, 0)
+        if step < 2:
+            core_copy(step).start()
 
 
 def pair_start(number, dp, spans):
@@ -1102,41 +1225,51 @@
     return pl.multiple_of(jnp.bitwise_xor(dp - lax.rem(dp, 2), bits) * LANES, 2 * LANES)
 
 
-def run_mixer(place, zvs, ys, norms, params, weights, rows, spans):
+def run_mixer(zvs, ys, norms, params, weights, rows, length, spans):
     tiles, tokens, _ = ys.shape
     width = weights.shape[1]
-
-    def at(i, place_ref):
-        half = jnp.bitwise_xor(i // 2, place_ref[1])
-        return i % 2 * 2 + half
-
+    dma = pltpu.SemaphoreType.DMA
     return pl.pallas_call(
-        functools.partial(mixer_kernel, spans=spans),
-        grid_spec=pltpu.PrefetchScalarGridSpec(
-            num_scalar_prefetch=1,
-            grid=(4,),
-            in_specs=[
-                pl.BlockSpec((tiles, rows, TILE), lambda i, p: (0, at(i, p), 0)),
-                pl.BlockSpec((tiles, rows, TILE), lambda i, p: (0, at(i, p), 0)),
-                pl.BlockSpec((8, rows), lambda i, p: (0, at(i, p))),
-                pl.BlockSpec((tiles, 8, TILE), lambda i, p: (0, 0, 0)),
-                pl.BlockSpec((tiles, width, TILE), lambda i, p: (0, 0, 2)),
-            ],
-            out_specs=pl.BlockSpec((None, rows, width), lambda i, p: (i, 0, 0)),
+        functools.partial(mixer_kernel, spans=spans, length=length),
+        grid=(1,),
+        in_specs=[
+            ANY,
+            ANY,
+            pl.BlockSpec((tokens, 8), lambda i: (0, 0)),
+            pl.BlockSpec((tiles, 8, TILE), lambda i: (0, 0, 0)),
+            pl.BlockSpec((tiles, width, TILE), lambda i: (0, 0, 2)),
+        ],
+        out_specs=[
+            pl.BlockSpec((rows, width), lambda i: (0, 0)),
+            pl.BlockSpec((rows, width), lambda i: (0, 0)),
+        ],
+        out_shape=[shaped((rows, width)), shaped((rows, width), BF16)],
+        scratch_shapes=[
+            pltpu.VMEM((2, tiles, rows, TILE), F32),
+            pltpu.VMEM((2, tiles, rows, TILE), F32),
+            pltpu.VMEM((rows, 8), F32),
+            pltpu.VMEM((2, rows, width), BF16),
+            pltpu.VMEM((2, rows, width), BF16),
+            dma((2,)),
+            dma((2,)),
+            dma((2,)),
+            dma((2,)),
+        ],
+        compiler_params=pltpu.CompilerParams(
+            vmem_limit_bytes=VMEM_LIMIT, collective_id=4, has_side_effects=True
         ),
-        out_shape=shaped((4, rows, width), BF16),
-        compiler_params=pltpu.CompilerParams(vmem_limit_bytes=VMEM_LIMIT),
         cost_estimate=cost(1e10),
-    )(place, zvs, ys, norms, params, weights)
+    )(zvs, ys, norms, params, weights)
 
 
 def tail_kernel(
     hidden_ref, cot_ref, inv_ref, gain_ref, grads_hbm, weights_hbm, small_ref, dt_ref, far_hbm, near_ref,
-    totals_ref, dbc_ref, proj_ref, col_ref, par_ref, normed_hbm, pack_ref, sums_ref,
-    grad_out, mine_ref, theirs_ref, bc_out_ref, pack_out_ref, last_ref,
+    z_own_ref, z_send_hbm, mine_ref, theirs_ref, dbc_ref, dbc_x_ref, proj_ref, col_ref, par_ref, normed_hbm,
+    smalls_ref, heads_ref, rate_ref, sums_ref,
+    grad_out, zx_ref, out_ref, steps_ref, bc_out_ref, pack_out_ref, last_ref,
     grads_seq, wblk, acc_ref, give_ref, core_recv, own_ref, x_give, x_recv, y_recv, z_send, z_own, z_recv, w_send,
-    dbc_core, dbc_x, dbc_low, dt_cols, normed_blk, bc_grad, bc_xs, bc_own, bc_xr, bc_yr, bc_zr, bc_core, pack_recv,
-    last_recv,
+    w_recv, dbc_core, dbc_low, dt_cols, normed_blk, bc_grad, bc_xs, bc_own, bc_xr, bc_yr, bc_zr, bc_core,
+    pack_recv, last_recv,
     seq_sem, blk_sem, out_sem, core_send, core_rsem, xs_sem, xr_sem, ys_sem, yr_sem, zs_sem, zr_sem, ws_sem, wr_sem,
     ds_sem, dr_sem, bs_sem, br_sem, ps_sem, pr_sem, ls_sem, lr_sem,
     *, spans, inside, extent,
@@ -1195,14 +1328,17 @@
     def y_copy(k):
         return remote(far_hbm.at[0, k], y_recv.at[k], ys_sem.at[k], yr_sem.at[k], along(2))
 
-    def z_copy(k):
-        return remote(z_send.at[k - 1], z_recv.at[k - 1], zs_sem.at[k - 1], zr_sem.at[k - 1], along(4 * k))
-
-    def w_copy(tile):
-        return remote(w_send.at[tile], theirs_ref.at[tile], ws_sem.at[tile], wr_sem.at[tile], along(1))
+    def z_copy(number, k):
+        src = z_send_hbm if number == 0 else z_send
+        return remote(
+            src.at[k - 1], z_recv.at[number, k - 1], zs_sem.at[number, k - 1], zr_sem.at[number, k - 1],
+            along(4 * k),
+        )
+
+    def w_copy(number):
+        return remote(w_send.at[number], w_recv.at[number], ws_sem.at[number], wr_sem.at[number], along(1))
 
     dbc_between = remote(dbc_ref, dbc_core, ds_sem.at[0], dr_sem.at[0], other_core)
-    dbc_across = remote(dbc_core.at[pl.ds(length, length), :], dbc_x, ds_sem.at[1], dr_sem.at[1], along(1))
     bc_x = remote(bc_xs, bc_xr, bs_sem.at[0], br_sem.at[0], along(1))
     bc_y = remote(bc_own.at[pl.ds(spans, spans)], bc_yr, bs_sem.at[1], br_sem.at[1], along(2))
 
@@ -1225,10 +1361,26 @@
         device = along(bits[step]) if step < len(bits) else other_core
         return remote(last_ref, last_recv.at[step], ls_sem.at[step], lr_sem.at[step], device)
 
-    def give_total(tile, total_ref):
-        mine_ref[tile] = total_ref[:, ours]
-        w_send[tile] = total_ref[:, others].astype(BF16)
-        w_copy(tile).start()
+    def emit(tile, share, owner):
+        channels = (owner * tiles + tile) * TILE
+        for plane in range(2):
+            lanes = pl.ds(pl.multiple_of(plane * 2 * tiles * TILE + channels, TILE), TILE)
+            zx_ref[:, lanes] = share[plane * TILE : (plane + 1) * TILE, :].astype(F32).T
+        out_ref[pl.ds(pl.multiple_of(channels, TILE), TILE), :] = share[OUT:, :].astype(F32)
+        steps_ref[tile, owner] = share[STEPS : STEPS + 16, :].astype(F32)[:8]
+
+    def give_total(number, total_ref):
+        w_send[number] = total_ref[:, others].astype(BF16)
+        w_copy(number).start()
+        emit(inside - 1 + number, total_ref[:, ours], side)
+
+    def finish_z(number, own):
+        total = own[...]
+        for k in range(1, spans):
+            z_copy(number, k).wait()
+            total = total + z_recv[number, k - 1].astype(F32)
+        z_own[...] = total
+        give_total(number, z_own)
 
     def products(sequence):
         dt_rows = jnp.concatenate(
@@ -1267,7 +1419,6 @@
 
     seq_fetch(1).start()
     w_fetch(0, 0).start()
-    pack_out_ref[...] = pack_ref[...]
     barrier = pltpu.get_barrier_semaphore()
     partners = [along(1), along(2), other_core] + [along(4 * k) for k in range(1, spans)]
     for device in partners:
@@ -1275,16 +1426,26 @@
     pl.semaphore_wait(barrier, len(partners))
     for k in range(spans):
         y_copy(k).start()
+    for k in range(1, spans):
+        z_copy(0, k).start()
     dbc_between.start()
+    pack_out_ref[...] = jnp.zeros_like(pack_out_ref)
+    head_row = jnp.zeros((1, LANES), F32)
+    for tile in range(tiles):
+        lanes = pl.ds(pl.multiple_of((side * tiles + tile) * TILE, TILE), TILE)
+        pack_out_ref[: GAIN + 1, lanes] = (smalls_ref[tile, 0] + smalls_ref[tile, 1])[: GAIN + 1]
+        heads = heads_ref[tile, 0] + heads_ref[tile, 1]
+        heads = jnp.concatenate([heads[:GROUP], heads[GROUP:] * rate_ref[tile, :GROUP]], axis=0)
+        row = iota((8, LANES), 0)
+        target = (row // GROUP) * 2 * HEADS + side * HEADS + tile * GROUP + row % GROUP
+        head_row = head_row + jnp.sum(
+            jnp.where(iota((8, LANES), 1) == target, heads, 0.0), axis=0, keepdims=True
+        )
+    pack_out_ref[GAIN + 1 : GAIN + 2, :LANES] = head_row
     pack_copy(0).start()
-    for tile in range(inside):
-        give_total(tile, totals_ref.at[tile])
     products(1)
     seq_fetch(0).start()
     w_fetch(0, 0).start()
-    dbc_between.wait()
-    dbc_core[...] += dbc_ref[...]
-    dbc_across.start()
     pack_step(0)
 
     def pass_on(number, carried):
@@ -1298,10 +1459,10 @@
     products(0)
     pack_step(1)
     normed_fetch(0, 0).start()
-    dbc_across.wait()
+    dbc_between.wait()
     conv = conv_of(proj_ref[...], col_ref[...], par_ref)
     gate = sigmoid(conv)
-    d_conv = (dbc_core[:length, :] + dbc_x[...]) * (gate * (1.0 + conv * (1.0 - gate)))
+    d_conv = (dbc_ref[...] + dbc_core[...] + dbc_x_ref[...].astype(F32)) * (gate * (1.0 + conv * (1.0 - gate)))
     d_proj = par_ref[TAPS + 3 : TAPS + 4, :] * d_conv
     small = [None] * 4
     small[3] = jnp.sum(d_conv * proj_ref[...], axis=0, keepdims=True)
@@ -1313,6 +1474,10 @@
     small.append(jnp.sum(d_conv, axis=0, keepdims=True))
     conv_grads = jnp.concatenate(small + [jnp.zeros((3, part), F32)], axis=0)
     dbc_low[...] = d_proj.astype(BF16)
+    finish_z(0, z_own_ref)
+    for tile in range(inside - 1):
+        emit(tile, mine_ref[tile], side)
+        emit(tile, theirs_ref[tile], 1 - side)
     for k in range(spans):
         y_copy(k).wait()
         total = near_ref[0, k] + y_recv[k].astype(F32)
@@ -1320,7 +1485,7 @@
             z_own[...] = total
         else:
             z_send[k - 1] = total.astype(BF16)
-            z_copy(k).start()
+            z_copy(1, k).start()
     half = pl.ds(pl.multiple_of(mp * LANES, LANES), LANES)
     turned = dbc_low[:, half].T
 
@@ -1358,12 +1523,7 @@
     bc_x.wait()
     bc_own[...] += bc_xr[...]
     bc_y.start()
-    total = z_own[...]
-    for k in range(1, spans):
-        z_copy(k).wait()
-        total = total + z_recv[k - 1].astype(F32)
-    z_own[...] = total
-    give_total(inside, z_own)
+    finish_z(1, z_own)
     bc_y.wait()
     bc_own[:spans] += bc_yr[...]
     for k in range(1, spans):
@@ -1410,8 +1570,9 @@
     first = jnp.where(mp == 0, 1.0, 0.0)
     bc_out_ref[:LANES, :] = first * bc_own[0] + (1.0 - first) * bc_core[...]
     bc_out_ref[LANES:, :] = (1.0 - first) * bc_own[0] + first * bc_core[...]
-    for tile in range(inside + 1):
-        w_copy(tile).wait()
+    for number in range(2):
+        w_copy(number).wait()
+        emit(inside - 1 + number, w_recv[number], 1 - side)
     for number in range(count):
         core_copy(0, number).wait_send()
         x_copy(number).wait_send()
@@ -1419,13 +1580,14 @@
 
 
 def run_tail(
-    hidden, cot, inv, gain, grads, weights, small, dts, far_share, near_share, totals, dbc, proj, col, bc_par,
-    normed, pack, sums, length, spans, extent,
+    hidden, cot, inv, gain, grads, weights, small, dts, far_share, near_share, z_own, z_send, mine, theirs, dbc,
+    dbc_x, proj, col, bc_par, normed, smalls, heads, rate, sums, length, spans, extent,
 ):
     rows, width = hidden.shape
     tiles, tokens = grads.shape[:2]
     part, inside = 2 * LANES, tiles - 1
     hops = extent.bit_length() - 1
+    channels = 2 * tiles * TILE
     dma = pltpu.SemaphoreType.DMA
 
     def full(*shape):
@@ -1445,29 +1607,37 @@
             full(*dts.shape),
             ANY,
             full(*near_share.shape),
-            full(*totals.shape),
-            full(*dbc.shape),
+            full(*z_own.shape),
+            ANY,
+            full(*mine.shape),
+            full(*theirs.shape),
+            full(length, part),
+            full(length, part),
             full(length, part),
             full(length, COLS),
             full(8, part),
             ANY,
-            full(*pack.shape),
+            full(*smalls.shape),
+            full(*heads.shape),
+            full(*rate.shape),
             full(8, LANES),
         ],
         out_specs=[
             ANY,
-            full(tiles, SHARE, LANES),
-            full(tiles, SHARE, LANES),
+            full(LANES, 2 * channels),
+            full(channels, LANES),
+            full(tiles, 2, 8, LANES),
             full(part, LANES),
-            full(*pack.shape),
+            full(8, channels),
             full(8, 3 * part),
         ],
         out_shape=[
             shaped((rows, width)),
-            shaped((tiles, SHARE, LANES)),
-            shaped((tiles, SHARE, LANES), BF16),
+            shaped((LANES, 2 * channels)),
+            shaped((channels, LANES)),
+            shaped((tiles, 2, 8, LANES)),
             shaped((part, LANES)),
-            shaped(pack.shape),
+            shaped((8, channels)),
             shaped((8, 3 * part)),
         ],
         scratch_shapes=[
@@ -1482,9 +1652,9 @@
             pltpu.VMEM((spans, SHARE, part), BF16),
             pltpu.VMEM((spans - 1, SHARE, part), BF16),
             pltpu.VMEM((SHARE, part), F32),
-            pltpu.VMEM((spans - 1, SHARE, part), BF16),
-            pltpu.VMEM((tiles, SHARE, LANES), BF16),
-            pltpu.VMEM((tokens, part), F32),
+            pltpu.VMEM((2, spans - 1, SHARE, part), BF16),
+            pltpu.VMEM((2, SHARE, LANES), BF16),
+            pltpu.VMEM((2, SHARE, LANES), BF16),
             pltpu.VMEM((length, part), F32),
             pltpu.VMEM((length, part), BF16),
             pltpu.VMEM((length, LANES), BF16),
@@ -1496,7 +1666,7 @@
             pltpu.VMEM((spans, LANES, LANES), F32),
             pltpu.VMEM((spans - 1, LANES, LANES), F32),
             pltpu.VMEM((LANES, LANES), F32),
-            pltpu.VMEM((hops,) + pack.shape, F32),
+            pltpu.VMEM((hops, 8, channels), F32),
             pltpu.VMEM((hops + 1, 8, 3 * part), F32),
             dma((1,)),
             dma((4,)),
@@ -1507,12 +1677,12 @@
             dma((2 * spans,)),
             dma((spans,)),
             dma((spans,)),
-            dma((spans - 1,)),
-            dma((spans - 1,)),
-            dma((tiles,)),
-            dma((tiles,)),
+            dma((2, spans - 1)),
+            dma((2, spans - 1)),
             dma((2,)),
             dma((2,)),
+            dma((1,)),
+            dma((1,)),
             dma((2 + spans,)),
             dma((2 + spans,)),
             dma((hops,)),
@@ -1525,8 +1695,8 @@
         ),
         cost_estimate=cost(1e11),
     )(
-        hidden, cot, inv, gain, grads, weights, small, dts, far_share, near_share, totals, dbc, proj, col, bc_par,
-        normed, pack, sums,
+        hidden, cot, inv, gain, grads, weights, small, dts, far_share, near_share, z_own, z_send, mine, theirs, dbc,
+        dbc_x, proj, col, bc_par, normed, smalls, heads, rate, sums,
     )
 
 
@@ -1664,35 +1834,28 @@
         sums = sums + jnp.concatenate([near[:, length:], near[:, :length]], axis=1)
         norms = norm_rows(sums, inner_total)
 
-    place = jnp.stack([dp, mp])
     inputs = hidden_in.astype(F32)
     usable = (lax.dynamic_slice_in_dim(segments, mp * rows, rows, 0) >= 0).astype(F32)[:, None]
     native = depth == LANES
+    norm_cols = norms.T
     ties = []
     if native:
-        mixer = run_mixer(place, zvs, ys, norms, params, weights, rows, far)
-        ties = [mixer]
-        mixer_near = flip(mixer[2:], "mp", 1)
-        mixer_send = (mixer[1].astype(F32) + mixer_near[1].astype(F32)).astype(BF16)
-        mixer_out = mixer[0].astype(F32) + mixer_near[0].astype(F32) + flip(mixer_send, "dp", 1).astype(F32)
+        mixer_own, mixer_give = run_mixer(zvs, ys, norm_cols, params, weights, rows, length, far)
+        ties = [mixer_own]
+        mixer_out = mixer_own + flip(mixer_give, "dp", 1).astype(F32)
 
     rate_rows = jnp.pad(rate.reshape(tiles, GROUP, 1), ((0, 0), (0, 8 - GROUP), (0, 0)))
-    inside, (grads, dbc, dts, head_sums, smalls, far_share, near_share, inner_totals) = run_backward(
-        ties, normed_all, cot_all, zvs, ys, dyns, bc, wide, col, rows_all, ids_all, turned, norms, params,
-        jnp.broadcast_to(rate_rows, (tiles, 8, LANES)), states, length, far,
+    rate_rows = jnp.broadcast_to(rate_rows, (tiles, 8, LANES))
+    inside, results = run_backward(
+        ties, normed_all, cot_all, zvs, ys, dyns, bc, wide, col, rows_all, ids_all, turned, norm_cols, params,
+        rate_rows, states, length, far,
     )
+    (
+        grads, dbc, dts, head_sums, smalls, far_share, near_share, z_own, z_send, mine, theirs, dbc_x,
+    ) = results
 
     def placed(a):
-        zero = jnp.zeros_like(a)
-        return by_side(a, zero, a.ndim - 1)
-
-    small = jnp.sum(smalls, axis=1).transpose(1, 0, 2).reshape(8, quarter)
-    head_sums = jnp.sum(head_sums[..., 0], axis=1)
-    grad_dt_bias = placed(head_sums[:, :GROUP].reshape(own_heads))
-    grad_a_log = placed(head_sums[:, GROUP:].reshape(own_heads) * rate)
-    channel = placed(small[: GAIN + 1])
-    head_row = jnp.pad(jnp.concatenate([grad_dt_bias, grad_a_log]), (0, inner - 2 * heads))
-    pack = jnp.concatenate([channel, head_row[None]], axis=0)
+        return by_side(a, jnp.zeros_like(a), a.ndim - 1)
 
     def summed(a, axes):
         for axis in axes:
@@ -1713,11 +1876,13 @@
 
     if native:
         sums = jnp.pad(mixer_sums(mixer_out)[None], ((0, 7), (0, LANES - 3)))
-        input_grad, mine, theirs, grad_bc, pack, last = run_tail(
+        input_grad, grad_zx, grad_out_weight, grad_steps, grad_bc, pack, last = run_tail(
             hidden_in, cotangent, inverse_rows, norm_gain[None], grads, weights, bc_weight, dts, far_share,
-            near_share, inner_totals, dbc, proj_bc, col, bc_par, normed_all, pack, sums, length, far, extent,
-        )
-        theirs = theirs.astype(F32)
+            near_share, z_own, z_send, mine, theirs, dbc, dbc_x, proj_bc, col, bc_par, normed_all, smalls,
+            head_sums, rate_rows, sums, length, far, extent,
+        )
+        grad_zx_weight = grad_zx.reshape(depth, 2, inner)
+        grad_dt_weight = grad_steps[:, :, :GROUP].transpose(1, 0, 2, 3).reshape(heads, depth).T
         grad_bc_weight = grad_bc.T
         part = 2 * LANES
         grad_norm_gain = last[:, :part].reshape(width)
@@ -1793,6 +1958,12 @@
             * inverse_cube_rows
             * jnp.mean(inputs * norm_gain * d_normed, axis=-1, keepdims=True)
         )
+        small = jnp.sum(smalls, axis=1).transpose(1, 0, 2).reshape(8, quarter)
+        head_sums = jnp.sum(head_sums[..., 0], axis=1)
+        grad_dt_bias = placed(head_sums[:, :GROUP].reshape(own_heads))
+        grad_a_log = placed(head_sums[:, GROUP:].reshape(own_heads) * rate)
+        head_row = jnp.pad(jnp.concatenate([grad_dt_bias, grad_a_log]), (0, inner - 2 * heads))
+        pack = jnp.concatenate([placed(small[: GAIN + 1]), head_row[None]], axis=0)
         pack = summed(pack, ("dp",))
         conv_sums = jnp.concatenate([grad_conv_bc, grad_conv_bc_bias[None]], axis=0)
         conv_sums = summed(conv_sums, ("dp",))
@@ -1800,17 +1971,17 @@
         last = summed(jnp.concatenate([grad_norm_gain, mixer_sums(mixer_out)]), ("mp", "dp"))
         grad_norm_gain, totals = last[:width], last[width:]
 
+        def assembled(first, last_row):
+            def columns(a):
+                return a[:, first:last_row].reshape(-1, depth)
+
+            return by_side(columns(mine), columns(theirs), 0)
+
+        grad_zx_weight = jnp.stack([assembled(0, TILE).T, assembled(TILE, STEPS).T], axis=1)
+        grad_dt_weight = assembled(STEPS, STEPS + GROUP).T
+        grad_out_weight = assembled(OUT, SHARE)
+
     residual_out = (inputs + mixer_out).astype(BF16)
-
-    def assembled(first, last_row):
-        def columns(a):
-            return a[:, first:last_row].reshape(-1, depth)
-
-        return by_side(columns(mine), columns(theirs), 0)
-
-    grad_zx_weight = jnp.stack([assembled(0, TILE).T, assembled(TILE, STEPS).T], axis=1)
-    grad_dt_weight = assembled(STEPS, STEPS + GROUP).T
-    grad_out_weight = assembled(OUT, SHARE)
     skip_grad = jnp.sum(pack[SKIP].reshape(heads, WIDTH), axis=1)
     sum_inputs, sum_mixer, usable_count = totals[0], totals[1], totals[2]
     rms_residual = jnp.sqrt(sum_inputs / (usable_count * width))

time: 677 us -> 584 us (0.86)
  Pallas kernels: 592 us -> 519 us
  other arithmetic: 23.9 us -> 16.3 us
    pallas_call x1, Pallas kernels: 224 us -> 160 us  [run_backward(): pl.pallas_call(functools.partial(backward_kernel, ties=len(ties), inside=...]
    pallas_call x1, Pallas kernels: 125 us -> 110 us  [run_tail(): pl.pallas_call(functools.partial(tail_kernel, spans=spans, inside=inside,...]
    slice x6 -> x0, local copies, waits for them, and re-layouts: 7.2 us -> none  [the longest x1 4.81 us: local(): mixer_near = flip(mixer[2:], 'mp', 1)]
  transfers between devices with their start and end apart: 3 -> 2, of which waited for: 1 -> 0; matrix products, arithmetic and copies ran while one was open for 3% -> 3% of each run, Pallas kernels for 34% -> 28%
where the time goes in v5:
time: 584 us; the launch traced here: 580 us
  Pallas kernels  519 us (89%)
  local copies, waits for them, and re-layouts  35.9 us (6%)
  other arithmetic  16.3 us (3%)
    pallas_call x1, Pallas kernels, run_gather(): pl.pallas_call(functools.partial(gather_kernel, tiles=tiles, spans=spans,...  218 us
    pallas_call x1, Pallas kernels, run_backward(): pl.pallas_call(functools.partial(backward_kernel, ties=len(ties), inside=...  160 us
    pallas_call x1, Pallas kernels, run_tail(): pl.pallas_call(functools.partial(tail_kernel, spans=spans, inside=inside,...  110 us
    pallas_call x1, Pallas kernels, run_mixer(): pl.pallas_call(functools.partial(mixer_kernel, spans=spans, length=length...  25.5 us
  transfers between devices with their start and end apart: 2, of which 0 were waited for; matrix products, arithmetic and copies ran while one was open for 3% of the time, Pallas kernels for 28%

profile of v5, /device:TPU:0, one launch (start us, length us, event | category | flops | bytes accessed | tf_op | source)
XLA Modules:
  0.0 580.2 jit_solution(14522148048767951685)
XLA Ops:
  0.7 3.0 collective-permute-start
  3.7 0.7 fusion.19
  4.5 0.7 exponential_negate_fusion
  5.2 1.9 fusion.14
  7.1 3.4 fusion.16
  10.6 0.9 copy.75
  11.5 0.9 copy.74
  15.2 0.7 fusion.4
  16.2 0.8 add_convert_fusion.pick_ref.refs_8_
  17.6 1.2 copy.66
  18.8 1.2 copy.67
  20.1 5.2 shard_map.287
  26.0 1.3 copy.70.seg_col_ref
  27.9 217.6 %shard_map.288 = (bf16[2048,2048]{1,0:T(8,128)(2,1)}, bf16[2048,2048]{1,0:T(8,128)(2,1)}, bf16[4,2048,768]{2,1,0:T(8,128)(2,1)}, bf16[2048,384]{1,0:T(8,128)(2,1...) custom-call(bf16[512,2048]{1,0:T(8,128)(2,1)} %get-tuple-element.56., ...), custom_call_target="tpu_custom_call" | custom-call | flops 199999995904 | bytes 10000000 | tf_op jit(solution)/shard_map/pallas_call | solution.py:971
  245.5 2.1 copy.71
  247.7 25.5 %shard_map.289 = (f32[512,2048]{1,0:T(8,128)}, bf16[512,2048]{1,0:T(8,128)(2,1)}) custom-call(f32[4,2048,512]{2,1,0:T(8,128)} %get-tuple-element.58.z_hbm.refs_3_, f32[4,2048,256]{2,1,0:T(8,128)} %get-tuple-element.59.y_hbm.refs_4_, f32[2048,8]{1,0:T(8,128)} %bitcast.53, f32[4,8,256]{2,1,0:T(8,128)} %bitcast.62, ...), custom_call_target="tpu_custom_call" | custom-call | flops 10000000000 | bytes 10000000 | tf_op jit(solution)/shard_map/pallas_call | solution.py:1232
  273.2 0.9 collective-permute-start.1
  274.7 160.0 %shard_map.290 = (bf16[4,2048,768]{2,1,0:T(8,128)(2,1)}, f32[2048,256]{1,0:T(8,128)}, bf16[64,2048]{1,0:T(8,128)(2,1)}, f32[4,2,8,128]{3,2,1,0:T(8,128)}, f32[4,...) custom-call(f32[512,2048]{1,0:T(8,128)} %get-tuple-element.62.refs_0, ...), custom_call_target="tpu_custom_call" | custom-call | flops 199999995904 | bytes 10000000 | tf_op jit(solution)/shard_map/pallas_call | solution.py:1072
  434.8 6.3 %fusion.1 = (f32[]{:T(128)}, f32[]{:T(128)}, bf16[512,2048]{1,0:T(8,128)(2,1)}) fusion(bf16[512,2048]{1,0:T(8,128)(2,1)S(1)} %copy-done.2, f32[512]{0:T(512)S(1)} %copy-done.8, f32[512,2048]{1,0:T(8,128)} %get-tuple-element.62.refs_0_, bf16[512,2048]{1,0:T(8,128)(2,1)} %collective-permute-done.1), kind=kLoop, calls=%fused_computation.4 | loop fusion | flops 11534334 | bytes 10487816 | tf_op jit(solution)/shard_map/reduce_sum | solution.py:1871
  441.1 2.0 maximum_bitcast_fusion.1
  443.7 110.4 %shard_map.291 = (f32[512,2048]{1,0:T(8,128)}, f32[128,4096]{1,0:T(8,128)}, f32[2048,128]{1,0:T(8,128)}, f32[4,2,8,128]{3,2,1,0:T(8,128)}, f32[256,128]{1,0:T(8,...) custom-call(bf16[512,2048]{1,0:T(8,128)(2,1)} %hidden_ref.3, bf16[512,2048]{1,0:T(8,128)(2,1)} %cot_ref.3, ...), custom_call_target="tpu_custom_call" | custom-call | flops 99999997952 | bytes 10000000 | tf_op jit(solution)/shard_map/pallas_call | solution.py:1596
  554.2 1.5 slice.56
  555.7 1.6 fusion.17
  557.2 0.7 slice_bitcast_fusion.1
  557.9 1.3 slice.58
  559.2 1.3 slice.59
  560.5 1.3 slice_bitcast_fusion.2
  561.8 1.4 fusion.18
  563.8 4.0 reshape.641
  568.4 0.8 copy.73
  572.0 4.8 copy.81
  576.7 1.0 copy.82
  (73 shorter events, 8.3 us)
Async XLA Ops:
  0.7 13.8 %copy-start = (f32[4,2048]{1,0:T(4,128)S(1)}, f32[4,2048]{1,0:T(4,128)}, u32[]{:S(2)}) copy-start(f32[4,2048]{1,0:T(4,128)} %param.22) | copy-start | bytes 98308
  0.7 25.3 %collective-permute-start = (s32[1024]{0:T(1024)}, s32[1024]{0:T(1024)S(1)}, u32[]{:S(2)}, u32[]{:S(2)}) collective-permute-start(s32[1024]{0:T(1024)} %param.17), channel_id=1, source_target_pairs={{0,2},{2,0},{4,6},{6,4},{8,10},{10,8},{12,14},{14,12},{16,18},{18,... | collective-permute-start | bytes 12296 | tf_op jit(solution)/shard_map/ppermute | solution.py:36
  10.6 1.7 copy-start.4
  12.5 0.7 copy-start.11
  12.5 0.9 copy-start.15
  12.7 1.8 copy-start.12
  12.7 1.8 copy-start.13
  12.7 2.5 copy-start.6
  15.9 4.0 copy-start.14
  20.1 5.2 dynamic-slice-start
  20.1 5.2 dynamic-slice-start.1
  20.1 5.9 %copy-start.7 = (s32[1024]{0:T(1024)S(1)}, s32[1024]{0:T(1024)}, u32[]{:S(2)}) copy-start(s32[1024]{0:T(1024)} %param.17) | copy-start | bytes 12292
  247.7 26.4 %copy-start.9 = (f32[4,8]{1,0:T(4,128)S(1)}, f32[4,8]{1,0:T(4,128)}, u32[]{:S(2)}) copy-start(f32[4,8]{1,0:T(4,128)} %pad_bitcast_fusion) | copy-start | bytes 388
  273.2 161.6 %collective-permute-start.1 = (bf16[512,2048]{1,0:T(8,128)(2,1)}, bf16[512,2048]{1,0:T(8,128)(2,1)}, u32[]{:S(2)}, u32[]{:S(2)}) collective-permute-start(bf16[512,2048]{1,0:T(8,128)(2,1)} %get-tuple-element.63), channel_id=1, source_target_pairs={{0,2},{2,0},{4,6},{6,4},{8,10},{10,8},{12,14},{14,12},{16,18},{18,... | collective-permute-start | bytes 6291464 | tf_op jit(solution)/shard_map/ppermute | solution.py:36
  274.7 160.0 %copy-start.2 = (bf16[512,2048]{1,0:T(8,128)(2,1)S(1)}, bf16[512,2048]{1,0:T(8,128)(2,1)}, u32[]{:S(2)}) copy-start(bf16[512,2048]{1,0:T(8,128)(2,1)} %hidden_ref.3) | copy-start | bytes 6291460
  274.7 160.0 %copy-start.8 = (f32[512]{0:T(512)S(1)}, f32[512]{0:T(512)}, u32[]{:S(2)}) copy-start(f32[512]{0:T(512)} %get-tuple-element.166) | copy-start | bytes 6148
  563.8 4.0 copy-start.10
  563.8 4.6 copy-start.5
  571.9 4.8 copy-start.3
  571.9 5.8 copy-start.1

commit v6 on v5

--- a/solution.py
+++ b/solution.py
@@ -2,6 +2,7 @@
 
 import jax
 import jax.numpy as jnp
+import numpy as np
 from jax import lax
 from jax.experimental import pallas as pl
 from jax.experimental.pallas import tpu as pltpu
@@ -16,7 +17,7 @@
 HIGH = lax.Precision.HIGHEST
 BF16 = jnp.bfloat16
 F32 = jnp.float32
-VMEM_LIMIT = 58 * 2**20
+VMEM_LIMIT = 60 * 2**20
 
 NN = (((1,), (0,)), ((), ()))
 NT = (((1,), (1,)), ((), ()))
@@ -166,7 +167,12 @@
 
     proj = dot(normed_ref[every, :], weight_ref[...])
     proj_ref[every, :] = proj[:, : 2 * LANES]
-    raw = proj[:, 2 * LANES : 2 * LANES + HEADS] + head_ref[0:1, :HEADS]
+    raw = jnp.where(
+        head_ref[2:3, :HEADS] == 0.0,
+        proj[:, 2 * LANES : 2 * LANES + HEADS],
+        proj[:, 2 * LANES + HEADS : 2 * LANES + 2 * HEADS],
+    )
+    raw = raw + head_ref[0:1, :HEADS]
     dt = jnp.maximum(raw, 0.0) + jnp.log1p(jnp.exp(-jnp.abs(raw)))
     step = dt * head_ref[1:2, :HEADS]
     seg = seg_col_ref[every, :]
@@ -225,35 +231,42 @@
 
 def forward_tile(
     origin, first_row, normed_ref, cot_ref, w_ref, bc_ref, wide_ref, pick_ref, col_ref, row_ref, score_ref,
-    par_ref, z_ref, dyn_ref, y_ref, state_ref, sum_ref, xs_ref, carry_ref,
+    par_ref, z_ref, dyn_ref, y_ref, state_ref, sum_ref, carry_ref,
 ):
-    length = xs_ref.shape[0]
+    length = z_ref.shape[0]
     blocks = length // BLOCK
 
     def spot(number):
         return pl.ds(pl.multiple_of(origin + number * BLOCK, BLOCK), BLOCK)
 
+
     def project(number, carried):
-        rows = pl.ds(pl.multiple_of(number * BLOCK, BLOCK), BLOCK)
-        z_ref[rows, :] = dot(normed_ref[spot(number), :], w_ref[:, : 2 * TILE])
-        dyn_ref[rows, :] = dot(cot_ref[spot(number), :], w_ref[:, 2 * TILE :])
+        rows = pl.ds(pl.multiple_of(number * 2 * BLOCK, 2 * BLOCK), 2 * BLOCK)
+        at = pl.ds(pl.multiple_of(origin + number * 2 * BLOCK, 2 * BLOCK), 2 * BLOCK)
+        z_ref[rows, :] = dot(normed_ref[at, :], w_ref[:, : 2 * TILE])
+        dyn_ref[rows, :] = dot(cot_ref[at, :], w_ref[:, 2 * TILE :])
         return carried
 
-    lax.fori_loop(0, blocks, project, 0)
-    conv = conv_of(z_ref[:, TILE:], col_ref[pl.ds(origin, length), :], par_ref)
-    xs_ref[...] = conv * sigmoid(conv)
+    lax.fori_loop(0, blocks // 2, project, 0)
     carry_ref[...] = jnp.zeros_like(carry_ref)
-    ones = jnp.ones((8, TILE), BF16)
 
     def row_sum(a):
-        return sum(dot(ones, part, NT) for part in halves(a))
+        return jnp.sum(a, axis=1, keepdims=True)
 
     def one_block(number, carried):
         rows, at = pl.ds(pl.multiple_of(number * BLOCK, BLOCK), BLOCK), spot(number)
         b_rows, c_rows = bc_ref[at, :LANES], bc_ref[at, LANES:]
         col = col_ref[at, :]
         scores = score_ref[at, :]
-        x = xs_ref[rows, :]
+        start = number * BLOCK
+        v = z_ref[rows, TILE:]
+        above = z_ref[pl.ds(pl.multiple_of(jnp.maximum(start - 8, 0), 8), 8), TILE:]
+        joined = jnp.concatenate([above, v], axis=0)
+        conv = par_ref[BIAS : BIAS + 1, :] + par_ref[TAPS + 3 : TAPS + 4, :] * v
+        for offset in range(1, 4):
+            moved = pltpu.roll(joined, offset, 0)[8:] * col[:, VALID + offset - 1 : VALID + offset]
+            conv = conv + par_ref[TAPS + 3 - offset : TAPS + 4 - offset, :] * moved
+        x = conv * sigmoid(conv)
         wide = dot(wide_ref[at, :], pick_ref[...])
         dt_wide, cum_wide = wide[:, :TILE], wide[:, TILE:]
         cum_rows = row_ref[pl.ds(first_row, 8), at]
@@ -276,8 +289,8 @@
         yg = y * z * sigmoid(z)
         first = row_sum(yg * yg)
         second = row_sum(yg * par_ref[GAIN : GAIN + 1, :] * dyn_ref[rows, :])
-        place = iota((8, BLOCK), 0)
-        sum_ref[:, at] += jnp.where(place == 0, first, jnp.where(place == 1, second, 0.0))
+        both = jnp.concatenate([first, second, jnp.zeros((BLOCK, LANES - 2), F32)], axis=1).T
+        sum_ref[:, at] += both[:8]
         return carried
 
     lax.fori_loop(0, blocks, one_block, 0)
@@ -285,7 +298,7 @@
 
 def forward_kernel(*refs, pieces):
     normed_ref, cot_ref, bc_ref, wide_ref, pick_ref, col_ref, row_ref, score_ref, par_ref = refs[pieces : pieces + 9]
-    w_ref, z_ref, dyn_ref, y_ref, state_ref, sum_ref, xs_ref, carry_ref = refs[pieces + 9 :]
+    w_ref, z_ref, dyn_ref, y_ref, state_ref, sum_ref, carry_ref = refs[pieces + 9 :]
 
     @pl.when(pl.program_id(0) == 0)
     def _():
@@ -296,22 +309,27 @@
     sum_ref[...] = jnp.zeros_like(sum_ref)
     forward_tile(
         0, 0, normed_ref, cot_ref, w_ref, bc_ref, wide_ref, pick_ref, col_ref, row_ref, score_ref, par_ref,
-        z_ref, dyn_ref, y_ref, state_ref, sum_ref, xs_ref, carry_ref,
+        z_ref, dyn_ref, y_ref, state_ref, sum_ref, carry_ref,
     )
 
 
+def step_of(step):
+    early = step < 4
+    return jnp.where(early, step % 2, step // 2), jnp.where(early, step // 2, step % 2)
+
+
 def gather_kernel(
-    normed_ref, cot_ref, own_ref, other_ref, small_own_ref, small_other_ref, seg_col_ref, seg_row_ref,
+    normed_ref, cot_ref, own_ref, other_ref, small_own_ref, seg_col_ref, seg_row_ref,
     bc_par_ref, head_ref, pick_ref, par_ref,
     normed_out, cot_out, w_out, small_out, z_ref, dyn_ref, y_ref, state_ref, proj_out, bc_out, wide_out, col_out, row_out,
     turned_out, norm_ref,
     normed_all, cot_all, w_all, small_all, proj_all, bc_all, wide_all, col_all, row_all, score_all, turned_all,
-    sum_ref, sum_recv, xs_ref, carry_ref,
+    sum_ref, sum_recv, carry_ref, small_side, small_mine, small_theirs,
     here_sem, out_sem, act_send, act_recv, x_send, x_recv, z_send, z_recv, y_send, y_recv, sum_send, sum_recv_sem,
     *, tiles, spans, inner_total,
 ):
-    tile, sequence = pl.program_id(0), pl.program_id(1)
-    length = xs_ref.shape[0]
+    tile, sequence = step_of(pl.program_id(0))
+    length = z_ref.shape[0]
     rows = normed_ref.shape[0]
     depth = own_ref.shape[1]
     part = 2 * depth
@@ -352,33 +370,60 @@
         )
 
     def weight_of(number):
-        return small_all if number == 0 else w_all.at[number - 1]
+        return small_side.at[side] if number == 0 else w_all.at[number - 1]
 
     def w_here(number):
-        src = small_own_ref if number == 0 else own_ref.at[number - 1]
-        return pltpu.make_async_copy(src, weight_of(number).at[slab, :], here_sem.at[2 + number])
+        if number == 0:
+            return pltpu.make_async_copy(
+                small_own_ref, weight_of(0).at[pl.ds(0, depth), :], here_sem.at[2]
+            )
+        return pltpu.make_async_copy(
+            own_ref.at[number - 1], weight_of(number).at[slab, :], here_sem.at[2 + number]
+        )
 
     def w_x(number):
-        src = small_other_ref if number == 0 else other_ref.at[number - 1]
-        return remote(src, weight_of(number).at[slab, :], x_send.at[number], x_recv.at[number], along(1))
+        if number == 0:
+            src, dst = small_side.at[side], small_side.at[side]
+        else:
+            src, dst = other_ref.at[number - 1], weight_of(number).at[slab, :]
+        return remote(src, dst, x_send.at[number], x_recv.at[number], along(1))
+
+    def rows_at(number, at):
+        size = depth if number == 0 else part
+        return weight_of(number).at[pl.ds(at * size, size), :]
 
     def w_z(number, k):
-        ref = weight_of(number)
         return remote(
-            ref.at[pl.ds(0, part), :], ref.at[pl.ds(k * part, part), :],
-            z_send.at[number, k - 1], z_recv.at[number, k - 1], along(4 * k),
+            rows_at(number, 0), rows_at(number, k), z_send.at[number, k - 1], z_recv.at[number, k - 1], along(4 * k)
         )
 
     def w_y(number, k):
-        ref = weight_of(number)
         return remote(
-            ref.at[pl.ds(k * part, part), :], ref.at[pl.ds((spans + k) * part, part), :],
-            y_send.at[number, k], y_recv.at[number, k], along(2),
-        )
+            rows_at(number, k), rows_at(number, spans + k), y_send.at[number, k], y_recv.at[number, k], along(2)
+        )
+
+    def small_core():
+        return remote(small_mine, small_theirs, sum_send.at[2], sum_recv_sem.at[2], other_core)
+
+    def gather_small():
+        for k in range(2 * spans):
+            for at in range(2):
+                small_mine[k * part + at * depth : k * part + (at + 1) * depth, :] = small_side[
+                    at, k * depth : (k + 1) * depth, :LANES
+                ]
+                small_all[k * part + at * depth : k * part + (at + 1) * depth, 2 * LANES :] = small_side[
+                    at, k * depth : (k + 1) * depth, LANES:
+                ]
+        small_core().start()
+        small_core().wait_recv()
+        first = mp == 0
+        small_all[:, :LANES] = jnp.where(first, small_mine[...], small_theirs[...])
+        small_all[:, LANES : 2 * LANES] = jnp.where(first, small_theirs[...], small_mine[...])
 
     def begin_z(number):
         w_here(number).wait()
-        w_x(number).wait_recv()
+        if number:
+            w_x(number).wait_recv()
         for k in range(1, spans):
             w_z(number, k).start()
         w_y(number, 0).start()
@@ -422,21 +467,24 @@
         act_here(1).start()
         sum_ref[...] = jnp.zeros_like(sum_ref)
         pl.semaphore_wait(barrier, len(partners))
-        w_x(0).start()
         w_x(1).start()
+        w_x(2).start()
+        begin_z(0)
         act_core(0).start()
         act_core(1).start()
+        begin_z(1)
+        begin_y(0)
+        complete(0)
+        w_x(0).start()
         act_x(0).start()
-        begin_z(0)
-        begin_z(1)
-        for number in range(2, tiles + 1):
+        for number in range(3, tiles + 1):
             w_x(number).start()
         act_x(1).start()
-        begin_y(0)
         begin_z(2)
         act_here(0).wait()
         act_core(0).wait_recv()
-        complete(0)
+        w_x(0).wait_recv()
+        gather_small()
         make_tables(0)
         begin_y(1)
         act_x(0).wait_recv()
@@ -444,21 +492,30 @@
         act_here(1).wait()
         act_core(1).wait_recv()
 
+    @pl.when((tile == 1) & (sequence == 0))
+    def _():
+        act_pass(0).wait_recv()
+        make_tables(length)
+
     for number in range(tiles):
 
         @pl.when((tile == number) & (sequence == 0))
         def _(number=number):
             if number + 3 <= tiles:
                 begin_z(number + 3)
-            if number + 2 <= tiles:
+            if number < 2:
                 begin_y(number + 2)
             complete(number + 1)
             weight_out(number).start()
 
+    for number in range(2, tiles - 1):
+
+        @pl.when((tile == number - 1) & (sequence == 1))
+        def _(number=number):
+            begin_y(number + 2)
+
     @pl.when((tile == 0) & (sequence == 1))
     def _():
-        act_pass(0).wait_recv()
-        make_tables(length)
         act_x(1).wait_recv()
         act_pass(1).start()
         act_pass(1).wait_recv()
@@ -467,7 +524,7 @@
 
     forward_tile(
         sequence * length, tile * 8, normed_all, cot_all, w_all.at[tile], bc_all, wide_all, pick_ref, col_all,
-        row_all, score_all, par_ref, z_ref, dyn_ref, y_ref, state_ref, sum_ref, xs_ref, carry_ref,
+        row_all, score_all, par_ref, z_ref, dyn_ref, y_ref, state_ref, sum_ref, carry_ref,
     )
 
     @pl.when((tile == tiles - 1) & (sequence == 1))
@@ -483,6 +540,7 @@
             sum_ref[...] + jnp.concatenate([sum_recv[1, :, length:], sum_recv[1, :, :length]], axis=1),
             inner_total,
         )
+        small_core().wait_send()
         for a in range(2):
             act_core(a).wait_send()
             act_x(a).wait_send()
@@ -553,9 +611,8 @@
         dt_wide, cum_wide = wide[:, :TILE], wide[:, TILE:]
         dtx = x * dt_wide
         dtx_low, e_low = dtx.astype(BF16), e.astype(BF16)
-        reach = (down >= across).astype(BF16)
         d_scores = jnp.zeros((BLOCK, BLOCK), F32)
-        parts, between = [], []
+        parts, leaving, arriving = [], [], []
         for head in range(GROUP):
             lanes = slice(head * WIDTH, (head + 1) * WIDTH)
             gap = row_ref[head : head + 1, rows] - cum_wide[:, head * WIDTH : head * WIDTH + 1]
@@ -564,8 +621,9 @@
             parts.append(dot(mixing.astype(BF16), e_low[:, lanes]))
             d_mixing = dot(dtx_low[:, lanes], e_low[:, lanes], NT)
             d_scores = d_scores + d_mixing * decay
-            later = dot((d_mixing * mixing).astype(BF16), reach)
-            between.append(jnp.sum(jnp.where(down < across, later, 0.0), axis=0, keepdims=True))
+            pairs = d_mixing * mixing
+            leaving.append(jnp.sum(pairs, axis=1, keepdims=True))
+            arriving.append(jnp.sum(pairs, axis=0, keepdims=True))
         d_dtx = jnp.concatenate(parts, axis=1)
         mask = pair_mask(col[:, SEG : SEG + 1], seg_ref[:, rows], True)
         d_scores = jnp.where(mask, d_scores, 0.0).astype(BF16)
@@ -609,17 +667,20 @@
         def head_sum(a):
             return sum(dot(part, owner) for part in halves(a))
 
-        def token_sum(reached, a):
-            both = dot(reached, jnp.concatenate(halves(a), axis=1))
-            return both[:, :8] + both[:, 8:]
-
-        run = token_sum((down <= across).astype(BF16), head_sum(from_state))
-        run = run + token_sum((down > across).astype(BF16), head_sum(to_state))
-        run = run + head_sum(jnp.broadcast_to(through, (8, TILE)))[:1]
+        through = through + jnp.sum(from_state, axis=0, keepdims=True)
         sums = jnp.concatenate(
-            [run, head_sum(d_dtx * x), jnp.zeros((BLOCK, LANES - 16), F32)], axis=1
+            [head_sum(to_state - from_state), head_sum(d_dtx * x)]
+            + leaving
+            + [jnp.zeros((BLOCK, LANES - 16 - GROUP), F32)],
+            axis=1,
         ).T
-        run_rows = sums[:GROUP] + jnp.concatenate(between, axis=0)
+        change = sums[:GROUP] + sums[16 : 16 + GROUP] - jnp.concatenate(arriving, axis=0)
+        terms = jnp.concatenate(
+            thirds(change) + [jnp.zeros((16 - 3 * GROUP, BLOCK), BF16)], axis=0
+        )
+        before = dot(terms, (down < across).astype(BF16))
+        const = head_sum(jnp.broadcast_to(through, (8, TILE))).T[:GROUP, :1]
+        run_rows = before[:GROUP] + before[GROUP : 2 * GROUP] + before[2 * GROUP : 3 * GROUP] + const
         raw = row_ref[GROUP : 2 * GROUP, rows]
         d_dt = (sums[8 : 8 + GROUP] + rate_ref[:GROUP, :1] * run_rows) * sigmoid(raw)
         dt = jnp.maximum(raw, 0.0) + jnp.log1p(jnp.exp(-jnp.abs(raw)))
@@ -899,9 +960,9 @@
 
 
 def pick_table(tile):
-    row, lane = jnp.arange(LANES)[:, None], jnp.arange(2 * TILE)[None, :]
+    row, lane = np.arange(LANES)[:, None], np.arange(2 * TILE)[None, :]
     head = tile * GROUP + (lane % TILE) // WIDTH
-    return ((row % HEADS == head) & (row // (3 * HEADS) == lane // TILE)).astype(BF16)
+    return ((row % HEADS == head) & (row // (3 * HEADS) == lane // TILE)).astype(np.float32)
 
 
 def run_forward(pieces, normed, cot, bc, wide, col, rows, score, par, tile, length):
@@ -938,26 +999,26 @@
             shaped((number * blocks, LANES, TILE)),
             shaped((8, tokens)),
         ],
-        scratch_shapes=[pltpu.VMEM((length, TILE), F32), pltpu.VMEM((LANES, TILE), F32)],
+        scratch_shapes=[pltpu.VMEM((LANES, TILE), F32)],
         compiler_params=pltpu.CompilerParams(vmem_limit_bytes=VMEM_LIMIT),
         cost_estimate=cost(2e10),
-    )(*pieces, normed, cot, bc, wide, pick_table(tile), col, rows, score, par)
-
-
-def run_gather(normed, cot, own, other, small_own, small_other, ids, bc_par, head_par, pars, length, spans, inner_total):
+    )(*pieces, normed, cot, bc, wide, jnp.asarray(pick_table(tile), BF16), col, rows, score, par)
+
+
+def run_gather(normed, cot, own, other, small_own, ids, bc_par, head_par, pars, length, spans, inner_total):
     rows, width = normed.shape
     tiles, _, cols = own.shape
-    small_cols = small_own.shape[1]
+    small_cols = small_own.shape[1] + LANES
     tokens, blocks = 2 * length, length // BLOCK
 
     def by_tile(size, count):
-        return pl.BlockSpec((None, size, count), lambda j, i: (j, i, 0))
+        return pl.BlockSpec((None, size, count), lambda i: step_of(i) + (0,))
 
     def fixed(*shape):
-        return pl.BlockSpec((None,) + shape, lambda j, i: (j,) + (0,) * len(shape))
+        return pl.BlockSpec((None,) + shape, lambda i: (step_of(i)[0],) + (0,) * len(shape))
 
     def constant(*shape):
-        return pl.BlockSpec(shape, lambda j, i: (0,) * len(shape))
+        return pl.BlockSpec(shape, lambda i: (0,) * len(shape))
 
     dma = pltpu.SemaphoreType.DMA
     table_shapes = [
@@ -970,8 +1031,8 @@
     ]
     return pl.pallas_call(
         functools.partial(gather_kernel, tiles=tiles, spans=spans, inner_total=inner_total),
-        grid=(tiles, 2),
-        in_specs=[ANY] * 6
+        grid=(2 * tiles,),
+        in_specs=[ANY] * 5
         + [
             constant(tokens, 1),
             constant(1, tokens),
@@ -988,7 +1049,7 @@
             by_tile(length, 2 * TILE),
             by_tile(length, TILE),
             by_tile(length, TILE),
-            pl.BlockSpec((None, blocks, LANES, TILE), lambda j, i: (j, i, 0, 0)),
+            pl.BlockSpec((None, blocks, LANES, TILE), lambda i: step_of(i) + (0, 0)),
         ]
         + [ANY] * 6
         + [constant(8, tokens)],
@@ -1016,8 +1077,10 @@
             pltpu.VMEM((tokens, BLOCK), F32),
             pltpu.VMEM((8, tokens), F32),
             pltpu.VMEM((2, 8, tokens), F32),
-            pltpu.VMEM((length, TILE), F32),
             pltpu.VMEM((LANES, TILE), F32),
+            pltpu.VMEM((2, width // 2, 2 * LANES), BF16),
+            pltpu.VMEM((width, LANES), BF16),
+            pltpu.VMEM((width, LANES), BF16),
             dma((3 + tiles,)),
             dma((9 + tiles,)),
             dma((2, 3)),
@@ -1028,16 +1091,16 @@
             dma((1 + tiles, spans - 1)),
             dma((1 + tiles, spans)),
             dma((1 + tiles, spans)),
-            dma((2,)),
-            dma((2,)),
+            dma((3,)),
+            dma((3,)),
         ],
         compiler_params=pltpu.CompilerParams(
             vmem_limit_bytes=VMEM_LIMIT, collective_id=2, has_side_effects=True
         ),
         cost_estimate=cost(2e11),
     )(
-        normed, cot, own, other, small_own, small_other, ids[:, None], ids[None, :], bc_par, head_par,
-        jnp.stack([pick_table(tile) for tile in range(tiles)]), pars,
+        normed, cot, own, other, small_own, ids[:, None], ids[None, :], bc_par, head_par,
+        jnp.asarray(np.stack([pick_table(tile) for tile in range(tiles)]), BF16), pars,
     )
 
 
@@ -1149,7 +1212,7 @@
         compiler_params=pltpu.CompilerParams(**params),
         cost_estimate=cost(2e11),
     )(
-        *ties, normed, cot, zv, y, dyn, bc, wide, jnp.stack([pick_table(tile) for tile in range(tiles)]), col,
+        *ties, normed, cot, zv, y, dyn, bc, wide, jnp.asarray(np.stack([pick_table(tile) for tile in range(tiles)]), BF16), col,
         rows, ids[None, :], turned, norms, par, rate, state,
     )
 
@@ -1212,7 +1275,7 @@
             elif step == 2:
                 give_ref[:, lanes] = (total + recv[0, :, lanes].astype(F32)).astype(BF16)
             else:
-                own_ref[:, lanes] = total + recv[1, :, lanes].astype(F32)
+                own_ref[:, lanes] = (total + recv[1, :, lanes].astype(F32)).astype(BF16)
             return carried
 
         lax.fori_loop(0, 2 * spans, columns, 0)
@@ -1243,7 +1306,7 @@
             pl.BlockSpec((rows, width), lambda i: (0, 0)),
             pl.BlockSpec((rows, width), lambda i: (0, 0)),
         ],
-        out_shape=[shaped((rows, width)), shaped((rows, width), BF16)],
+        out_shape=[shaped((rows, width), BF16), shaped((rows, width), BF16)],
         scratch_shapes=[
             pltpu.VMEM((2, tiles, rows, TILE), F32),
             pltpu.VMEM((2, tiles, rows, TILE), F32),
@@ -1263,20 +1326,26 @@
 
 
 def tail_kernel(
-    hidden_ref, cot_ref, inv_ref, gain_ref, grads_hbm, weights_hbm, small_ref, dt_ref, far_hbm, near_ref,
+    hidden_hbm, cot_hbm, inv_ref, gain_ref, grads_hbm, weights_hbm, small_ref, dt_ref, far_hbm, near_hbm,
     z_own_ref, z_send_hbm, mine_ref, theirs_ref, dbc_ref, dbc_x_ref, proj_ref, col_ref, par_ref, normed_hbm,
-    smalls_ref, heads_ref, rate_ref, sums_ref,
-    grad_out, zx_ref, out_ref, steps_ref, bc_out_ref, pack_out_ref, last_ref,
-    grads_seq, wblk, acc_ref, give_ref, core_recv, own_ref, x_give, x_recv, y_recv, z_send, z_own, z_recv, w_send,
+    smalls_ref, heads_ref, rate_ref, usable_ref, mixer_own_hbm, mixer_x_hbm,
+    grad_out, residual_out, zx_ref, out_ref, steps_ref, bc_out_ref, pack_out_ref, last_ref,
+    grads_seq, wblk, acc_ref, give_ref, core_recv, own_ref, x_give, x_recv, y_recv, z_send, z_own, z_total, z_recv, w_send,
     w_recv, dbc_core, dbc_low, dt_cols, normed_blk, bc_grad, bc_xs, bc_own, bc_xr, bc_yr, bc_zr, bc_core,
-    pack_recv, last_recv,
-    seq_sem, blk_sem, out_sem, core_send, core_rsem, xs_sem, xr_sem, ys_sem, yr_sem, zs_sem, zr_sem, ws_sem, wr_sem,
+    pack_recv, last_recv, hidden_ref, cot_ref, near_ref,
+    load_sem, seq_sem, w_sem, blk_sem, out_sem, core_send, core_rsem, xs_sem, xr_sem, ys_sem, yr_sem, zs_sem, zr_sem, ws_sem, wr_sem,
     ds_sem, dr_sem, bs_sem, br_sem, ps_sem, pr_sem, ls_sem, lr_sem,
     *, spans, inside, extent,
 ):
-    tiles = grads_seq.shape[0]
-    length = grads_seq.shape[1]
+    tiles = weights_hbm.shape[0]
+    length = grads_seq.shape[0]
     rows, width = hidden_ref.shape
+    loads = [
+        pltpu.make_async_copy(src, dst, load_sem.at[at])
+        for at, (src, dst) in enumerate(
+            [(near_hbm.at[0], near_ref), (hidden_hbm, hidden_ref), (cot_hbm, cot_ref)]
+        )
+    ]
     part = 2 * LANES
     count = 2 * spans
     dp, mp = lax.axis_index("dp"), lax.axis_index("mp")
@@ -1298,20 +1367,38 @@
         return pl.ds(pair_start(number, dp, spans), part)
 
     def seq_fetch(sequence):
-        return pltpu.make_async_copy(
-            grads_hbm.at[:, pl.ds(sequence * length, length), pl.ds(0, 2 * TILE)], grads_seq, seq_sem.at[0]
-        )
+        return [
+            pltpu.make_async_copy(
+                grads_hbm.at[tile, pl.ds(sequence * length, length), pl.ds(0, 2 * TILE)],
+                grads_seq.at[:, pl.ds(tile * 2 * TILE, 2 * TILE)],
+                seq_sem.at[tile],
+            )
+            for tile in range(tiles)
+        ]
 
     def w_fetch(number, slot):
         at = pl.ds(pl.multiple_of(number * part, part), part)
-        return pltpu.make_async_copy(
-            weights_hbm.at[:, at, pl.ds(0, 2 * TILE)], wblk.at[slot], blk_sem.at[slot]
-        )
+        return [
+            pltpu.make_async_copy(
+                weights_hbm.at[tile, at, pl.ds(0, 2 * TILE)],
+                wblk.at[slot, :, pl.ds(tile * 2 * TILE, 2 * TILE)],
+                w_sem.at[slot, tile],
+            )
+            for tile in range(tiles)
+        ]
+
+    def begin(copies):
+        for copy in copies:
+            copy.start()
+
+    def end(copies):
+        for copy in copies:
+            copy.wait()
 
     def normed_fetch(number, slot):
         at = pl.ds(pl.multiple_of(number * part, part), part)
         return pltpu.make_async_copy(
-            normed_hbm.at[pl.ds(0, length), at], normed_blk.at[slot], blk_sem.at[2 + slot]
+            normed_hbm.at[pl.ds(0, length), at], normed_blk.at[slot], blk_sem.at[slot]
         )
 
     def core_copy(sequence, number):
@@ -1358,7 +1445,7 @@
             pack_copy(step + 1).start()
 
     def last_copy(step):
-        device = along(bits[step]) if step < len(bits) else other_core
+        device = along(bits[step - 1]) if step else other_core
         return remote(last_ref, last_recv.at[step], ls_sem.at[step], lr_sem.at[step], device)
 
     def emit(tile, share, owner):
@@ -1379,8 +1466,14 @@
         for k in range(1, spans):
             z_copy(number, k).wait()
             total = total + z_recv[number, k - 1].astype(F32)
-        z_own[...] = total
-        give_total(number, z_own)
+        z_total[...] = total
+        give_total(number, z_total)
+
+    def relay(number):
+        core_copy(1, number).wait()
+        lanes = lanes_of(number)
+        x_give[:, lanes] = (own_ref[:, lanes] + core_recv[1, :, lanes].astype(F32)).astype(BF16)
+        x_copy(number).start()
 
     def products(sequence):
         dt_rows = jnp.concatenate(
@@ -1390,45 +1483,60 @@
             ],
             axis=0,
         )
-        dt_rows = jnp.concatenate([dt_rows, jnp.zeros((LANES - tiles * GROUP, length), F32)], axis=0)
+        blank = jnp.zeros_like(dt_rows)
+        dt_rows = jnp.concatenate(
+            [
+                jnp.where(side == 0, dt_rows, blank),
+                jnp.where(side == 0, blank, dt_rows),
+                jnp.zeros((LANES - 2 * tiles * GROUP, length), F32),
+            ],
+            axis=0,
+        )
         dt_cols[...] = dt_rows.T.astype(BF16)
-        seq_fetch(sequence).wait()
+        end(seq_fetch(sequence))
 
         def one(number, carried):
             slot = lax.rem(number, 2)
 
             @pl.when(number + 1 < count)
             def _():
-                w_fetch(number + 1, 1 - slot).start()
-
-            w_fetch(number, slot).wait()
+                begin(w_fetch(number + 1, 1 - slot))
+
+            end(w_fetch(number, slot))
             at = pl.ds(pl.multiple_of(number * part, part), part)
-            total = dot(dt_cols[...], small_ref[at, 2 * LANES :], NT)
-            for tile in range(tiles):
-                total = total + dot(grads_seq[tile], wblk[slot, tile], NT)
-            acc_ref[...] = total
+            acc_ref[...] = dot(grads_seq[...], wblk[slot], NT) + dot(
+                dt_cols[...], small_ref[at, 2 * LANES :], NT
+            )
             lanes = lanes_of(number)
             away = pl.ds(pl.multiple_of((1 - mp) * rows, rows), rows)
             here = pl.ds(pl.multiple_of(mp * rows, rows), rows)
             give_ref[:, lanes] = acc_ref[away, :].astype(BF16)
             core_copy(sequence, number).start()
             own_ref[:, lanes] = acc_ref[here, :]
+            if sequence == 1:
+
+                @pl.when(number > 0)
+                def _():
+                    relay(number - 1)
+
             return carried
 
         lax.fori_loop(0, count, one, 0)
 
-    seq_fetch(1).start()
-    w_fetch(0, 0).start()
+    begin(seq_fetch(1))
+    begin(w_fetch(0, 0))
     barrier = pltpu.get_barrier_semaphore()
     partners = [along(1), along(2), other_core] + [along(4 * k) for k in range(1, spans)]
     for device in partners:
         pl.semaphore_signal(barrier, inc=1, device_id=device, device_id_type=pl.DeviceIdType.MESH)
     pl.semaphore_wait(barrier, len(partners))
-    for k in range(spans):
+    for k in range(spans - 1, -1, -1):
         y_copy(k).start()
-    for k in range(1, spans):
+    for k in range(spans - 1, 0, -1):
         z_copy(0, k).start()
     dbc_between.start()
+    for load in loads:
+        load.start()
     pack_out_ref[...] = jnp.zeros_like(pack_out_ref)
     head_row = jnp.zeros((1, LANES), F32)
     for tile in range(tiles):
@@ -1444,20 +1552,23 @@
     pack_out_ref[GAIN + 1 : GAIN + 2, :LANES] = head_row
     pack_copy(0).start()
     products(1)
-    seq_fetch(0).start()
-    w_fetch(0, 0).start()
+    begin(seq_fetch(0))
+    begin(w_fetch(0, 0))
+    relay(count - 1)
     pack_step(0)
 
-    def pass_on(number, carried):
-        core_copy(1, number).wait()
-        lanes = lanes_of(number)
-        x_give[:, lanes] = (own_ref[:, lanes] + core_recv[1, :, lanes].astype(F32)).astype(BF16)
-        x_copy(number).start()
-        return carried
-
-    lax.fori_loop(0, count, pass_on, 0)
-    products(0)
-    pack_step(1)
+    def y_pass(k):
+        y_copy(k).wait()
+        total = near_ref[k] + y_recv[k].astype(F32)
+        if k == 0:
+            z_own[...] = total
+        else:
+            z_send[k - 1] = total.astype(BF16)
+            z_copy(1, k).start()
+
+    loads[0].wait()
+    for k in range(spans - 1, spans // 2 - 1, -1):
+        y_pass(k)
     normed_fetch(0, 0).start()
     dbc_between.wait()
     conv = conv_of(proj_ref[...], col_ref[...], par_ref)
@@ -1474,37 +1585,36 @@
     small.append(jnp.sum(d_conv, axis=0, keepdims=True))
     conv_grads = jnp.concatenate(small + [jnp.zeros((3, part), F32)], axis=0)
     dbc_low[...] = d_proj.astype(BF16)
-    finish_z(0, z_own_ref)
+    half = pl.ds(pl.multiple_of(mp * LANES, LANES), LANES)
+    turned = dbc_low[:, half].T
+
+    def bc_product(number, carried):
+        slot = lax.rem(number, 2)
+
+        @pl.when(number + 1 < count)
+        def _():
+            normed_fetch(number + 1, 1 - slot).start()
+
+        normed_fetch(number, slot).wait()
+        bc_grad[...] = dot(turned, normed_blk[slot])
+        bc_own[number] = bc_grad[:, ours]
+        bc_xs[number] = bc_grad[:, others].astype(BF16)
+        return carried
+
+    lax.fori_loop(0, count, bc_product, 0)
+    bc_x.start()
+    products(0)
+    mixer_copies = [
+        pltpu.make_async_copy(mixer_own_hbm, grads_seq.at[pl.ds(0, rows), :], seq_sem.at[0]),
+        pltpu.make_async_copy(mixer_x_hbm, grads_seq.at[pl.ds(rows, rows), :], seq_sem.at[1]),
+    ]
+    begin(mixer_copies)
+    pack_step(1)
+    for k in range(spans // 2 - 1, -1, -1):
+        y_pass(k)
     for tile in range(inside - 1):
         emit(tile, mine_ref[tile], side)
         emit(tile, theirs_ref[tile], 1 - side)
-    for k in range(spans):
-        y_copy(k).wait()
-        total = near_ref[0, k] + y_recv[k].astype(F32)
-        if k == 0:
-            z_own[...] = total
-        else:
-            z_send[k - 1] = total.astype(BF16)
-            z_copy(1, k).start()
-    half = pl.ds(pl.multiple_of(mp * LANES, LANES), LANES)
-    turned = dbc_low[:, half].T
-
-    def bc_product(number, carried):
-        slot = lax.rem(number, 2)
-
-        @pl.when(number + 1 < count)
-        def _():
-            normed_fetch(number + 1, 1 - slot).start()
-
-        normed_fetch(number, slot).wait()
-        bc_grad[...] = dot(turned, normed_blk[slot])
-        bc_own[number] = bc_grad[:, ours]
-        bc_xs[number] = bc_grad[:, others]
-        return carried
-
-    lax.fori_loop(0, count, bc_product, 0)
-    bc_x.start()
-    pack_step(2)
     here = pl.ds(pl.multiple_of(mp * rows, rows), rows)
 
     def add_core(number, carried):
@@ -1517,17 +1627,31 @@
         return carried
 
     lax.fori_loop(0, count, add_core, 0)
-    pack_step(3)
-    for step in range(4, len(bits)):
-        pack_step(step)
-    bc_x.wait()
-    bc_own[...] += bc_xr[...]
-    bc_y.start()
-    finish_z(1, z_own)
-    bc_y.wait()
-    bc_own[:spans] += bc_yr[...]
-    for k in range(1, spans):
-        bc_z(k).start()
+    step_rows = 64
+    end(mixer_copies + loads[1:])
+
+    def residual(number, carried):
+        at = pl.ds(pl.multiple_of(number * step_rows, step_rows), step_rows)
+        away = pl.ds(pl.multiple_of(rows + number * step_rows, step_rows), step_rows)
+        u = hidden_ref[at, :].astype(F32)
+        mixer = grads_seq[at, :].astype(F32) + grads_seq[away, :].astype(F32)
+        slot = number // (part // step_rows)
+        place = lax.rem(number, part // step_rows) * step_rows
+        wblk[slot, pl.ds(pl.multiple_of(place, step_rows), step_rows), :] = (u + mixer).astype(BF16)
+        usable = usable_ref[at, :]
+        return (
+            carried[0] + jnp.sum(usable * (u * u), axis=0, keepdims=True),
+            carried[1] + jnp.sum(usable * (mixer * mixer), axis=0, keepdims=True),
+        )
+
+    zero_row = jnp.zeros((1, width), F32)
+    squares = lax.fori_loop(0, rows // step_rows, residual, (zero_row, zero_row))
+    residual_copies = [
+        pltpu.make_async_copy(wblk.at[slot], residual_out.at[pl.ds(slot * part, part), :], seq_sem.at[2 + slot])
+        for slot in range(2)
+    ]
+    begin(residual_copies)
+    finish_z(0, z_own_ref)
 
     def add_x(number, carried):
         x_copy(number).wait_recv()
@@ -1538,8 +1662,14 @@
     lax.fori_loop(0, count, add_x, 0)
     last_ref[...] = jnp.zeros_like(last_ref)
     last_ref[:, part : 2 * part] = 0.5 * conv_grads
-    last_ref[:, 2 * part : 2 * part + LANES] = sums_ref[...]
-    step_rows = 64
+    for at, total in enumerate(
+        [
+            jnp.sum(squares[0], axis=1, keepdims=True),
+            jnp.sum(squares[1], axis=1, keepdims=True),
+            jnp.sum(usable_ref[...], axis=0, keepdims=True),
+        ]
+    ):
+        last_ref[at : at + 1, 2 * part : 2 * part + LANES] = jnp.broadcast_to(total, (1, LANES))
 
     def finish(number, gain_sum):
         at = pl.ds(pl.multiple_of(number * step_rows, step_rows), step_rows)
@@ -1555,17 +1685,34 @@
     out.start()
     for number in range(8):
         last_ref[number : number + 1, :part] = gain_sum[:, number * part : (number + 1) * part]
-    for step in range(len(bits) + 1):
-        last_copy(step).start()
-        if step == 1:
-            total = bc_own[0]
-            for k in range(1, spans):
-                bc_z(k).wait()
-                total = total + bc_zr[k - 1]
-            bc_own[0] = total
-            bc_between.start()
+
+    def last_step(step):
         last_copy(step).wait()
         last_ref[...] += last_recv[step]
+        if step < len(bits):
+            last_copy(step + 1).start()
+
+    last_copy(0).start()
+    bc_x.wait()
+    bc_own[...] += bc_xr[...].astype(F32)
+    bc_y.start()
+    last_step(0)
+    last_step(1)
+    bc_y.wait()
+    bc_own[:spans] += bc_yr[...]
+    for k in range(1, spans):
+        bc_z(k).start()
+    last_step(2)
+    finish_z(1, z_own)
+    for step in range(2, len(bits)):
+        pack_step(step)
+        last_step(step + 1)
+    total = bc_own[0]
+    for k in range(1, spans):
+        bc_z(k).wait()
+        total = total + bc_zr[k - 1]
+    bc_own[0] = total
+    bc_between.start()
     bc_between.wait()
     first = jnp.where(mp == 0, 1.0, 0.0)
     bc_out_ref[:LANES, :] = first * bc_own[0] + (1.0 - first) * bc_core[...]
@@ -1577,11 +1724,12 @@
         core_copy(0, number).wait_send()
         x_copy(number).wait_send()
     out.wait()
+    end(residual_copies)
 
 
 def run_tail(
     hidden, cot, inv, gain, grads, weights, small, dts, far_share, near_share, z_own, z_send, mine, theirs, dbc,
-    dbc_x, proj, col, bc_par, normed, smalls, heads, rate, sums, length, spans, extent,
+    dbc_x, proj, col, bc_par, normed, smalls, heads, rate, usable, mixer_own, mixer_x, length, spans, extent,
 ):
     rows, width = hidden.shape
     tiles, tokens = grads.shape[:2]
@@ -1597,8 +1745,8 @@
         functools.partial(tail_kernel, spans=spans, inside=inside, extent=extent),
         grid=(1,),
         in_specs=[
-            full(rows, width),
-            full(rows, width),
+            ANY,
+            ANY,
             full(rows, 1),
             full(1, width),
             ANY,
@@ -1606,7 +1754,7 @@
             full(*small.shape),
             full(*dts.shape),
             ANY,
-            full(*near_share.shape),
+            ANY,
             full(*z_own.shape),
             ANY,
             full(*mine.shape),
@@ -1620,9 +1768,12 @@
             full(*smalls.shape),
             full(*heads.shape),
             full(*rate.shape),
-            full(8, LANES),
+            full(rows, 1),
+            ANY,
+            ANY,
         ],
         out_specs=[
+            ANY,
             ANY,
             full(LANES, 2 * channels),
             full(channels, LANES),
@@ -1633,6 +1784,7 @@
         ],
         out_shape=[
             shaped((rows, width)),
+            shaped((rows, width), BF16),
             shaped((LANES, 2 * channels)),
             shaped((channels, LANES)),
             shaped((tiles, 2, 8, LANES)),
@@ -1641,8 +1793,8 @@
             shaped((8, 3 * part)),
         ],
         scratch_shapes=[
-            pltpu.VMEM((tiles, length, 2 * TILE), BF16),
-            pltpu.VMEM((2, tiles, part, 2 * TILE), BF16),
+            pltpu.VMEM((length, tiles * 2 * TILE), BF16),
+            pltpu.VMEM((2, part, tiles * 2 * TILE), BF16),
             pltpu.VMEM((length, part), F32),
             pltpu.VMEM((rows, width), BF16),
             pltpu.VMEM((2, rows, width), BF16),
@@ -1652,6 +1804,7 @@
             pltpu.VMEM((spans, SHARE, part), BF16),
             pltpu.VMEM((spans - 1, SHARE, part), BF16),
             pltpu.VMEM((SHARE, part), F32),
+            pltpu.VMEM((SHARE, part), F32),
             pltpu.VMEM((2, spans - 1, SHARE, part), BF16),
             pltpu.VMEM((2, SHARE, LANES), BF16),
             pltpu.VMEM((2, SHARE, LANES), BF16),
@@ -1660,16 +1813,21 @@
             pltpu.VMEM((length, LANES), BF16),
             pltpu.VMEM((2, length, part), BF16),
             pltpu.VMEM((LANES, part), F32),
+            pltpu.VMEM((2 * spans, LANES, LANES), BF16),
             pltpu.VMEM((2 * spans, LANES, LANES), F32),
-            pltpu.VMEM((2 * spans, LANES, LANES), F32),
-            pltpu.VMEM((2 * spans, LANES, LANES), F32),
+            pltpu.VMEM((2 * spans, LANES, LANES), BF16),
             pltpu.VMEM((spans, LANES, LANES), F32),
             pltpu.VMEM((spans - 1, LANES, LANES), F32),
             pltpu.VMEM((LANES, LANES), F32),
             pltpu.VMEM((hops, 8, channels), F32),
             pltpu.VMEM((hops + 1, 8, 3 * part), F32),
-            dma((1,)),
-            dma((4,)),
+            pltpu.VMEM((rows, width), BF16),
+            pltpu.VMEM((rows, width), BF16),
+            pltpu.VMEM((spans, SHARE, part), F32),
+            dma((3,)),
+            dma((tiles,)),
+            dma((2, tiles)),
+            dma((2,)),
             dma((1,)),
             dma((2, 2 * spans)),
             dma((2, 2 * spans)),
@@ -1696,7 +1854,7 @@
         cost_estimate=cost(1e11),
     )(
         hidden, cot, inv, gain, grads, weights, small, dts, far_share, near_share, z_own, z_send, mine, theirs, dbc,
-        dbc_x, proj, col, bc_par, normed, smalls, heads, rate, sums,
+        dbc_x, proj, col, bc_par, normed, smalls, heads, rate, usable, mixer_own, mixer_x,
     )
 
 
@@ -1762,14 +1920,14 @@
         size = a.shape[axis] // 2
         return lax.dynamic_slice_in_dim(a, side * size, size, axis)
 
+    def of_core(a):
+        return lax.dynamic_slice_in_dim(a, mp * LANES, LANES, 1)
+
     packed = jnp.concatenate([w_zx[:, 0], w_zx[:, 1], w_out.T], axis=1)
     packed = packed.reshape(depth, 3, 2, tiles, TILE).transpose(2, 3, 0, 1, 4)
     packed = packed.reshape(2, tiles, depth, 3 * TILE)
 
-    def small_weights(side):
-        filler = jnp.zeros((depth, LANES - own_heads), BF16)
-        return jnp.concatenate([w_bc, of_side(w_dt, side, 1), filler], axis=1)
-
+    filler = jnp.zeros((depth, LANES - heads), BF16)
     packed_own = lax.dynamic_index_in_dim(packed, x_side, 0, False)
     packed_other = lax.dynamic_index_in_dim(packed, 1 - x_side, 0, False)
 
@@ -1784,7 +1942,8 @@
     side_bias = of_side(dt_bias, x_side, 0)
     rate = -jnp.exp(of_side(a_log, x_side, 0))
     bc_par = jnp.concatenate([conv_bc, conv_bc_bias[None], jnp.zeros((3, 2 * LANES), F32)], axis=0)
-    head_par = jnp.pad(jnp.stack([side_bias, rate]), ((0, 6), (0, LANES - own_heads)))
+    head_par = jnp.stack([side_bias, rate, jnp.full_like(rate, x_side)])
+    head_par = jnp.pad(head_par, ((0, 5), (0, LANES - own_heads)))
     params = jnp.concatenate(
         [
             of_side(conv_x, x_side, 1),
@@ -1801,8 +1960,8 @@
         (
             normed_all, cot_all, weights, bc_weight, zvs, dyns, ys, states, proj_bc, bc, wide, col, rows_all, turned, norms,
         ) = run_gather(
-            normed, cot, packed_own, packed_other, small_weights(x_side), small_weights(1 - x_side), ids_all,
-            bc_par, head_par, params, length, far, inner_total,
+            normed, cot, packed_own, packed_other, jnp.concatenate([of_core(w_bc), w_dt, filler], axis=1),
+            ids_all, bc_par, head_par, params, length, far, inner_total,
         )
     else:
 
@@ -1814,8 +1973,10 @@
 
         normed_all, cot_all = both_sequences(normed), both_sequences(cot)
         packed_other = flip(packed_other, "dp", 1)
-        small_other = flip(small_weights(1 - x_side), "dp", 1)
-        bc_weight = jnp.concatenate(gathered(by_side(small_weights(x_side), small_other, 0)), axis=0)
+        small_weights = jnp.concatenate([w_bc, w_dt, filler], axis=1)
+        bc_weight = jnp.concatenate(
+            gathered(by_side(small_weights, flip(small_weights, "dp", 1), 0)), axis=0
+        )
         proj_bc, bc, wide, col, rows_all, score, turned = run_tables(
             normed_all, bc_weight, ids_all, bc_par, head_par, length
         )
@@ -1842,7 +2003,7 @@
     if native:
         mixer_own, mixer_give = run_mixer(zvs, ys, norm_cols, params, weights, rows, length, far)
         ties = [mixer_own]
-        mixer_out = mixer_own + flip(mixer_give, "dp", 1).astype(F32)
+        mixer_x = flip(mixer_give, "dp", 1)
 
     rate_rows = jnp.pad(rate.reshape(tiles, GROUP, 1), ((0, 0), (0, 8 - GROUP), (0, 0)))
     rate_rows = jnp.broadcast_to(rate_rows, (tiles, 8, LANES))
@@ -1875,11 +2036,10 @@
         )
 
     if native:
-        sums = jnp.pad(mixer_sums(mixer_out)[None], ((0, 7), (0, LANES - 3)))
-        input_grad, grad_zx, grad_out_weight, grad_steps, grad_bc, pack, last = run_tail(
+        input_grad, residual_out, grad_zx, grad_out_weight, grad_steps, grad_bc, pack, last = run_tail(
             hidden_in, cotangent, inverse_rows, norm_gain[None], grads, weights, bc_weight, dts, far_share,
             near_share, z_own, z_send, mine, theirs, dbc, dbc_x, proj_bc, col, bc_par, normed_all, smalls,
-            head_sums, rate_rows, sums, length, far, extent,
+            head_sums, rate_rows, usable, mixer_own, mixer_x, length, far, extent,
         )
         grad_zx_weight = grad_zx.reshape(depth, 2, inner)
         grad_dt_weight = grad_steps[:, :, :GROUP].transpose(1, 0, 2, 3).reshape(heads, depth).T
@@ -1887,7 +2047,7 @@
         part = 2 * LANES
         grad_norm_gain = last[:, :part].reshape(width)
         grad_conv_bc, grad_conv_bc_bias = last[:4, part : 2 * part], last[4, part : 2 * part]
-        totals = last[0, 2 * part : 2 * part + 3]
+        totals = last[:3, 2 * part]
     else:
 
         def spread_sum(far_part, near_part):
@@ -1939,7 +2099,7 @@
         yn_all = jnp.concatenate([g[:, 2 * TILE :] for g in grads], axis=1)
         mixer_out = restore_order(token_sum(lambda pick: dot(pick(yn_all), out_all, NT)), dp, extent)
         zv_all = jnp.concatenate([w[:, : 2 * TILE] for w in weights], axis=1)
-        dt_weight = bc_weight[:, 2 * LANES : 2 * LANES + own_heads]
+        dt_weight = of_side(bc_weight[:, 2 * LANES : 2 * LANES + heads], x_side, 1)
         dzx_all = jnp.concatenate([g[:, : 2 * TILE] for g in grads], axis=1)
         dt_grad = dts.reshape(tiles, 16, tokens)[:, :GROUP].reshape(own_heads, tokens).T
         d_normed = token_sum(
@@ -1980,8 +2140,8 @@
         grad_zx_weight = jnp.stack([assembled(0, TILE).T, assembled(TILE, STEPS).T], axis=1)
         grad_dt_weight = assembled(STEPS, STEPS + GROUP).T
         grad_out_weight = assembled(OUT, SHARE)
-
-    residual_out = (inputs + mixer_out).astype(BF16)
+        residual_out = (inputs + mixer_out).astype(BF16)
+
     skip_grad = jnp.sum(pack[SKIP].reshape(heads, WIDTH), axis=1)
     sum_inputs, sum_mixer, usable_count = totals[0], totals[1], totals[2]
     rms_residual = jnp.sqrt(sum_inputs / (usable_count * width))

time: 584 us -> 525 us (0.90)
  Pallas kernels: 519 us -> 470 us
  other arithmetic: 16.3 us -> 4.34 us
    pallas_call x1, Pallas kernels: 218 us -> 195 us  [run_gather(): pl.pallas_call(functools.partial(gather_kernel, tiles=tiles, spans=spans,...]
    pallas_call x1, Pallas kernels: 110 us -> 88.9 us  [run_tail(): pl.pallas_call(functools.partial(tail_kernel, spans=spans, inside=inside,...]
    reduce_sum x2 -> x0, other arithmetic: 8.28 us -> none  [the longest x1 6.34 us: mixer_sums(): jnp.sum(usable * inputs * inputs)]
  transfers between devices with their start and end apart: 2 -> 2, of which waited for: 0 -> 0; matrix products, arithmetic and copies ran while one was open for 3% -> 3% of each run, Pallas kernels for 28% -> 31%
where the time goes in v6:
time: 525 us; the launch traced here: 521 us
  Pallas kernels  470 us (90%)
  local copies, waits for them, and re-layouts  36.9 us (7%)
  between operations  5.64 us (1%)
    pallas_call x1, Pallas kernels, run_gather(): pl.pallas_call(functools.partial(gather_kernel, tiles=tiles, spans=spans,...  195 us
    pallas_call x1, Pallas kernels, run_backward(): pl.pallas_call(functools.partial(backward_kernel, ties=len(ties), inside=...  156 us
    pallas_call x1, Pallas kernels, run_tail(): pl.pallas_call(functools.partial(tail_kernel, spans=spans, inside=inside,...  88.9 us
    pallas_call x1, Pallas kernels, run_mixer(): pl.pallas_call(functools.partial(mixer_kernel, spans=spans, length=length...  24.7 us
  transfers between devices with their start and end apart: 2, of which 0 were waited for; matrix products, arithmetic and copies ran while one was open for 3% of the time, Pallas kernels for 31%

profile of v6, /device:TPU:0, one launch (start us, length us, event | category | flops | bytes accessed | tf_op | source)
XLA Modules:
  0.0 521.1 jit_solution(507451471005860696)
XLA Ops:
  0.7 3.0 collective-permute-start
  3.7 0.7 fusion.4
  4.4 0.7 exponential_negate_fusion
  5.1 3.4 fusion.1
  8.6 0.9 copy.76
  9.5 0.9 copy.75
  13.1 0.7 maximum_maximum_fusion.1.bc_par_ref.par_ref
  13.9 1.2 copy.67
  15.1 1.2 copy.68
  17.0 0.9 copy.72.usable_ref
  17.9 5.2 shard_map.305
  23.8 1.3 copy.70.seg_col_ref
  25.7 194.8 %shard_map.306 = (bf16[2048,2048]{1,0:T(8,128)(2,1)}, bf16[2048,2048]{1,0:T(8,128)(2,1)}, bf16[4,2048,768]{2,1,0:T(8,128)(2,1)}, bf16[2048,384]{1,0:T(8,128)(2,1...) custom-call(bf16[512,2048]{1,0:T(8,128)(2,1)} %get-tuple-element.58., ...), custom_call_target="tpu_custom_call" | custom-call | flops 199999995904 | bytes 10000000 | tf_op jit(solution)/shard_map/pallas_call | solution.py:1032
  220.5 2.1 copy.71
  222.7 24.7 %shard_map.307 = (bf16[512,2048]{1,0:T(8,128)(2,1)}, bf16[512,2048]{1,0:T(8,128)(2,1)}) custom-call(f32[4,2048,512]{2,1,0:T(8,128)} %get-tuple-element.60.z_hbm.refs_3_, f32[4,2048,256]{2,1,0:T(8,128)} %get-tuple-element.61.y_hbm.refs_4_, f32[2048,8]{1,0:T(8,128)} %bitcast.50, f32[4,8,256]{2,1,0:T(8,128)} %bitcast.59, ...), custom_call_target="tpu_custom_call" | custom-call | flops 10000000000 | bytes 10000000 | tf_op jit(solution)/shard_map/pallas_call | solution.py:1295
  247.4 1.5 collective-permute-start.1
  248.9 0.7 broadcast_in_dim.40.refs_15_.rate_ref
  249.6 156.2 %shard_map.308 = (bf16[4,2048,768]{2,1,0:T(8,128)(2,1)}, f32[2048,256]{1,0:T(8,128)}, bf16[64,2048]{1,0:T(8,128)(2,1)}, f32[4,2,8,128]{3,2,1,0:T(8,128)}, f32[4,...) custom-call(bf16[512,2048]{1,0:T(8,128)(2,1)} %get-tuple-element.64., ...), custom_call_target="tpu_custom_call" | custom-call | flops 199999995904 | bytes 10000000 | tf_op jit(solution)/shard_map/pallas_call | solution.py:1135
  405.8 88.9 %shard_map.309 = (f32[512,2048]{1,0:T(8,128)}, bf16[512,2048]{1,0:T(8,128)(2,1)}, f32[128,4096]{1,0:T(8,128)}, f32[2048,128]{1,0:T(8,128)}, f32[4,2,8,128]{3,2,1...) custom-call(bf16[512,2048]{1,0:T(8,128)(2,1)} %hidden_hbm.1, bf16[512,2048]{1,0:T(8,128)(2,1)} %cot_hbm.1, ...), custom_call_target="tpu_custom_call" | custom-call | flops 99999997952 | bytes 10000000 | tf_op jit(solution)/shard_map/pallas_call | solution.py:1744
  494.7 1.5 slice.56
  496.1 1.6 fusion.2
  497.7 0.7 slice_bitcast_fusion.1
  498.4 1.3 slice.58
  499.7 1.3 slice.59
  500.9 1.3 slice_bitcast_fusion.2
  502.3 1.3 fusion.3
  504.2 4.1 reshape.149
  509.0 0.8 copy.74
  512.5 1.3 copy.81
  513.8 1.6 copy-done.2
  515.4 2.0 copy.82
  517.4 1.0 copy.83
  (67 shorter events, 6.8 us)
Async XLA Ops:
  0.7 11.6 %copy-start = (bf16[128,256]{1,0:T(8,128)(2,1)S(1)}, bf16[128,256]{1,0:T(8,128)(2,1)}, u32[]{:S(2)}) copy-start(bf16[128,256]{1,0:T(8,128)(2,1)} %param.23) | copy-start | bytes 196612
  0.7 23.1 %collective-permute-start = (s32[1024]{0:T(1024)}, s32[1024]{0:T(1024)S(1)}, u32[]{:S(2)}, u32[]{:S(2)}) collective-permute-start(s32[1024]{0:T(1024)} %param.19), channel_id=1, source_target_pairs={{0,2},{2,0},{4,6},{6,4},{8,10},{10,8},{12,14},{14,12},{16,18},{18,... | collective-permute-start | bytes 12296 | tf_op jit(solution)/shard_map/ppermute | solution.py:37
  8.6 1.7 copy-start.5
  10.5 0.7 copy-start.8
  10.5 0.8 copy-start.15
  10.6 1.8 copy-start.10
  10.7 2.4 copy-start.12
  10.7 2.4 copy-start.13
  10.7 3.1 copy-start.7
  12.5 4.4 copy-start.14
  17.9 5.2 dynamic-slice-start
  17.9 5.2 dynamic-slice-start.1
  222.7 26.2 %copy-start.9 = (f32[4,8]{1,0:T(4,128)S(1)}, f32[4,8]{1,0:T(4,128)}, u32[]{:S(2)}) copy-start(f32[4,8]{1,0:T(4,128)} %pad_bitcast_fusion) | copy-start | bytes 388
  247.4 158.4 %collective-permute-start.1 = (bf16[512,2048]{1,0:T(8,128)(2,1)}, bf16[512,2048]{1,0:T(8,128)(2,1)}, u32[]{:S(2)}, u32[]{:S(2)}) collective-permute-start(bf16[512,2048]{1,0:T(8,128)(2,1)} %get-tuple-element.88), channel_id=1, source_target_pairs={{0,2},{2,0},{4,6},{6,4},{8,10},{10,8},{12,14},{14,12},{16,18},{18,... | collective-permute-start | bytes 6291464 | tf_op jit(solution)/shard_map/ppermute | solution.py:37
  504.2 4.1 copy-start.11
  504.2 4.8 copy-start.6
  504.2 8.3 %copy-start.3 = (bf16[512,2048]{1,0:T(8,128)(2,1)S(1)}, bf16[512,2048]{1,0:T(8,128)(2,1)}, u32[]{:S(2)}) copy-start(bf16[512,2048]{1,0:T(8,128)(2,1)} %get-tuple-element.194) | copy-start | bytes 6291460
  512.5 2.9 copy-start.2
  515.4 2.0 copy-start.4
  515.4 3.0 copy-start.1
